TPU v7x, 32 devices: a whole 2x2x4 slice. The times are simulated.
32 devices in a mesh: slab: 8 (over z, y), pair: 4 (over x, core).
Axes of the slice: x: 2, y: 2, z: 4, core: 2. Of those that a mesh axis runs over, the one named last changes fastest.
Arguments:
- orbitals: bfloat16 [128, 32768], P('pair', 'slab'), may hold values from -6 to 6
- centers: int32 [128, 3], replicated, may hold values from 0 to 16
- matchings: int32 [8, 4, 16], P('slab'), may hold values from 0 to 15, as said below
Outputs:
- exchange_force: float32 [128, 32768], P('pair', 'slab')
Inputs may be any that keep to these rules, and one draw needn't show every extreme that they name: `centers`: box corners relative to a common reference cell. `matchings`: entry [s, r, t] is the partner of member t of team s in round r; in each round every member has exactly one partner other than itself, and the partner's partner is the member.
All inputs are finite; a program needn't handle non-finite values.
Results may differ from a plain program's by a relative error of at most 0.0003.
Values may be sent and summed in bfloat16 or wider, within the bound.
No kernel may reach another device: no remote copies, remote signals or barrier semaphores. Data moves between devices by JAX's collectives and lax.ppermute only.
A program may use at most 128 MiB of HBM per device.

v0:
```python
import jax
import jax.numpy as jnp
from jax import lax
from jax.sharding import PartitionSpec as P

BOX = 32
STEPS = 16
CUT2 = 192


SCREEN = 0.1
LOWER_BOUND = 0.1
UPPER_BOUND = 12.1


def cell_coords(box_side):
    cell_index = jnp.arange(box_side * box_side * box_side, dtype=jnp.int32)
    return (
        cell_index // (box_side * box_side),
        cell_index // box_side % box_side,
        cell_index % box_side,
    )


def shift_table(offset_part, box_side):
    target = jnp.arange(box_side, dtype=jnp.int32)
    source = target[None, :, None] - offset_part[:, None, None]
    return (source == target[None, None, :]).astype(jnp.float32)


def shift_rows(field, offset, box_side):
    row_count = field.shape[0]
    grid = field.astype(jnp.float32).reshape(row_count, box_side, box_side, box_side)
    best = lax.Precision.HIGHEST
    grid = jnp.einsum("rix,rxyz->riyz", shift_table(offset[:, 0], box_side), grid, precision=best)
    grid = jnp.einsum("riy,rxyz->rxiz", shift_table(offset[:, 1], box_side), grid, precision=best)
    grid = jnp.einsum("riz,rxyz->rxyi", shift_table(offset[:, 2], box_side), grid, precision=best)
    return grid.reshape(row_count, box_side * box_side * box_side)


def boundary_masks(box_side):
    plane_index, line_index, point_index = cell_coords(box_side)
    return jnp.stack(
        [line_index > 0, line_index < box_side - 1, point_index > 0, point_index < box_side - 1]
    ).astype(jnp.float32)


def apply_operator(field, box_side, masks):
    face_cells = box_side * box_side
    cell_count = field.shape[1]
    padded = jnp.pad(field, ((0, 0), (face_cells, face_cells)))

    def window(offset_cells):
        return padded[:, face_cells + offset_cells : face_cells + offset_cells + cell_count]

    neighbours = window(-face_cells) + window(face_cells)
    neighbours = neighbours + masks[0] * window(-box_side) + masks[1] * window(box_side)
    neighbours = neighbours + masks[2] * window(-1) + masks[3] * window(1)
    return (6.0 + SCREEN) * field - neighbours


def chebyshev_solve(source, box_side, sweeps):
    masks = boundary_masks(box_side)
    middle = (UPPER_BOUND + LOWER_BOUND) / 2.0
    spread = (UPPER_BOUND - LOWER_BOUND) / 2.0
    ratio = middle / spread

    def sweep(step, carry):
        solution, residual, direction, factor = carry
        solution = solution + direction
        residual = residual - apply_operator(direction, box_side, masks)
        factor_next = 1.0 / (2.0 * ratio - factor)
        direction = factor_next * factor * direction + 2.0 * factor_next / spread * residual
        return (solution, residual, direction, factor_next)

    start = (
        jnp.zeros_like(source),
        source,
        source / middle,
        jnp.asarray(1.0 / ratio, source.dtype),
    )
    return lax.fori_loop(0, sweeps, sweep, start)[0]


def pair_geometry(own_centers, partner_centers, cut_squared):
    anchor = (own_centers + partner_centers) // 2
    difference = own_centers - partner_centers
    active = (jnp.sum(difference * difference, axis=1) <= cut_squared).astype(jnp.float32)
    return (own_centers - anchor, partner_centers - anchor, active)


def pair_potential(own_rows, partner_rows, own_offset, partner_offset, active, box_side, sweeps):
    own_field = shift_rows(own_rows, own_offset, box_side)
    partner_field = shift_rows(partner_rows, partner_offset, box_side)
    density = active[:, None] * own_field * partner_field
    return (chebyshev_solve(density, box_side, sweeps), own_field, partner_field)


def shards(orbitals, centers, matchings):
    slab_count = lax.axis_size("slab")
    pair_count = lax.axis_size("pair")
    slab_index = lax.axis_index("slab")
    pair_index = lax.axis_index("pair")
    local_rows, plane_cells = orbitals.shape
    own_count = local_rows // slab_count
    match = matchings[0]
    rounds, team_size = match.shape
    member_iota = jnp.arange(team_size, dtype=jnp.int32)
    team_centers = lax.dynamic_index_in_dim(
        centers.reshape(pair_count, slab_count, own_count, 3), slab_index, 1, keepdims=False
    ).reshape(team_size, 3)
    half_count = own_count // 2
    lower = match > member_iota[None, :]
    position = jnp.cumsum(lower.astype(jnp.int32), axis=1) - 1
    slot_index = pair_index * half_count + jnp.arange(half_count, dtype=jnp.int32)
    picked = lower[:, None, :] & (position[:, None, :] == slot_index[None, :, None])
    low_index = jnp.sum(jnp.where(picked, member_iota[None, None, :], 0), axis=2)
    high_index = jnp.sum(jnp.where(picked, match[:, None, :], 0), axis=2)
    wanted = jnp.concatenate([low_index.reshape(-1), high_index.reshape(-1)])
    boxes = lax.all_to_all(orbitals, "slab", split_axis=0, concat_axis=1, tiled=True)
    empty_rows = jnp.zeros((wanted.shape[0], boxes.shape[1]), boxes.dtype)
    piece = lax.all_gather(boxes, "pair", axis=0, tiled=True)
    inside_piece = (wanted >= 0) & (wanted < piece.shape[0])
    chosen = piece[jnp.clip(wanted, 0, piece.shape[0] - 1)]
    rows = jnp.where(inside_piece[:, None], chosen, empty_rows)
    high_start = rounds * half_count
    term_list = []
    member_list = []
    for round_index in range(rounds):
        begin = round_index * half_count
        low_rows = rows[begin : begin + half_count]
        high_rows = rows[high_start + begin : high_start + begin + half_count]
        low_members = low_index[round_index]
        high_members = high_index[round_index]
        low_offset, high_offset, active = pair_geometry(
            team_centers[low_members], team_centers[high_members], CUT2
        )
        potential, low_field, high_field = pair_potential(
            low_rows, high_rows, low_offset, high_offset, active, BOX, STEPS
        )
        term_list.append(shift_rows(potential * high_field, -low_offset, BOX))
        term_list.append(shift_rows(potential * low_field, -high_offset, BOX))
        member_list.append(low_members)
        member_list.append(high_members)
    stacked_terms = jnp.concatenate(term_list, axis=0)
    stacked_members = jnp.concatenate(member_list, axis=0)
    buffer = (
        jnp.zeros((team_size, rows.shape[1]), jnp.float32).at[stacked_members].add(stacked_terms)
    )
    force = lax.psum_scatter(buffer, "pair", scatter_dimension=0, tiled=True)
    return lax.all_to_all(force, "slab", split_axis=1, concat_axis=0, tiled=True)


def solution(mesh):
    in_specs = (P("pair", "slab"), P(), P("slab", None, None))
    out_specs = P("pair", "slab")
    return jax.shard_map(shards, mesh=mesh, in_specs=in_specs, out_specs=out_specs, check_vma=False)
```

profile of v0, /device:TPU:0, one launch (start us, length us, event | category | flops | bytes accessed | tf_op | source)
XLA Modules:
  0.0 361.3 jit_solution(15478612166352143774)
XLA Ops:
  6.5 1.8 all_to_all.28
  8.3 7.3 %all-to-all-start = ((bf16[8,4,4096]{2,1,0:T(4,128)(2,1)}), bf16[8,4,4096]{2,1,0:T(4,128)(2,1)S(1)}, u32[]{:S(2)}, u32[]{:S(2)}) async-start(bf16[8,4,4096]{2,1,0:T(4,128)(2,1)} %all_to_all.28), calls=%async_computation | async-start | bytes 524288 | tf_op jit(solution)/shard_map/all_to_all | solution.py:120
  57.9 15.3 %all-gather.3.cloned.1.call-done = bf16[4,4,32768]{2,1,0:T(4,128)(2,1)} async-done(((bf16[1,4,32768]{2,1,0:T(4,128)(2,1)}), bf16[4,4,32768]{2,1,0:T(4,128)(2,1)}) %all-gather.3.cloned.1.call-update) | async-done | bytes 1048592 | tf_op jit(solution)/shard_map/all_gather | solution.py:122
  74.6 2.2 gather_fusion.2
  78.2 1.6 fusion.234
  80.3 1.4 convolution_bitcast_fusion.14
  83.9 1.4 convolution_bitcast_fusion.15
  87.2 29.1 %while.76 = (s32[]{:T(128)}, f32[2,32768]{1,0:T(2,128)S(1)}, f32[2,32768]{1,0:T(2,128)S(1)}, f32[2,32768]{1,0:T(2,128)S(1)}, f32[]{:T(128)}, /*index=5*/f32[4,32...) while((s32[]{:T(128)}, f32[2,32768]{1,0:T(2,128)S(1)}, ...), condition=%wide.region_5.6_spmd.clone, body=%wide.region_4.5_spmd.clone.sunk | while | flops 1114119 | bytes 3670207 | solution.py:82
  117.1 1.9 fusion.28
  119.1 1.4 convolution_bitcast_fusion.13
  128.3 1.4 convolution_bitcast_fusion.10
  132.2 1.4 convolution_bitcast_fusion.11
  135.5 29.4 %while.77 = (s32[]{:T(128)}, f32[2,32768]{1,0:T(2,128)S(1)}, f32[2,32768]{1,0:T(2,128)S(1)}, f32[2,32768]{1,0:T(2,128)S(1)}, f32[]{:T(128)}, /*index=5*/f32[4,32...) while((s32[]{:T(128)}, f32[2,32768]{1,0:T(2,128)S(1)}, ...), condition=%wide.region_8.9_spmd.clone, body=%wide.region_7.8_spmd.clone.sunk | while | flops 1114119 | bytes 3670207 | solution.py:82
  165.7 1.9 fusion.20
  172.5 1.4 convolution_bitcast_fusion.8
  176.8 1.4 convolution_bitcast_fusion.6
  184.0 29.0 %while.78 = (s32[]{:T(128)}, f32[2,32768]{1,0:T(2,128)S(1)}, f32[2,32768]{1,0:T(2,128)S(1)}, f32[2,32768]{1,0:T(2,128)S(1)}, f32[]{:T(128)}, /*index=5*/f32[4,32...) while((s32[]{:T(128)}, f32[2,32768]{1,0:T(2,128)S(1)}, ...), condition=%wide.region_11.12_spmd.clone, body=%wide.region_10.11_spmd.clone.sunk | while | flops 1114119 | bytes 3670207 | solution.py:82
  213.7 1.9 fusion.12
  226.3 1.4 fusion.149
  232.3 29.1 %while.79 = (s32[]{:T(128)}, f32[2,32768]{1,0:T(2,128)S(1)}, f32[2,32768]{1,0:T(2,128)S(1)}, f32[2,32768]{1,0:T(2,128)S(1)}, f32[]{:T(128)}, /*index=5*/f32[4,32...) while((s32[]{:T(128)}, f32[2,32768]{1,0:T(2,128)S(1)}, ...), condition=%wide.region_14.15_spmd.clone, body=%wide.region_13.14_spmd.clone.sunk | while | flops 1114119 | bytes 3670207 | solution.py:82
  272.7 3.3 concatenate.83
  276.0 4.6 %scatter_custom_fusion = f32[16,32768]{1,0:T(8,128)} fusion(s32[16]{0:T(128)} %fusion.211, f32[16,32768]{1,0:T(8,128)S(1)} %concatenate.83, f32[]{:T(128)} %constant.277.clone.1), kind=kCustom, calls=%fused_computation.70 | custom fusion | flops 524288 | bytes 2097664 | tf_op jit(solution)/shard_map/scatter-add | solution.py:148
  281.9 50.3 %all-reduce.7.cloned.1.call-done = f32[16,32768]{1,0:T(8,128)} async-done(((f32[16,32768]{1,0:T(8,128)}), f32[16,32768]{1,0:T(8,128)}) %all-reduce.7.cloned.1.call-update) | async-done | bytes 2097168
  333.5 19.8 %all_to_all.38 = f32[4,8,4096]{2,0,1:T(4,128)S(1)} all-to-all(f32[4,8,4096]{2,0,1:T(4,128)S(1)} %bitcast.432), channel_id=1, replica_groups=mesh['slab'=8,'pair'=4] {'slab'}, dimensions={1} | all-to-all | bytes 1048576 | tf_op jit(solution)/shard_map/all_to_all | solution.py:151
  (500 shorter events, 216.6 us)
Async XLA Ops:
  8.3 45.9 %all-to-all-start = ((bf16[8,4,4096]{2,1,0:T(4,128)(2,1)}), bf16[8,4,4096]{2,1,0:T(4,128)(2,1)S(1)}, u32[]{:S(2)}, u32[]{:S(2)}) async-start(bf16[8,4,4096]{2,1,0:T(4,128)(2,1)} %all_to_all.28), calls=%async_computation | async-start | bytes 524288 | tf_op jit(solution)/shard_map/all_to_all | solution.py:120
  15.6 57.6 %all-gather.3.cloned.1.call-start = ((), (), s32[]{:S(2)}) async-start(), calls=%async_computation.2 | async-start | bytes 1310720 | tf_op jit(solution)/shard_map/all_gather | solution.py:122
  55.0 277.2 %all-reduce.7.cloned.1.call-start = ((), (), s32[]{:S(2)}) async-start(), calls=%async_computation.3 | async-start | bytes 4194304
  116.6 2.4 copy-start.30
  117.1 3.4 copy-start.31
  121.5 2.4 copy-start.28
  122.6 2.7 copy-start.29
  125.3 2.3 copy-start.7
  125.3 2.6 copy-start.41
  165.2 2.4 copy-start.21
  165.7 3.4 copy-start.22
  170.1 2.4 copy-start.19
  171.2 2.7 copy-start.20
  173.9 2.6 copy-start.39
  213.2 2.4 copy-start.12
  213.7 3.4 copy-start.13
  218.1 2.4 copy-start.10
  219.2 2.7 copy-start.11
  221.9 2.3 copy-start.3
  221.9 2.6 copy-start.37
  262.2 2.7 copy-start.8
  270.3 2.3 copy-start
  270.3 2.3 copy-start.1
  276.0 4.6 %copy-start.46 = (u32[32]{0:T(128)S(1)}, u32[32]{0:T(128)}, u32[]{:S(2)}) copy-start(u32[32]{0:T(128)} %constant.306) | copy-start | bytes 388
  (26 other events, 46.7 us)
Sparse Core Ops, SparseCore 0:
  55.1 18.0 all-gather.2
  280.7 51.3 all-reduce.6
where the time goes:
time: 365 us; the launch traced here: 361 us
  other arithmetic  124 us (34%)
  local copies, waits for them, and re-layouts  67.6 us (19%)
  waiting for transfers between devices  65.7 us (18%)
  matrix products  54.4 us (15%)
  blocking collectives  19.8 us (5%)
  between operations  15.6 us (4%)
  starting transfers between devices  7.88 us (2%)
  loops' own time  5.96 us (2%)
    add x64, other arithmetic, sweep(): factor_next * factor * direction + 2.0 * factor_next / spread * residual  85.3 us
    unnamed x3, waiting for transfers between devices  50.3 us
    sub x48, other arithmetic, shift_table(): source = target[None, :, None] - offset_part[:, None, None]  25.2 us
    slice x64, local copies, waits for them, and re-layouts, apply_operator(): masks[0] * window(-box_side)  24.2 us
    dot_general x16, matrix products, shift_rows(): jnp.einsum('riy,rxyz->rxiz', shift_table(offset[:, 1], box_side), grid, p...  22.3 us
    all_to_all x1, blocking collectives, shards(): lax.all_to_all(force, 'slab', split_axis=1, concat_axis=0, tiled=True)  19.8 us
    dot_general x16, matrix products, shift_rows(): jnp.einsum('riz,rxyz->rxyi', shift_table(offset[:, 2], box_side), grid, p...  17.1 us
    all_gather x1, waiting for transfers between devices, shards(): piece = lax.all_gather(boxes, 'pair', axis=0, tiled=True)  15.3 us
  transfers between devices with their start and end apart: 3, of which 2 were waited for; matrix products, arithmetic and copies ran while one was open for 11% of the time, Pallas kernels for 0%

commit v1 on v0

v1 whole, which is shorter than its diff:
```python
import functools
import math

import jax
import jax.numpy as jnp
import ml_dtypes
import numpy as np
from jax import lax
from jax.experimental import pallas as pl
from jax.experimental.pallas import tpu as pltpu
from jax.sharding import PartitionSpec as P

STEPS = 16
CUT2 = 192
REACH = 8
SCREEN = 0.1
LOWER_BOUND = 0.1
UPPER_BOUND = 12.1
LANES = 128
TILE_ROWS = 8


def split_constant(matrix):
    high = matrix.astype(ml_dtypes.bfloat16)
    low = (matrix - high.astype(np.float64)).astype(ml_dtypes.bfloat16)
    return high, low


def sine_basis(side):
    index = np.arange(1, side + 1, dtype=np.float64)
    return np.sqrt(2.0 / (side + 1)) * np.sin(np.pi * np.outer(index, index) / (side + 1))


def chebyshev_gain(side):
    shifts = -2.0 * np.cos(np.pi * np.arange(1, side + 1, dtype=np.float64) / (side + 1))
    eigenvalue = 6.0 + SCREEN + shifts[:, None, None] + shifts[None, :, None] + shifts[None, None, :]
    middle = (UPPER_BOUND + LOWER_BOUND) / 2.0
    spread = (UPPER_BOUND - LOWER_BOUND) / 2.0
    ratio = middle / spread
    total = np.zeros_like(eigenvalue)
    residual = np.ones_like(eigenvalue)
    direction = residual / middle
    factor = 1.0 / ratio
    for _ in range(STEPS):
        total = total + direction
        residual = residual - eigenvalue * direction
        factor_next = 1.0 / (2.0 * ratio - factor)
        direction = factor_next * factor * direction + 2.0 * factor_next / spread * residual
        factor = factor_next
    return total.reshape(side, side * side).astype(np.float32)


def split_pair(value):
    high = value.astype(jnp.bfloat16)
    low = (value - high.astype(jnp.float32)).astype(jnp.bfloat16)
    return high, low


def dot(left, right):
    return jnp.dot(left, right, preferred_element_type=jnp.float32)


def force_kernel(
    sizes,
    where_ref,
    match_ref,
    centers_ref,
    boxes_ref,
    mix_high_ref,
    mix_low_ref,
    gain_ref,
    basis_high_hbm,
    basis_low_hbm,
    out_ref,
    fields,
    partner,
    first_high,
    first_low,
    second_high,
    second_low,
    terms,
    total,
    basis_high,
    basis_low,
    sems,
):
    side, rounds, own_count, slab_count, pair_count = sizes
    planes = side // slab_count
    tiles = side * side // LANES
    lines = LANES // side
    pitch = side + 2 * REACH
    solves = own_count * rounds
    group = min(solves, 8)
    group_rows = group * side
    cells = tiles * LANES
    width = 2 * LANES

    high_copy = pltpu.make_async_copy(basis_high_hbm, basis_high, sems.at[0])
    low_copy = pltpu.make_async_copy(basis_low_hbm, basis_low, sems.at[1])
    high_copy.start()
    low_copy.start()

    zeros = jnp.zeros((REACH, LANES), jnp.float32)

    def clear(index, carry):
        fields[pl.ds(pl.multiple_of(index * pitch, 8), REACH), :] = zeros
        fields[pl.ds(pl.multiple_of(index * pitch + REACH + side, 8), REACH), :] = zeros
        return carry

    lax.fori_loop(0, pair_count * own_count * tiles, clear, 0, unroll=8)

    def clear_terms(index, carry):
        terms[pl.ds(pl.multiple_of(index * pitch, 8), REACH), :] = zeros
        terms[pl.ds(pl.multiple_of(index * pitch + REACH + side, 8), REACH), :] = zeros
        return carry

    lax.fori_loop(0, solves * tiles, clear_terms, 0, unroll=8)

    def unpack(index, carry):
        pair = index // slab_count
        slab = index % slab_count
        for chunk in range(own_count * planes // 2):
            block = boxes_ref[pair, slab, 16 * chunk : 16 * chunk + 16, :].astype(jnp.float32)
            for half in range(2):
                own, plane = divmod(2 * chunk + half, planes)
                start = (pair * own_count + own) * tiles * pitch + REACH + slab * planes + plane
                fields[pl.ds(start, tiles, stride=pitch), :] = block[8 * half : 8 * half + 8, :]
        return carry

    lax.fori_loop(0, pair_count * slab_count, unpack, 0)

    lane = lax.broadcasted_iota(jnp.int32, (side, LANES), 1)
    lane_row = lax.broadcasted_iota(jnp.int32, (1, LANES), 1)
    lane_line = lane_row // side
    lane_point = lane_row % side

    def rolled(ref, base, offset_x, offset_flat):
        whole = (offset_flat >> 7) & (tiles - 1)
        part = offset_flat & (LANES - 1)
        start = base * pitch + REACH - offset_x
        moved = []
        for tile in range(tiles):
            row = start + ((tile - whole) & (tiles - 1)) * pitch
            moved.append(pltpu.roll(ref[pl.ds(row, side), :], part, axis=1))
        keep = lane >= part
        return [jnp.where(keep, moved[t], moved[(t - 1) % tiles]) for t in range(tiles)]

    def geometry(index):
        own = index // rounds
        turn = index % rounds
        member = where_ref[0] * own_count + own
        mate = match_ref[turn, member]
        own_offset = []
        mate_offset = []
        distance = 0
        for axis in range(3):
            mine = centers_ref[member, axis]
            other = centers_ref[mate, axis]
            anchor = (mine + other) >> 1
            own_offset.append(mine - anchor)
            mate_offset.append(other - anchor)
            distance = distance + (mine - other) * (mine - other)
        return own, member, mate, own_offset, mate_offset, distance <= CUT2

    def densities(index, carry):
        own, member, mate, a, b, active = geometry(index)
        mine = rolled(fields, member * tiles, a[0], a[1] * side + a[2])
        other = rolled(fields, mate * tiles, b[0], b[1] * side + b[2])
        low_line = jnp.maximum(jnp.maximum(a[1], b[1]), 0)
        high_line = jnp.where(active, side + jnp.minimum(jnp.minimum(a[1], b[1]), 0), 0)
        low_point = jnp.maximum(jnp.maximum(a[2], b[2]), 0)
        high_point = side + jnp.minimum(jnp.minimum(a[2], b[2]), 0)
        point_ok = (lane_point >= low_point) & (lane_point < high_point)
        rows = pl.ds(pl.multiple_of(index * side, side), side)
        for tile in range(tiles):
            line = lane_line + tile * lines
            ok = jnp.where(point_ok & (line >= low_line) & (line < high_line), 1.0, 0.0)
            masked = other[tile] * ok
            columns = slice(tile * LANES, (tile + 1) * LANES)
            partner[rows, columns] = masked.astype(jnp.bfloat16)
            high, low = split_pair(mine[tile] * masked)
            first_high[rows, columns] = high
            first_low[rows, columns] = low
        return carry

    lax.fori_loop(0, solves, densities, 0)

    mix_high = mix_high_ref[...]
    mix_low = mix_low_ref[...]
    column_steps = cells // width
    group_steps = solves // group

    def block_of(index):
        rows = pl.ds(pl.multiple_of((index // column_steps) * group_rows, group_rows), group_rows)
        columns = pl.ds(pl.multiple_of((index % column_steps) * width, width), width)
        return rows, columns

    def along_x(index, carry):
        rows, columns = block_of(index)
        high = first_high[rows, columns]
        low = first_low[rows, columns]
        value = dot(mix_high, high) + (dot(mix_high, low) + dot(mix_low, high))
        second_high[rows, columns], second_low[rows, columns] = split_pair(value)
        return carry

    lax.fori_loop(0, group_steps * column_steps, along_x, 0)
    high_copy.wait()
    low_copy.wait()

    def in_plane(index, source_high, source_low):
        rows, columns = block_of(index)
        high = source_high[rows, :]
        low = source_low[rows, :]
        basis = basis_high[:, columns]
        return dot(high, basis) + (dot(low, basis) + dot(high, basis_low[:, columns]))

    def forward(index, carry):
        rows, columns = block_of(index)
        value = in_plane(index, second_high, second_low)
        gain = gain_ref[:, columns]
        value = (value.reshape(group, side, width) * gain[None]).reshape(group_rows, width)
        first_high[rows, columns], first_low[rows, columns] = split_pair(value)
        return carry

    lax.fori_loop(0, group_steps * column_steps, forward, 0)

    def backward(index, carry):
        rows, columns = block_of(index)
        value = in_plane(index, first_high, first_low)
        second_high[rows, columns], second_low[rows, columns] = split_pair(value)
        return carry

    lax.fori_loop(0, group_steps * column_steps, backward, 0)

    def back_along_x(index, carry):
        rows, columns = block_of(index)
        high = second_high[rows, columns]
        low = second_low[rows, columns]
        value = dot(mix_high, high) + (dot(mix_high, low) + dot(mix_low, high))
        value = value * partner[rows, columns].astype(jnp.float32)
        first_solve = (index // column_steps) * group
        first_tile = (index % column_steps) * 2
        for solve in range(group):
            for half in range(2):
                start = ((first_solve + solve) * tiles + first_tile + half) * pitch + REACH
                terms[pl.ds(pl.multiple_of(start, 8), side), :] = value[
                    solve * side : (solve + 1) * side, half * LANES : (half + 1) * LANES
                ]
        return carry

    lax.fori_loop(0, group_steps * column_steps, back_along_x, 0)

    def collect(own, carry):
        sums = None
        for turn in range(rounds):
            index = own * rounds + turn
            _, _, _, a, _, _ = geometry(index)
            term = rolled(terms, index * tiles, -a[0], -(a[1] * side + a[2]))
            sums = term if sums is None else [s + t for s, t in zip(sums, term)]
        for tile in range(tiles):
            start = (own * tiles + tile) * side
            total[pl.ds(pl.multiple_of(start, side), side), :] = sums[tile]
        return carry

    lax.fori_loop(0, own_count, collect, 0)

    def pack(slab, carry):
        for own in range(own_count):
            for plane in range(planes):
                start = own * tiles * side + slab * planes + plane
                row = (own * planes + plane) * tiles
                out_ref[slab, row : row + tiles, :] = total[pl.ds(start, tiles, stride=side), :]
        return carry

    lax.fori_loop(0, slab_count, pack, 0)


def team_forces(place, match, centers, boxes, side):
    rounds, team = match.shape
    pair_count, slab_count, rows, _ = boxes.shape
    own_count = team // pair_count
    tiles = side * side // LANES
    solves = own_count * rounds
    group = min(solves, 8)
    cells = side * side
    pitch = side + 2 * REACH
    basis = sine_basis(side)
    mix_high, mix_low = split_constant(np.kron(np.eye(group), basis))
    basis_high, basis_low = split_constant(np.kron(basis, basis))
    gain = chebyshev_gain(side)
    sizes = (side, rounds, own_count, slab_count, pair_count)
    scalars = pl.BlockSpec(memory_space=pltpu.SMEM)
    vectors = pl.BlockSpec(memory_space=pltpu.VMEM)
    wide = pltpu.VMEM((solves * side, cells), jnp.bfloat16)
    flops = 2 * solves * side * 3 * 2 * (cells * cells + cells * group * side)
    return pl.pallas_call(
        functools.partial(force_kernel, sizes),
        out_shape=jax.ShapeDtypeStruct((slab_count, rows, LANES), jnp.float32),
        in_specs=[scalars] * 3 + [vectors] * 4 + [pl.BlockSpec(memory_space=pl.ANY)] * 2,
        out_specs=vectors,
        scratch_shapes=[
            pltpu.VMEM((team * tiles * pitch, LANES), jnp.float32),
            wide,
            wide,
            wide,
            wide,
            wide,
            pltpu.VMEM((solves * tiles * pitch, LANES), jnp.float32),
            pltpu.VMEM((own_count * tiles * side, LANES), jnp.float32),
            pltpu.VMEM((cells, cells), jnp.bfloat16),
            pltpu.VMEM((cells, cells), jnp.bfloat16),
            pltpu.SemaphoreType.DMA((2,)),
        ],
        compiler_params=pltpu.CompilerParams(vmem_limit_bytes=40 * 1024 * 1024),
        cost_estimate=pl.CostEstimate(flops=flops, bytes_accessed=8 * 1024 * 1024, transcendentals=0),
    )(
        place,
        match,
        centers,
        boxes,
        jnp.asarray(mix_high),
        jnp.asarray(mix_low),
        jnp.asarray(gain),
        jnp.asarray(basis_high),
        jnp.asarray(basis_low),
    )


def shards(orbitals, centers, matchings):
    slab_count = lax.axis_size("slab")
    pair_count = lax.axis_size("pair")
    slab_index = lax.axis_index("slab")
    pair_index = lax.axis_index("pair")
    local_rows, plane_cells = orbitals.shape
    own_count = local_rows // slab_count
    side = round((plane_cells * slab_count) ** (1.0 / 3.0))
    match = matchings[0]
    team = match.shape[1]
    team_centers = lax.dynamic_index_in_dim(
        centers.reshape(pair_count, slab_count, own_count, 3), slab_index, 1, keepdims=False
    ).reshape(team, 3)
    place = pair_index.astype(jnp.int32).reshape(1)
    rows = own_count * plane_cells // LANES
    sent = orbitals.reshape(slab_count, rows, LANES)
    boxes = lax.all_to_all(sent, "slab", split_axis=0, concat_axis=0, tiled=True)
    gathered = lax.all_gather(boxes, "pair", axis=0, tiled=False)
    force = team_forces(place, match, team_centers, gathered, side)
    planes = lax.all_to_all(force, "slab", split_axis=0, concat_axis=0, tiled=True)
    return planes.reshape(local_rows, plane_cells)


def solution(mesh):
    in_specs = (P("pair", "slab"), P(), P("slab", None, None))
    out_specs = P("pair", "slab")
    return jax.shard_map(shards, mesh=mesh, in_specs=in_specs, out_specs=out_specs, check_vma=False)
```

time: 365 us -> 96 us (0.26)
  other arithmetic: 124 us -> 0 us
  local copies, waits for them, and re-layouts: 67.6 us -> 10.7 us
  matrix products: 54.4 us -> 0 us
  waiting for transfers between devices: 65.7 us -> 15 us
  Pallas kernels: 0 us -> 20.2 us
  blocking collectives: 19.8 us -> 36.3 us
  starting transfers between devices: 7.88 us -> 0.01 us
  loops' own time: 5.96 us -> 0 us
    add x65 -> x0, other arithmetic: 85.3 us -> none  [the longest x64 85.3 us: sweep(): factor_next * factor * direction + 2.0 * factor_next / spread * residual]
    dot_general x48 -> x0, matrix products: 54.4 us -> none  [the longest x16 22.3 us: shift_rows(): jnp.einsum('riy,rxyz->rxiz', shift_table(offset[:, 1], box_side), grid, p...]
    unnamed x3 -> x1, waiting for transfers between devices: 50.3 us -> 0.02 us
    slice x82 -> x0, local copies, waits for them, and re-layouts: 29.5 us -> none  [the longest x64 24.2 us: apply_operator(): masks[0] * window(-box_side)]
    sub x49 -> x0, other arithmetic: 25.2 us -> none  [the longest x48 25.2 us: shift_table(): source = target[None, :, None] - offset_part[:, None, None]]
    pallas_call x0 -> x1, Pallas kernels: none -> 20.2 us  [team_forces(): pl.pallas_call(functools.partial(force_kernel, sizes), out_shape=jax.Shap...]
    all_to_all x1 -> x2, blocking collectives: 19.8 us -> 36.3 us  [the longest x1 20.2 us: shards(): lax.all_to_all(force, 'slab', split_axis=0, concat_axis=0, tiled=True)]
    reshape x32 -> x2, local copies, waits for them, and re-layouts: 18.4 us -> 1.96 us  [the longest x1 1.07 us: shards(): sent = orbitals.reshape(slab_count, rows, LANES)]
  transfers between devices with their start and end apart: 3 -> 1, of which waited for: 2 -> 1; matrix products, arithmetic and copies ran while one was open for 11% -> 1% of each run, Pallas kernels for 0% -> 0%
where the time goes in v1:
time: 96 us; the launch traced here: 95.6 us
  blocking collectives  36.3 us (38%)
  Pallas kernels  20.2 us (21%)
  waiting for transfers between devices  15 us (16%)
  between operations  13.4 us (14%)
  local copies, waits for them, and re-layouts  10.7 us (11%)
    pallas_call x1, Pallas kernels, team_forces(): pl.pallas_call(functools.partial(force_kernel, sizes), out_shape=jax.Shap...  20.2 us
    all_to_all x1, blocking collectives, shards(): lax.all_to_all(force, 'slab', split_axis=0, concat_axis=0, tiled=True)  20.2 us
    all_to_all x1, blocking collectives, shards(): lax.all_to_all(sent, 'slab', split_axis=0, concat_axis=0, tiled=True)  16.1 us
    all_gather x1, waiting for transfers between devices, shards(): gathered = lax.all_gather(boxes, 'pair', axis=0, tiled=False)  15 us
    unnamed x14, local copies, waits for them, and re-layouts  7.8 us
  transfers between devices with their start and end apart: 1, of which 1 were waited for; matrix products, arithmetic and copies ran while one was open for 1% of the time, Pallas kernels for 0%

profile of v1, /device:TPU:0, one launch (start us, length us, event | category | flops | bytes accessed | tf_op | source)
XLA Modules:
  0.0 95.6 jit_solution(9411134418323435010)
XLA Ops:
  6.5 0.0 all-gather.3.cloned.1.call-start
  6.5 1.1 %reshape.19 = bf16[8,128,128]{2,1,0:T(8,128)(2,1)S(1)} reshape(bf16[32,4096]{1,0:T(8,128)(2,1)} %param.8) | data formatting | bytes 524288 | tf_op jit(solution)/shard_map/reshape | solution.py:344
  7.6 16.1 %all_to_all.10 = bf16[8,128,128]{2,1,0:T(8,128)(2,1)} all-to-all(bf16[8,128,128]{2,1,0:T(8,128)(2,1)S(1)} %reshape.19), channel_id=1, replica_groups=mesh['slab'=8,'pair'=4] {'slab'}, dimensions={0} | all-to-all | bytes 524288 | tf_op jit(solution)/shard_map/all_to_all | solution.py:345
  23.7 0.0 all-gather.3.cloned.1.call-update
  23.7 0.8 reshape.17
  24.6 0.1 copy.13
  24.7 15.0 %all-gather.3.cloned.1.call-done = bf16[32,128,128]{2,1,0:T(8,128)(2,1)} async-done(((bf16[8,128,128]{2,1,0:T(8,128)(2,1)}), bf16[32,128,128]{2,1,0:T(8,128)(2,1)}) %all-gather.3.cloned.1.call-update) | async-done | bytes 1048592 | tf_op jit(solution)/shard_map/all_gather | solution.py:346
  39.6 0.0 copy-start
  39.6 1.2 %copy-done = bf16[32,128,128]{2,1,0:T(8,128)(2,1)S(1)} copy-done((bf16[32,128,128]{2,1,0:T(8,128)(2,1)S(1)}, bf16[32,128,128]{2,1,0:T(8,128)(2,1)}, u32[]{:S(2)}) %copy-start) | copy-done | bytes 1048600
  40.8 0.0 copy-start.1
  40.9 0.7 copy-done.1
  41.5 0.0 copy-start.2
  41.5 1.6 %copy-done.2 = bf16[1024,1024]{1,0:T(8,128)(2,1)S(1)} copy-done((bf16[1024,1024]{1,0:T(8,128)(2,1)S(1)}, bf16[1024,1024]{1,0:T(8,128)(2,1)}, u32[]{:S(2)}) %copy-start.2) | copy-done | bytes 2097176
  43.1 0.0 copy-start.3
  43.1 1.6 %copy-done.3 = bf16[1024,1024]{1,0:T(8,128)(2,1)S(1)} copy-done((bf16[1024,1024]{1,0:T(8,128)(2,1)S(1)}, bf16[1024,1024]{1,0:T(8,128)(2,1)}, u32[]{:S(2)}) %copy-start.3) | copy-done | bytes 2097176
  44.7 0.0 copy-start.4
  44.7 0.9 copy-done.4
  45.6 0.0 copy-start.5
  45.6 0.9 copy-done.5
  46.5 0.0 copy-start.6
  46.5 0.9 copy-done.6
  47.4 20.2 %shard_map.82 = f32[8,128,128]{2,1,0:T(8,128)S(1)} custom-call(s32[1]{0:T(128)} %bitcast.where_ref, s32[4,16]{1,0:T(4,128)S(1)} %bitcast.8, s32[16,3]{1,0:T(8,128)S(1)} %bitcast.6, bf16[4,8,128,128]{3,2,1,0:T(8,128)(2,1)S(1)} %bitcast.7, bf16[256,256]{1,0:T(8,128)(2,1)S(1)} %copy-done.6, bf16[256,256]{1,0:T(8,128)(2,1)S(1)} %copy-done.5, ...), custom_call_target="tpu_custom_call" | custom-call | flops 8053063680 | bytes 8388608 | tf_op jit(solution)/shard_map/pallas_call | solution.py:296
  67.6 20.2 %all_to_all.11 = f32[8,128,128]{2,1,0:T(8,128)S(1)} all-to-all(f32[8,128,128]{2,1,0:T(8,128)S(1)} %shard_map.82), channel_id=1, replica_groups=mesh['slab'=8,'pair'=4] {'slab'}, dimensions={0} | all-to-all | bytes 1048576 | tf_op jit(solution)/shard_map/all_to_all | solution.py:348
  87.8 0.9 reshape.20
  (1 shorter events, 0.0 us)
Async XLA Ops:
  6.5 33.1 %all-gather.3.cloned.1.call-start = ((), (), s32[]{:S(2)}) async-start(), calls=%async_computation.2 | async-start | bytes 1310720 | tf_op jit(solution)/shard_map/all_gather | solution.py:346
  39.6 1.2 %copy-start = (bf16[32,128,128]{2,1,0:T(8,128)(2,1)S(1)}, bf16[32,128,128]{2,1,0:T(8,128)(2,1)}, u32[]{:S(2)}) copy-start(bf16[32,128,128]{2,1,0:T(8,128)(2,1)} %all-gather.3.cloned.1.call-done) | copy-start | bytes 3145732
  40.8 0.7 copy-start.1
  41.5 1.6 %copy-start.2 = (bf16[1024,1024]{1,0:T(8,128)(2,1)S(1)}, bf16[1024,1024]{1,0:T(8,128)(2,1)}, u32[]{:S(2)}) copy-start(bf16[1024,1024]{1,0:T(8,128)(2,1)} %constant.29.clone.basis_low_hbm) | copy-start | bytes 6291460
  43.1 1.6 %copy-start.3 = (bf16[1024,1024]{1,0:T(8,128)(2,1)S(1)}, bf16[1024,1024]{1,0:T(8,128)(2,1)}, u32[]{:S(2)}) copy-start(bf16[1024,1024]{1,0:T(8,128)(2,1)} %constant.28.clone.basis_high_hbm) | copy-start | bytes 6291460
  44.7 0.9 copy-start.4
  45.6 0.9 copy-start.5
  46.5 0.9 copy-start.6
Sparse Core Ops, SparseCore 0:
  23.9 15.7 all-gather.2

commit v2 on v1

--- a/solution.py
+++ b/solution.py
@@ -1,5 +1,4 @@
 import functools
-import math
 
 import jax
 import jax.numpy as jnp
@@ -17,7 +16,7 @@
 LOWER_BOUND = 0.1
 UPPER_BOUND = 12.1
 LANES = 128
-TILE_ROWS = 8
+CORES = 2
 
 
 def split_constant(matrix):
@@ -65,13 +64,29 @@
     where_ref,
     match_ref,
     centers_ref,
+    *refs,
+):
+    side, rounds, own_count, slab_count, pair_count = sizes
+    block_count = slab_count * pair_count
+    block_refs = refs[:block_count]
+    constant_refs = refs[block_count : block_count + 5]
+    out_refs = refs[block_count + 5 : block_count + 5 + slab_count]
+    scratch = refs[block_count + 5 + slab_count :]
+    force_body(sizes, where_ref, match_ref, centers_ref, block_refs, constant_refs, out_refs, *scratch)
+
+
+def force_body(
+    sizes,
+    where_ref,
+    match_ref,
+    centers_ref,
+    block_refs,
+    constant_refs,
+    out_refs,
     boxes_ref,
     mix_high_ref,
     mix_low_ref,
     gain_ref,
-    basis_high_hbm,
-    basis_low_hbm,
-    out_ref,
     fields,
     partner,
     first_high,
@@ -95,10 +110,19 @@
     cells = tiles * LANES
     width = 2 * LANES
 
-    high_copy = pltpu.make_async_copy(basis_high_hbm, basis_high, sems.at[0])
-    low_copy = pltpu.make_async_copy(basis_low_hbm, basis_low, sems.at[1])
-    high_copy.start()
-    low_copy.start()
+    slab_index = where_ref[0]
+    pair_index = where_ref[1]
+    copies = []
+    for index, (pair, slab) in enumerate(block_places(slab_index, pair_index, slab_count, pair_count)):
+        copies.append(
+            pltpu.make_async_copy(block_refs[index], boxes_ref.at[pair, slab], sems.at[index])
+        )
+    constants = (mix_high_ref, mix_low_ref, gain_ref, basis_high, basis_low)
+    constant_copies = []
+    for index, (source, target) in enumerate(zip(constant_refs, constants)):
+        constant_copies.append(pltpu.make_async_copy(source, target, sems.at[len(copies) + index]))
+    for copy in copies + constant_copies:
+        copy.start()
 
     zeros = jnp.zeros((REACH, LANES), jnp.float32)
 
@@ -115,6 +139,9 @@
         return carry
 
     lax.fori_loop(0, solves * tiles, clear_terms, 0, unroll=8)
+
+    for copy in copies:
+        copy.wait()
 
     def unpack(index, carry):
         pair = index // slab_count
@@ -148,7 +175,7 @@
     def geometry(index):
         own = index // rounds
         turn = index % rounds
-        member = where_ref[0] * own_count + own
+        member = pair_index * own_count + own
         mate = match_ref[turn, member]
         own_offset = []
         mate_offset = []
@@ -185,6 +212,8 @@
 
     lax.fori_loop(0, solves, densities, 0)
 
+    for copy in constant_copies:
+        copy.wait()
     mix_high = mix_high_ref[...]
     mix_low = mix_low_ref[...]
     column_steps = cells // width
@@ -204,8 +233,6 @@
         return carry
 
     lax.fori_loop(0, group_steps * column_steps, along_x, 0)
-    high_copy.wait()
-    low_copy.wait()
 
     def in_plane(index, source_high, source_low):
         rows, columns = block_of(index)
@@ -264,20 +291,107 @@
 
     lax.fori_loop(0, own_count, collect, 0)
 
-    def pack(slab, carry):
+    for step in range(slab_count):
+        slab = (slab_index + step) % slab_count
         for own in range(own_count):
             for plane in range(planes):
                 start = own * tiles * side + slab * planes + plane
                 row = (own * planes + plane) * tiles
-                out_ref[slab, row : row + tiles, :] = total[pl.ds(start, tiles, stride=side), :]
-        return carry
-
-    lax.fori_loop(0, slab_count, pack, 0)
-
-
-def team_forces(place, match, centers, boxes, side):
+                out_refs[step][row : row + tiles, :] = total[pl.ds(start, tiles, stride=side), :]
+
+
+def block_places(slab_index, pair_index, slab_count, pair_count):
+    chips = pair_count // CORES
+    chip = pair_index // CORES
+    core = pair_index % CORES
+    for core_step in range(CORES):
+        for chip_step in range(chips):
+            pair = (chip + chips - chip_step) % chips * CORES + (core + core_step) % CORES
+            for step in range(slab_count):
+                yield pair, (slab_index + slab_count - step) % slab_count
+
+
+def gather_boxes(blocks, slab_count, pair_count):
+    chips = pair_count // CORES
+    own = [blocks[0]]
+    for step in range(1, slab_count):
+        perm = [(i, (i + step) % slab_count) for i in range(slab_count)]
+        own.append(lax.ppermute(blocks[step], "slab", perm))
+    pieces = [own]
+    for step in range(1, chips):
+        perm = [(i, (i + step * CORES) % pair_count) for i in range(pair_count)]
+        pieces.append([lax.ppermute(block, "pair", perm) for block in own])
+    swap = [(i, i ^ 1) for i in range(pair_count)]
+    other = [[lax.ppermute(block, "pair", swap) for block in piece] for piece in pieces]
+    return [block for piece in pieces + other for block in piece]
+
+
+def pack_kernel(sizes, where_ref, orbitals_ref, *refs):
+    own_count, slab_count = sizes
+    out_refs, lines = refs[:slab_count], refs[slab_count]
+    row_count, cells = orbitals_ref.shape
+    tiles = cells // LANES
+    for tile in range(tiles):
+        columns = slice(tile * LANES, (tile + 1) * LANES)
+        lines[tile * row_count : (tile + 1) * row_count, :] = orbitals_ref[:, columns].astype(jnp.float32)
+    for step in range(slab_count):
+        first = (where_ref[0] + step) % slab_count * own_count
+        for chunk in range(own_count * tiles // 16):
+            halves = []
+            for half in range(2):
+                own, tile = divmod(16 * chunk + 8 * half, tiles)
+                halves.append(lines[pl.ds(tile * row_count + first + own, 8, stride=row_count), :])
+            out_refs[step][16 * chunk : 16 * chunk + 16, :] = jnp.concatenate(halves, axis=0).astype(
+                jnp.bfloat16
+            )
+
+
+def pack(place, orbitals, own_count, slab_count):
+    row_count, cells = orbitals.shape
+    rows = own_count * cells // LANES
+    vectors = pl.BlockSpec(memory_space=pltpu.VMEM)
+    return pl.pallas_call(
+        functools.partial(pack_kernel, (own_count, slab_count)),
+        out_shape=[jax.ShapeDtypeStruct((rows, LANES), jnp.bfloat16)] * slab_count,
+        in_specs=[pl.BlockSpec(memory_space=pltpu.SMEM), vectors],
+        out_specs=[vectors] * slab_count,
+        scratch_shapes=[pltpu.VMEM((row_count * cells // LANES, LANES), jnp.float32)],
+    )(place, orbitals)
+
+
+def unpack_kernel(sizes, where_ref, *refs):
+    own_count, slab_count = sizes
+    block_refs, out_ref, lines = refs[:slab_count], refs[slab_count], refs[slab_count + 1]
+    row_count, cells = out_ref.shape
+    tiles = cells // LANES
+    for step in range(slab_count):
+        first = (where_ref[0] + slab_count - step) % slab_count * own_count
+        for own in range(own_count):
+            for tile in range(0, tiles, 8):
+                start = tile * row_count + first + own
+                row = own * tiles + tile
+                lines[pl.ds(start, 8, stride=row_count), :] = block_refs[step][row : row + 8, :]
+    for tile in range(tiles):
+        columns = slice(tile * LANES, (tile + 1) * LANES)
+        out_ref[:, columns] = lines[tile * row_count : (tile + 1) * row_count, :]
+
+
+def unpack(place, blocks, own_count, cells):
+    slab_count = len(blocks)
+    row_count = own_count * slab_count
+    vectors = pl.BlockSpec(memory_space=pltpu.VMEM)
+    return pl.pallas_call(
+        functools.partial(unpack_kernel, (own_count, slab_count)),
+        out_shape=jax.ShapeDtypeStruct((row_count, cells), jnp.float32),
+        in_specs=[pl.BlockSpec(memory_space=pltpu.SMEM)] + [vectors] * slab_count,
+        out_specs=vectors,
+        scratch_shapes=[pltpu.VMEM((row_count * cells // LANES, LANES), jnp.float32)],
+    )(place, *blocks)
+
+
+def team_forces(place, match, centers, blocks, side, slab_count, pair_count):
     rounds, team = match.shape
-    pair_count, slab_count, rows, _ = boxes.shape
+    rows = blocks[0].shape[0]
     own_count = team // pair_count
     tiles = side * side // LANES
     solves = own_count * rounds
@@ -295,10 +409,14 @@
     flops = 2 * solves * side * 3 * 2 * (cells * cells + cells * group * side)
     return pl.pallas_call(
         functools.partial(force_kernel, sizes),
-        out_shape=jax.ShapeDtypeStruct((slab_count, rows, LANES), jnp.float32),
-        in_specs=[scalars] * 3 + [vectors] * 4 + [pl.BlockSpec(memory_space=pl.ANY)] * 2,
-        out_specs=vectors,
+        out_shape=[jax.ShapeDtypeStruct((rows, LANES), jnp.float32)] * slab_count,
+        in_specs=[scalars] * 3 + [pl.BlockSpec(memory_space=pl.ANY)] * (len(blocks) + 5),
+        out_specs=[vectors] * slab_count,
         scratch_shapes=[
+            pltpu.VMEM((pair_count, slab_count, rows, LANES), jnp.bfloat16),
+            pltpu.VMEM((group * side, group * side), jnp.bfloat16),
+            pltpu.VMEM((group * side, group * side), jnp.bfloat16),
+            pltpu.VMEM((side, cells), jnp.float32),
             pltpu.VMEM((team * tiles * pitch, LANES), jnp.float32),
             wide,
             wide,
@@ -309,7 +427,7 @@
             pltpu.VMEM((own_count * tiles * side, LANES), jnp.float32),
             pltpu.VMEM((cells, cells), jnp.bfloat16),
             pltpu.VMEM((cells, cells), jnp.bfloat16),
-            pltpu.SemaphoreType.DMA((2,)),
+            pltpu.SemaphoreType.DMA((len(blocks) + 5,)),
         ],
         compiler_params=pltpu.CompilerParams(vmem_limit_bytes=40 * 1024 * 1024),
         cost_estimate=pl.CostEstimate(flops=flops, bytes_accessed=8 * 1024 * 1024, transcendentals=0),
@@ -317,7 +435,7 @@
         place,
         match,
         centers,
-        boxes,
+        *blocks,
         jnp.asarray(mix_high),
         jnp.asarray(mix_low),
         jnp.asarray(gain),
@@ -339,14 +457,15 @@
     team_centers = lax.dynamic_index_in_dim(
         centers.reshape(pair_count, slab_count, own_count, 3), slab_index, 1, keepdims=False
     ).reshape(team, 3)
-    place = pair_index.astype(jnp.int32).reshape(1)
-    rows = own_count * plane_cells // LANES
-    sent = orbitals.reshape(slab_count, rows, LANES)
-    boxes = lax.all_to_all(sent, "slab", split_axis=0, concat_axis=0, tiled=True)
-    gathered = lax.all_gather(boxes, "pair", axis=0, tiled=False)
-    force = team_forces(place, match, team_centers, gathered, side)
-    planes = lax.all_to_all(force, "slab", split_axis=0, concat_axis=0, tiled=True)
-    return planes.reshape(local_rows, plane_cells)
+    place = jnp.stack([slab_index, pair_index]).astype(jnp.int32)
+    blocks = pack(place, orbitals, own_count, slab_count)
+    team_blocks = gather_boxes(blocks, slab_count, pair_count)
+    forces = team_forces(place, match, team_centers, team_blocks, side, slab_count, pair_count)
+    received = [forces[0]]
+    for step in range(1, slab_count):
+        perm = [(i, (i + step) % slab_count) for i in range(slab_count)]
+        received.append(lax.ppermute(forces[step], "slab", perm))
+    return unpack(place, received, own_count, plane_cells)
 
 
 def solution(mesh):

time: 96 us -> 82.5 us (0.86)
  starting transfers between devices: 0.01 us -> 36.7 us
  blocking collectives: 36.3 us -> 0 us
  between operations: 13.4 us -> 0.15 us
  waiting for transfers between devices: 15 us -> 7.53 us
  Pallas kernels: 20.2 us -> 27.1 us
    ppermute x0 -> x38, starting transfers between devices: none -> 36.7 us  [the longest x7 13.7 us: gather_boxes(): own.append(lax.ppermute(blocks[step], 'slab', perm))]
    all_to_all x2 -> x0, blocking collectives: 36.3 us -> none  [the longest x1 20.2 us: shards(): lax.all_to_all(force, 'slab', split_axis=0, concat_axis=0, tiled=True)]
    all_gather x1 -> x0, waiting for transfers between devices: 15 us -> none  [shards(): gathered = lax.all_gather(boxes, 'pair', axis=0, tiled=False)]
    ppermute x0 -> x38, waiting for transfers between devices: none -> 7.53 us  [the longest x7 4.71 us: shards(): received.append(lax.ppermute(forces[step], 'slab', perm))]
    pallas_call x1 -> x3, Pallas kernels: 20.2 us -> 27.1 us  [the longest x1 22.7 us: team_forces(): pl.pallas_call(functools.partial(force_kernel, sizes), out_shape=[jax.Sha...]
    reshape x2 -> x0, local copies, waits for them, and re-layouts: 1.96 us -> none  [the longest x1 1.07 us: shards(): sent = orbitals.reshape(slab_count, rows, LANES)]
    unnamed x14 -> x32, local copies, waits for them, and re-layouts: 7.8 us -> 9.17 us
  transfers between devices with their start and end apart: 1 -> 38, of which waited for: 1 -> 13; matrix products, arithmetic and copies ran while one was open for 1% -> 1% of each run, Pallas kernels for 0% -> 0%
where the time goes in v2:
time: 82.5 us; the launch traced here: 82.1 us
  starting transfers between devices  36.7 us (44%)
  Pallas kernels  27.1 us (33%)
  local copies, waits for them, and re-layouts  10.1 us (12%)
  waiting for transfers between devices  7.53 us (9%)
    pallas_call x1, Pallas kernels, team_forces(): pl.pallas_call(functools.partial(force_kernel, sizes), out_shape=[jax.Sha...  22.7 us
    ppermute x7, starting transfers between devices, gather_boxes(): own.append(lax.ppermute(blocks[step], 'slab', perm))  13.7 us
    ppermute x7, starting transfers between devices, shards(): received.append(lax.ppermute(forces[step], 'slab', perm))  10.7 us
    ppermute x8, starting transfers between devices, gather_boxes(): pieces.append([lax.ppermute(block, 'pair', perm) for block in own])  9.29 us
    unnamed x32, local copies, waits for them, and re-layouts  9.17 us
    ppermute x7, waiting for transfers between devices, shards(): received.append(lax.ppermute(forces[step], 'slab', perm))  4.71 us
    ppermute x16, starting transfers between devices, gather_boxes(): lax.ppermute(block, 'pair', swap)  2.95 us
    pallas_call x1, Pallas kernels, unpack(): pl.pallas_call(functools.partial(unpack_kernel, (own_count, slab_count)),...  2.39 us
  transfers between devices with their start and end apart: 38, of which 13 were waited for; matrix products, arithmetic and copies ran while one was open for 1% of the time, Pallas kernels for 0%

profile of v2, /device:TPU:0, one launch (start us, length us, event | category | flops | bytes accessed | tf_op | source)
XLA Modules:
  0.0 82.1 jit_solution(14673479213953904354)
XLA Ops:
  0.6 1.9 %shard_map.82 = (bf16[128,128]{1,0:T(8,128)(2,1)}, bf16[128,128]{1,0:T(8,128)(2,1)}, bf16[128,128]{1,0:T(8,128)(2,1)}, bf16[128,128]{1,0:T(8,128)(2,1)}, bf16[12...) custom-call(s32[2]{0:T(128)} %pad_add_fusion.where_ref, ...), custom_call_target="tpu_custom_call" | custom-call | tf_op jit(solution)/shard_map/pallas_call | solution.py:353
  2.5 3.0 %collective-permute-start = (bf16[128,128]{1,0:T(8,128)(2,1)}, bf16[128,128]{1,0:T(8,128)(2,1)S(1)}, u32[]{:S(2)}, u32[]{:S(2)}) collective-permute-start(bf16[128,128]{1,0:T(8,128)(2,1)} %get-tuple-element.22), channel_id=1, source_target_pairs={{0,4},{4,8},{8,12},{12,16},{16,20},{20,24},{24,28},{28,0},{1,5},{5... | collective-permute-start | bytes 98312 | tf_op jit(solution)/shard_map/ppermute | solution.py:319
  5.5 1.6 %collective-permute-start.1 = (bf16[128,128]{1,0:T(8,128)(2,1)}, bf16[128,128]{1,0:T(8,128)(2,1)S(1)}, u32[]{:S(2)}, u32[]{:S(2)}) collective-permute-start(bf16[128,128]{1,0:T(8,128)(2,1)} %get-tuple-element.23), channel_id=1, source_target_pairs={{0,8},{4,12},{8,16},{12,20},{16,24},{20,28},{24,0},{28,4},{1,9},{5... | collective-permute-start | bytes 98312 | tf_op jit(solution)/shard_map/ppermute | solution.py:319
  7.1 2.5 %collective-permute-start.2 = (bf16[128,128]{1,0:T(8,128)(2,1)}, bf16[128,128]{1,0:T(8,128)(2,1)S(1)}, u32[]{:S(2)}, u32[]{:S(2)}) collective-permute-start(bf16[128,128]{1,0:T(8,128)(2,1)} %get-tuple-element.24), channel_id=1, source_target_pairs={{0,12},{4,16},{8,20},{12,24},{16,28},{20,0},{24,4},{28,8},{1,13},{... | collective-permute-start | bytes 98312 | tf_op jit(solution)/shard_map/ppermute | solution.py:319
  9.6 1.2 %collective-permute-start.3 = (bf16[128,128]{1,0:T(8,128)(2,1)}, bf16[128,128]{1,0:T(8,128)(2,1)S(1)}, u32[]{:S(2)}, u32[]{:S(2)}) collective-permute-start(bf16[128,128]{1,0:T(8,128)(2,1)} %get-tuple-element.25), channel_id=1, source_target_pairs={{0,16},{4,20},{8,24},{12,28},{16,0},{20,4},{24,8},{28,12},{1,17},{... | collective-permute-start | bytes 98312 | tf_op jit(solution)/shard_map/ppermute | solution.py:319
  10.9 2.6 %collective-permute-start.4 = (bf16[128,128]{1,0:T(8,128)(2,1)}, bf16[128,128]{1,0:T(8,128)(2,1)S(1)}, u32[]{:S(2)}, u32[]{:S(2)}) collective-permute-start(bf16[128,128]{1,0:T(8,128)(2,1)} %get-tuple-element.26), channel_id=1, source_target_pairs={{0,20},{4,24},{8,28},{12,0},{16,4},{20,8},{24,12},{28,16},{1,21},{... | collective-permute-start | bytes 98312 | tf_op jit(solution)/shard_map/ppermute | solution.py:319
  13.5 1.3 %collective-permute-start.5 = (bf16[128,128]{1,0:T(8,128)(2,1)}, bf16[128,128]{1,0:T(8,128)(2,1)S(1)}, u32[]{:S(2)}, u32[]{:S(2)}) collective-permute-start(bf16[128,128]{1,0:T(8,128)(2,1)} %get-tuple-element.27), channel_id=1, source_target_pairs={{0,24},{4,28},{8,0},{12,4},{16,8},{20,12},{24,16},{28,20},{1,25},{... | collective-permute-start | bytes 98312 | tf_op jit(solution)/shard_map/ppermute | solution.py:319
  14.9 1.4 %collective-permute-start.6 = (bf16[128,128]{1,0:T(8,128)(2,1)}, bf16[128,128]{1,0:T(8,128)(2,1)S(1)}, u32[]{:S(2)}, u32[]{:S(2)}) collective-permute-start(bf16[128,128]{1,0:T(8,128)(2,1)} %get-tuple-element.28), channel_id=1, source_target_pairs={{0,28},{4,0},{8,4},{12,8},{16,12},{20,16},{24,20},{28,24},{1,29},{... | collective-permute-start | bytes 98312 | tf_op jit(solution)/shard_map/ppermute | solution.py:319
  16.3 1.6 %collective-permute-start.7 = (bf16[128,128]{1,0:T(8,128)(2,1)}, bf16[128,128]{1,0:T(8,128)(2,1)S(1)}, u32[]{:S(2)}, u32[]{:S(2)}) collective-permute-start(bf16[128,128]{1,0:T(8,128)(2,1)} %get-tuple-element.21.refs_0_), channel_id=1, source_target_pairs={{0,2},{1,3},{2,0},{3,1},{4,6},{5,7},{6,4},{7,5},{8,10},{9,11},{10,... | collective-permute-start | bytes 98312 | tf_op jit(solution)/shard_map/ppermute | solution.py:323
  19.1 1.3 %collective-permute-start.9 = (bf16[128,128]{1,0:T(8,128)(2,1)S(1)}, bf16[128,128]{1,0:T(8,128)(2,1)S(1)}, u32[]{:S(2)}, u32[]{:S(2)}) collective-permute-start(bf16[128,128]{1,0:T(8,128)(2,1)S(1)} %collective-permute-done.1.refs_2_), channel_id=1, source_target_pairs={{0,2},{1,3},{2,0},{3,1},{4,6},{5,7},{6,4},{7,5},{8,10},{9,11},{10,... | collective-permute-start | bytes 98312 | tf_op jit(solution)/shard_map/ppermute | solution.py:323
  20.7 1.5 %collective-permute-start.10 = (bf16[128,128]{1,0:T(8,128)(2,1)S(1)}, bf16[128,128]{1,0:T(8,128)(2,1)S(1)}, u32[]{:S(2)}, u32[]{:S(2)}) collective-permute-start(bf16[128,128]{1,0:T(8,128)(2,1)S(1)} %collective-permute-done.2.refs_3_), channel_id=1, source_target_pairs={{0,2},{1,3},{2,0},{3,1},{4,6},{5,7},{6,4},{7,5},{8,10},{9,11},{10,... | collective-permute-start | bytes 98312 | tf_op jit(solution)/shard_map/ppermute | solution.py:323
  23.3 1.2 %collective-permute-start.12 = (bf16[128,128]{1,0:T(8,128)(2,1)S(1)}, bf16[128,128]{1,0:T(8,128)(2,1)S(1)}, u32[]{:S(2)}, u32[]{:S(2)}) collective-permute-start(bf16[128,128]{1,0:T(8,128)(2,1)S(1)} %collective-permute-done.4.refs_5_), channel_id=1, source_target_pairs={{0,2},{1,3},{2,0},{3,1},{4,6},{5,7},{6,4},{7,5},{8,10},{9,11},{10,... | collective-permute-start | bytes 98312 | tf_op jit(solution)/shard_map/ppermute | solution.py:323
  24.7 1.4 %collective-permute-start.13 = (bf16[128,128]{1,0:T(8,128)(2,1)S(1)}, bf16[128,128]{1,0:T(8,128)(2,1)S(1)}, u32[]{:S(2)}, u32[]{:S(2)}) collective-permute-start(bf16[128,128]{1,0:T(8,128)(2,1)S(1)} %collective-permute-done.5.refs_6_), channel_id=1, source_target_pairs={{0,2},{1,3},{2,0},{3,1},{4,6},{5,7},{6,4},{7,5},{8,10},{9,11},{10,... | collective-permute-start | bytes 98312 | tf_op jit(solution)/shard_map/ppermute | solution.py:323
  34.3 1.6 %copy-done.4 = bf16[1024,1024]{1,0:T(8,128)(2,1)S(1)} copy-done((bf16[1024,1024]{1,0:T(8,128)(2,1)S(1)}, bf16[1024,1024]{1,0:T(8,128)(2,1)}, u32[]{:S(2)}) %copy-start.4) | copy-done | bytes 2097176
  35.9 1.6 %copy-done.5 = bf16[1024,1024]{1,0:T(8,128)(2,1)S(1)} copy-done((bf16[1024,1024]{1,0:T(8,128)(2,1)S(1)}, bf16[1024,1024]{1,0:T(8,128)(2,1)}, u32[]{:S(2)}) %copy-start.5) | copy-done | bytes 2097176
  40.2 22.7 %shard_map.83 = (f32[128,128]{1,0:T(8,128)S(1)}, f32[128,128]{1,0:T(8,128)S(1)}, f32[128,128]{1,0:T(8,128)S(1)}, f32[128,128]{1,0:T(8,128)S(1)}, f32[128,128]{1,...) custom-call(s32[2]{0:T(128)S(1)} %copy-done.1, s32[4,16]{1,0:T(4,128)S(1)} %bitcast.7, ...), custom_call_target="tpu_custom_call" | custom-call | flops 8053063680 | bytes 8388608 | tf_op jit(solution)/shard_map/pallas_call | solution.py:410
  63.6 1.2 %collective-permute-start.31 = (f32[128,128]{1,0:T(8,128)S(1)}, f32[128,128]{1,0:T(8,128)S(1)}, u32[]{:S(2)}, u32[]{:S(2)}) collective-permute-start(f32[128,128]{1,0:T(8,128)S(1)} %get-tuple-element.30), channel_id=1, source_target_pairs={{0,4},{4,8},{8,12},{12,16},{16,20},{20,24},{24,28},{28,0},{1,5},{5... | collective-permute-start | bytes 196616 | tf_op jit(solution)/shard_map/ppermute | solution.py:467
  64.9 3.2 %collective-permute-start.33 = (f32[128,128]{1,0:T(8,128)S(1)}, f32[128,128]{1,0:T(8,128)S(1)}, u32[]{:S(2)}, u32[]{:S(2)}) collective-permute-start(f32[128,128]{1,0:T(8,128)S(1)} %get-tuple-element.32), channel_id=1, source_target_pairs={{0,12},{4,16},{8,20},{12,24},{16,28},{20,0},{24,4},{28,8},{1,13},{... | collective-permute-start | bytes 196616 | tf_op jit(solution)/shard_map/ppermute | solution.py:467
  68.1 1.6 %collective-permute-start.34 = (f32[128,128]{1,0:T(8,128)S(1)}, f32[128,128]{1,0:T(8,128)S(1)}, u32[]{:S(2)}, u32[]{:S(2)}) collective-permute-start(f32[128,128]{1,0:T(8,128)S(1)} %get-tuple-element.33), channel_id=1, source_target_pairs={{0,16},{4,20},{8,24},{12,28},{16,0},{20,4},{24,8},{28,12},{1,17},{... | collective-permute-start | bytes 196616 | tf_op jit(solution)/shard_map/ppermute | solution.py:467
  69.8 3.1 %collective-permute-start.35 = (f32[128,128]{1,0:T(8,128)S(1)}, f32[128,128]{1,0:T(8,128)S(1)}, u32[]{:S(2)}, u32[]{:S(2)}) collective-permute-start(f32[128,128]{1,0:T(8,128)S(1)} %get-tuple-element.34), channel_id=1, source_target_pairs={{0,20},{4,24},{8,28},{12,0},{16,4},{20,8},{24,12},{28,16},{1,21},{... | collective-permute-start | bytes 196616 | tf_op jit(solution)/shard_map/ppermute | solution.py:467
  72.9 1.5 %collective-permute-start.37 = (f32[128,128]{1,0:T(8,128)S(1)}, f32[128,128]{1,0:T(8,128)S(1)}, u32[]{:S(2)}, u32[]{:S(2)}) collective-permute-start(f32[128,128]{1,0:T(8,128)S(1)} %get-tuple-element.36), channel_id=1, source_target_pairs={{0,28},{4,0},{8,4},{12,8},{16,12},{20,16},{24,20},{28,24},{1,29},{... | collective-permute-start | bytes 196616 | tf_op jit(solution)/shard_map/ppermute | solution.py:467
  74.4 2.1 %collective-permute-done.33.refs_3_ = f32[128,128]{1,0:T(8,128)S(1)} collective-permute-done((f32[128,128]{1,0:T(8,128)S(1)}, f32[128,128]{1,0:T(8,128)S(1)}, u32[]{:S(2)}, u32[]{:S(2)}) %collective-permute-start.33) | collective-permute-done | bytes 65568 | tf_op jit(solution)/shard_map/ppermute | solution.py:467
  76.6 1.8 %collective-permute-done.35.refs_5_ = f32[128,128]{1,0:T(8,128)S(1)} collective-permute-done((f32[128,128]{1,0:T(8,128)S(1)}, f32[128,128]{1,0:T(8,128)S(1)}, u32[]{:S(2)}, u32[]{:S(2)}) %collective-permute-start.35) | collective-permute-done | bytes 65568 | tf_op jit(solution)/shard_map/ppermute | solution.py:467
  79.7 2.4 %shard_map.84 = f32[32,4096]{1,0:T(8,128)} custom-call(s32[2]{0:T(128)} %pad_add_fusion.where_ref, f32[128,128]{1,0:T(8,128)} %copy-done, f32[128,128]{1,0:T(8,128)} %copy-done.9, f32[128,128]{1,0:T(8,128)} %copy-done.10, f32[128,128]{1,0:T(8,128)} %copy-done.11, f32[128,128]{1,0:T(8,128)} %copy-done.12, f32[128,128]{1,0:T(8,128)} %copy-done.13, ...), custom_call_target="tpu_custom_call" | custom-call | tf_op jit(solution)/shard_map/pallas_call | solution.py:383
  (91 shorter events, 16.5 us)
Async XLA Ops:
  2.5 11.0 %collective-permute-start = (bf16[128,128]{1,0:T(8,128)(2,1)}, bf16[128,128]{1,0:T(8,128)(2,1)S(1)}, u32[]{:S(2)}, u32[]{:S(2)}) collective-permute-start(bf16[128,128]{1,0:T(8,128)(2,1)} %get-tuple-element.22), channel_id=1, source_target_pairs={{0,4},{4,8},{8,12},{12,16},{16,20},{20,24},{24,28},{28,0},{1,5},{5... | collective-permute-start | bytes 98312 | tf_op jit(solution)/shard_map/ppermute | solution.py:319
  5.5 9.3 %collective-permute-start.1 = (bf16[128,128]{1,0:T(8,128)(2,1)}, bf16[128,128]{1,0:T(8,128)(2,1)S(1)}, u32[]{:S(2)}, u32[]{:S(2)}) collective-permute-start(bf16[128,128]{1,0:T(8,128)(2,1)} %get-tuple-element.23), channel_id=1, source_target_pairs={{0,8},{4,12},{8,16},{12,20},{16,24},{20,28},{24,0},{28,4},{1,9},{5... | collective-permute-start | bytes 98312 | tf_op jit(solution)/shard_map/ppermute | solution.py:319
  7.1 9.2 %collective-permute-start.2 = (bf16[128,128]{1,0:T(8,128)(2,1)}, bf16[128,128]{1,0:T(8,128)(2,1)S(1)}, u32[]{:S(2)}, u32[]{:S(2)}) collective-permute-start(bf16[128,128]{1,0:T(8,128)(2,1)} %get-tuple-element.24), channel_id=1, source_target_pairs={{0,12},{4,16},{8,20},{12,24},{16,28},{20,0},{24,4},{28,8},{1,13},{... | collective-permute-start | bytes 98312 | tf_op jit(solution)/shard_map/ppermute | solution.py:319
  9.6 6.7 %collective-permute-start.3 = (bf16[128,128]{1,0:T(8,128)(2,1)}, bf16[128,128]{1,0:T(8,128)(2,1)S(1)}, u32[]{:S(2)}, u32[]{:S(2)}) collective-permute-start(bf16[128,128]{1,0:T(8,128)(2,1)} %get-tuple-element.25), channel_id=1, source_target_pairs={{0,16},{4,20},{8,24},{12,28},{16,0},{20,4},{24,8},{28,12},{1,17},{... | collective-permute-start | bytes 98312 | tf_op jit(solution)/shard_map/ppermute | solution.py:319
  10.9 7.0 %collective-permute-start.4 = (bf16[128,128]{1,0:T(8,128)(2,1)}, bf16[128,128]{1,0:T(8,128)(2,1)S(1)}, u32[]{:S(2)}, u32[]{:S(2)}) collective-permute-start(bf16[128,128]{1,0:T(8,128)(2,1)} %get-tuple-element.26), channel_id=1, source_target_pairs={{0,20},{4,24},{8,28},{12,0},{16,4},{20,8},{24,12},{28,16},{1,21},{... | collective-permute-start | bytes 98312 | tf_op jit(solution)/shard_map/ppermute | solution.py:319
  13.5 4.5 %collective-permute-start.5 = (bf16[128,128]{1,0:T(8,128)(2,1)}, bf16[128,128]{1,0:T(8,128)(2,1)S(1)}, u32[]{:S(2)}, u32[]{:S(2)}) collective-permute-start(bf16[128,128]{1,0:T(8,128)(2,1)} %get-tuple-element.27), channel_id=1, source_target_pairs={{0,24},{4,28},{8,0},{12,4},{16,8},{20,12},{24,16},{28,20},{1,25},{... | collective-permute-start | bytes 98312 | tf_op jit(solution)/shard_map/ppermute | solution.py:319
  14.9 4.3 %collective-permute-start.6 = (bf16[128,128]{1,0:T(8,128)(2,1)}, bf16[128,128]{1,0:T(8,128)(2,1)S(1)}, u32[]{:S(2)}, u32[]{:S(2)}) collective-permute-start(bf16[128,128]{1,0:T(8,128)(2,1)} %get-tuple-element.28), channel_id=1, source_target_pairs={{0,28},{4,0},{8,4},{12,8},{16,12},{20,16},{24,20},{28,24},{1,29},{... | collective-permute-start | bytes 98312 | tf_op jit(solution)/shard_map/ppermute | solution.py:319
  16.3 4.2 %collective-permute-start.7 = (bf16[128,128]{1,0:T(8,128)(2,1)}, bf16[128,128]{1,0:T(8,128)(2,1)S(1)}, u32[]{:S(2)}, u32[]{:S(2)}) collective-permute-start(bf16[128,128]{1,0:T(8,128)(2,1)} %get-tuple-element.21.refs_0_), channel_id=1, source_target_pairs={{0,2},{1,3},{2,0},{3,1},{4,6},{5,7},{6,4},{7,5},{8,10},{9,11},{10,... | collective-permute-start | bytes 98312 | tf_op jit(solution)/shard_map/ppermute | solution.py:323
  18.0 4.2 %collective-permute-start.8 = (bf16[128,128]{1,0:T(8,128)(2,1)S(1)}, bf16[128,128]{1,0:T(8,128)(2,1)S(1)}, u32[]{:S(2)}, u32[]{:S(2)}) collective-permute-start(bf16[128,128]{1,0:T(8,128)(2,1)S(1)} %collective-permute-done.refs_1_), channel_id=1, source_target_pairs={{0,2},{1,3},{2,0},{3,1},{4,6},{5,7},{6,4},{7,5},{8,10},{9,11},{10,... | collective-permute-start | bytes 98312 | tf_op jit(solution)/shard_map/ppermute | solution.py:323
  19.1 4.0 %collective-permute-start.9 = (bf16[128,128]{1,0:T(8,128)(2,1)S(1)}, bf16[128,128]{1,0:T(8,128)(2,1)S(1)}, u32[]{:S(2)}, u32[]{:S(2)}) collective-permute-start(bf16[128,128]{1,0:T(8,128)(2,1)S(1)} %collective-permute-done.1.refs_2_), channel_id=1, source_target_pairs={{0,2},{1,3},{2,0},{3,1},{4,6},{5,7},{6,4},{7,5},{8,10},{9,11},{10,... | collective-permute-start | bytes 98312 | tf_op jit(solution)/shard_map/ppermute | solution.py:323
  20.7 3.9 %collective-permute-start.10 = (bf16[128,128]{1,0:T(8,128)(2,1)S(1)}, bf16[128,128]{1,0:T(8,128)(2,1)S(1)}, u32[]{:S(2)}, u32[]{:S(2)}) collective-permute-start(bf16[128,128]{1,0:T(8,128)(2,1)S(1)} %collective-permute-done.2.refs_3_), channel_id=1, source_target_pairs={{0,2},{1,3},{2,0},{3,1},{4,6},{5,7},{6,4},{7,5},{8,10},{9,11},{10,... | collective-permute-start | bytes 98312 | tf_op jit(solution)/shard_map/ppermute | solution.py:323
  22.4 4.0 %collective-permute-start.11 = (bf16[128,128]{1,0:T(8,128)(2,1)S(1)}, bf16[128,128]{1,0:T(8,128)(2,1)S(1)}, u32[]{:S(2)}, u32[]{:S(2)}) collective-permute-start(bf16[128,128]{1,0:T(8,128)(2,1)S(1)} %collective-permute-done.3.refs_4_), channel_id=1, source_target_pairs={{0,2},{1,3},{2,0},{3,1},{4,6},{5,7},{6,4},{7,5},{8,10},{9,11},{10,... | collective-permute-start | bytes 98312 | tf_op jit(solution)/shard_map/ppermute | solution.py:323
  23.1 3.3 %collective-permute-start.20 = (bf16[128,128]{1,0:T(8,128)(2,1)S(1)}, bf16[128,128]{1,0:T(8,128)(2,1)S(1)}, u32[]{:S(2)}, u32[]{:S(2)}) collective-permute-start(bf16[128,128]{1,0:T(8,128)(2,1)S(1)} %collective-permute-done.4.refs_5_), channel_id=1, source_target_pairs={{0,1},{1,0},{2,3},{3,2},{4,5},{5,4},{6,7},{7,6},{8,9},{9,8},{10,11... | collective-permute-start | bytes 98312 | tf_op jit(solution)/shard_map/ppermute | solution.py:325
  23.3 3.9 %collective-permute-start.12 = (bf16[128,128]{1,0:T(8,128)(2,1)S(1)}, bf16[128,128]{1,0:T(8,128)(2,1)S(1)}, u32[]{:S(2)}, u32[]{:S(2)}) collective-permute-start(bf16[128,128]{1,0:T(8,128)(2,1)S(1)} %collective-permute-done.4.refs_5_), channel_id=1, source_target_pairs={{0,2},{1,3},{2,0},{3,1},{4,6},{5,7},{6,4},{7,5},{8,10},{9,11},{10,... | collective-permute-start | bytes 98312 | tf_op jit(solution)/shard_map/ppermute | solution.py:323
  24.7 3.9 %collective-permute-start.13 = (bf16[128,128]{1,0:T(8,128)(2,1)S(1)}, bf16[128,128]{1,0:T(8,128)(2,1)S(1)}, u32[]{:S(2)}, u32[]{:S(2)}) collective-permute-start(bf16[128,128]{1,0:T(8,128)(2,1)S(1)} %collective-permute-done.5.refs_6_), channel_id=1, source_target_pairs={{0,2},{1,3},{2,0},{3,1},{4,6},{5,7},{6,4},{7,5},{8,10},{9,11},{10,... | collective-permute-start | bytes 98312 | tf_op jit(solution)/shard_map/ppermute | solution.py:323
  26.5 3.9 %collective-permute-start.14 = (bf16[128,128]{1,0:T(8,128)(2,1)S(1)}, bf16[128,128]{1,0:T(8,128)(2,1)S(1)}, u32[]{:S(2)}, u32[]{:S(2)}) collective-permute-start(bf16[128,128]{1,0:T(8,128)(2,1)S(1)} %collective-permute-done.6.refs_7_), channel_id=1, source_target_pairs={{0,2},{1,3},{2,0},{3,1},{4,6},{5,7},{6,4},{7,5},{8,10},{9,11},{10,... | collective-permute-start | bytes 98312 | tf_op jit(solution)/shard_map/ppermute | solution.py:323
  27.2 3.7 %collective-permute-start.24 = (bf16[128,128]{1,0:T(8,128)(2,1)S(1)}, bf16[128,128]{1,0:T(8,128)(2,1)S(1)}, u32[]{:S(2)}, u32[]{:S(2)}) collective-permute-start(bf16[128,128]{1,0:T(8,128)(2,1)S(1)} %collective-permute-done.8.refs_9_), channel_id=1, source_target_pairs={{0,1},{1,0},{2,3},{3,2},{4,5},{5,4},{6,7},{7,6},{8,9},{9,8},{10,11... | collective-permute-start | bytes 98312 | tf_op jit(solution)/shard_map/ppermute | solution.py:325
  63.6 9.2 %collective-permute-start.31 = (f32[128,128]{1,0:T(8,128)S(1)}, f32[128,128]{1,0:T(8,128)S(1)}, u32[]{:S(2)}, u32[]{:S(2)}) collective-permute-start(f32[128,128]{1,0:T(8,128)S(1)} %get-tuple-element.30), channel_id=1, source_target_pairs={{0,4},{4,8},{8,12},{12,16},{16,20},{20,24},{24,28},{28,0},{1,5},{5... | collective-permute-start | bytes 196616 | tf_op jit(solution)/shard_map/ppermute | solution.py:467
  64.8 8.0 %collective-permute-start.32 = (f32[128,128]{1,0:T(8,128)S(1)}, f32[128,128]{1,0:T(8,128)S(1)}, u32[]{:S(2)}, u32[]{:S(2)}) collective-permute-start(f32[128,128]{1,0:T(8,128)S(1)} %get-tuple-element.31), channel_id=1, source_target_pairs={{0,8},{4,12},{8,16},{12,20},{16,24},{20,28},{24,0},{28,4},{1,9},{5... | collective-permute-start | bytes 196616 | tf_op jit(solution)/shard_map/ppermute | solution.py:467
  64.9 11.5 %collective-permute-start.33 = (f32[128,128]{1,0:T(8,128)S(1)}, f32[128,128]{1,0:T(8,128)S(1)}, u32[]{:S(2)}, u32[]{:S(2)}) collective-permute-start(f32[128,128]{1,0:T(8,128)S(1)} %get-tuple-element.32), channel_id=1, source_target_pairs={{0,12},{4,16},{8,20},{12,24},{16,28},{20,0},{24,4},{28,8},{1,13},{... | collective-permute-start | bytes 196616 | tf_op jit(solution)/shard_map/ppermute | solution.py:467
  68.1 8.4 %collective-permute-start.34 = (f32[128,128]{1,0:T(8,128)S(1)}, f32[128,128]{1,0:T(8,128)S(1)}, u32[]{:S(2)}, u32[]{:S(2)}) collective-permute-start(f32[128,128]{1,0:T(8,128)S(1)} %get-tuple-element.33), channel_id=1, source_target_pairs={{0,16},{4,20},{8,24},{12,28},{16,0},{20,4},{24,8},{28,12},{1,17},{... | collective-permute-start | bytes 196616 | tf_op jit(solution)/shard_map/ppermute | solution.py:467
  69.8 8.5 %collective-permute-start.35 = (f32[128,128]{1,0:T(8,128)S(1)}, f32[128,128]{1,0:T(8,128)S(1)}, u32[]{:S(2)}, u32[]{:S(2)}) collective-permute-start(f32[128,128]{1,0:T(8,128)S(1)} %get-tuple-element.34), channel_id=1, source_target_pairs={{0,20},{4,24},{8,28},{12,0},{16,4},{20,8},{24,12},{28,16},{1,21},{... | collective-permute-start | bytes 196616 | tf_op jit(solution)/shard_map/ppermute | solution.py:467
  72.8 6.2 %collective-permute-start.36 = (f32[128,128]{1,0:T(8,128)S(1)}, f32[128,128]{1,0:T(8,128)S(1)}, u32[]{:S(2)}, u32[]{:S(2)}) collective-permute-start(f32[128,128]{1,0:T(8,128)S(1)} %get-tuple-element.35), channel_id=1, source_target_pairs={{0,24},{4,28},{8,0},{12,4},{16,8},{20,12},{24,16},{28,20},{1,25},{... | collective-permute-start | bytes 196616 | tf_op jit(solution)/shard_map/ppermute | solution.py:467
  72.9 6.2 %collective-permute-start.37 = (f32[128,128]{1,0:T(8,128)S(1)}, f32[128,128]{1,0:T(8,128)S(1)}, u32[]{:S(2)}, u32[]{:S(2)}) collective-permute-start(f32[128,128]{1,0:T(8,128)S(1)} %get-tuple-element.36), channel_id=1, source_target_pairs={{0,28},{4,0},{8,4},{12,8},{16,12},{20,16},{24,20},{28,24},{1,29},{... | collective-permute-start | bytes 196616 | tf_op jit(solution)/shard_map/ppermute | solution.py:467
  (30 other events, 60.9 us)

commit v3 on v2

--- a/solution.py
+++ b/solution.py
@@ -59,30 +59,46 @@
     return jnp.dot(left, right, preferred_element_type=jnp.float32)
 
 
-def force_kernel(
-    sizes,
-    where_ref,
-    match_ref,
-    centers_ref,
-    *refs,
-):
-    side, rounds, own_count, slab_count, pair_count = sizes
-    block_count = slab_count * pair_count
+def partner_of(index, step, count):
+    if count & (count - 1) == 0:
+        return index ^ step, index ^ step
+    return (index + step) % count, (index + count - step) % count
+
+
+def slab_step(turn, core):
+    return CORES * turn + CORES - 1 - core
+
+
+def block_places(slab_index, pair_index, slab_count, pair_count):
+    chips = pair_count // CORES
+    chip = pair_index // CORES
+    for core_step in range(CORES):
+        core = (pair_index + core_step) % CORES
+        for chip_step in range(chips):
+            for turn in range(slab_count // CORES):
+                step = slab_step(turn, core)
+                yield (chip + chips - chip_step) % chips, partner_of(slab_index, step, slab_count)[1]
+
+
+def force_kernel(sizes, match_ref, centers_ref, *refs):
+    slab_count, pair_count = sizes[3:]
+    block_count = slab_count * pair_count // CORES
     block_refs = refs[:block_count]
     constant_refs = refs[block_count : block_count + 5]
     out_refs = refs[block_count + 5 : block_count + 5 + slab_count]
     scratch = refs[block_count + 5 + slab_count :]
-    force_body(sizes, where_ref, match_ref, centers_ref, block_refs, constant_refs, out_refs, *scratch)
+    force_body(sizes, match_ref, centers_ref, block_refs, constant_refs, out_refs, *scratch)
 
 
 def force_body(
     sizes,
-    where_ref,
-    match_ref,
-    centers_ref,
+    match_hbm,
+    centers_hbm,
     block_refs,
     constant_refs,
     out_refs,
+    match_ref,
+    centers_ref,
     boxes_ref,
     mix_high_ref,
     mix_low_ref,
@@ -109,14 +125,15 @@
     group_rows = group * side
     cells = tiles * LANES
     width = 2 * LANES
-
-    slab_index = where_ref[0]
-    pair_index = where_ref[1]
+    slab_index = lax.axis_index("slab")
+    pair_index = lax.axis_index("pair")
+
+    targets = [boxes_ref.at[place] for place in block_places(slab_index, pair_index, slab_count, pair_count)]
+    sources = list(block_refs) + [match_hbm, centers_hbm]
+    targets += [match_ref, centers_ref]
     copies = []
-    for index, (pair, slab) in enumerate(block_places(slab_index, pair_index, slab_count, pair_count)):
-        copies.append(
-            pltpu.make_async_copy(block_refs[index], boxes_ref.at[pair, slab], sems.at[index])
-        )
+    for source, target in zip(sources, targets):
+        copies.append(pltpu.make_async_copy(source, target, sems.at[len(copies)]))
     constants = (mix_high_ref, mix_low_ref, gain_ref, basis_high, basis_low)
     constant_copies = []
     for index, (source, target) in enumerate(zip(constant_refs, constants)):
@@ -143,18 +160,18 @@
     for copy in copies:
         copy.wait()
 
-    def unpack(index, carry):
-        pair = index // slab_count
+    def spread(index, carry):
+        chip = index // slab_count
         slab = index % slab_count
-        for chunk in range(own_count * planes // 2):
-            block = boxes_ref[pair, slab, 16 * chunk : 16 * chunk + 16, :].astype(jnp.float32)
+        for chunk in range(CORES * own_count * planes // 2):
+            block = boxes_ref[chip, slab, 16 * chunk : 16 * chunk + 16, :].astype(jnp.float32)
             for half in range(2):
-                own, plane = divmod(2 * chunk + half, planes)
-                start = (pair * own_count + own) * tiles * pitch + REACH + slab * planes + plane
+                member, plane = divmod(2 * chunk + half, planes)
+                start = (chip * CORES * own_count + member) * tiles * pitch + REACH + slab * planes + plane
                 fields[pl.ds(start, tiles, stride=pitch), :] = block[8 * half : 8 * half + 8, :]
         return carry
 
-    lax.fori_loop(0, pair_count * slab_count, unpack, 0)
+    lax.fori_loop(0, pair_count // CORES * slab_count, spread, 0)
 
     lane = lax.broadcasted_iota(jnp.int32, (side, LANES), 1)
     lane_row = lax.broadcasted_iota(jnp.int32, (1, LANES), 1)
@@ -172,17 +189,20 @@
         keep = lane >= part
         return [jnp.where(keep, moved[t], moved[(t - 1) % tiles]) for t in range(tiles)]
 
+    def orbital_of(member):
+        return (member // own_count * slab_count + slab_index) * own_count + member % own_count
+
     def geometry(index):
         own = index // rounds
         turn = index % rounds
         member = pair_index * own_count + own
-        mate = match_ref[turn, member]
+        mate = match_ref[0, turn, member]
         own_offset = []
         mate_offset = []
         distance = 0
         for axis in range(3):
-            mine = centers_ref[member, axis]
-            other = centers_ref[mate, axis]
+            mine = centers_ref[axis, orbital_of(member)]
+            other = centers_ref[axis, orbital_of(mate)]
             anchor = (mine + other) >> 1
             own_offset.append(mine - anchor)
             mate_offset.append(other - anchor)
@@ -292,7 +312,7 @@
     lax.fori_loop(0, own_count, collect, 0)
 
     for step in range(slab_count):
-        slab = (slab_index + step) % slab_count
+        slab = partner_of(slab_index, step, slab_count)[0]
         for own in range(own_count):
             for plane in range(planes):
                 start = own * tiles * side + slab * planes + plane
@@ -300,98 +320,110 @@
                 out_refs[step][row : row + tiles, :] = total[pl.ds(start, tiles, stride=side), :]
 
 
-def block_places(slab_index, pair_index, slab_count, pair_count):
-    chips = pair_count // CORES
-    chip = pair_index // CORES
-    core = pair_index % CORES
-    for core_step in range(CORES):
-        for chip_step in range(chips):
-            pair = (chip + chips - chip_step) % chips * CORES + (core + core_step) % CORES
-            for step in range(slab_count):
-                yield pair, (slab_index + slab_count - step) % slab_count
-
-
 def gather_boxes(blocks, slab_count, pair_count):
     chips = pair_count // CORES
-    own = [blocks[0]]
-    for step in range(1, slab_count):
-        perm = [(i, (i + step) % slab_count) for i in range(slab_count)]
-        own.append(lax.ppermute(blocks[step], "slab", perm))
+    own = []
+    for turn, block in enumerate(blocks):
+        perm = []
+        for slab in range(slab_count):
+            for pair in range(pair_count):
+                target = partner_of(slab, slab_step(turn, pair % CORES), slab_count)[0]
+                perm.append((slab * pair_count + pair, target * pair_count + pair))
+        own.append((turn, lax.ppermute(block, ("slab", "pair"), perm)))
     pieces = [own]
     for step in range(1, chips):
         perm = [(i, (i + step * CORES) % pair_count) for i in range(pair_count)]
-        pieces.append([lax.ppermute(block, "pair", perm) for block in own])
-    swap = [(i, i ^ 1) for i in range(pair_count)]
-    other = [[lax.ppermute(block, "pair", swap) for block in piece] for piece in pieces]
-    return [block for piece in pieces + other for block in piece]
-
-
-def pack_kernel(sizes, where_ref, orbitals_ref, *refs):
+        pieces.append([(turn, lax.ppermute(block, "pair", perm)) for turn, block in own])
+    other = [[(turn, swap_cores(block, pair_count)) for turn, block in piece] for piece in pieces]
+    return [block for piece in pieces + other for _, block in sorted(piece, key=lambda item: item[0])]
+
+
+def swap_cores(block, pair_count):
+    return lax.ppermute(block, "pair", [(i, i ^ 1) for i in range(pair_count)])
+
+
+def pack_kernel(sizes, *refs):
     own_count, slab_count = sizes
-    out_refs, lines = refs[:slab_count], refs[slab_count]
-    row_count, cells = orbitals_ref.shape
+    orbital_refs, out_refs, lines = refs[:CORES], refs[CORES:-1], refs[-1]
+    row_count, cells = orbital_refs[0].shape
     tiles = cells // LANES
-    for tile in range(tiles):
-        columns = slice(tile * LANES, (tile + 1) * LANES)
-        lines[tile * row_count : (tile + 1) * row_count, :] = orbitals_ref[:, columns].astype(jnp.float32)
-    for step in range(slab_count):
-        first = (where_ref[0] + step) % slab_count * own_count
-        for chunk in range(own_count * tiles // 16):
+    slab_index = lax.axis_index("slab")
+    core = lax.axis_index("pair") % CORES
+    for side in range(CORES):
+        base = (core ^ side) * tiles * row_count
+        for tile in range(tiles):
+            columns = slice(tile * LANES, (tile + 1) * LANES)
+            rows = pl.ds(pl.multiple_of(base + tile * row_count, 8), row_count)
+            lines[rows, :] = orbital_refs[side][:, columns].astype(jnp.float32)
+    for turn, out_ref in enumerate(out_refs):
+        first = partner_of(slab_index, slab_step(turn, core), slab_count)[0] * own_count
+        for chunk in range(CORES * own_count * tiles // 16):
             halves = []
             for half in range(2):
-                own, tile = divmod(16 * chunk + 8 * half, tiles)
-                halves.append(lines[pl.ds(tile * row_count + first + own, 8, stride=row_count), :])
-            out_refs[step][16 * chunk : 16 * chunk + 16, :] = jnp.concatenate(halves, axis=0).astype(
-                jnp.bfloat16
-            )
-
-
-def pack(place, orbitals, own_count, slab_count):
+                member, tile = divmod(16 * chunk + 8 * half, tiles)
+                side, own = divmod(member, own_count)
+                start = (side * tiles + tile) * row_count + first + own
+                halves.append(lines[pl.ds(start, 8, stride=row_count), :])
+            block = jnp.concatenate(halves, axis=0).astype(jnp.bfloat16)
+            out_ref[16 * chunk : 16 * chunk + 16, :] = block
+
+
+def pack(orbitals, other, own_count, slab_count):
     row_count, cells = orbitals.shape
-    rows = own_count * cells // LANES
+    rows = CORES * own_count * cells // LANES
     vectors = pl.BlockSpec(memory_space=pltpu.VMEM)
+    turns = slab_count // CORES
     return pl.pallas_call(
         functools.partial(pack_kernel, (own_count, slab_count)),
-        out_shape=[jax.ShapeDtypeStruct((rows, LANES), jnp.bfloat16)] * slab_count,
-        in_specs=[pl.BlockSpec(memory_space=pltpu.SMEM), vectors],
-        out_specs=[vectors] * slab_count,
-        scratch_shapes=[pltpu.VMEM((row_count * cells // LANES, LANES), jnp.float32)],
-    )(place, orbitals)
-
-
-def unpack_kernel(sizes, where_ref, *refs):
+        out_shape=[jax.ShapeDtypeStruct((rows, LANES), jnp.bfloat16)] * turns,
+        in_specs=[vectors] * CORES,
+        out_specs=[vectors] * turns,
+        scratch_shapes=[pltpu.VMEM((CORES * row_count * cells // LANES, LANES), jnp.float32)],
+    )(orbitals, other)
+
+
+def unpack_kernel(sizes, *refs):
     own_count, slab_count = sizes
-    block_refs, out_ref, lines = refs[:slab_count], refs[slab_count], refs[slab_count + 1]
+    block_refs, out_ref, blocks, lines, sems = refs[:slab_count], *refs[slab_count:]
     row_count, cells = out_ref.shape
     tiles = cells // LANES
+    slab_index = lax.axis_index("slab")
+    copies = []
     for step in range(slab_count):
-        first = (where_ref[0] + slab_count - step) % slab_count * own_count
+        copies.append(pltpu.make_async_copy(block_refs[step], blocks.at[step], sems.at[step]))
+        copies[-1].start()
+    for step in range(slab_count):
+        copies[step].wait()
+        first = partner_of(slab_index, step, slab_count)[1] * own_count
         for own in range(own_count):
             for tile in range(0, tiles, 8):
                 start = tile * row_count + first + own
                 row = own * tiles + tile
-                lines[pl.ds(start, 8, stride=row_count), :] = block_refs[step][row : row + 8, :]
+                lines[pl.ds(start, 8, stride=row_count), :] = blocks[step, row : row + 8, :]
     for tile in range(tiles):
         columns = slice(tile * LANES, (tile + 1) * LANES)
         out_ref[:, columns] = lines[tile * row_count : (tile + 1) * row_count, :]
 
 
-def unpack(place, blocks, own_count, cells):
+def unpack(blocks, own_count, cells):
     slab_count = len(blocks)
     row_count = own_count * slab_count
-    vectors = pl.BlockSpec(memory_space=pltpu.VMEM)
     return pl.pallas_call(
         functools.partial(unpack_kernel, (own_count, slab_count)),
         out_shape=jax.ShapeDtypeStruct((row_count, cells), jnp.float32),
-        in_specs=[pl.BlockSpec(memory_space=pltpu.SMEM)] + [vectors] * slab_count,
-        out_specs=vectors,
-        scratch_shapes=[pltpu.VMEM((row_count * cells // LANES, LANES), jnp.float32)],
-    )(place, *blocks)
-
-
-def team_forces(place, match, centers, blocks, side, slab_count, pair_count):
-    rounds, team = match.shape
-    rows = blocks[0].shape[0]
+        in_specs=[pl.BlockSpec(memory_space=pl.ANY)] * slab_count,
+        out_specs=pl.BlockSpec(memory_space=pltpu.VMEM),
+        scratch_shapes=[
+            pltpu.VMEM((slab_count,) + blocks[0].shape, jnp.float32),
+            pltpu.VMEM((row_count * cells // LANES, LANES), jnp.float32),
+            pltpu.SemaphoreType.DMA((slab_count,)),
+        ],
+    )(*blocks)
+
+
+def team_forces(match, centers, blocks, side, slab_count, pair_count):
+    _, rounds, team = match.shape
+    rows = blocks[0].shape[0] // CORES
     own_count = team // pair_count
     tiles = side * side // LANES
     solves = own_count * rounds
@@ -403,17 +435,20 @@
     basis_high, basis_low = split_constant(np.kron(basis, basis))
     gain = chebyshev_gain(side)
     sizes = (side, rounds, own_count, slab_count, pair_count)
-    scalars = pl.BlockSpec(memory_space=pltpu.SMEM)
+    either = pl.BlockSpec(memory_space=pl.ANY)
+    distant = pl.BlockSpec(memory_space=pltpu.HBM)
     vectors = pl.BlockSpec(memory_space=pltpu.VMEM)
     wide = pltpu.VMEM((solves * side, cells), jnp.bfloat16)
     flops = 2 * solves * side * 3 * 2 * (cells * cells + cells * group * side)
     return pl.pallas_call(
         functools.partial(force_kernel, sizes),
         out_shape=[jax.ShapeDtypeStruct((rows, LANES), jnp.float32)] * slab_count,
-        in_specs=[scalars] * 3 + [pl.BlockSpec(memory_space=pl.ANY)] * (len(blocks) + 5),
+        in_specs=[distant] * 2 + [either] * len(blocks) + [distant] * 5,
         out_specs=[vectors] * slab_count,
         scratch_shapes=[
-            pltpu.VMEM((pair_count, slab_count, rows, LANES), jnp.bfloat16),
+            pltpu.SMEM(match.shape, jnp.int32),
+            pltpu.SMEM(centers.shape, jnp.int32),
+            pltpu.VMEM((pair_count // CORES, slab_count, CORES * rows, LANES), jnp.bfloat16),
             pltpu.VMEM((group * side, group * side), jnp.bfloat16),
             pltpu.VMEM((group * side, group * side), jnp.bfloat16),
             pltpu.VMEM((side, cells), jnp.float32),
@@ -427,12 +462,11 @@
             pltpu.VMEM((own_count * tiles * side, LANES), jnp.float32),
             pltpu.VMEM((cells, cells), jnp.bfloat16),
             pltpu.VMEM((cells, cells), jnp.bfloat16),
-            pltpu.SemaphoreType.DMA((len(blocks) + 5,)),
+            pltpu.SemaphoreType.DMA((len(blocks) + 7,)),
         ],
         compiler_params=pltpu.CompilerParams(vmem_limit_bytes=40 * 1024 * 1024),
         cost_estimate=pl.CostEstimate(flops=flops, bytes_accessed=8 * 1024 * 1024, transcendentals=0),
     )(
-        place,
         match,
         centers,
         *blocks,
@@ -447,25 +481,18 @@
 def shards(orbitals, centers, matchings):
     slab_count = lax.axis_size("slab")
     pair_count = lax.axis_size("pair")
-    slab_index = lax.axis_index("slab")
-    pair_index = lax.axis_index("pair")
     local_rows, plane_cells = orbitals.shape
     own_count = local_rows // slab_count
     side = round((plane_cells * slab_count) ** (1.0 / 3.0))
-    match = matchings[0]
-    team = match.shape[1]
-    team_centers = lax.dynamic_index_in_dim(
-        centers.reshape(pair_count, slab_count, own_count, 3), slab_index, 1, keepdims=False
-    ).reshape(team, 3)
-    place = jnp.stack([slab_index, pair_index]).astype(jnp.int32)
-    blocks = pack(place, orbitals, own_count, slab_count)
+    other = swap_cores(orbitals, pair_count)
+    blocks = pack(orbitals, other, own_count, slab_count)
     team_blocks = gather_boxes(blocks, slab_count, pair_count)
-    forces = team_forces(place, match, team_centers, team_blocks, side, slab_count, pair_count)
+    forces = team_forces(matchings, centers.T, team_blocks, side, slab_count, pair_count)
     received = [forces[0]]
     for step in range(1, slab_count):
-        perm = [(i, (i + step) % slab_count) for i in range(slab_count)]
+        perm = [(i, partner_of(i, step, slab_count)[0]) for i in range(slab_count)]
         received.append(lax.ppermute(forces[step], "slab", perm))
-    return unpack(place, received, own_count, plane_cells)
+    return unpack(received, own_count, plane_cells)
 
 
 def solution(mesh):

time: 82.5 us -> 77.1 us (0.935)
  starting transfers between devices: 36.7 us -> 27.5 us
  waiting for transfers between devices: 7.53 us -> 13.7 us
  Pallas kernels: 27.1 us -> 26.2 us
  local copies, waits for them, and re-layouts: 10.1 us -> 9.21 us
    ppermute x31 -> x17, starting transfers between devices: 26 us -> 16.4 us  [the longest x4 9.92 us: gather_boxes(): own.append((turn, lax.ppermute(block, ('slab', 'pair'), perm)))]
    ppermute x31 -> x17, waiting for transfers between devices: 2.81 us -> 9.7 us  [the longest x4 3.79 us: gather_boxes(): own.append((turn, lax.ppermute(block, ('slab', 'pair'), perm)))]
    reshape x2 -> x0, local copies, waits for them, and re-layouts: 0.89 us -> none  [the longest x1 0.78 us: shards(): centers.reshape(pair_count, slab_count, own_count, 3)]
    pallas_call x1, Pallas kernels: 22.7 us -> 21.9 us  [team_forces(): pl.pallas_call(functools.partial(force_kernel, sizes), out_shape=[jax.Sha...]
  transfers between devices with their start and end apart: 38 -> 24, of which waited for: 13 -> 9; matrix products, arithmetic and copies ran while one was open for 1% -> 0% of each run, Pallas kernels for 0% -> 0%
where the time goes in v3:
time: 77.1 us; the launch traced here: 76.7 us
  starting transfers between devices  27.5 us (36%)
  Pallas kernels  26.2 us (34%)
  waiting for transfers between devices  13.7 us (18%)
  local copies, waits for them, and re-layouts  9.21 us (12%)
    pallas_call x1, Pallas kernels, team_forces(): pl.pallas_call(functools.partial(force_kernel, sizes), out_shape=[jax.Sha...  21.9 us
    ppermute x7, starting transfers between devices, shards(): received.append(lax.ppermute(forces[step], 'slab', perm))  11.1 us
    ppermute x4, starting transfers between devices, gather_boxes(): own.append((turn, lax.ppermute(block, ('slab', 'pair'), perm)))  9.92 us
    unnamed x32, local copies, waits for them, and re-layouts  9.21 us
    ppermute x4, starting transfers between devices, gather_boxes(): lax.ppermute(block, 'pair', perm)  5.17 us
    ppermute x7, waiting for transfers between devices, shards(): received.append(lax.ppermute(forces[step], 'slab', perm))  3.99 us
    ppermute x4, waiting for transfers between devices, gather_boxes(): own.append((turn, lax.ppermute(block, ('slab', 'pair'), perm)))  3.79 us
    ppermute x4, waiting for transfers between devices, gather_boxes(): lax.ppermute(block, 'pair', perm)  3.29 us
  transfers between devices with their start and end apart: 24, of which 9 were waited for; matrix products, arithmetic and copies ran while one was open for 0% of the time, Pallas kernels for 0%

profile of v3, /device:TPU:0, one launch (start us, length us, event | category | flops | bytes accessed | tf_op | source)
XLA Modules:
  0.0 76.7 jit_solution(13769507585872142839)
XLA Ops:
  0.5 1.4 %collective-permute-done.refs_1_ = bf16[32,4096]{1,0:T(8,128)(2,1)S(1)} collective-permute-done((bf16[32,4096]{1,0:T(8,128)(2,1)}, bf16[32,4096]{1,0:T(8,128)(2,1)S(1)}, u32[]{:S(2)}, u32[]{:S(2)}) %collective-permute-start) | collective-permute-done | bytes 262176 | tf_op jit(solution)/shard_map/ppermute | solution.py:342
  2.5 2.1 %shard_map.82 = (bf16[256,128]{1,0:T(8,128)(2,1)}, bf16[256,128]{1,0:T(8,128)(2,1)}, bf16[256,128]{1,0:T(8,128)(2,1)}, bf16[256,128]{1,0:T(8,128)(2,1)}) custom-call(bf16[32,4096]{1,0:T(8,128)(2,1)} %refs_0_.1, bf16[32,4096]{1,0:T(8,128)(2,1)} %copy-done.8), custom_call_target="tpu_custom_call" | custom-call | tf_op jit(solution)/shard_map/pallas_call | solution.py:376
  4.6 4.8 %collective-permute-start.1 = (bf16[256,128]{1,0:T(8,128)(2,1)}, bf16[256,128]{1,0:T(8,128)(2,1)S(1)}, u32[]{:S(2)}, u32[]{:S(2)}) collective-permute-start(bf16[256,128]{1,0:T(8,128)(2,1)} %get-tuple-element.17), channel_id=1, source_target_pairs={{0,4},{1,1},{2,6},{3,3},{4,0},{5,5},{6,2},{7,7},{8,12},{9,9},{10,1... | collective-permute-start | bytes 196616 | tf_op jit(solution)/shard_map/ppermute | solution.py:332
  9.4 1.6 %collective-permute-start.2 = (bf16[256,128]{1,0:T(8,128)(2,1)}, bf16[256,128]{1,0:T(8,128)(2,1)S(1)}, u32[]{:S(2)}, u32[]{:S(2)}) collective-permute-start(bf16[256,128]{1,0:T(8,128)(2,1)} %get-tuple-element.18), channel_id=1, source_target_pairs={{0,12},{1,9},{2,14},{3,11},{4,8},{5,13},{6,10},{7,15},{8,4},{9,1},... | collective-permute-start | bytes 196616 | tf_op jit(solution)/shard_map/ppermute | solution.py:332
  11.0 3.5 %collective-permute-start.3 = (bf16[256,128]{1,0:T(8,128)(2,1)}, bf16[256,128]{1,0:T(8,128)(2,1)S(1)}, u32[]{:S(2)}, u32[]{:S(2)}) collective-permute-start(bf16[256,128]{1,0:T(8,128)(2,1)} %get-tuple-element.19), channel_id=1, source_target_pairs={{0,20},{1,17},{2,22},{3,19},{4,16},{5,21},{6,18},{7,23},{8,28},{9,... | collective-permute-start | bytes 196616 | tf_op jit(solution)/shard_map/ppermute | solution.py:332
  14.6 1.6 %collective-permute-start.5 = (bf16[256,128]{1,0:T(8,128)(2,1)S(1)}, bf16[256,128]{1,0:T(8,128)(2,1)S(1)}, u32[]{:S(2)}, u32[]{:S(2)}) collective-permute-start(bf16[256,128]{1,0:T(8,128)(2,1)S(1)} %collective-permute-done.1.refs_0_), channel_id=1, source_target_pairs={{0,2},{1,3},{2,0},{3,1},{4,6},{5,7},{6,4},{7,5},{8,10},{9,11},{10,... | collective-permute-start | bytes 196616 | tf_op jit(solution)/shard_map/ppermute | solution.py:336
  16.4 2.2 %collective-permute-done.3.refs_2_ = bf16[256,128]{1,0:T(8,128)(2,1)S(1)} collective-permute-done((bf16[256,128]{1,0:T(8,128)(2,1)}, bf16[256,128]{1,0:T(8,128)(2,1)S(1)}, u32[]{:S(2)}, u32[]{:S(2)}) %collective-permute-start.3) | collective-permute-done | bytes 65568 | tf_op jit(solution)/shard_map/ppermute | solution.py:332
  18.7 1.5 %collective-permute-start.6 = (bf16[256,128]{1,0:T(8,128)(2,1)S(1)}, bf16[256,128]{1,0:T(8,128)(2,1)S(1)}, u32[]{:S(2)}, u32[]{:S(2)}) collective-permute-start(bf16[256,128]{1,0:T(8,128)(2,1)S(1)} %collective-permute-done.2.refs_1_), channel_id=1, source_target_pairs={{0,2},{1,3},{2,0},{3,1},{4,6},{5,7},{6,4},{7,5},{8,10},{9,11},{10,... | collective-permute-start | bytes 196616 | tf_op jit(solution)/shard_map/ppermute | solution.py:336
  20.2 1.5 %collective-permute-done.4.refs_3_ = bf16[256,128]{1,0:T(8,128)(2,1)S(1)} collective-permute-done((bf16[256,128]{1,0:T(8,128)(2,1)}, bf16[256,128]{1,0:T(8,128)(2,1)S(1)}, u32[]{:S(2)}, u32[]{:S(2)}) %collective-permute-start.4) | collective-permute-done | bytes 65568 | tf_op jit(solution)/shard_map/ppermute | solution.py:332
  21.7 1.5 %collective-permute-start.7 = (bf16[256,128]{1,0:T(8,128)(2,1)S(1)}, bf16[256,128]{1,0:T(8,128)(2,1)S(1)}, u32[]{:S(2)}, u32[]{:S(2)}) collective-permute-start(bf16[256,128]{1,0:T(8,128)(2,1)S(1)} %collective-permute-done.3.refs_2_), channel_id=1, source_target_pairs={{0,2},{1,3},{2,0},{3,1},{4,6},{5,7},{6,4},{7,5},{8,10},{9,11},{10,... | collective-permute-start | bytes 196616 | tf_op jit(solution)/shard_map/ppermute | solution.py:336
  24.3 2.1 %collective-permute-done.7.refs_6_ = bf16[256,128]{1,0:T(8,128)(2,1)S(1)} collective-permute-done((bf16[256,128]{1,0:T(8,128)(2,1)S(1)}, bf16[256,128]{1,0:T(8,128)(2,1)S(1)}, u32[]{:S(2)}, u32[]{:S(2)}) %collective-permute-start.7) | collective-permute-done | bytes 65568 | tf_op jit(solution)/shard_map/ppermute | solution.py:336
  26.4 1.2 %collective-permute-done.8.refs_7_ = bf16[256,128]{1,0:T(8,128)(2,1)S(1)} collective-permute-done((bf16[256,128]{1,0:T(8,128)(2,1)S(1)}, bf16[256,128]{1,0:T(8,128)(2,1)S(1)}, u32[]{:S(2)}, u32[]{:S(2)}) %collective-permute-start.8) | collective-permute-done | bytes 65568 | tf_op jit(solution)/shard_map/ppermute | solution.py:336
  27.7 1.2 %collective-permute-done.16.refs_15_ = bf16[256,128]{1,0:T(8,128)(2,1)S(1)} collective-permute-done((bf16[256,128]{1,0:T(8,128)(2,1)S(1)}, bf16[256,128]{1,0:T(8,128)(2,1)S(1)}, u32[]{:S(2)}, u32[]{:S(2)}) %collective-permute-start.16) | collective-permute-done | bytes 65568 | tf_op jit(solution)/shard_map/ppermute | solution.py:342
  30.2 1.6 %copy-done.3 = bf16[1024,1024]{1,0:T(8,128)(2,1)S(1)} copy-done((bf16[1024,1024]{1,0:T(8,128)(2,1)S(1)}, bf16[1024,1024]{1,0:T(8,128)(2,1)}, u32[]{:S(2)}) %copy-start.3) | copy-done | bytes 2097176
  31.8 1.6 %copy-done.4 = bf16[1024,1024]{1,0:T(8,128)(2,1)S(1)} copy-done((bf16[1024,1024]{1,0:T(8,128)(2,1)S(1)}, bf16[1024,1024]{1,0:T(8,128)(2,1)}, u32[]{:S(2)}) %copy-start.4) | copy-done | bytes 2097176
  33.4 0.9 %copy-done.5 = f32[32,1024]{1,0:T(8,128)S(1)} copy-done((f32[32,1024]{1,0:T(8,128)S(1)}, f32[32,1024]{1,0:T(8,128)}, u32[]{:S(2)}) %copy-start.5) | copy-done | bytes 131096
  34.3 0.9 %copy-done.6 = bf16[256,256]{1,0:T(8,128)(2,1)S(1)} copy-done((bf16[256,256]{1,0:T(8,128)(2,1)S(1)}, bf16[256,256]{1,0:T(8,128)(2,1)}, u32[]{:S(2)}) %copy-start.6) | copy-done | bytes 131096
  36.1 21.9 %shard_map.83 = (f32[128,128]{1,0:T(8,128)S(1)}, f32[128,128]{1,0:T(8,128)S(1)}, f32[128,128]{1,0:T(8,128)S(1)}, f32[128,128]{1,0:T(8,128)S(1)}, f32[128,128]{1,...) custom-call(s32[1,4,16]{2,1,0:T(4,128)S(1)} %copy-done.1, ...), custom_call_target="tpu_custom_call" | custom-call | flops 8053063680 | bytes 8388608 | tf_op jit(solution)/shard_map/pallas_call | solution.py:443
  59.2 3.0 %collective-permute-start.19 = (f32[128,128]{1,0:T(8,128)S(1)}, f32[128,128]{1,0:T(8,128)S(1)}, u32[]{:S(2)}, u32[]{:S(2)}) collective-permute-start(f32[128,128]{1,0:T(8,128)S(1)} %get-tuple-element.24), channel_id=1, source_target_pairs={{0,12},{4,8},{8,4},{12,0},{16,28},{20,24},{24,20},{28,16},{1,13},{... | collective-permute-start | bytes 196616 | tf_op jit(solution)/shard_map/ppermute | solution.py:494
  62.2 2.9 %collective-permute-start.21 = (f32[128,128]{1,0:T(8,128)S(1)}, f32[128,128]{1,0:T(8,128)S(1)}, u32[]{:S(2)}, u32[]{:S(2)}) collective-permute-start(f32[128,128]{1,0:T(8,128)S(1)} %get-tuple-element.26), channel_id=1, source_target_pairs={{0,20},{4,16},{8,28},{12,24},{16,4},{20,0},{24,12},{28,8},{1,21},{... | collective-permute-start | bytes 196616 | tf_op jit(solution)/shard_map/ppermute | solution.py:494
  65.9 3.9 %collective-permute-start.23 = (f32[128,128]{1,0:T(8,128)S(1)}, f32[128,128]{1,0:T(8,128)S(1)}, u32[]{:S(2)}, u32[]{:S(2)}) collective-permute-start(f32[128,128]{1,0:T(8,128)S(1)} %get-tuple-element.28), channel_id=1, source_target_pairs={{0,28},{4,24},{8,20},{12,16},{16,12},{20,8},{24,4},{28,0},{1,29},{... | collective-permute-start | bytes 196616 | tf_op jit(solution)/shard_map/ppermute | solution.py:494
  69.8 1.3 %collective-permute-done.20.refs_4_ = f32[128,128]{1,0:T(8,128)S(1)} collective-permute-done((f32[128,128]{1,0:T(8,128)S(1)}, f32[128,128]{1,0:T(8,128)S(1)}, u32[]{:S(2)}, u32[]{:S(2)}) %collective-permute-start.20) | collective-permute-done | bytes 65568 | tf_op jit(solution)/shard_map/ppermute | solution.py:494
  71.1 2.7 %collective-permute-done.21.refs_5_ = f32[128,128]{1,0:T(8,128)S(1)} collective-permute-done((f32[128,128]{1,0:T(8,128)S(1)}, f32[128,128]{1,0:T(8,128)S(1)}, u32[]{:S(2)}, u32[]{:S(2)}) %collective-permute-start.21) | collective-permute-done | bytes 65568 | tf_op jit(solution)/shard_map/ppermute | solution.py:494
  74.5 2.2 %shard_map.84 = f32[32,4096]{1,0:T(8,128)} custom-call(f32[128,128]{1,0:T(8,128)} %copy-done, f32[128,128]{1,0:T(8,128)} %copy-done.9, f32[128,128]{1,0:T(8,128)} %copy-done.10, f32[128,128]{1,0:T(8,128)} %copy-done.11, f32[128,128]{1,0:T(8,128)} %copy-done.12, f32[128,128]{1,0:T(8,128)} %copy-done.13, f32[128,128]{1,0:T(8,128)} %copy-done.14, ...), custom_call_target="tpu_custom_call" | custom-call | tf_op jit(solution)/shard_map/pallas_call | solution.py:411
  (59 shorter events, 7.5 us)
Async XLA Ops:
  0.0 1.8 %collective-permute-start = (bf16[32,4096]{1,0:T(8,128)(2,1)}, bf16[32,4096]{1,0:T(8,128)(2,1)S(1)}, u32[]{:S(2)}, u32[]{:S(2)}) collective-permute-start(bf16[32,4096]{1,0:T(8,128)(2,1)} %refs_0_.1), channel_id=1, source_target_pairs={{0,1},{1,0},{2,3},{3,2},{4,5},{5,4},{6,7},{7,6},{8,9},{9,8},{10,11... | collective-permute-start | bytes 786440 | tf_op jit(solution)/shard_map/ppermute | solution.py:342
  4.6 9.9 %collective-permute-start.1 = (bf16[256,128]{1,0:T(8,128)(2,1)}, bf16[256,128]{1,0:T(8,128)(2,1)S(1)}, u32[]{:S(2)}, u32[]{:S(2)}) collective-permute-start(bf16[256,128]{1,0:T(8,128)(2,1)} %get-tuple-element.17), channel_id=1, source_target_pairs={{0,4},{1,1},{2,6},{3,3},{4,0},{5,5},{6,2},{7,7},{8,12},{9,9},{10,1... | collective-permute-start | bytes 196616 | tf_op jit(solution)/shard_map/ppermute | solution.py:332
  9.4 6.8 %collective-permute-start.2 = (bf16[256,128]{1,0:T(8,128)(2,1)}, bf16[256,128]{1,0:T(8,128)(2,1)S(1)}, u32[]{:S(2)}, u32[]{:S(2)}) collective-permute-start(bf16[256,128]{1,0:T(8,128)(2,1)} %get-tuple-element.18), channel_id=1, source_target_pairs={{0,12},{1,9},{2,14},{3,11},{4,8},{5,13},{6,10},{7,15},{8,4},{9,1},... | collective-permute-start | bytes 196616 | tf_op jit(solution)/shard_map/ppermute | solution.py:332
  11.0 7.7 %collective-permute-start.3 = (bf16[256,128]{1,0:T(8,128)(2,1)}, bf16[256,128]{1,0:T(8,128)(2,1)S(1)}, u32[]{:S(2)}, u32[]{:S(2)}) collective-permute-start(bf16[256,128]{1,0:T(8,128)(2,1)} %get-tuple-element.19), channel_id=1, source_target_pairs={{0,20},{1,17},{2,22},{3,19},{4,16},{5,21},{6,18},{7,23},{8,28},{9,... | collective-permute-start | bytes 196616 | tf_op jit(solution)/shard_map/ppermute | solution.py:332
  14.5 7.2 %collective-permute-start.4 = (bf16[256,128]{1,0:T(8,128)(2,1)}, bf16[256,128]{1,0:T(8,128)(2,1)S(1)}, u32[]{:S(2)}, u32[]{:S(2)}) collective-permute-start(bf16[256,128]{1,0:T(8,128)(2,1)} %get-tuple-element.20), channel_id=1, source_target_pairs={{0,28},{1,25},{2,30},{3,27},{4,24},{5,29},{6,26},{7,31},{8,20},{9,... | collective-permute-start | bytes 196616 | tf_op jit(solution)/shard_map/ppermute | solution.py:332
  14.5 7.2 %collective-permute-start.9 = (bf16[256,128]{1,0:T(8,128)(2,1)S(1)}, bf16[256,128]{1,0:T(8,128)(2,1)S(1)}, u32[]{:S(2)}, u32[]{:S(2)}) collective-permute-start(bf16[256,128]{1,0:T(8,128)(2,1)S(1)} %collective-permute-done.1.refs_0_), channel_id=1, source_target_pairs={{0,1},{1,0},{2,3},{3,2},{4,5},{5,4},{6,7},{7,6},{8,9},{9,8},{10,11... | collective-permute-start | bytes 196616 | tf_op jit(solution)/shard_map/ppermute | solution.py:342
  14.6 8.7 %collective-permute-start.5 = (bf16[256,128]{1,0:T(8,128)(2,1)S(1)}, bf16[256,128]{1,0:T(8,128)(2,1)S(1)}, u32[]{:S(2)}, u32[]{:S(2)}) collective-permute-start(bf16[256,128]{1,0:T(8,128)(2,1)S(1)} %collective-permute-done.1.refs_0_), channel_id=1, source_target_pairs={{0,2},{1,3},{2,0},{3,1},{4,6},{5,7},{6,4},{7,5},{8,10},{9,11},{10,... | collective-permute-start | bytes 196616 | tf_op jit(solution)/shard_map/ppermute | solution.py:336
  16.2 7.5 %collective-permute-start.10 = (bf16[256,128]{1,0:T(8,128)(2,1)S(1)}, bf16[256,128]{1,0:T(8,128)(2,1)S(1)}, u32[]{:S(2)}, u32[]{:S(2)}) collective-permute-start(bf16[256,128]{1,0:T(8,128)(2,1)S(1)} %collective-permute-done.2.refs_1_), channel_id=1, source_target_pairs={{0,1},{1,0},{2,3},{3,2},{4,5},{5,4},{6,7},{7,6},{8,9},{9,8},{10,11... | collective-permute-start | bytes 196616 | tf_op jit(solution)/shard_map/ppermute | solution.py:342
  18.7 5.1 %collective-permute-start.6 = (bf16[256,128]{1,0:T(8,128)(2,1)S(1)}, bf16[256,128]{1,0:T(8,128)(2,1)S(1)}, u32[]{:S(2)}, u32[]{:S(2)}) collective-permute-start(bf16[256,128]{1,0:T(8,128)(2,1)S(1)} %collective-permute-done.2.refs_1_), channel_id=1, source_target_pairs={{0,2},{1,3},{2,0},{3,1},{4,6},{5,7},{6,4},{7,5},{8,10},{9,11},{10,... | collective-permute-start | bytes 196616 | tf_op jit(solution)/shard_map/ppermute | solution.py:336
  21.7 2.6 %collective-permute-start.11 = (bf16[256,128]{1,0:T(8,128)(2,1)S(1)}, bf16[256,128]{1,0:T(8,128)(2,1)S(1)}, u32[]{:S(2)}, u32[]{:S(2)}) collective-permute-start(bf16[256,128]{1,0:T(8,128)(2,1)S(1)} %collective-permute-done.3.refs_2_), channel_id=1, source_target_pairs={{0,1},{1,0},{2,3},{3,2},{4,5},{5,4},{6,7},{7,6},{8,9},{9,8},{10,11... | collective-permute-start | bytes 196616 | tf_op jit(solution)/shard_map/ppermute | solution.py:342
  21.7 4.7 %collective-permute-start.7 = (bf16[256,128]{1,0:T(8,128)(2,1)S(1)}, bf16[256,128]{1,0:T(8,128)(2,1)S(1)}, u32[]{:S(2)}, u32[]{:S(2)}) collective-permute-start(bf16[256,128]{1,0:T(8,128)(2,1)S(1)} %collective-permute-done.3.refs_2_), channel_id=1, source_target_pairs={{0,2},{1,3},{2,0},{3,1},{4,6},{5,7},{6,4},{7,5},{8,10},{9,11},{10,... | collective-permute-start | bytes 196616 | tf_op jit(solution)/shard_map/ppermute | solution.py:336
  23.2 4.4 %collective-permute-start.8 = (bf16[256,128]{1,0:T(8,128)(2,1)S(1)}, bf16[256,128]{1,0:T(8,128)(2,1)S(1)}, u32[]{:S(2)}, u32[]{:S(2)}) collective-permute-start(bf16[256,128]{1,0:T(8,128)(2,1)S(1)} %collective-permute-done.4.refs_3_), channel_id=1, source_target_pairs={{0,2},{1,3},{2,0},{3,1},{4,6},{5,7},{6,4},{7,5},{8,10},{9,11},{10,... | collective-permute-start | bytes 196616 | tf_op jit(solution)/shard_map/ppermute | solution.py:336
  23.8 3.9 %collective-permute-start.12 = (bf16[256,128]{1,0:T(8,128)(2,1)S(1)}, bf16[256,128]{1,0:T(8,128)(2,1)S(1)}, u32[]{:S(2)}, u32[]{:S(2)}) collective-permute-start(bf16[256,128]{1,0:T(8,128)(2,1)S(1)} %collective-permute-done.4.refs_3_), channel_id=1, source_target_pairs={{0,1},{1,0},{2,3},{3,2},{4,5},{5,4},{6,7},{7,6},{8,9},{9,8},{10,11... | collective-permute-start | bytes 196616 | tf_op jit(solution)/shard_map/ppermute | solution.py:342
  23.8 3.9 %collective-permute-start.13 = (bf16[256,128]{1,0:T(8,128)(2,1)S(1)}, bf16[256,128]{1,0:T(8,128)(2,1)S(1)}, u32[]{:S(2)}, u32[]{:S(2)}) collective-permute-start(bf16[256,128]{1,0:T(8,128)(2,1)S(1)} %collective-permute-done.5.refs_4_), channel_id=1, source_target_pairs={{0,1},{1,0},{2,3},{3,2},{4,5},{5,4},{6,7},{7,6},{8,9},{9,8},{10,11... | collective-permute-start | bytes 196616 | tf_op jit(solution)/shard_map/ppermute | solution.py:342
  24.3 3.4 %collective-permute-start.14 = (bf16[256,128]{1,0:T(8,128)(2,1)S(1)}, bf16[256,128]{1,0:T(8,128)(2,1)S(1)}, u32[]{:S(2)}, u32[]{:S(2)}) collective-permute-start(bf16[256,128]{1,0:T(8,128)(2,1)S(1)} %collective-permute-done.6.refs_5_), channel_id=1, source_target_pairs={{0,1},{1,0},{2,3},{3,2},{4,5},{5,4},{6,7},{7,6},{8,9},{9,8},{10,11... | collective-permute-start | bytes 196616 | tf_op jit(solution)/shard_map/ppermute | solution.py:342
  26.4 1.3 %collective-permute-start.15 = (bf16[256,128]{1,0:T(8,128)(2,1)S(1)}, bf16[256,128]{1,0:T(8,128)(2,1)S(1)}, u32[]{:S(2)}, u32[]{:S(2)}) collective-permute-start(bf16[256,128]{1,0:T(8,128)(2,1)S(1)} %collective-permute-done.7.refs_6_), channel_id=1, source_target_pairs={{0,1},{1,0},{2,3},{3,2},{4,5},{5,4},{6,7},{7,6},{8,9},{9,8},{10,11... | collective-permute-start | bytes 196616 | tf_op jit(solution)/shard_map/ppermute | solution.py:342
  27.6 1.3 %collective-permute-start.16 = (bf16[256,128]{1,0:T(8,128)(2,1)S(1)}, bf16[256,128]{1,0:T(8,128)(2,1)S(1)}, u32[]{:S(2)}, u32[]{:S(2)}) collective-permute-start(bf16[256,128]{1,0:T(8,128)(2,1)S(1)} %collective-permute-done.8.refs_7_), channel_id=1, source_target_pairs={{0,1},{1,0},{2,3},{3,2},{4,5},{5,4},{6,7},{7,6},{8,9},{9,8},{10,11... | collective-permute-start | bytes 196616 | tf_op jit(solution)/shard_map/ppermute | solution.py:342
  58.7 6.4 %collective-permute-start.17 = (f32[128,128]{1,0:T(8,128)S(1)}, f32[128,128]{1,0:T(8,128)S(1)}, u32[]{:S(2)}, u32[]{:S(2)}) collective-permute-start(f32[128,128]{1,0:T(8,128)S(1)} %get-tuple-element.22), channel_id=1, source_target_pairs={{0,4},{4,0},{8,12},{12,8},{16,20},{20,16},{24,28},{28,24},{1,5},{5... | collective-permute-start | bytes 196616 | tf_op jit(solution)/shard_map/ppermute | solution.py:494
  59.2 6.7 %collective-permute-start.18 = (f32[128,128]{1,0:T(8,128)S(1)}, f32[128,128]{1,0:T(8,128)S(1)}, u32[]{:S(2)}, u32[]{:S(2)}) collective-permute-start(f32[128,128]{1,0:T(8,128)S(1)} %get-tuple-element.23), channel_id=1, source_target_pairs={{0,8},{4,12},{8,0},{12,4},{16,24},{20,28},{24,16},{28,20},{1,9},{5... | collective-permute-start | bytes 196616 | tf_op jit(solution)/shard_map/ppermute | solution.py:494
  59.2 10.7 %collective-permute-start.19 = (f32[128,128]{1,0:T(8,128)S(1)}, f32[128,128]{1,0:T(8,128)S(1)}, u32[]{:S(2)}, u32[]{:S(2)}) collective-permute-start(f32[128,128]{1,0:T(8,128)S(1)} %get-tuple-element.24), channel_id=1, source_target_pairs={{0,12},{4,8},{8,4},{12,0},{16,28},{20,24},{24,20},{28,16},{1,13},{... | collective-permute-start | bytes 196616 | tf_op jit(solution)/shard_map/ppermute | solution.py:494
  62.2 9.0 %collective-permute-start.20 = (f32[128,128]{1,0:T(8,128)S(1)}, f32[128,128]{1,0:T(8,128)S(1)}, u32[]{:S(2)}, u32[]{:S(2)}) collective-permute-start(f32[128,128]{1,0:T(8,128)S(1)} %get-tuple-element.25), channel_id=1, source_target_pairs={{0,16},{4,20},{8,24},{12,28},{16,0},{20,4},{24,8},{28,12},{1,17},{... | collective-permute-start | bytes 196616 | tf_op jit(solution)/shard_map/ppermute | solution.py:494
  62.2 11.6 %collective-permute-start.21 = (f32[128,128]{1,0:T(8,128)S(1)}, f32[128,128]{1,0:T(8,128)S(1)}, u32[]{:S(2)}, u32[]{:S(2)}) collective-permute-start(f32[128,128]{1,0:T(8,128)S(1)} %get-tuple-element.26), channel_id=1, source_target_pairs={{0,20},{4,16},{8,28},{12,24},{16,4},{20,0},{24,12},{28,8},{1,21},{... | collective-permute-start | bytes 196616 | tf_op jit(solution)/shard_map/ppermute | solution.py:494
  65.0 8.8 %collective-permute-start.22 = (f32[128,128]{1,0:T(8,128)S(1)}, f32[128,128]{1,0:T(8,128)S(1)}, u32[]{:S(2)}, u32[]{:S(2)}) collective-permute-start(f32[128,128]{1,0:T(8,128)S(1)} %get-tuple-element.27), channel_id=1, source_target_pairs={{0,24},{4,28},{8,16},{12,20},{16,8},{20,12},{24,0},{28,4},{1,25},{... | collective-permute-start | bytes 196616 | tf_op jit(solution)/shard_map/ppermute | solution.py:494
  65.9 7.9 %collective-permute-start.23 = (f32[128,128]{1,0:T(8,128)S(1)}, f32[128,128]{1,0:T(8,128)S(1)}, u32[]{:S(2)}, u32[]{:S(2)}) collective-permute-start(f32[128,128]{1,0:T(8,128)S(1)} %get-tuple-element.28), channel_id=1, source_target_pairs={{0,28},{4,24},{8,20},{12,16},{16,12},{20,8},{24,4},{28,0},{1,29},{... | collective-permute-start | bytes 196616 | tf_op jit(solution)/shard_map/ppermute | solution.py:494
  (16 other events, 34.0 us)

commit v4 on v3

--- a/solution.py
+++ b/solution.py
@@ -84,9 +84,9 @@
     slab_count, pair_count = sizes[3:]
     block_count = slab_count * pair_count // CORES
     block_refs = refs[:block_count]
-    constant_refs = refs[block_count : block_count + 5]
-    out_refs = refs[block_count + 5 : block_count + 5 + slab_count]
-    scratch = refs[block_count + 5 + slab_count :]
+    constant_refs = refs[block_count : block_count + 6]
+    out_refs = refs[block_count + 6 : block_count + 6 + slab_count]
+    scratch = refs[block_count + 6 + slab_count :]
     force_body(sizes, match_ref, centers_ref, block_refs, constant_refs, out_refs, *scratch)
 
 
@@ -100,19 +100,18 @@
     match_ref,
     centers_ref,
     boxes_ref,
-    mix_high_ref,
-    mix_low_ref,
+    mix_ref,
     gain_ref,
+    there_high,
+    there_low,
+    back_high,
+    back_low,
     fields,
     partner,
-    first_high,
-    first_low,
-    second_high,
-    second_low,
+    first,
+    second,
     terms,
     total,
-    basis_high,
-    basis_low,
     sems,
 ):
     side, rounds, own_count, slab_count, pair_count = sizes
@@ -134,7 +133,7 @@
     copies = []
     for source, target in zip(sources, targets):
         copies.append(pltpu.make_async_copy(source, target, sems.at[len(copies)]))
-    constants = (mix_high_ref, mix_low_ref, gain_ref, basis_high, basis_low)
+    constants = (mix_ref, gain_ref, there_high, there_low, back_high, back_low)
     constant_copies = []
     for index, (source, target) in enumerate(zip(constant_refs, constants)):
         constant_copies.append(pltpu.make_async_copy(source, target, sems.at[len(copies) + index]))
@@ -173,21 +172,32 @@
 
     lax.fori_loop(0, pair_count // CORES * slab_count, spread, 0)
 
-    lane = lax.broadcasted_iota(jnp.int32, (side, LANES), 1)
+    step_rows = 16
+    lane = lax.broadcasted_iota(jnp.int32, (step_rows, LANES), 1)
     lane_row = lax.broadcasted_iota(jnp.int32, (1, LANES), 1)
     lane_line = lane_row // side
     lane_point = lane_row % side
 
-    def rolled(ref, base, offset_x, offset_flat):
+    def rolled(ref, base, row, offset_x, offset_flat):
         whole = (offset_flat >> 7) & (tiles - 1)
         part = offset_flat & (LANES - 1)
-        start = base * pitch + REACH - offset_x
+        start = base * pitch + REACH + row - offset_x
         moved = []
         for tile in range(tiles):
-            row = start + ((tile - whole) & (tiles - 1)) * pitch
-            moved.append(pltpu.roll(ref[pl.ds(row, side), :], part, axis=1))
+            first_row = start + ((tile - whole) & (tiles - 1)) * pitch
+            moved.append(pltpu.roll(ref[pl.ds(first_row, step_rows), :], part, axis=1))
         keep = lane >= part
         return [jnp.where(keep, moved[t], moved[(t - 1) % tiles]) for t in range(tiles)]
+
+    def mirrored(tile):
+        line = lax.broadcasted_iota(jnp.int32, tile.shape, 1) // side
+        result = None
+        for index in range(lines):
+            amount = (2 * index - lines + 1) * side % LANES
+            if index < 2:
+                moved = pltpu.roll(tile, amount, axis=1)
+                result = moved if result is None else jnp.where(line % 2 == index, moved, result)
+        return result
 
     def orbital_of(member):
         return (member // own_count * slab_count + slab_index) * own_count + member % own_count
@@ -209,107 +219,114 @@
             distance = distance + (mine - other) * (mine - other)
         return own, member, mate, own_offset, mate_offset, distance <= CUT2
 
-    def densities(index, carry):
+    row_count = solves * side
+    half_tiles = tiles // 2
+    half_cells = cells // 2
+
+    def store_split(ref, start, count, columns, value):
+        high, low = split_pair(value)
+        if isinstance(start, int):
+            ref[start : start + count, columns] = high
+            ref[row_count + start : row_count + start + count, columns] = low
+        else:
+            ref[pl.ds(pl.multiple_of(start, count), count), columns] = high
+            ref[pl.ds(pl.multiple_of(row_count + start, count), count), columns] = low
+
+    def densities(step, carry):
+        index = step // (side // step_rows)
+        row = step % (side // step_rows) * step_rows
         own, member, mate, a, b, active = geometry(index)
-        mine = rolled(fields, member * tiles, a[0], a[1] * side + a[2])
-        other = rolled(fields, mate * tiles, b[0], b[1] * side + b[2])
+        mine = rolled(fields, member * tiles, row, a[0], a[1] * side + a[2])
+        other = rolled(fields, mate * tiles, row, b[0], b[1] * side + b[2])
         low_line = jnp.maximum(jnp.maximum(a[1], b[1]), 0)
         high_line = jnp.where(active, side + jnp.minimum(jnp.minimum(a[1], b[1]), 0), 0)
         low_point = jnp.maximum(jnp.maximum(a[2], b[2]), 0)
         high_point = side + jnp.minimum(jnp.minimum(a[2], b[2]), 0)
         point_ok = (lane_point >= low_point) & (lane_point < high_point)
-        rows = pl.ds(pl.multiple_of(index * side, side), side)
+        start = step * step_rows
+        rows = pl.ds(pl.multiple_of(start, step_rows), step_rows)
+        density = []
         for tile in range(tiles):
             line = lane_line + tile * lines
             ok = jnp.where(point_ok & (line >= low_line) & (line < high_line), 1.0, 0.0)
             masked = other[tile] * ok
-            columns = slice(tile * LANES, (tile + 1) * LANES)
-            partner[rows, columns] = masked.astype(jnp.bfloat16)
-            high, low = split_pair(mine[tile] * masked)
-            first_high[rows, columns] = high
-            first_low[rows, columns] = low
+            partner[rows, tile * LANES : (tile + 1) * LANES] = masked.astype(jnp.bfloat16)
+            density.append(mine[tile] * masked)
+        for tile in range(half_tiles):
+            mirror = mirrored(density[tiles - 1 - tile])
+            for parity, value in enumerate((density[tile] + mirror, density[tile] - mirror)):
+                column = parity * half_cells + tile * LANES
+                store_split(first, start, step_rows, slice(column, column + LANES), value)
         return carry
 
-    lax.fori_loop(0, solves, densities, 0)
+    lax.fori_loop(0, solves * side // step_rows, densities, 0, unroll=2)
 
     for copy in constant_copies:
         copy.wait()
-    mix_high = mix_high_ref[...]
-    mix_low = mix_low_ref[...]
-    column_steps = cells // width
-    group_steps = solves // group
-
-    def block_of(index):
-        rows = pl.ds(pl.multiple_of((index // column_steps) * group_rows, group_rows), group_rows)
-        columns = pl.ds(pl.multiple_of((index % column_steps) * width, width), width)
-        return rows, columns
-
-    def along_x(index, carry):
-        rows, columns = block_of(index)
-        high = first_high[rows, columns]
-        low = first_low[rows, columns]
-        value = dot(mix_high, high) + (dot(mix_high, low) + dot(mix_low, high))
-        second_high[rows, columns], second_low[rows, columns] = split_pair(value)
-        return carry
-
-    lax.fori_loop(0, group_steps * column_steps, along_x, 0)
-
-    def in_plane(index, source_high, source_low):
-        rows, columns = block_of(index)
-        high = source_high[rows, :]
-        low = source_low[rows, :]
-        basis = basis_high[:, columns]
-        return dot(high, basis) + (dot(low, basis) + dot(high, basis_low[:, columns]))
-
-    def forward(index, carry):
-        rows, columns = block_of(index)
-        value = in_plane(index, second_high, second_low)
-        gain = gain_ref[:, columns]
-        value = (value.reshape(group, side, width) * gain[None]).reshape(group_rows, width)
-        first_high[rows, columns], first_low[rows, columns] = split_pair(value)
-        return carry
-
-    lax.fori_loop(0, group_steps * column_steps, forward, 0)
-
-    def backward(index, carry):
-        rows, columns = block_of(index)
-        value = in_plane(index, first_high, first_low)
-        second_high[rows, columns], second_low[rows, columns] = split_pair(value)
-        return carry
-
-    lax.fori_loop(0, group_steps * column_steps, backward, 0)
-
-    def back_along_x(index, carry):
-        rows, columns = block_of(index)
-        high = second_high[rows, columns]
-        low = second_low[rows, columns]
-        value = dot(mix_high, high) + (dot(mix_high, low) + dot(mix_low, high))
-        value = value * partner[rows, columns].astype(jnp.float32)
-        first_solve = (index // column_steps) * group
-        first_tile = (index % column_steps) * 2
-        for solve in range(group):
-            for half in range(2):
-                start = ((first_solve + solve) * tiles + first_tile + half) * pitch + REACH
-                terms[pl.ds(pl.multiple_of(start, 8), side), :] = value[
-                    solve * side : (solve + 1) * side, half * LANES : (half + 1) * LANES
-                ]
-        return carry
-
-    lax.fori_loop(0, group_steps * column_steps, back_along_x, 0)
-
-    def collect(own, carry):
+
+    def along_x(start, columns, source):
+        high = source[start : start + group_rows, columns]
+        low = source[row_count + start : row_count + start + group_rows, columns]
+        value = dot(mix_ref[...], high)
+        return value[:group_rows] + (value[group_rows:] + dot(mix_ref[:group_rows, :], low))
+
+    def in_plane(parity, columns, source, high_ref, low_ref):
+        inner = slice(parity * half_cells, (parity + 1) * half_cells)
+        value = dot(source[:, inner], high_ref[parity, :, columns])
+        rest = dot(source[:row_count, inner], low_ref[parity, :, columns])
+        return value[:row_count] + (value[row_count:] + rest)
+
+    for start in range(0, row_count, group_rows):
+        for column in range(0, cells, width):
+            columns = slice(column, column + width)
+            store_split(second, start, group_rows, columns, along_x(start, columns, first))
+
+    for parity in range(2):
+        for column in range(0, half_cells, width):
+            columns = slice(column, column + width)
+            value = in_plane(parity, columns, second, there_high, there_low)
+            columns = slice(parity * half_cells + column, parity * half_cells + column + width)
+            gain = gain_ref[:, columns]
+            value = (value.reshape(solves, side, width) * gain[None]).reshape(row_count, width)
+            store_split(first, 0, row_count, columns, value)
+
+    for parity in range(2):
+        for column in range(0, half_cells, width):
+            value = in_plane(parity, slice(column, column + width), first, back_high, back_low)
+            columns = slice(parity * half_cells + column, parity * half_cells + column + width)
+            store_split(second, 0, row_count, columns, value)
+
+    for start in range(0, row_count, group_rows):
+        for column in range(0, half_cells, width):
+            even = along_x(start, slice(column, column + width), second)
+            odd = along_x(start, slice(half_cells + column, half_cells + column + width), second)
+            for part in range(width // LANES):
+                tile = column // LANES + part
+                lanes = slice(part * LANES, (part + 1) * LANES)
+                near = even[:, lanes] + odd[:, lanes]
+                far = mirrored(even[:, lanes] - odd[:, lanes])
+                for place, value in ((tile, near), (tiles - 1 - tile, far)):
+                    columns = slice(place * LANES, (place + 1) * LANES)
+                    value = value * partner[start : start + group_rows, columns].astype(jnp.float32)
+                    for solve in range(group):
+                        row = ((start // side + solve) * tiles + place) * pitch + REACH
+                        terms[row : row + side, :] = value[solve * side : (solve + 1) * side, :]
+
+    def collect(step, carry):
+        own = step // (side // step_rows)
+        row = step % (side // step_rows) * step_rows
         sums = None
         for turn in range(rounds):
             index = own * rounds + turn
             _, _, _, a, _, _ = geometry(index)
-            term = rolled(terms, index * tiles, -a[0], -(a[1] * side + a[2]))
+            term = rolled(terms, index * tiles, row, -a[0], -(a[1] * side + a[2]))
             sums = term if sums is None else [s + t for s, t in zip(sums, term)]
         for tile in range(tiles):
-            start = (own * tiles + tile) * side
-            total[pl.ds(pl.multiple_of(start, side), side), :] = sums[tile]
+            start = (own * tiles + tile) * side + row
+            total[pl.ds(pl.multiple_of(start, step_rows), step_rows), :] = sums[tile]
         return carry
 
-    lax.fori_loop(0, own_count, collect, 0)
+    lax.fori_loop(0, own_count * side // step_rows, collect, 0)
 
     for step in range(slab_count):
         slab = partner_of(slab_index, step, slab_count)[0]
@@ -323,7 +340,8 @@
 def gather_boxes(blocks, slab_count, pair_count):
     chips = pair_count // CORES
     own = []
-    for turn, block in enumerate(blocks):
+    for turn in reversed(range(len(blocks))):
+        block = blocks[turn]
         perm = []
         for slab in range(slab_count):
             for pair in range(pair_count):
@@ -431,50 +449,42 @@
     cells = side * side
     pitch = side + 2 * REACH
     basis = sine_basis(side)
-    mix_high, mix_low = split_constant(np.kron(np.eye(group), basis))
-    basis_high, basis_low = split_constant(np.kron(basis, basis))
-    gain = chebyshev_gain(side)
+    mix = np.concatenate(split_constant(np.kron(np.eye(group), basis)), axis=0)
+    there = np.stack([np.kron(basis[parity::2, : side // 2].T, basis) for parity in range(2)])
+    gain = chebyshev_gain(side).reshape(side, side, side)
+    gain = np.concatenate([gain[:, parity::2].reshape(side, -1) for parity in range(2)], axis=1)
+    constants = (mix, gain, *split_constant(there), *split_constant(there.transpose(0, 2, 1)))
     sizes = (side, rounds, own_count, slab_count, pair_count)
     either = pl.BlockSpec(memory_space=pl.ANY)
     distant = pl.BlockSpec(memory_space=pltpu.HBM)
     vectors = pl.BlockSpec(memory_space=pltpu.VMEM)
-    wide = pltpu.VMEM((solves * side, cells), jnp.bfloat16)
-    flops = 2 * solves * side * 3 * 2 * (cells * cells + cells * group * side)
+    wide = pltpu.VMEM((2 * solves * side, cells), jnp.bfloat16)
+    flops = 2 * solves * side * 3 * 2 * (cells * cells // 2 + cells * group * side)
     return pl.pallas_call(
         functools.partial(force_kernel, sizes),
         out_shape=[jax.ShapeDtypeStruct((rows, LANES), jnp.float32)] * slab_count,
-        in_specs=[distant] * 2 + [either] * len(blocks) + [distant] * 5,
+        in_specs=[distant] * 2 + [either] * len(blocks) + [distant] * len(constants),
         out_specs=[vectors] * slab_count,
         scratch_shapes=[
             pltpu.SMEM(match.shape, jnp.int32),
             pltpu.SMEM(centers.shape, jnp.int32),
             pltpu.VMEM((pair_count // CORES, slab_count, CORES * rows, LANES), jnp.bfloat16),
-            pltpu.VMEM((group * side, group * side), jnp.bfloat16),
-            pltpu.VMEM((group * side, group * side), jnp.bfloat16),
-            pltpu.VMEM((side, cells), jnp.float32),
+            *[pltpu.VMEM(constant.shape, constant.dtype) for constant in constants],
             pltpu.VMEM((team * tiles * pitch, LANES), jnp.float32),
-            wide,
-            wide,
-            wide,
+            pltpu.VMEM((solves * side, cells), jnp.bfloat16),
             wide,
             wide,
             pltpu.VMEM((solves * tiles * pitch, LANES), jnp.float32),
             pltpu.VMEM((own_count * tiles * side, LANES), jnp.float32),
-            pltpu.VMEM((cells, cells), jnp.bfloat16),
-            pltpu.VMEM((cells, cells), jnp.bfloat16),
-            pltpu.SemaphoreType.DMA((len(blocks) + 7,)),
+            pltpu.SemaphoreType.DMA((len(blocks) + 2 + len(constants),)),
         ],
-        compiler_params=pltpu.CompilerParams(vmem_limit_bytes=40 * 1024 * 1024),
+        compiler_params=pltpu.CompilerParams(vmem_limit_bytes=60 * 1024 * 1024),
         cost_estimate=pl.CostEstimate(flops=flops, bytes_accessed=8 * 1024 * 1024, transcendentals=0),
     )(
         match,
         centers,
         *blocks,
-        jnp.asarray(mix_high),
-        jnp.asarray(mix_low),
-        jnp.asarray(gain),
-        jnp.asarray(basis_high),
-        jnp.asarray(basis_low),
+        *[jnp.asarray(constant) for constant in constants],
     )
 
 
@@ -489,9 +499,9 @@
     team_blocks = gather_boxes(blocks, slab_count, pair_count)
     forces = team_forces(matchings, centers.T, team_blocks, side, slab_count, pair_count)
     received = [forces[0]]
-    for step in range(1, slab_count):
+    for step in reversed(range(1, slab_count)):
         perm = [(i, partner_of(i, step, slab_count)[0]) for i in range(slab_count)]
-        received.append(lax.ppermute(forces[step], "slab", perm))
+        received.insert(1, lax.ppermute(forces[step], "slab", perm))
     return unpack(received, own_count, plane_cells)
 
 

time: 77.1 us -> 62.8 us (0.81)
  local copies, waits for them, and re-layouts: 9.21 us -> 1.87 us
  Pallas kernels: 26.2 us -> 19.1 us
    unnamed x32 -> x48, local copies, waits for them, and re-layouts: 9.21 us -> 1.87 us
    pallas_call x1, Pallas kernels: 21.9 us -> 14.8 us  [team_forces(): pl.pallas_call(functools.partial(force_kernel, sizes), out_shape=[jax.Sha...]
  transfers between devices with their start and end apart: 24 -> 24, of which waited for: 9 -> 8; matrix products, arithmetic and copies ran while one was open for 0% -> 0% of each run, Pallas kernels for 0% -> 0%
where the time goes in v4:
time: 62.8 us; the launch traced here: 62.6 us
  starting transfers between devices  27.6 us (44%)
  Pallas kernels  19.1 us (30%)
  waiting for transfers between devices  13.7 us (22%)
  local copies, waits for them, and re-layouts  1.87 us (3%)
    pallas_call x1, Pallas kernels, team_forces(): pl.pallas_call(functools.partial(force_kernel, sizes), out_shape=[jax.Sha...  14.8 us
    ppermute x7, starting transfers between devices, shards(): received.insert(1, lax.ppermute(forces[step], 'slab', perm))  11.2 us
    ppermute x4, starting transfers between devices, gather_boxes(): own.append((turn, lax.ppermute(block, ('slab', 'pair'), perm)))  9.92 us
    ppermute x4, starting transfers between devices, gather_boxes(): lax.ppermute(block, 'pair', perm)  5.22 us
    ppermute x7, waiting for transfers between devices, shards(): received.insert(1, lax.ppermute(forces[step], 'slab', perm))  4.18 us
    ppermute x4, waiting for transfers between devices, gather_boxes(): own.append((turn, lax.ppermute(block, ('slab', 'pair'), perm)))  3.79 us
    ppermute x4, waiting for transfers between devices, gather_boxes(): lax.ppermute(block, 'pair', perm)  3.2 us
    ppermute x9, waiting for transfers between devices, swap_cores(): return lax.ppermute(block, 'pair', [(i, i ^ 1) for i in range(pair_count)])  2.58 us
  transfers between devices with their start and end apart: 24, of which 8 were waited for; matrix products, arithmetic and copies ran while one was open for 0% of the time, Pallas kernels for 0%

profile of v4, /device:TPU:0, one launch (start us, length us, event | category | flops | bytes accessed | tf_op | source)
XLA Modules:
  0.0 62.6 jit_solution(6270159145114699146)
XLA Ops:
  0.5 1.4 %collective-permute-done.refs_1_ = bf16[32,4096]{1,0:T(8,128)(2,1)S(1)} collective-permute-done((bf16[32,4096]{1,0:T(8,128)(2,1)}, bf16[32,4096]{1,0:T(8,128)(2,1)S(1)}, u32[]{:S(2)}, u32[]{:S(2)}) %collective-permute-start) | collective-permute-done | bytes 262176 | tf_op jit(solution)/shard_map/ppermute | solution.py:360
  1.8 0.7 %copy-done = bf16[32,4096]{1,0:T(8,128)(2,1)} copy-done((bf16[32,4096]{1,0:T(8,128)(2,1)}, bf16[32,4096]{1,0:T(8,128)(2,1)S(1)}, u32[]{:S(2)}) %copy-start) | copy-done | bytes 262168
  2.5 2.1 %shard_map.91 = (bf16[256,128]{1,0:T(8,128)(2,1)}, bf16[256,128]{1,0:T(8,128)(2,1)}, bf16[256,128]{1,0:T(8,128)(2,1)}, bf16[256,128]{1,0:T(8,128)(2,1)}) custom-call(bf16[32,4096]{1,0:T(8,128)(2,1)} %refs_0_.1, bf16[32,4096]{1,0:T(8,128)(2,1)} %copy-done), custom_call_target="tpu_custom_call" | custom-call | tf_op jit(solution)/shard_map/pallas_call | solution.py:394
  4.6 4.8 %collective-permute-start.1 = (bf16[256,128]{1,0:T(8,128)(2,1)}, bf16[256,128]{1,0:T(8,128)(2,1)S(1)}, u32[]{:S(2)}, u32[]{:S(2)}) collective-permute-start(bf16[256,128]{1,0:T(8,128)(2,1)} %get-tuple-element.17), channel_id=1, source_target_pairs={{0,4},{1,1},{2,6},{3,3},{4,0},{5,5},{6,2},{7,7},{8,12},{9,9},{10,1... | collective-permute-start | bytes 196616 | tf_op jit(solution)/shard_map/ppermute | solution.py:350
  9.4 1.6 %collective-permute-start.2 = (bf16[256,128]{1,0:T(8,128)(2,1)}, bf16[256,128]{1,0:T(8,128)(2,1)S(1)}, u32[]{:S(2)}, u32[]{:S(2)}) collective-permute-start(bf16[256,128]{1,0:T(8,128)(2,1)} %get-tuple-element.18), channel_id=1, source_target_pairs={{0,12},{1,9},{2,14},{3,11},{4,8},{5,13},{6,10},{7,15},{8,4},{9,1},... | collective-permute-start | bytes 196616 | tf_op jit(solution)/shard_map/ppermute | solution.py:350
  11.0 3.5 %collective-permute-start.3 = (bf16[256,128]{1,0:T(8,128)(2,1)}, bf16[256,128]{1,0:T(8,128)(2,1)S(1)}, u32[]{:S(2)}, u32[]{:S(2)}) collective-permute-start(bf16[256,128]{1,0:T(8,128)(2,1)} %get-tuple-element.19), channel_id=1, source_target_pairs={{0,20},{1,17},{2,22},{3,19},{4,16},{5,21},{6,18},{7,23},{8,28},{9,... | collective-permute-start | bytes 196616 | tf_op jit(solution)/shard_map/ppermute | solution.py:350
  14.6 1.6 %collective-permute-start.5 = (bf16[256,128]{1,0:T(8,128)(2,1)S(1)}, bf16[256,128]{1,0:T(8,128)(2,1)S(1)}, u32[]{:S(2)}, u32[]{:S(2)}) collective-permute-start(bf16[256,128]{1,0:T(8,128)(2,1)S(1)} %collective-permute-done.1.refs_0_), channel_id=1, source_target_pairs={{0,2},{1,3},{2,0},{3,1},{4,6},{5,7},{6,4},{7,5},{8,10},{9,11},{10,... | collective-permute-start | bytes 196616 | tf_op jit(solution)/shard_map/ppermute | solution.py:354
  16.4 2.2 %collective-permute-done.3.refs_2_ = bf16[256,128]{1,0:T(8,128)(2,1)S(1)} collective-permute-done((bf16[256,128]{1,0:T(8,128)(2,1)}, bf16[256,128]{1,0:T(8,128)(2,1)S(1)}, u32[]{:S(2)}, u32[]{:S(2)}) %collective-permute-start.3) | collective-permute-done | bytes 65568 | tf_op jit(solution)/shard_map/ppermute | solution.py:350
  18.7 1.5 %collective-permute-start.6 = (bf16[256,128]{1,0:T(8,128)(2,1)S(1)}, bf16[256,128]{1,0:T(8,128)(2,1)S(1)}, u32[]{:S(2)}, u32[]{:S(2)}) collective-permute-start(bf16[256,128]{1,0:T(8,128)(2,1)S(1)} %collective-permute-done.2.refs_1_), channel_id=1, source_target_pairs={{0,2},{1,3},{2,0},{3,1},{4,6},{5,7},{6,4},{7,5},{8,10},{9,11},{10,... | collective-permute-start | bytes 196616 | tf_op jit(solution)/shard_map/ppermute | solution.py:354
  20.2 1.5 %collective-permute-done.4.refs_3_ = bf16[256,128]{1,0:T(8,128)(2,1)S(1)} collective-permute-done((bf16[256,128]{1,0:T(8,128)(2,1)}, bf16[256,128]{1,0:T(8,128)(2,1)S(1)}, u32[]{:S(2)}, u32[]{:S(2)}) %collective-permute-start.4) | collective-permute-done | bytes 65568 | tf_op jit(solution)/shard_map/ppermute | solution.py:350
  21.7 1.6 %collective-permute-start.7 = (bf16[256,128]{1,0:T(8,128)(2,1)S(1)}, bf16[256,128]{1,0:T(8,128)(2,1)S(1)}, u32[]{:S(2)}, u32[]{:S(2)}) collective-permute-start(bf16[256,128]{1,0:T(8,128)(2,1)S(1)} %collective-permute-done.3.refs_2_), channel_id=1, source_target_pairs={{0,2},{1,3},{2,0},{3,1},{4,6},{5,7},{6,4},{7,5},{8,10},{9,11},{10,... | collective-permute-start | bytes 196616 | tf_op jit(solution)/shard_map/ppermute | solution.py:354
  24.4 2.0 %collective-permute-done.7.refs_6_ = bf16[256,128]{1,0:T(8,128)(2,1)S(1)} collective-permute-done((bf16[256,128]{1,0:T(8,128)(2,1)S(1)}, bf16[256,128]{1,0:T(8,128)(2,1)S(1)}, u32[]{:S(2)}, u32[]{:S(2)}) %collective-permute-start.7) | collective-permute-done | bytes 65568 | tf_op jit(solution)/shard_map/ppermute | solution.py:354
  26.5 1.2 %collective-permute-done.8.refs_7_ = bf16[256,128]{1,0:T(8,128)(2,1)S(1)} collective-permute-done((bf16[256,128]{1,0:T(8,128)(2,1)S(1)}, bf16[256,128]{1,0:T(8,128)(2,1)S(1)}, u32[]{:S(2)}, u32[]{:S(2)}) %collective-permute-start.8) | collective-permute-done | bytes 65568 | tf_op jit(solution)/shard_map/ppermute | solution.py:354
  27.7 1.2 %collective-permute-done.16.refs_15_ = bf16[256,128]{1,0:T(8,128)(2,1)S(1)} collective-permute-done((bf16[256,128]{1,0:T(8,128)(2,1)S(1)}, bf16[256,128]{1,0:T(8,128)(2,1)S(1)}, u32[]{:S(2)}, u32[]{:S(2)}) %collective-permute-start.16) | collective-permute-done | bytes 65568 | tf_op jit(solution)/shard_map/ppermute | solution.py:360
  29.5 14.8 %shard_map.92 = (f32[128,128]{1,0:T(8,128)}, f32[128,128]{1,0:T(8,128)}, f32[128,128]{1,0:T(8,128)}, f32[128,128]{1,0:T(8,128)}, f32[128,128]{1,0:T(8,128)}, /*i...) custom-call(s32[1,4,16]{2,1,0:T(4,128)} %match_ref.1, s32[3,128]{1,0:T(4,128)} %bitcast.1, ...), custom_call_target="tpu_custom_call" | custom-call | flops 4831838208 | bytes 8388608 | tf_op jit(solution)/shard_map/pallas_call | solution.py:463
  44.3 0.6 collective-permute-start.17
  44.9 3.0 %collective-permute-start.19 = (f32[128,128]{1,0:T(8,128)}, f32[128,128]{1,0:T(8,128)S(1)}, u32[]{:S(2)}, u32[]{:S(2)}) collective-permute-start(f32[128,128]{1,0:T(8,128)} %get-tuple-element.24), channel_id=1, source_target_pairs={{0,12},{4,8},{8,4},{12,0},{16,28},{20,24},{24,20},{28,16},{1,13},{... | collective-permute-start | bytes 196616 | tf_op jit(solution)/shard_map/ppermute | solution.py:504
  47.9 2.9 %collective-permute-start.21 = (f32[128,128]{1,0:T(8,128)}, f32[128,128]{1,0:T(8,128)S(1)}, u32[]{:S(2)}, u32[]{:S(2)}) collective-permute-start(f32[128,128]{1,0:T(8,128)} %get-tuple-element.26), channel_id=1, source_target_pairs={{0,20},{4,16},{8,28},{12,24},{16,4},{20,0},{24,12},{28,8},{1,21},{... | collective-permute-start | bytes 196616 | tf_op jit(solution)/shard_map/ppermute | solution.py:504
  50.8 0.9 %collective-permute-start.22 = (f32[128,128]{1,0:T(8,128)}, f32[128,128]{1,0:T(8,128)S(1)}, u32[]{:S(2)}, u32[]{:S(2)}) collective-permute-start(f32[128,128]{1,0:T(8,128)} %get-tuple-element.27), channel_id=1, source_target_pairs={{0,24},{4,28},{8,16},{12,20},{16,8},{20,12},{24,0},{28,4},{1,25},{... | collective-permute-start | bytes 196616 | tf_op jit(solution)/shard_map/ppermute | solution.py:504
  51.6 3.9 %collective-permute-start.23 = (f32[128,128]{1,0:T(8,128)}, f32[128,128]{1,0:T(8,128)S(1)}, u32[]{:S(2)}, u32[]{:S(2)}) collective-permute-start(f32[128,128]{1,0:T(8,128)} %get-tuple-element.28), channel_id=1, source_target_pairs={{0,28},{4,24},{8,20},{12,16},{16,12},{20,8},{24,4},{28,0},{1,29},{... | collective-permute-start | bytes 196616 | tf_op jit(solution)/shard_map/ppermute | solution.py:504
  55.6 0.8 %collective-permute-done.20.refs_4_ = f32[128,128]{1,0:T(8,128)S(1)} collective-permute-done((f32[128,128]{1,0:T(8,128)}, f32[128,128]{1,0:T(8,128)S(1)}, u32[]{:S(2)}, u32[]{:S(2)}) %collective-permute-start.20) | collective-permute-done | bytes 65568 | tf_op jit(solution)/shard_map/ppermute | solution.py:504
  56.4 3.4 %collective-permute-done.21.refs_5_ = f32[128,128]{1,0:T(8,128)S(1)} collective-permute-done((f32[128,128]{1,0:T(8,128)}, f32[128,128]{1,0:T(8,128)S(1)}, u32[]{:S(2)}, u32[]{:S(2)}) %collective-permute-start.21) | collective-permute-done | bytes 65568 | tf_op jit(solution)/shard_map/ppermute | solution.py:504
  59.8 0.6 copy-done.5
  60.4 2.2 %shard_map.93 = f32[32,4096]{1,0:T(8,128)} custom-call(f32[128,128]{1,0:T(8,128)} %get-tuple-element.21.refs_0_, f32[128,128]{1,0:T(8,128)} %copy-done.1, f32[128,128]{1,0:T(8,128)} %copy-done.2, f32[128,128]{1,0:T(8,128)} %copy-done.3, f32[128,128]{1,0:T(8,128)} %copy-done.4, f32[128,128]{1,0:T(8,128)} %copy-done.5, f32[128,128]{1,0:T(8,128)} %copy-done.6, ...), custom_call_target="tpu_custom_call" | custom-call | tf_op jit(solution)/shard_map/pallas_call | solution.py:429
  (75 shorter events, 2.5 us)
Async XLA Ops:
  0.0 1.8 %collective-permute-start = (bf16[32,4096]{1,0:T(8,128)(2,1)}, bf16[32,4096]{1,0:T(8,128)(2,1)S(1)}, u32[]{:S(2)}, u32[]{:S(2)}) collective-permute-start(bf16[32,4096]{1,0:T(8,128)(2,1)} %refs_0_.1), channel_id=1, source_target_pairs={{0,1},{1,0},{2,3},{3,2},{4,5},{5,4},{6,7},{7,6},{8,9},{9,8},{10,11... | collective-permute-start | bytes 786440 | tf_op jit(solution)/shard_map/ppermute | solution.py:360
  4.6 9.9 %collective-permute-start.1 = (bf16[256,128]{1,0:T(8,128)(2,1)}, bf16[256,128]{1,0:T(8,128)(2,1)S(1)}, u32[]{:S(2)}, u32[]{:S(2)}) collective-permute-start(bf16[256,128]{1,0:T(8,128)(2,1)} %get-tuple-element.17), channel_id=1, source_target_pairs={{0,4},{1,1},{2,6},{3,3},{4,0},{5,5},{6,2},{7,7},{8,12},{9,9},{10,1... | collective-permute-start | bytes 196616 | tf_op jit(solution)/shard_map/ppermute | solution.py:350
  9.4 6.9 %collective-permute-start.2 = (bf16[256,128]{1,0:T(8,128)(2,1)}, bf16[256,128]{1,0:T(8,128)(2,1)S(1)}, u32[]{:S(2)}, u32[]{:S(2)}) collective-permute-start(bf16[256,128]{1,0:T(8,128)(2,1)} %get-tuple-element.18), channel_id=1, source_target_pairs={{0,12},{1,9},{2,14},{3,11},{4,8},{5,13},{6,10},{7,15},{8,4},{9,1},... | collective-permute-start | bytes 196616 | tf_op jit(solution)/shard_map/ppermute | solution.py:350
  11.0 7.7 %collective-permute-start.3 = (bf16[256,128]{1,0:T(8,128)(2,1)}, bf16[256,128]{1,0:T(8,128)(2,1)S(1)}, u32[]{:S(2)}, u32[]{:S(2)}) collective-permute-start(bf16[256,128]{1,0:T(8,128)(2,1)} %get-tuple-element.19), channel_id=1, source_target_pairs={{0,20},{1,17},{2,22},{3,19},{4,16},{5,21},{6,18},{7,23},{8,28},{9,... | collective-permute-start | bytes 196616 | tf_op jit(solution)/shard_map/ppermute | solution.py:350
  14.5 7.2 %collective-permute-start.4 = (bf16[256,128]{1,0:T(8,128)(2,1)}, bf16[256,128]{1,0:T(8,128)(2,1)S(1)}, u32[]{:S(2)}, u32[]{:S(2)}) collective-permute-start(bf16[256,128]{1,0:T(8,128)(2,1)} %get-tuple-element.20), channel_id=1, source_target_pairs={{0,28},{1,25},{2,30},{3,27},{4,24},{5,29},{6,26},{7,31},{8,20},{9,... | collective-permute-start | bytes 196616 | tf_op jit(solution)/shard_map/ppermute | solution.py:350
  14.5 7.2 %collective-permute-start.9 = (bf16[256,128]{1,0:T(8,128)(2,1)S(1)}, bf16[256,128]{1,0:T(8,128)(2,1)S(1)}, u32[]{:S(2)}, u32[]{:S(2)}) collective-permute-start(bf16[256,128]{1,0:T(8,128)(2,1)S(1)} %collective-permute-done.1.refs_0_), channel_id=1, source_target_pairs={{0,1},{1,0},{2,3},{3,2},{4,5},{5,4},{6,7},{7,6},{8,9},{9,8},{10,11... | collective-permute-start | bytes 196616 | tf_op jit(solution)/shard_map/ppermute | solution.py:360
  14.6 8.7 %collective-permute-start.5 = (bf16[256,128]{1,0:T(8,128)(2,1)S(1)}, bf16[256,128]{1,0:T(8,128)(2,1)S(1)}, u32[]{:S(2)}, u32[]{:S(2)}) collective-permute-start(bf16[256,128]{1,0:T(8,128)(2,1)S(1)} %collective-permute-done.1.refs_0_), channel_id=1, source_target_pairs={{0,2},{1,3},{2,0},{3,1},{4,6},{5,7},{6,4},{7,5},{8,10},{9,11},{10,... | collective-permute-start | bytes 196616 | tf_op jit(solution)/shard_map/ppermute | solution.py:354
  16.3 7.6 %collective-permute-start.10 = (bf16[256,128]{1,0:T(8,128)(2,1)S(1)}, bf16[256,128]{1,0:T(8,128)(2,1)S(1)}, u32[]{:S(2)}, u32[]{:S(2)}) collective-permute-start(bf16[256,128]{1,0:T(8,128)(2,1)S(1)} %collective-permute-done.2.refs_1_), channel_id=1, source_target_pairs={{0,1},{1,0},{2,3},{3,2},{4,5},{5,4},{6,7},{7,6},{8,9},{9,8},{10,11... | collective-permute-start | bytes 196616 | tf_op jit(solution)/shard_map/ppermute | solution.py:360
  18.7 5.2 %collective-permute-start.6 = (bf16[256,128]{1,0:T(8,128)(2,1)S(1)}, bf16[256,128]{1,0:T(8,128)(2,1)S(1)}, u32[]{:S(2)}, u32[]{:S(2)}) collective-permute-start(bf16[256,128]{1,0:T(8,128)(2,1)S(1)} %collective-permute-done.2.refs_1_), channel_id=1, source_target_pairs={{0,2},{1,3},{2,0},{3,1},{4,6},{5,7},{6,4},{7,5},{8,10},{9,11},{10,... | collective-permute-start | bytes 196616 | tf_op jit(solution)/shard_map/ppermute | solution.py:354
  21.7 2.6 %collective-permute-start.11 = (bf16[256,128]{1,0:T(8,128)(2,1)S(1)}, bf16[256,128]{1,0:T(8,128)(2,1)S(1)}, u32[]{:S(2)}, u32[]{:S(2)}) collective-permute-start(bf16[256,128]{1,0:T(8,128)(2,1)S(1)} %collective-permute-done.3.refs_2_), channel_id=1, source_target_pairs={{0,1},{1,0},{2,3},{3,2},{4,5},{5,4},{6,7},{7,6},{8,9},{9,8},{10,11... | collective-permute-start | bytes 196616 | tf_op jit(solution)/shard_map/ppermute | solution.py:360
  21.7 4.7 %collective-permute-start.7 = (bf16[256,128]{1,0:T(8,128)(2,1)S(1)}, bf16[256,128]{1,0:T(8,128)(2,1)S(1)}, u32[]{:S(2)}, u32[]{:S(2)}) collective-permute-start(bf16[256,128]{1,0:T(8,128)(2,1)S(1)} %collective-permute-done.3.refs_2_), channel_id=1, source_target_pairs={{0,2},{1,3},{2,0},{3,1},{4,6},{5,7},{6,4},{7,5},{8,10},{9,11},{10,... | collective-permute-start | bytes 196616 | tf_op jit(solution)/shard_map/ppermute | solution.py:354
  23.3 4.4 %collective-permute-start.8 = (bf16[256,128]{1,0:T(8,128)(2,1)S(1)}, bf16[256,128]{1,0:T(8,128)(2,1)S(1)}, u32[]{:S(2)}, u32[]{:S(2)}) collective-permute-start(bf16[256,128]{1,0:T(8,128)(2,1)S(1)} %collective-permute-done.4.refs_3_), channel_id=1, source_target_pairs={{0,2},{1,3},{2,0},{3,1},{4,6},{5,7},{6,4},{7,5},{8,10},{9,11},{10,... | collective-permute-start | bytes 196616 | tf_op jit(solution)/shard_map/ppermute | solution.py:354
  23.8 3.8 %collective-permute-start.12 = (bf16[256,128]{1,0:T(8,128)(2,1)S(1)}, bf16[256,128]{1,0:T(8,128)(2,1)S(1)}, u32[]{:S(2)}, u32[]{:S(2)}) collective-permute-start(bf16[256,128]{1,0:T(8,128)(2,1)S(1)} %collective-permute-done.4.refs_3_), channel_id=1, source_target_pairs={{0,1},{1,0},{2,3},{3,2},{4,5},{5,4},{6,7},{7,6},{8,9},{9,8},{10,11... | collective-permute-start | bytes 196616 | tf_op jit(solution)/shard_map/ppermute | solution.py:360
  23.9 3.8 %collective-permute-start.13 = (bf16[256,128]{1,0:T(8,128)(2,1)S(1)}, bf16[256,128]{1,0:T(8,128)(2,1)S(1)}, u32[]{:S(2)}, u32[]{:S(2)}) collective-permute-start(bf16[256,128]{1,0:T(8,128)(2,1)S(1)} %collective-permute-done.5.refs_4_), channel_id=1, source_target_pairs={{0,1},{1,0},{2,3},{3,2},{4,5},{5,4},{6,7},{7,6},{8,9},{9,8},{10,11... | collective-permute-start | bytes 196616 | tf_op jit(solution)/shard_map/ppermute | solution.py:360
  24.4 3.3 %collective-permute-start.14 = (bf16[256,128]{1,0:T(8,128)(2,1)S(1)}, bf16[256,128]{1,0:T(8,128)(2,1)S(1)}, u32[]{:S(2)}, u32[]{:S(2)}) collective-permute-start(bf16[256,128]{1,0:T(8,128)(2,1)S(1)} %collective-permute-done.6.refs_5_), channel_id=1, source_target_pairs={{0,1},{1,0},{2,3},{3,2},{4,5},{5,4},{6,7},{7,6},{8,9},{9,8},{10,11... | collective-permute-start | bytes 196616 | tf_op jit(solution)/shard_map/ppermute | solution.py:360
  26.5 1.3 %collective-permute-start.15 = (bf16[256,128]{1,0:T(8,128)(2,1)S(1)}, bf16[256,128]{1,0:T(8,128)(2,1)S(1)}, u32[]{:S(2)}, u32[]{:S(2)}) collective-permute-start(bf16[256,128]{1,0:T(8,128)(2,1)S(1)} %collective-permute-done.7.refs_6_), channel_id=1, source_target_pairs={{0,1},{1,0},{2,3},{3,2},{4,5},{5,4},{6,7},{7,6},{8,9},{9,8},{10,11... | collective-permute-start | bytes 196616 | tf_op jit(solution)/shard_map/ppermute | solution.py:360
  27.6 1.3 %collective-permute-start.16 = (bf16[256,128]{1,0:T(8,128)(2,1)S(1)}, bf16[256,128]{1,0:T(8,128)(2,1)S(1)}, u32[]{:S(2)}, u32[]{:S(2)}) collective-permute-start(bf16[256,128]{1,0:T(8,128)(2,1)S(1)} %collective-permute-done.8.refs_7_), channel_id=1, source_target_pairs={{0,1},{1,0},{2,3},{3,2},{4,5},{5,4},{6,7},{7,6},{8,9},{9,8},{10,11... | collective-permute-start | bytes 196616 | tf_op jit(solution)/shard_map/ppermute | solution.py:360
  44.3 6.4 %collective-permute-start.17 = (f32[128,128]{1,0:T(8,128)}, f32[128,128]{1,0:T(8,128)S(1)}, u32[]{:S(2)}, u32[]{:S(2)}) collective-permute-start(f32[128,128]{1,0:T(8,128)} %get-tuple-element.22), channel_id=1, source_target_pairs={{0,4},{4,0},{8,12},{12,8},{16,20},{20,16},{24,28},{28,24},{1,5},{5... | collective-permute-start | bytes 196616 | tf_op jit(solution)/shard_map/ppermute | solution.py:504
  44.9 6.7 %collective-permute-start.18 = (f32[128,128]{1,0:T(8,128)}, f32[128,128]{1,0:T(8,128)S(1)}, u32[]{:S(2)}, u32[]{:S(2)}) collective-permute-start(f32[128,128]{1,0:T(8,128)} %get-tuple-element.23), channel_id=1, source_target_pairs={{0,8},{4,12},{8,0},{12,4},{16,24},{20,28},{24,16},{28,20},{1,9},{5... | collective-permute-start | bytes 196616 | tf_op jit(solution)/shard_map/ppermute | solution.py:504
  44.9 10.6 %collective-permute-start.19 = (f32[128,128]{1,0:T(8,128)}, f32[128,128]{1,0:T(8,128)S(1)}, u32[]{:S(2)}, u32[]{:S(2)}) collective-permute-start(f32[128,128]{1,0:T(8,128)} %get-tuple-element.24), channel_id=1, source_target_pairs={{0,12},{4,8},{8,4},{12,0},{16,28},{20,24},{24,20},{28,16},{1,13},{... | collective-permute-start | bytes 196616 | tf_op jit(solution)/shard_map/ppermute | solution.py:504
  47.9 8.5 %collective-permute-start.20 = (f32[128,128]{1,0:T(8,128)}, f32[128,128]{1,0:T(8,128)S(1)}, u32[]{:S(2)}, u32[]{:S(2)}) collective-permute-start(f32[128,128]{1,0:T(8,128)} %get-tuple-element.25), channel_id=1, source_target_pairs={{0,16},{4,20},{8,24},{12,28},{16,0},{20,4},{24,8},{28,12},{1,17},{... | collective-permute-start | bytes 196616 | tf_op jit(solution)/shard_map/ppermute | solution.py:504
  47.9 11.8 %collective-permute-start.21 = (f32[128,128]{1,0:T(8,128)}, f32[128,128]{1,0:T(8,128)S(1)}, u32[]{:S(2)}, u32[]{:S(2)}) collective-permute-start(f32[128,128]{1,0:T(8,128)} %get-tuple-element.26), channel_id=1, source_target_pairs={{0,20},{4,16},{8,28},{12,24},{16,4},{20,0},{24,12},{28,8},{1,21},{... | collective-permute-start | bytes 196616 | tf_op jit(solution)/shard_map/ppermute | solution.py:504
  50.8 9.0 %collective-permute-start.22 = (f32[128,128]{1,0:T(8,128)}, f32[128,128]{1,0:T(8,128)S(1)}, u32[]{:S(2)}, u32[]{:S(2)}) collective-permute-start(f32[128,128]{1,0:T(8,128)} %get-tuple-element.27), channel_id=1, source_target_pairs={{0,24},{4,28},{8,16},{12,20},{16,8},{20,12},{24,0},{28,4},{1,25},{... | collective-permute-start | bytes 196616 | tf_op jit(solution)/shard_map/ppermute | solution.py:504
  51.6 8.1 %collective-permute-start.23 = (f32[128,128]{1,0:T(8,128)}, f32[128,128]{1,0:T(8,128)S(1)}, u32[]{:S(2)}, u32[]{:S(2)}) collective-permute-start(f32[128,128]{1,0:T(8,128)} %get-tuple-element.28), channel_id=1, source_target_pairs={{0,28},{4,24},{8,20},{12,16},{16,12},{20,8},{24,4},{28,0},{1,29},{... | collective-permute-start | bytes 196616 | tf_op jit(solution)/shard_map/ppermute | solution.py:504
  (24 other events, 109.3 us)

commit v5 on v4

--- a/solution.py
+++ b/solution.py
@@ -69,20 +69,27 @@
     return CORES * turn + CORES - 1 - core
 
 
+def turn_groups(slab_count):
+    turns = list(reversed(range(slab_count // CORES)))
+    middle = (len(turns) + 1) // 2
+    return [group for group in (turns[:middle], turns[middle:]) if group]
+
+
 def block_places(slab_index, pair_index, slab_count, pair_count):
     chips = pair_count // CORES
     chip = pair_index // CORES
     for core_step in range(CORES):
         core = (pair_index + core_step) % CORES
         for chip_step in range(chips):
-            for turn in range(slab_count // CORES):
-                step = slab_step(turn, core)
-                yield (chip + chips - chip_step) % chips, partner_of(slab_index, step, slab_count)[1]
+            source = (chip + chips - chip_step) % chips
+            for turns in turn_groups(slab_count):
+                steps = [slab_step(turn, core) for turn in turns]
+                yield [(source, partner_of(slab_index, step, slab_count)[1]) for step in steps]
 
 
 def force_kernel(sizes, match_ref, centers_ref, *refs):
     slab_count, pair_count = sizes[3:]
-    block_count = slab_count * pair_count // CORES
+    block_count = len(turn_groups(slab_count)) * pair_count
     block_refs = refs[:block_count]
     constant_refs = refs[block_count : block_count + 6]
     out_refs = refs[block_count + 6 : block_count + 6 + slab_count]
@@ -127,9 +134,14 @@
     slab_index = lax.axis_index("slab")
     pair_index = lax.axis_index("pair")
 
-    targets = [boxes_ref.at[place] for place in block_places(slab_index, pair_index, slab_count, pair_count)]
-    sources = list(block_refs) + [match_hbm, centers_hbm]
-    targets += [match_ref, centers_ref]
+    sources = [match_hbm, centers_hbm]
+    targets = [match_ref, centers_ref]
+    block_rows = boxes_ref.shape[2]
+    places = block_places(slab_index, pair_index, slab_count, pair_count)
+    for block_ref, group_places in zip(block_refs, places):
+        for index, place in enumerate(group_places):
+            sources.append(block_ref.at[index * block_rows : (index + 1) * block_rows])
+            targets.append(boxes_ref.at[place])
     copies = []
     for source, target in zip(sources, targets):
         copies.append(pltpu.make_async_copy(source, target, sems.at[len(copies)]))
@@ -339,21 +351,22 @@
 
 def gather_boxes(blocks, slab_count, pair_count):
     chips = pair_count // CORES
-    own = []
-    for turn in reversed(range(len(blocks))):
-        block = blocks[turn]
-        perm = []
-        for slab in range(slab_count):
-            for pair in range(pair_count):
-                target = partner_of(slab, slab_step(turn, pair % CORES), slab_count)[0]
-                perm.append((slab * pair_count + pair, target * pair_count + pair))
-        own.append((turn, lax.ppermute(block, ("slab", "pair"), perm)))
+    arrived = {}
+    for turns in turn_groups(slab_count):
+        for turn in turns:
+            perm = []
+            for slab in range(slab_count):
+                for pair in range(pair_count):
+                    target = partner_of(slab, slab_step(turn, pair % CORES), slab_count)[0]
+                    perm.append((slab * pair_count + pair, target * pair_count + pair))
+            arrived[turn] = lax.ppermute(blocks[turn], ("slab", "pair"), perm)
+    own = [jnp.concatenate([arrived[t] for t in turns]) for turns in turn_groups(slab_count)]
     pieces = [own]
     for step in range(1, chips):
         perm = [(i, (i + step * CORES) % pair_count) for i in range(pair_count)]
-        pieces.append([(turn, lax.ppermute(block, "pair", perm)) for turn, block in own])
-    other = [[(turn, swap_cores(block, pair_count)) for turn, block in piece] for piece in pieces]
-    return [block for piece in pieces + other for _, block in sorted(piece, key=lambda item: item[0])]
+        pieces.append([lax.ppermute(block, "pair", perm) for block in own])
+    other = [[swap_cores(block, pair_count) for block in piece] for piece in pieces]
+    return [block for piece in pieces + other for block in piece]
 
 
 def swap_cores(block, pair_count):
@@ -407,17 +420,18 @@
     tiles = cells // LANES
     slab_index = lax.axis_index("slab")
     copies = []
-    for step in range(slab_count):
-        copies.append(pltpu.make_async_copy(block_refs[step], blocks.at[step], sems.at[step]))
+    for index in range(slab_count):
+        copies.append(pltpu.make_async_copy(block_refs[index], blocks.at[index], sems.at[index]))
         copies[-1].start()
-    for step in range(slab_count):
-        copies[step].wait()
+    for index in reversed(range(slab_count)):
+        step = slab_count - 1 - index
+        copies[index].wait()
         first = partner_of(slab_index, step, slab_count)[1] * own_count
         for own in range(own_count):
             for tile in range(0, tiles, 8):
                 start = tile * row_count + first + own
                 row = own * tiles + tile
-                lines[pl.ds(start, 8, stride=row_count), :] = blocks[step, row : row + 8, :]
+                lines[pl.ds(start, 8, stride=row_count), :] = blocks[index, row : row + 8, :]
     for tile in range(tiles):
         columns = slice(tile * LANES, (tile + 1) * LANES)
         out_ref[:, columns] = lines[tile * row_count : (tile + 1) * row_count, :]
@@ -441,8 +455,9 @@
 
 def team_forces(match, centers, blocks, side, slab_count, pair_count):
     _, rounds, team = match.shape
-    rows = blocks[0].shape[0] // CORES
     own_count = team // pair_count
+    rows = own_count * side * side // LANES * (side // slab_count)
+    block_count = slab_count * pair_count // CORES
     tiles = side * side // LANES
     solves = own_count * rounds
     group = min(solves, 8)
@@ -476,7 +491,7 @@
             wide,
             pltpu.VMEM((solves * tiles * pitch, LANES), jnp.float32),
             pltpu.VMEM((own_count * tiles * side, LANES), jnp.float32),
-            pltpu.SemaphoreType.DMA((len(blocks) + 2 + len(constants),)),
+            pltpu.SemaphoreType.DMA((block_count + 2 + len(constants),)),
         ],
         compiler_params=pltpu.CompilerParams(vmem_limit_bytes=60 * 1024 * 1024),
         cost_estimate=pl.CostEstimate(flops=flops, bytes_accessed=8 * 1024 * 1024, transcendentals=0),
@@ -498,11 +513,11 @@
     blocks = pack(orbitals, other, own_count, slab_count)
     team_blocks = gather_boxes(blocks, slab_count, pair_count)
     forces = team_forces(matchings, centers.T, team_blocks, side, slab_count, pair_count)
-    received = [forces[0]]
+    received = []
     for step in reversed(range(1, slab_count)):
         perm = [(i, partner_of(i, step, slab_count)[0]) for i in range(slab_count)]
-        received.insert(1, lax.ppermute(forces[step], "slab", perm))
-    return unpack(received, own_count, plane_cells)
+        received.append(lax.ppermute(forces[step], "slab", perm))
+    return unpack(received + [forces[0]], own_count, plane_cells)
 
 
 def solution(mesh):

time: 62.8 us -> 61.1 us (0.973)
  starting transfers between devices: 27.6 us -> 26.4 us
  waiting for transfers between devices: 13.7 us -> 13 us
    ppermute x15 -> x13, starting transfers between devices: 26.3 us -> 25.4 us  [the longest x7 13.4 us: shards(): received.append(lax.ppermute(forces[step], 'slab', perm))]
    ppermute x15 -> x13, waiting for transfers between devices: 11.2 us -> 10.4 us  [the longest x2 3.91 us: gather_boxes(): pieces.append([lax.ppermute(block, 'pair', perm) for block in own])]
    ppermute x9 -> x5, starting transfers between devices: 1.27 us -> 0.97 us  [swap_cores(): return lax.ppermute(block, 'pair', [(i, i ^ 1) for i in range(pair_count)])]
    unnamed x48 -> x34, local copies, waits for them, and re-layouts: 1.87 us -> 1.98 us
    ppermute x9 -> x5, waiting for transfers between devices: 2.58 us -> 2.67 us  [swap_cores(): return lax.ppermute(block, 'pair', [(i, i ^ 1) for i in range(pair_count)])]
  transfers between devices with their start and end apart: 24 -> 18, of which waited for: 8 -> 8; matrix products, arithmetic and copies ran while one was open for 0% -> 0% of each run, Pallas kernels for 0% -> 0%
where the time goes in v5:
time: 61.1 us; the launch traced here: 60.9 us
  starting transfers between devices  26.4 us (43%)
  Pallas kernels  19.3 us (32%)
  waiting for transfers between devices  13 us (21%)
  local copies, waits for them, and re-layouts  2 us (3%)
    pallas_call x1, Pallas kernels, team_forces(): pl.pallas_call(functools.partial(force_kernel, sizes), out_shape=[jax.Sha...  14.8 us
    ppermute x7, starting transfers between devices, shards(): received.append(lax.ppermute(forces[step], 'slab', perm))  13.4 us
    ppermute x4, starting transfers between devices, gather_boxes(): arrived[turn] = lax.ppermute(blocks[turn], ('slab', 'pair'), perm)  9.85 us
    ppermute x2, waiting for transfers between devices, gather_boxes(): pieces.append([lax.ppermute(block, 'pair', perm) for block in own])  3.91 us
    ppermute x4, waiting for transfers between devices, gather_boxes(): arrived[turn] = lax.ppermute(blocks[turn], ('slab', 'pair'), perm)  3.71 us
    ppermute x7, waiting for transfers between devices, shards(): received.append(lax.ppermute(forces[step], 'slab', perm))  2.76 us
    ppermute x5, waiting for transfers between devices, swap_cores(): return lax.ppermute(block, 'pair', [(i, i ^ 1) for i in range(pair_count)])  2.67 us
    pallas_call x1, Pallas kernels, unpack(): pl.pallas_call(functools.partial(unpack_kernel, (own_count, slab_count)),...  2.45 us
  transfers between devices with their start and end apart: 18, of which 8 were waited for; matrix products, arithmetic and copies ran while one was open for 0% of the time, Pallas kernels for 0%

profile of v5, /device:TPU:0, one launch (start us, length us, event | category | flops | bytes accessed | tf_op | source)
XLA Modules:
  0.0 60.9 jit_solution(5125698992438458017)
XLA Ops:
  0.5 1.4 %collective-permute-done.refs_1_ = bf16[32,4096]{1,0:T(8,128)(2,1)S(1)} collective-permute-done((bf16[32,4096]{1,0:T(8,128)(2,1)}, bf16[32,4096]{1,0:T(8,128)(2,1)S(1)}, u32[]{:S(2)}, u32[]{:S(2)}) %collective-permute-start) | collective-permute-done | bytes 262176 | tf_op jit(solution)/shard_map/ppermute | solution.py:373
  1.8 0.7 %copy-done = bf16[32,4096]{1,0:T(8,128)(2,1)} copy-done((bf16[32,4096]{1,0:T(8,128)(2,1)}, bf16[32,4096]{1,0:T(8,128)(2,1)S(1)}, u32[]{:S(2)}) %copy-start) | copy-done | bytes 262168
  2.5 2.1 %shard_map.91 = (bf16[256,128]{1,0:T(8,128)(2,1)}, bf16[256,128]{1,0:T(8,128)(2,1)}, bf16[256,128]{1,0:T(8,128)(2,1)}, bf16[256,128]{1,0:T(8,128)(2,1)}) custom-call(bf16[32,4096]{1,0:T(8,128)(2,1)} %refs_0_.1, bf16[32,4096]{1,0:T(8,128)(2,1)} %copy-done), custom_call_target="tpu_custom_call" | custom-call | tf_op jit(solution)/shard_map/pallas_call | solution.py:407
  4.6 3.9 %collective-permute-start.3 = (bf16[256,128]{1,0:T(8,128)(2,1)}, bf16[256,128]{1,0:T(8,128)(2,1)S(1)}, u32[]{:S(2)}, u32[]{:S(2)}) collective-permute-start(bf16[256,128]{1,0:T(8,128)(2,1)} %get-tuple-element.19), channel_id=1, source_target_pairs={{0,12},{1,9},{2,14},{3,11},{4,8},{5,13},{6,10},{7,15},{8,4},{9,1},... | collective-permute-start | bytes 196616 | tf_op jit(solution)/shard_map/ppermute | solution.py:362
  8.5 2.4 %collective-permute-start.1 = (bf16[256,128]{1,0:T(8,128)(2,1)}, bf16[256,128]{1,0:T(8,128)(2,1)S(1)}, u32[]{:S(2)}, u32[]{:S(2)}) collective-permute-start(bf16[256,128]{1,0:T(8,128)(2,1)} %get-tuple-element.17), channel_id=1, source_target_pairs={{0,28},{1,25},{2,30},{3,27},{4,24},{5,29},{6,26},{7,31},{8,20},{9,... | collective-permute-start | bytes 196616 | tf_op jit(solution)/shard_map/ppermute | solution.py:362
  11.3 3.1 %collective-permute-start.4 = (bf16[256,128]{1,0:T(8,128)(2,1)}, bf16[256,128]{1,0:T(8,128)(2,1)S(1)}, u32[]{:S(2)}, u32[]{:S(2)}) collective-permute-start(bf16[256,128]{1,0:T(8,128)(2,1)} %get-tuple-element.20), channel_id=1, source_target_pairs={{0,4},{1,1},{2,6},{3,3},{4,0},{5,5},{6,2},{7,7},{8,12},{9,9},{10,1... | collective-permute-start | bytes 196616 | tf_op jit(solution)/shard_map/ppermute | solution.py:362
  14.5 3.7 %collective-permute-done.4 = bf16[256,128]{1,0:T(8,128)(2,1)S(1)} collective-permute-done((bf16[256,128]{1,0:T(8,128)(2,1)}, bf16[256,128]{1,0:T(8,128)(2,1)S(1)}, u32[]{:S(2)}, u32[]{:S(2)}) %collective-permute-start.4) | collective-permute-done | bytes 65568 | tf_op jit(solution)/shard_map/ppermute | solution.py:362
  18.2 1.6 %collective-permute-start.6 = (bf16[512,128]{1,0:T(8,128)(2,1)S(1)}, bf16[512,128]{1,0:T(8,128)(2,1)S(1)}, u32[]{:S(2)}, u32[]{:S(2)}) collective-permute-start(bf16[512,128]{1,0:T(8,128)(2,1)S(1)} %constant_dynamic-update-slice_fusion.2.refs_1_), channel_id=1, source_target_pairs={{0,2},{1,3},{2,0},{3,1},{4,6},{5,7},{6,4},{7,5},{8,10},{9,11},{10,... | collective-permute-start | bytes 393224 | tf_op jit(solution)/shard_map/ppermute | solution.py:367
  19.8 0.6 collective-permute-start.5
  20.4 0.5 collective-permute-start.7
  20.9 2.3 %collective-permute-done.6.refs_3_ = bf16[512,128]{1,0:T(8,128)(2,1)S(1)} collective-permute-done((bf16[512,128]{1,0:T(8,128)(2,1)S(1)}, bf16[512,128]{1,0:T(8,128)(2,1)S(1)}, u32[]{:S(2)}, u32[]{:S(2)}) %collective-permute-start.6) | collective-permute-done | bytes 131104 | tf_op jit(solution)/shard_map/ppermute | solution.py:367
  23.2 1.6 %collective-permute-done.5.refs_2_ = bf16[512,128]{1,0:T(8,128)(2,1)S(1)} collective-permute-done((bf16[512,128]{1,0:T(8,128)(2,1)S(1)}, bf16[512,128]{1,0:T(8,128)(2,1)S(1)}, u32[]{:S(2)}, u32[]{:S(2)}) %collective-permute-start.5) | collective-permute-done | bytes 131104 | tf_op jit(solution)/shard_map/ppermute | solution.py:367
  24.9 1.3 %collective-permute-done.9.refs_6_ = bf16[512,128]{1,0:T(8,128)(2,1)S(1)} collective-permute-done((bf16[512,128]{1,0:T(8,128)(2,1)S(1)}, bf16[512,128]{1,0:T(8,128)(2,1)S(1)}, u32[]{:S(2)}, u32[]{:S(2)}) %collective-permute-start.9) | collective-permute-done | bytes 131104 | tf_op jit(solution)/shard_map/ppermute | solution.py:373
  26.2 0.6 copy-done.15
  26.8 14.8 %shard_map.92 = (f32[128,128]{1,0:T(8,128)}, f32[128,128]{1,0:T(8,128)}, f32[128,128]{1,0:T(8,128)}, f32[128,128]{1,0:T(8,128)}, f32[128,128]{1,0:T(8,128)}, /*i...) custom-call(s32[1,4,16]{2,1,0:T(4,128)} %match_ref.1, s32[3,128]{1,0:T(4,128)} %bitcast.1, ...), custom_call_target="tpu_custom_call" | custom-call | flops 4831838208 | bytes 8388608 | tf_op jit(solution)/shard_map/pallas_call | solution.py:478
  41.7 3.1 %collective-permute-start.11 = (f32[128,128]{1,0:T(8,128)}, f32[128,128]{1,0:T(8,128)S(1)}, u32[]{:S(2)}, u32[]{:S(2)}) collective-permute-start(f32[128,128]{1,0:T(8,128)} %get-tuple-element.21), channel_id=1, source_target_pairs={{0,28},{4,24},{8,20},{12,16},{16,12},{20,8},{24,4},{28,0},{1,29},{... | collective-permute-start | bytes 196616 | tf_op jit(solution)/shard_map/ppermute | solution.py:519
  44.8 1.0 %collective-permute-start.12 = (f32[128,128]{1,0:T(8,128)}, f32[128,128]{1,0:T(8,128)S(1)}, u32[]{:S(2)}, u32[]{:S(2)}) collective-permute-start(f32[128,128]{1,0:T(8,128)} %get-tuple-element.22), channel_id=1, source_target_pairs={{0,24},{4,28},{8,16},{12,20},{16,8},{20,12},{24,0},{28,4},{1,25},{... | collective-permute-start | bytes 196616 | tf_op jit(solution)/shard_map/ppermute | solution.py:519
  45.8 1.9 %collective-permute-start.13 = (f32[128,128]{1,0:T(8,128)}, f32[128,128]{1,0:T(8,128)S(1)}, u32[]{:S(2)}, u32[]{:S(2)}) collective-permute-start(f32[128,128]{1,0:T(8,128)} %get-tuple-element.23), channel_id=1, source_target_pairs={{0,20},{4,16},{8,28},{12,24},{16,4},{20,0},{24,12},{28,8},{1,21},{... | collective-permute-start | bytes 196616 | tf_op jit(solution)/shard_map/ppermute | solution.py:519
  47.6 1.8 %collective-permute-start.14 = (f32[128,128]{1,0:T(8,128)}, f32[128,128]{1,0:T(8,128)S(1)}, u32[]{:S(2)}, u32[]{:S(2)}) collective-permute-start(f32[128,128]{1,0:T(8,128)} %get-tuple-element.24), channel_id=1, source_target_pairs={{0,16},{4,20},{8,24},{12,28},{16,0},{20,4},{24,8},{28,12},{1,17},{... | collective-permute-start | bytes 196616 | tf_op jit(solution)/shard_map/ppermute | solution.py:519
  49.4 0.7 %collective-permute-start.15 = (f32[128,128]{1,0:T(8,128)}, f32[128,128]{1,0:T(8,128)S(1)}, u32[]{:S(2)}, u32[]{:S(2)}) collective-permute-start(f32[128,128]{1,0:T(8,128)} %get-tuple-element.25), channel_id=1, source_target_pairs={{0,12},{4,8},{8,4},{12,0},{16,28},{20,24},{24,20},{28,16},{1,13},{... | collective-permute-start | bytes 196616 | tf_op jit(solution)/shard_map/ppermute | solution.py:519
  50.1 3.0 %collective-permute-start.16 = (f32[128,128]{1,0:T(8,128)}, f32[128,128]{1,0:T(8,128)S(1)}, u32[]{:S(2)}, u32[]{:S(2)}) collective-permute-start(f32[128,128]{1,0:T(8,128)} %get-tuple-element.26), channel_id=1, source_target_pairs={{0,8},{4,12},{8,0},{12,4},{16,24},{20,28},{24,16},{28,20},{1,9},{5... | collective-permute-start | bytes 196616 | tf_op jit(solution)/shard_map/ppermute | solution.py:519
  53.2 1.9 %collective-permute-start.17 = (f32[128,128]{1,0:T(8,128)}, f32[128,128]{1,0:T(8,128)S(1)}, u32[]{:S(2)}, u32[]{:S(2)}) collective-permute-start(f32[128,128]{1,0:T(8,128)} %get-tuple-element.27), channel_id=1, source_target_pairs={{0,4},{4,0},{8,12},{12,8},{16,20},{20,16},{24,28},{28,24},{1,5},{5... | collective-permute-start | bytes 196616 | tf_op jit(solution)/shard_map/ppermute | solution.py:519
  55.1 2.3 %collective-permute-done.13.refs_2_ = f32[128,128]{1,0:T(8,128)S(1)} collective-permute-done((f32[128,128]{1,0:T(8,128)}, f32[128,128]{1,0:T(8,128)S(1)}, u32[]{:S(2)}, u32[]{:S(2)}) %collective-permute-start.13) | collective-permute-done | bytes 65568 | tf_op jit(solution)/shard_map/ppermute | solution.py:519
  58.5 2.4 %shard_map.93 = f32[32,4096]{1,0:T(8,128)} custom-call(f32[128,128]{1,0:T(8,128)} %copy-done.1, f32[128,128]{1,0:T(8,128)} %copy-done.2, f32[128,128]{1,0:T(8,128)} %copy-done.3, f32[128,128]{1,0:T(8,128)} %copy-done.4, f32[128,128]{1,0:T(8,128)} %copy-done.5, f32[128,128]{1,0:T(8,128)} %copy-done.6, f32[128,128]{1,0:T(8,128)} %copy-done.7, ...), custom_call_target="tpu_custom_call" | custom-call | tf_op jit(solution)/shard_map/pallas_call | solution.py:443
  (51 shorter events, 2.0 us)
Async XLA Ops:
  0.0 1.8 %collective-permute-start = (bf16[32,4096]{1,0:T(8,128)(2,1)}, bf16[32,4096]{1,0:T(8,128)(2,1)S(1)}, u32[]{:S(2)}, u32[]{:S(2)}) collective-permute-start(bf16[32,4096]{1,0:T(8,128)(2,1)} %refs_0_.1), channel_id=1, source_target_pairs={{0,1},{1,0},{2,3},{3,2},{4,5},{5,4},{6,7},{7,6},{8,9},{9,8},{10,11... | collective-permute-start | bytes 786440 | tf_op jit(solution)/shard_map/ppermute | solution.py:373
  4.6 9.9 %collective-permute-start.3 = (bf16[256,128]{1,0:T(8,128)(2,1)}, bf16[256,128]{1,0:T(8,128)(2,1)S(1)}, u32[]{:S(2)}, u32[]{:S(2)}) collective-permute-start(bf16[256,128]{1,0:T(8,128)(2,1)} %get-tuple-element.19), channel_id=1, source_target_pairs={{0,12},{1,9},{2,14},{3,11},{4,8},{5,13},{6,10},{7,15},{8,4},{9,1},... | collective-permute-start | bytes 196616 | tf_op jit(solution)/shard_map/ppermute | solution.py:362
  8.5 11.3 %collective-permute-start.1 = (bf16[256,128]{1,0:T(8,128)(2,1)}, bf16[256,128]{1,0:T(8,128)(2,1)S(1)}, u32[]{:S(2)}, u32[]{:S(2)}) collective-permute-start(bf16[256,128]{1,0:T(8,128)(2,1)} %get-tuple-element.17), channel_id=1, source_target_pairs={{0,28},{1,25},{2,30},{3,27},{4,24},{5,29},{6,26},{7,31},{8,20},{9,... | collective-permute-start | bytes 196616 | tf_op jit(solution)/shard_map/ppermute | solution.py:362
  10.9 8.9 %collective-permute-start.2 = (bf16[256,128]{1,0:T(8,128)(2,1)}, bf16[256,128]{1,0:T(8,128)(2,1)S(1)}, u32[]{:S(2)}, u32[]{:S(2)}) collective-permute-start(bf16[256,128]{1,0:T(8,128)(2,1)} %get-tuple-element.18), channel_id=1, source_target_pairs={{0,20},{1,17},{2,22},{3,19},{4,16},{5,21},{6,18},{7,23},{8,28},{9,... | collective-permute-start | bytes 196616 | tf_op jit(solution)/shard_map/ppermute | solution.py:362
  11.3 6.9 %collective-permute-start.4 = (bf16[256,128]{1,0:T(8,128)(2,1)}, bf16[256,128]{1,0:T(8,128)(2,1)S(1)}, u32[]{:S(2)}, u32[]{:S(2)}) collective-permute-start(bf16[256,128]{1,0:T(8,128)(2,1)} %get-tuple-element.20), channel_id=1, source_target_pairs={{0,4},{1,1},{2,6},{3,3},{4,0},{5,5},{6,2},{7,7},{8,12},{9,9},{10,1... | collective-permute-start | bytes 196616 | tf_op jit(solution)/shard_map/ppermute | solution.py:362
  18.2 2.2 %copy-start.8 = (bf16[512,128]{1,0:T(8,128)(2,1)}, bf16[512,128]{1,0:T(8,128)(2,1)S(1)}, u32[]{:S(2)}) copy-start(bf16[512,128]{1,0:T(8,128)(2,1)S(1)} %constant_dynamic-update-slice_fusion.2.refs_1_) | copy-start | bytes 393220
  18.2 5.0 %collective-permute-start.6 = (bf16[512,128]{1,0:T(8,128)(2,1)S(1)}, bf16[512,128]{1,0:T(8,128)(2,1)S(1)}, u32[]{:S(2)}, u32[]{:S(2)}) collective-permute-start(bf16[512,128]{1,0:T(8,128)(2,1)S(1)} %constant_dynamic-update-slice_fusion.2.refs_1_), channel_id=1, source_target_pairs={{0,2},{1,3},{2,0},{3,1},{4,6},{5,7},{6,4},{7,5},{8,10},{9,11},{10,... | collective-permute-start | bytes 393224 | tf_op jit(solution)/shard_map/ppermute | solution.py:367
  19.8 6.4 %copy-start.9 = (bf16[512,128]{1,0:T(8,128)(2,1)}, bf16[512,128]{1,0:T(8,128)(2,1)S(1)}, u32[]{:S(2)}) copy-start(bf16[512,128]{1,0:T(8,128)(2,1)S(1)} %constant_dynamic-update-slice_fusion.refs_0_) | copy-start | bytes 393220
  19.8 5.0 %collective-permute-start.5 = (bf16[512,128]{1,0:T(8,128)(2,1)S(1)}, bf16[512,128]{1,0:T(8,128)(2,1)S(1)}, u32[]{:S(2)}, u32[]{:S(2)}) collective-permute-start(bf16[512,128]{1,0:T(8,128)(2,1)S(1)} %constant_dynamic-update-slice_fusion.refs_0_), channel_id=1, source_target_pairs={{0,2},{1,3},{2,0},{3,1},{4,6},{5,7},{6,4},{7,5},{8,10},{9,11},{10,... | collective-permute-start | bytes 393224 | tf_op jit(solution)/shard_map/ppermute | solution.py:367
  20.4 4.4 %collective-permute-start.8 = (bf16[512,128]{1,0:T(8,128)(2,1)S(1)}, bf16[512,128]{1,0:T(8,128)(2,1)S(1)}, u32[]{:S(2)}, u32[]{:S(2)}) collective-permute-start(bf16[512,128]{1,0:T(8,128)(2,1)S(1)} %constant_dynamic-update-slice_fusion.2.refs_1_), channel_id=1, source_target_pairs={{0,1},{1,0},{2,3},{3,2},{4,5},{5,4},{6,7},{7,6},{8,9},{9,8},{10,11... | collective-permute-start | bytes 393224 | tf_op jit(solution)/shard_map/ppermute | solution.py:373
  20.4 4.5 %collective-permute-start.7 = (bf16[512,128]{1,0:T(8,128)(2,1)S(1)}, bf16[512,128]{1,0:T(8,128)(2,1)S(1)}, u32[]{:S(2)}, u32[]{:S(2)}) collective-permute-start(bf16[512,128]{1,0:T(8,128)(2,1)S(1)} %constant_dynamic-update-slice_fusion.refs_0_), channel_id=1, source_target_pairs={{0,1},{1,0},{2,3},{3,2},{4,5},{5,4},{6,7},{7,6},{8,9},{9,8},{10,11... | collective-permute-start | bytes 393224 | tf_op jit(solution)/shard_map/ppermute | solution.py:373
  23.2 3.0 %copy-start.10 = (bf16[512,128]{1,0:T(8,128)(2,1)}, bf16[512,128]{1,0:T(8,128)(2,1)S(1)}, u32[]{:S(2)}) copy-start(bf16[512,128]{1,0:T(8,128)(2,1)S(1)} %collective-permute-done.6.refs_3_) | copy-start | bytes 393220
  23.2 1.7 %collective-permute-start.10 = (bf16[512,128]{1,0:T(8,128)(2,1)S(1)}, bf16[512,128]{1,0:T(8,128)(2,1)S(1)}, u32[]{:S(2)}, u32[]{:S(2)}) collective-permute-start(bf16[512,128]{1,0:T(8,128)(2,1)S(1)} %collective-permute-done.6.refs_3_), channel_id=1, source_target_pairs={{0,1},{1,0},{2,3},{3,2},{4,5},{5,4},{6,7},{7,6},{8,9},{9,8},{10,11... | collective-permute-start | bytes 393224 | tf_op jit(solution)/shard_map/ppermute | solution.py:373
  24.9 1.4 %copy-start.11 = (bf16[512,128]{1,0:T(8,128)(2,1)}, bf16[512,128]{1,0:T(8,128)(2,1)S(1)}, u32[]{:S(2)}) copy-start(bf16[512,128]{1,0:T(8,128)(2,1)S(1)} %collective-permute-done.5.refs_2_) | copy-start | bytes 393220
  24.9 1.3 %collective-permute-start.9 = (bf16[512,128]{1,0:T(8,128)(2,1)S(1)}, bf16[512,128]{1,0:T(8,128)(2,1)S(1)}, u32[]{:S(2)}, u32[]{:S(2)}) collective-permute-start(bf16[512,128]{1,0:T(8,128)(2,1)S(1)} %collective-permute-done.5.refs_2_), channel_id=1, source_target_pairs={{0,1},{1,0},{2,3},{3,2},{4,5},{5,4},{6,7},{7,6},{8,9},{9,8},{10,11... | collective-permute-start | bytes 393224 | tf_op jit(solution)/shard_map/ppermute | solution.py:373
  41.7 8.4 %collective-permute-start.11 = (f32[128,128]{1,0:T(8,128)}, f32[128,128]{1,0:T(8,128)S(1)}, u32[]{:S(2)}, u32[]{:S(2)}) collective-permute-start(f32[128,128]{1,0:T(8,128)} %get-tuple-element.21), channel_id=1, source_target_pairs={{0,28},{4,24},{8,20},{12,16},{16,12},{20,8},{24,4},{28,0},{1,29},{... | collective-permute-start | bytes 196616 | tf_op jit(solution)/shard_map/ppermute | solution.py:519
  44.8 8.4 %collective-permute-start.12 = (f32[128,128]{1,0:T(8,128)}, f32[128,128]{1,0:T(8,128)S(1)}, u32[]{:S(2)}, u32[]{:S(2)}) collective-permute-start(f32[128,128]{1,0:T(8,128)} %get-tuple-element.22), channel_id=1, source_target_pairs={{0,24},{4,28},{8,16},{12,20},{16,8},{20,12},{24,0},{28,4},{1,25},{... | collective-permute-start | bytes 196616 | tf_op jit(solution)/shard_map/ppermute | solution.py:519
  45.8 11.6 %collective-permute-start.13 = (f32[128,128]{1,0:T(8,128)}, f32[128,128]{1,0:T(8,128)S(1)}, u32[]{:S(2)}, u32[]{:S(2)}) collective-permute-start(f32[128,128]{1,0:T(8,128)} %get-tuple-element.23), channel_id=1, source_target_pairs={{0,20},{4,16},{8,28},{12,24},{16,4},{20,0},{24,12},{28,8},{1,21},{... | collective-permute-start | bytes 196616 | tf_op jit(solution)/shard_map/ppermute | solution.py:519
  47.6 9.8 %collective-permute-start.14 = (f32[128,128]{1,0:T(8,128)}, f32[128,128]{1,0:T(8,128)S(1)}, u32[]{:S(2)}, u32[]{:S(2)}) collective-permute-start(f32[128,128]{1,0:T(8,128)} %get-tuple-element.24), channel_id=1, source_target_pairs={{0,16},{4,20},{8,24},{12,28},{16,0},{20,4},{24,8},{28,12},{1,17},{... | collective-permute-start | bytes 196616 | tf_op jit(solution)/shard_map/ppermute | solution.py:519
  49.4 8.0 %collective-permute-start.15 = (f32[128,128]{1,0:T(8,128)}, f32[128,128]{1,0:T(8,128)S(1)}, u32[]{:S(2)}, u32[]{:S(2)}) collective-permute-start(f32[128,128]{1,0:T(8,128)} %get-tuple-element.25), channel_id=1, source_target_pairs={{0,12},{4,8},{8,4},{12,0},{16,28},{20,24},{24,20},{28,16},{1,13},{... | collective-permute-start | bytes 196616 | tf_op jit(solution)/shard_map/ppermute | solution.py:519
  50.1 7.7 %copy-start.1 = (f32[128,128]{1,0:T(8,128)}, f32[128,128]{1,0:T(8,128)S(1)}, u32[]{:S(2)}) copy-start(f32[128,128]{1,0:T(8,128)S(1)} %collective-permute-done.11.refs_0_) | copy-start | bytes 196612
  50.1 7.5 %collective-permute-start.16 = (f32[128,128]{1,0:T(8,128)}, f32[128,128]{1,0:T(8,128)S(1)}, u32[]{:S(2)}, u32[]{:S(2)}) collective-permute-start(f32[128,128]{1,0:T(8,128)} %get-tuple-element.26), channel_id=1, source_target_pairs={{0,8},{4,12},{8,0},{12,4},{16,24},{20,28},{24,16},{28,20},{1,9},{5... | collective-permute-start | bytes 196616 | tf_op jit(solution)/shard_map/ppermute | solution.py:519
  53.2 4.7 %copy-start.2 = (f32[128,128]{1,0:T(8,128)}, f32[128,128]{1,0:T(8,128)S(1)}, u32[]{:S(2)}) copy-start(f32[128,128]{1,0:T(8,128)S(1)} %collective-permute-done.12.refs_1_) | copy-start | bytes 196612
  53.2 4.7 %collective-permute-start.17 = (f32[128,128]{1,0:T(8,128)}, f32[128,128]{1,0:T(8,128)S(1)}, u32[]{:S(2)}, u32[]{:S(2)}) collective-permute-start(f32[128,128]{1,0:T(8,128)} %get-tuple-element.27), channel_id=1, source_target_pairs={{0,4},{4,0},{8,12},{12,8},{16,20},{20,16},{24,28},{28,24},{1,5},{5... | collective-permute-start | bytes 196616 | tf_op jit(solution)/shard_map/ppermute | solution.py:519
  (10 other events, 8.5 us)

commit v6 on v5

--- a/solution.py
+++ b/solution.py
@@ -17,6 +17,11 @@
 UPPER_BOUND = 12.1
 LANES = 128
 CORES = 2
+CODE_LIMIT = 32767.0
+FACTOR_UNIT = 8192.0
+LOWEST_EXPONENT = -120.0
+TINY = 1e-37
+HEADER_ROWS = 16
 
 
 def split_constant(matrix):
@@ -340,13 +345,38 @@
 
     lax.fori_loop(0, own_count * side // step_rows, collect, 0)
 
+    lane_index = lax.broadcasted_iota(jnp.int32, (tiles, LANES), 1)
     for step in range(slab_count):
         slab = partner_of(slab_index, step, slab_count)[0]
-        for own in range(own_count):
-            for plane in range(planes):
-                start = own * tiles * side + slab * planes + plane
-                row = (own * planes + plane) * tiles
-                out_refs[step][row : row + tiles, :] = total[pl.ds(start, tiles, stride=side), :]
+        exponents = jnp.zeros((tiles, LANES), jnp.float32)
+        factors = jnp.zeros((tiles, LANES), jnp.float32)
+        codes = []
+        for chunk in range(own_count * planes):
+            own, plane = divmod(chunk, planes)
+            start = own * tiles * side + slab * planes + plane
+            value = total[pl.ds(start, tiles, stride=side), :]
+            code, exponent, factor = encode(value)
+            codes.append(code)
+            exponents = jnp.where(lane_index == chunk, exponent, exponents)
+            factors = jnp.where(lane_index == chunk, factor, factors)
+            if chunk % 2:
+                pair = jnp.concatenate(codes[-2:], axis=0)
+                out_refs[step][tiles * (chunk - 1) : tiles * (chunk + 1), :] = whole_codes(pair)
+        header = jnp.concatenate([exponents, factors], axis=0)
+        out_refs[step][tiles * own_count * planes :, :] = whole_codes(header)
+
+
+def whole_codes(value):
+    return value.astype(jnp.int32).astype(jnp.int16)
+
+
+def encode(value):
+    largest = jnp.max(jnp.abs(value), axis=1, keepdims=True)
+    exponent = jnp.maximum(jnp.floor(jnp.log2(jnp.maximum(largest, TINY))), LOWEST_EXPONENT)
+    lifted = 1.0 / jnp.exp2(exponent)
+    factor = jnp.maximum(jnp.ceil(largest * lifted * FACTOR_UNIT), 1.0)
+    code = jnp.floor(value * lifted * (CODE_LIMIT * FACTOR_UNIT / factor) + 0.5)
+    return jnp.clip(code, -CODE_LIMIT, CODE_LIMIT), exponent, factor
 
 
 def gather_boxes(blocks, slab_count, pair_count):
@@ -410,14 +440,13 @@
         in_specs=[vectors] * CORES,
         out_specs=[vectors] * turns,
         scratch_shapes=[pltpu.VMEM((CORES * row_count * cells // LANES, LANES), jnp.float32)],
+        compiler_params=pltpu.CompilerParams(vmem_limit_bytes=60 * 1024 * 1024),
     )(orbitals, other)
 
 
 def unpack_kernel(sizes, *refs):
-    own_count, slab_count = sizes
-    block_refs, out_ref, blocks, lines, sems = refs[:slab_count], *refs[slab_count:]
-    row_count, cells = out_ref.shape
-    tiles = cells // LANES
+    own_count, slab_count, tiles = sizes
+    block_refs, out_ref, blocks, sems = refs[:slab_count], *refs[slab_count:]
     slab_index = lax.axis_index("slab")
     copies = []
     for index in range(slab_count):
@@ -427,30 +456,36 @@
         step = slab_count - 1 - index
         copies[index].wait()
         first = partner_of(slab_index, step, slab_count)[1] * own_count
-        for own in range(own_count):
-            for tile in range(0, tiles, 8):
-                start = tile * row_count + first + own
-                row = own * tiles + tile
-                lines[pl.ds(start, 8, stride=row_count), :] = blocks[index, row : row + 8, :]
-    for tile in range(tiles):
-        columns = slice(tile * LANES, (tile + 1) * LANES)
-        out_ref[:, columns] = lines[tile * row_count : (tile + 1) * row_count, :]
+        row_count = own_count * tiles
+        header = blocks[index, row_count:, :].astype(jnp.int32).astype(jnp.float32)
+        units = jnp.exp2(header[:8, :])
+        factors = header[8:, :] * (1.0 / (CODE_LIMIT * FACTOR_UNIT))
+        for pair in range(row_count // 16):
+            codes = blocks[index, 16 * pair : 16 * pair + 16, :].astype(jnp.int32).astype(jnp.float32)
+            for half in range(2):
+                chunk = 2 * pair + half
+                own, tile = divmod(8 * chunk, tiles)
+                row = first + own
+                start = (row // 8 * tiles + tile) * 8 + row % 8
+                value = codes[8 * half : 8 * half + 8, :] * factors[:, chunk : chunk + 1]
+                out_ref[pl.ds(start, 8, stride=8), :] = value * units[:, chunk : chunk + 1]
 
 
 def unpack(blocks, own_count, cells):
     slab_count = len(blocks)
     row_count = own_count * slab_count
-    return pl.pallas_call(
-        functools.partial(unpack_kernel, (own_count, slab_count)),
-        out_shape=jax.ShapeDtypeStruct((row_count, cells), jnp.float32),
+    tiles = cells // LANES
+    out = pl.pallas_call(
+        functools.partial(unpack_kernel, (own_count, slab_count, tiles)),
+        out_shape=jax.ShapeDtypeStruct((row_count * tiles, LANES), jnp.float32),
         in_specs=[pl.BlockSpec(memory_space=pl.ANY)] * slab_count,
         out_specs=pl.BlockSpec(memory_space=pltpu.VMEM),
         scratch_shapes=[
-            pltpu.VMEM((slab_count,) + blocks[0].shape, jnp.float32),
-            pltpu.VMEM((row_count * cells // LANES, LANES), jnp.float32),
+            pltpu.VMEM((slab_count,) + blocks[0].shape, jnp.int16),
             pltpu.SemaphoreType.DMA((slab_count,)),
         ],
     )(*blocks)
+    return out.reshape(row_count // 8, tiles, 8, LANES).transpose(0, 2, 1, 3).reshape(row_count, cells)
 
 
 def team_forces(match, centers, blocks, side, slab_count, pair_count):
@@ -477,7 +512,7 @@
     flops = 2 * solves * side * 3 * 2 * (cells * cells // 2 + cells * group * side)
     return pl.pallas_call(
         functools.partial(force_kernel, sizes),
-        out_shape=[jax.ShapeDtypeStruct((rows, LANES), jnp.float32)] * slab_count,
+        out_shape=[jax.ShapeDtypeStruct((rows + HEADER_ROWS, LANES), jnp.int16)] * slab_count,
         in_specs=[distant] * 2 + [either] * len(blocks) + [distant] * len(constants),
         out_specs=[vectors] * slab_count,
         scratch_shapes=[

time: 61.1 us -> 59.5 us (0.974)
  starting transfers between devices: 26.4 us -> 24.2 us
    ppermute x7, starting transfers between devices: 13.4 us -> 11.2 us  [shards(): received.append(lax.ppermute(forces[step], 'slab', perm))]
where the time goes in v6:
time: 59.5 us; the launch traced here: 59.3 us
  starting transfers between devices  24.2 us (41%)
  Pallas kernels  19.8 us (33%)
  waiting for transfers between devices  13.2 us (22%)
  local copies, waits for them, and re-layouts  1.95 us (3%)
    pallas_call x1, Pallas kernels, team_forces(): pl.pallas_call(functools.partial(force_kernel, sizes), out_shape=[jax.Sha...  15 us
    ppermute x7, starting transfers between devices, shards(): received.append(lax.ppermute(forces[step], 'slab', perm))  11.2 us
    ppermute x4, starting transfers between devices, gather_boxes(): arrived[turn] = lax.ppermute(blocks[turn], ('slab', 'pair'), perm)  9.85 us
    ppermute x2, waiting for transfers between devices, gather_boxes(): pieces.append([lax.ppermute(block, 'pair', perm) for block in own])  3.91 us
    ppermute x4, waiting for transfers between devices, gather_boxes(): arrived[turn] = lax.ppermute(blocks[turn], ('slab', 'pair'), perm)  3.71 us
    ppermute x7, waiting for transfers between devices, shards(): received.append(lax.ppermute(forces[step], 'slab', perm))  2.9 us
    pallas_call x1, Pallas kernels, unpack(): pl.pallas_call(functools.partial(unpack_kernel, (own_count, slab_count, t...  2.74 us
    ppermute x5, waiting for transfers between devices, swap_cores(): return lax.ppermute(block, 'pair', [(i, i ^ 1) for i in range(pair_count)])  2.67 us
  transfers between devices with their start and end apart: 18, of which 8 were waited for; matrix products, arithmetic and copies ran while one was open for 0% of the time, Pallas kernels for 0%

profile of v6, /device:TPU:0, one launch (start us, length us, event | category | flops | bytes accessed | tf_op | source)
XLA Modules:
  0.0 59.3 jit_solution(18171905866166909790)
XLA Ops:
  0.5 1.4 %collective-permute-done.refs_1_ = bf16[32,4096]{1,0:T(8,128)(2,1)S(1)} collective-permute-done((bf16[32,4096]{1,0:T(8,128)(2,1)}, bf16[32,4096]{1,0:T(8,128)(2,1)S(1)}, u32[]{:S(2)}, u32[]{:S(2)}) %collective-permute-start) | collective-permute-done | bytes 262176 | tf_op jit(solution)/shard_map/ppermute | solution.py:403
  1.8 0.7 %copy-done = bf16[32,4096]{1,0:T(8,128)(2,1)} copy-done((bf16[32,4096]{1,0:T(8,128)(2,1)}, bf16[32,4096]{1,0:T(8,128)(2,1)S(1)}, u32[]{:S(2)}) %copy-start) | copy-done | bytes 262168
  2.5 2.1 %shard_map.91 = (bf16[256,128]{1,0:T(8,128)(2,1)}, bf16[256,128]{1,0:T(8,128)(2,1)}, bf16[256,128]{1,0:T(8,128)(2,1)}, bf16[256,128]{1,0:T(8,128)(2,1)}) custom-call(bf16[32,4096]{1,0:T(8,128)(2,1)} %refs_0_.1, bf16[32,4096]{1,0:T(8,128)(2,1)} %copy-done), custom_call_target="tpu_custom_call" | custom-call | tf_op jit(solution)/shard_map/pallas_call | solution.py:437
  4.6 3.9 %collective-permute-start.3 = (bf16[256,128]{1,0:T(8,128)(2,1)}, bf16[256,128]{1,0:T(8,128)(2,1)S(1)}, u32[]{:S(2)}, u32[]{:S(2)}) collective-permute-start(bf16[256,128]{1,0:T(8,128)(2,1)} %get-tuple-element.19), channel_id=1, source_target_pairs={{0,12},{1,9},{2,14},{3,11},{4,8},{5,13},{6,10},{7,15},{8,4},{9,1},... | collective-permute-start | bytes 196616 | tf_op jit(solution)/shard_map/ppermute | solution.py:392
  8.5 2.4 %collective-permute-start.1 = (bf16[256,128]{1,0:T(8,128)(2,1)}, bf16[256,128]{1,0:T(8,128)(2,1)S(1)}, u32[]{:S(2)}, u32[]{:S(2)}) collective-permute-start(bf16[256,128]{1,0:T(8,128)(2,1)} %get-tuple-element.17), channel_id=1, source_target_pairs={{0,28},{1,25},{2,30},{3,27},{4,24},{5,29},{6,26},{7,31},{8,20},{9,... | collective-permute-start | bytes 196616 | tf_op jit(solution)/shard_map/ppermute | solution.py:392
  11.3 3.1 %collective-permute-start.4 = (bf16[256,128]{1,0:T(8,128)(2,1)}, bf16[256,128]{1,0:T(8,128)(2,1)S(1)}, u32[]{:S(2)}, u32[]{:S(2)}) collective-permute-start(bf16[256,128]{1,0:T(8,128)(2,1)} %get-tuple-element.20), channel_id=1, source_target_pairs={{0,4},{1,1},{2,6},{3,3},{4,0},{5,5},{6,2},{7,7},{8,12},{9,9},{10,1... | collective-permute-start | bytes 196616 | tf_op jit(solution)/shard_map/ppermute | solution.py:392
  14.5 3.7 %collective-permute-done.4 = bf16[256,128]{1,0:T(8,128)(2,1)S(1)} collective-permute-done((bf16[256,128]{1,0:T(8,128)(2,1)}, bf16[256,128]{1,0:T(8,128)(2,1)S(1)}, u32[]{:S(2)}, u32[]{:S(2)}) %collective-permute-start.4) | collective-permute-done | bytes 65568 | tf_op jit(solution)/shard_map/ppermute | solution.py:392
  18.2 1.6 %collective-permute-start.6 = (bf16[512,128]{1,0:T(8,128)(2,1)S(1)}, bf16[512,128]{1,0:T(8,128)(2,1)S(1)}, u32[]{:S(2)}, u32[]{:S(2)}) collective-permute-start(bf16[512,128]{1,0:T(8,128)(2,1)S(1)} %constant_dynamic-update-slice_fusion.2.refs_1_), channel_id=1, source_target_pairs={{0,2},{1,3},{2,0},{3,1},{4,6},{5,7},{6,4},{7,5},{8,10},{9,11},{10,... | collective-permute-start | bytes 393224 | tf_op jit(solution)/shard_map/ppermute | solution.py:397
  19.8 0.6 %collective-permute-start.5 = (bf16[512,128]{1,0:T(8,128)(2,1)S(1)}, bf16[512,128]{1,0:T(8,128)(2,1)S(1)}, u32[]{:S(2)}, u32[]{:S(2)}) collective-permute-start(bf16[512,128]{1,0:T(8,128)(2,1)S(1)} %constant_dynamic-update-slice_fusion.refs_0_), channel_id=1, source_target_pairs={{0,2},{1,3},{2,0},{3,1},{4,6},{5,7},{6,4},{7,5},{8,10},{9,11},{10,... | collective-permute-start | bytes 393224 | tf_op jit(solution)/shard_map/ppermute | solution.py:397
  20.9 2.3 %collective-permute-done.6.refs_3_ = bf16[512,128]{1,0:T(8,128)(2,1)S(1)} collective-permute-done((bf16[512,128]{1,0:T(8,128)(2,1)S(1)}, bf16[512,128]{1,0:T(8,128)(2,1)S(1)}, u32[]{:S(2)}, u32[]{:S(2)}) %collective-permute-start.6) | collective-permute-done | bytes 131104 | tf_op jit(solution)/shard_map/ppermute | solution.py:397
  23.2 1.6 %collective-permute-done.5.refs_2_ = bf16[512,128]{1,0:T(8,128)(2,1)S(1)} collective-permute-done((bf16[512,128]{1,0:T(8,128)(2,1)S(1)}, bf16[512,128]{1,0:T(8,128)(2,1)S(1)}, u32[]{:S(2)}, u32[]{:S(2)}) %collective-permute-start.5) | collective-permute-done | bytes 131104 | tf_op jit(solution)/shard_map/ppermute | solution.py:397
  24.9 1.3 %collective-permute-done.9.refs_6_ = bf16[512,128]{1,0:T(8,128)(2,1)S(1)} collective-permute-done((bf16[512,128]{1,0:T(8,128)(2,1)S(1)}, bf16[512,128]{1,0:T(8,128)(2,1)S(1)}, u32[]{:S(2)}, u32[]{:S(2)}) %collective-permute-start.9) | collective-permute-done | bytes 131104 | tf_op jit(solution)/shard_map/ppermute | solution.py:403
  26.2 0.6 copy-done.15
  26.8 15.0 %shard_map.92 = (s16[144,128]{1,0:T(8,128)(2,1)}, s16[144,128]{1,0:T(8,128)(2,1)}, s16[144,128]{1,0:T(8,128)(2,1)}, s16[144,128]{1,0:T(8,128)(2,1)}, s16[144,128...) custom-call(s32[1,4,16]{2,1,0:T(4,128)} %match_ref.1, ...), custom_call_target="tpu_custom_call" | custom-call | flops 4831838208 | bytes 8388608 | tf_op jit(solution)/shard_map/pallas_call | solution.py:513
  41.8 3.1 %collective-permute-start.11 = (s16[144,128]{1,0:T(8,128)(2,1)}, s16[144,128]{1,0:T(8,128)(2,1)S(1)}, u32[]{:S(2)}, u32[]{:S(2)}) collective-permute-start(s16[144,128]{1,0:T(8,128)(2,1)} %get-tuple-element.21), channel_id=1, source_target_pairs={{0,28},{4,24},{8,20},{12,16},{16,12},{20,8},{24,4},{28,0},{1,29},{... | collective-permute-start | bytes 110600 | tf_op jit(solution)/shard_map/ppermute | solution.py:554
  44.9 1.0 %collective-permute-start.12 = (s16[144,128]{1,0:T(8,128)(2,1)}, s16[144,128]{1,0:T(8,128)(2,1)S(1)}, u32[]{:S(2)}, u32[]{:S(2)}) collective-permute-start(s16[144,128]{1,0:T(8,128)(2,1)} %get-tuple-element.22), channel_id=1, source_target_pairs={{0,24},{4,28},{8,16},{12,20},{16,8},{20,12},{24,0},{28,4},{1,25},{... | collective-permute-start | bytes 110600 | tf_op jit(solution)/shard_map/ppermute | solution.py:554
  45.9 1.9 %collective-permute-start.13 = (s16[144,128]{1,0:T(8,128)(2,1)}, s16[144,128]{1,0:T(8,128)(2,1)S(1)}, u32[]{:S(2)}, u32[]{:S(2)}) collective-permute-start(s16[144,128]{1,0:T(8,128)(2,1)} %get-tuple-element.23), channel_id=1, source_target_pairs={{0,20},{4,16},{8,28},{12,24},{16,4},{20,0},{24,12},{28,8},{1,21},{... | collective-permute-start | bytes 110600 | tf_op jit(solution)/shard_map/ppermute | solution.py:554
  47.8 1.8 %collective-permute-start.14 = (s16[144,128]{1,0:T(8,128)(2,1)}, s16[144,128]{1,0:T(8,128)(2,1)S(1)}, u32[]{:S(2)}, u32[]{:S(2)}) collective-permute-start(s16[144,128]{1,0:T(8,128)(2,1)} %get-tuple-element.24), channel_id=1, source_target_pairs={{0,16},{4,20},{8,24},{12,28},{16,0},{20,4},{24,8},{28,12},{1,17},{... | collective-permute-start | bytes 110600 | tf_op jit(solution)/shard_map/ppermute | solution.py:554
  49.5 0.7 %collective-permute-start.15 = (s16[144,128]{1,0:T(8,128)(2,1)}, s16[144,128]{1,0:T(8,128)(2,1)S(1)}, u32[]{:S(2)}, u32[]{:S(2)}) collective-permute-start(s16[144,128]{1,0:T(8,128)(2,1)} %get-tuple-element.25), channel_id=1, source_target_pairs={{0,12},{4,8},{8,4},{12,0},{16,28},{20,24},{24,20},{28,16},{1,13},{... | collective-permute-start | bytes 110600 | tf_op jit(solution)/shard_map/ppermute | solution.py:554
  50.3 1.5 %collective-permute-start.16 = (s16[144,128]{1,0:T(8,128)(2,1)}, s16[144,128]{1,0:T(8,128)(2,1)S(1)}, u32[]{:S(2)}, u32[]{:S(2)}) collective-permute-start(s16[144,128]{1,0:T(8,128)(2,1)} %get-tuple-element.26), channel_id=1, source_target_pairs={{0,8},{4,12},{8,0},{12,4},{16,24},{20,28},{24,16},{28,20},{1,9},{5... | collective-permute-start | bytes 110600 | tf_op jit(solution)/shard_map/ppermute | solution.py:554
  51.8 1.3 %collective-permute-start.17 = (s16[144,128]{1,0:T(8,128)(2,1)}, s16[144,128]{1,0:T(8,128)(2,1)S(1)}, u32[]{:S(2)}, u32[]{:S(2)}) collective-permute-start(s16[144,128]{1,0:T(8,128)(2,1)} %get-tuple-element.27), channel_id=1, source_target_pairs={{0,4},{4,0},{8,12},{12,8},{16,20},{20,16},{24,28},{28,24},{1,5},{5... | collective-permute-start | bytes 110600 | tf_op jit(solution)/shard_map/ppermute | solution.py:554
  53.4 1.2 %collective-permute-done.15.refs_4_ = s16[144,128]{1,0:T(8,128)(2,1)S(1)} collective-permute-done((s16[144,128]{1,0:T(8,128)(2,1)}, s16[144,128]{1,0:T(8,128)(2,1)S(1)}, u32[]{:S(2)}, u32[]{:S(2)}) %collective-permute-start.15) | collective-permute-done | bytes 36896 | tf_op jit(solution)/shard_map/ppermute | solution.py:554
  54.6 1.3 %collective-permute-done.17.refs_6_ = s16[144,128]{1,0:T(8,128)(2,1)S(1)} collective-permute-done((s16[144,128]{1,0:T(8,128)(2,1)}, s16[144,128]{1,0:T(8,128)(2,1)S(1)}, u32[]{:S(2)}, u32[]{:S(2)}) %collective-permute-start.17) | collective-permute-done | bytes 36896 | tf_op jit(solution)/shard_map/ppermute | solution.py:554
  56.5 2.7 %shard_map.93 = f32[1024,128]{1,0:T(8,128)} custom-call(s16[144,128]{1,0:T(8,128)(2,1)} %copy-done.1, s16[144,128]{1,0:T(8,128)(2,1)} %copy-done.2, s16[144,128]{1,0:T(8,128)(2,1)} %copy-done.3, s16[144,128]{1,0:T(8,128)(2,1)} %copy-done.4, s16[144,128]{1,0:T(8,128)(2,1)} %copy-done.5, s16[144,128]{1,0:T(8,128)(2,1)} %copy-done.6, ...), custom_call_target="tpu_custom_call" | custom-call | tf_op jit(solution)/shard_map/pallas_call | solution.py:478
  (51 shorter events, 2.4 us)
Async XLA Ops:
  0.0 1.8 %collective-permute-start = (bf16[32,4096]{1,0:T(8,128)(2,1)}, bf16[32,4096]{1,0:T(8,128)(2,1)S(1)}, u32[]{:S(2)}, u32[]{:S(2)}) collective-permute-start(bf16[32,4096]{1,0:T(8,128)(2,1)} %refs_0_.1), channel_id=1, source_target_pairs={{0,1},{1,0},{2,3},{3,2},{4,5},{5,4},{6,7},{7,6},{8,9},{9,8},{10,11... | collective-permute-start | bytes 786440 | tf_op jit(solution)/shard_map/ppermute | solution.py:403
  4.6 9.9 %collective-permute-start.3 = (bf16[256,128]{1,0:T(8,128)(2,1)}, bf16[256,128]{1,0:T(8,128)(2,1)S(1)}, u32[]{:S(2)}, u32[]{:S(2)}) collective-permute-start(bf16[256,128]{1,0:T(8,128)(2,1)} %get-tuple-element.19), channel_id=1, source_target_pairs={{0,12},{1,9},{2,14},{3,11},{4,8},{5,13},{6,10},{7,15},{8,4},{9,1},... | collective-permute-start | bytes 196616 | tf_op jit(solution)/shard_map/ppermute | solution.py:392
  8.5 11.3 %collective-permute-start.1 = (bf16[256,128]{1,0:T(8,128)(2,1)}, bf16[256,128]{1,0:T(8,128)(2,1)S(1)}, u32[]{:S(2)}, u32[]{:S(2)}) collective-permute-start(bf16[256,128]{1,0:T(8,128)(2,1)} %get-tuple-element.17), channel_id=1, source_target_pairs={{0,28},{1,25},{2,30},{3,27},{4,24},{5,29},{6,26},{7,31},{8,20},{9,... | collective-permute-start | bytes 196616 | tf_op jit(solution)/shard_map/ppermute | solution.py:392
  10.9 8.9 %collective-permute-start.2 = (bf16[256,128]{1,0:T(8,128)(2,1)}, bf16[256,128]{1,0:T(8,128)(2,1)S(1)}, u32[]{:S(2)}, u32[]{:S(2)}) collective-permute-start(bf16[256,128]{1,0:T(8,128)(2,1)} %get-tuple-element.18), channel_id=1, source_target_pairs={{0,20},{1,17},{2,22},{3,19},{4,16},{5,21},{6,18},{7,23},{8,28},{9,... | collective-permute-start | bytes 196616 | tf_op jit(solution)/shard_map/ppermute | solution.py:392
  11.3 6.9 %collective-permute-start.4 = (bf16[256,128]{1,0:T(8,128)(2,1)}, bf16[256,128]{1,0:T(8,128)(2,1)S(1)}, u32[]{:S(2)}, u32[]{:S(2)}) collective-permute-start(bf16[256,128]{1,0:T(8,128)(2,1)} %get-tuple-element.20), channel_id=1, source_target_pairs={{0,4},{1,1},{2,6},{3,3},{4,0},{5,5},{6,2},{7,7},{8,12},{9,9},{10,1... | collective-permute-start | bytes 196616 | tf_op jit(solution)/shard_map/ppermute | solution.py:392
  18.2 5.0 %collective-permute-start.6 = (bf16[512,128]{1,0:T(8,128)(2,1)S(1)}, bf16[512,128]{1,0:T(8,128)(2,1)S(1)}, u32[]{:S(2)}, u32[]{:S(2)}) collective-permute-start(bf16[512,128]{1,0:T(8,128)(2,1)S(1)} %constant_dynamic-update-slice_fusion.2.refs_1_), channel_id=1, source_target_pairs={{0,2},{1,3},{2,0},{3,1},{4,6},{5,7},{6,4},{7,5},{8,10},{9,11},{10,... | collective-permute-start | bytes 393224 | tf_op jit(solution)/shard_map/ppermute | solution.py:397
  19.8 6.4 %copy-start.9 = (bf16[512,128]{1,0:T(8,128)(2,1)}, bf16[512,128]{1,0:T(8,128)(2,1)S(1)}, u32[]{:S(2)}) copy-start(bf16[512,128]{1,0:T(8,128)(2,1)S(1)} %constant_dynamic-update-slice_fusion.refs_0_) | copy-start | bytes 393220
  19.8 5.0 %collective-permute-start.5 = (bf16[512,128]{1,0:T(8,128)(2,1)S(1)}, bf16[512,128]{1,0:T(8,128)(2,1)S(1)}, u32[]{:S(2)}, u32[]{:S(2)}) collective-permute-start(bf16[512,128]{1,0:T(8,128)(2,1)S(1)} %constant_dynamic-update-slice_fusion.refs_0_), channel_id=1, source_target_pairs={{0,2},{1,3},{2,0},{3,1},{4,6},{5,7},{6,4},{7,5},{8,10},{9,11},{10,... | collective-permute-start | bytes 393224 | tf_op jit(solution)/shard_map/ppermute | solution.py:397
  20.4 4.4 %collective-permute-start.8 = (bf16[512,128]{1,0:T(8,128)(2,1)S(1)}, bf16[512,128]{1,0:T(8,128)(2,1)S(1)}, u32[]{:S(2)}, u32[]{:S(2)}) collective-permute-start(bf16[512,128]{1,0:T(8,128)(2,1)S(1)} %constant_dynamic-update-slice_fusion.2.refs_1_), channel_id=1, source_target_pairs={{0,1},{1,0},{2,3},{3,2},{4,5},{5,4},{6,7},{7,6},{8,9},{9,8},{10,11... | collective-permute-start | bytes 393224 | tf_op jit(solution)/shard_map/ppermute | solution.py:403
  20.4 4.5 %collective-permute-start.7 = (bf16[512,128]{1,0:T(8,128)(2,1)S(1)}, bf16[512,128]{1,0:T(8,128)(2,1)S(1)}, u32[]{:S(2)}, u32[]{:S(2)}) collective-permute-start(bf16[512,128]{1,0:T(8,128)(2,1)S(1)} %constant_dynamic-update-slice_fusion.refs_0_), channel_id=1, source_target_pairs={{0,1},{1,0},{2,3},{3,2},{4,5},{5,4},{6,7},{7,6},{8,9},{9,8},{10,11... | collective-permute-start | bytes 393224 | tf_op jit(solution)/shard_map/ppermute | solution.py:403
  23.2 3.0 %copy-start.10 = (bf16[512,128]{1,0:T(8,128)(2,1)}, bf16[512,128]{1,0:T(8,128)(2,1)S(1)}, u32[]{:S(2)}) copy-start(bf16[512,128]{1,0:T(8,128)(2,1)S(1)} %collective-permute-done.6.refs_3_) | copy-start | bytes 393220
  23.2 1.7 %collective-permute-start.10 = (bf16[512,128]{1,0:T(8,128)(2,1)S(1)}, bf16[512,128]{1,0:T(8,128)(2,1)S(1)}, u32[]{:S(2)}, u32[]{:S(2)}) collective-permute-start(bf16[512,128]{1,0:T(8,128)(2,1)S(1)} %collective-permute-done.6.refs_3_), channel_id=1, source_target_pairs={{0,1},{1,0},{2,3},{3,2},{4,5},{5,4},{6,7},{7,6},{8,9},{9,8},{10,11... | collective-permute-start | bytes 393224 | tf_op jit(solution)/shard_map/ppermute | solution.py:403
  24.9 1.3 %collective-permute-start.9 = (bf16[512,128]{1,0:T(8,128)(2,1)S(1)}, bf16[512,128]{1,0:T(8,128)(2,1)S(1)}, u32[]{:S(2)}, u32[]{:S(2)}) collective-permute-start(bf16[512,128]{1,0:T(8,128)(2,1)S(1)} %collective-permute-done.5.refs_2_), channel_id=1, source_target_pairs={{0,1},{1,0},{2,3},{3,2},{4,5},{5,4},{6,7},{7,6},{8,9},{9,8},{10,11... | collective-permute-start | bytes 393224 | tf_op jit(solution)/shard_map/ppermute | solution.py:403
  41.8 8.4 %collective-permute-start.11 = (s16[144,128]{1,0:T(8,128)(2,1)}, s16[144,128]{1,0:T(8,128)(2,1)S(1)}, u32[]{:S(2)}, u32[]{:S(2)}) collective-permute-start(s16[144,128]{1,0:T(8,128)(2,1)} %get-tuple-element.21), channel_id=1, source_target_pairs={{0,28},{4,24},{8,20},{12,16},{16,12},{20,8},{24,4},{28,0},{1,29},{... | collective-permute-start | bytes 110600 | tf_op jit(solution)/shard_map/ppermute | solution.py:554
  44.9 6.9 %collective-permute-start.12 = (s16[144,128]{1,0:T(8,128)(2,1)}, s16[144,128]{1,0:T(8,128)(2,1)S(1)}, u32[]{:S(2)}, u32[]{:S(2)}) collective-permute-start(s16[144,128]{1,0:T(8,128)(2,1)} %get-tuple-element.22), channel_id=1, source_target_pairs={{0,24},{4,28},{8,16},{12,20},{16,8},{20,12},{24,0},{28,4},{1,25},{... | collective-permute-start | bytes 110600 | tf_op jit(solution)/shard_map/ppermute | solution.py:554
  45.9 7.5 %collective-permute-start.13 = (s16[144,128]{1,0:T(8,128)(2,1)}, s16[144,128]{1,0:T(8,128)(2,1)S(1)}, u32[]{:S(2)}, u32[]{:S(2)}) collective-permute-start(s16[144,128]{1,0:T(8,128)(2,1)} %get-tuple-element.23), channel_id=1, source_target_pairs={{0,20},{4,16},{8,28},{12,24},{16,4},{20,0},{24,12},{28,8},{1,21},{... | collective-permute-start | bytes 110600 | tf_op jit(solution)/shard_map/ppermute | solution.py:554
  47.8 5.6 %collective-permute-start.14 = (s16[144,128]{1,0:T(8,128)(2,1)}, s16[144,128]{1,0:T(8,128)(2,1)S(1)}, u32[]{:S(2)}, u32[]{:S(2)}) collective-permute-start(s16[144,128]{1,0:T(8,128)(2,1)} %get-tuple-element.24), channel_id=1, source_target_pairs={{0,16},{4,20},{8,24},{12,28},{16,0},{20,4},{24,8},{28,12},{1,17},{... | collective-permute-start | bytes 110600 | tf_op jit(solution)/shard_map/ppermute | solution.py:554
  49.5 5.1 %collective-permute-start.15 = (s16[144,128]{1,0:T(8,128)(2,1)}, s16[144,128]{1,0:T(8,128)(2,1)S(1)}, u32[]{:S(2)}, u32[]{:S(2)}) collective-permute-start(s16[144,128]{1,0:T(8,128)(2,1)} %get-tuple-element.25), channel_id=1, source_target_pairs={{0,12},{4,8},{8,4},{12,0},{16,28},{20,24},{24,20},{28,16},{1,13},{... | collective-permute-start | bytes 110600 | tf_op jit(solution)/shard_map/ppermute | solution.py:554
  50.3 5.7 %copy-start.1 = (s16[144,128]{1,0:T(8,128)(2,1)}, s16[144,128]{1,0:T(8,128)(2,1)S(1)}, u32[]{:S(2)}) copy-start(s16[144,128]{1,0:T(8,128)(2,1)S(1)} %collective-permute-done.11.refs_0_) | copy-start | bytes 110596
  50.3 4.3 %collective-permute-start.16 = (s16[144,128]{1,0:T(8,128)(2,1)}, s16[144,128]{1,0:T(8,128)(2,1)S(1)}, u32[]{:S(2)}, u32[]{:S(2)}) collective-permute-start(s16[144,128]{1,0:T(8,128)(2,1)} %get-tuple-element.26), channel_id=1, source_target_pairs={{0,8},{4,12},{8,0},{12,4},{16,24},{20,28},{24,16},{28,20},{1,9},{5... | collective-permute-start | bytes 110600 | tf_op jit(solution)/shard_map/ppermute | solution.py:554
  51.8 4.2 %copy-start.2 = (s16[144,128]{1,0:T(8,128)(2,1)}, s16[144,128]{1,0:T(8,128)(2,1)S(1)}, u32[]{:S(2)}) copy-start(s16[144,128]{1,0:T(8,128)(2,1)S(1)} %collective-permute-done.12.refs_1_) | copy-start | bytes 110596
  51.8 4.2 %collective-permute-start.17 = (s16[144,128]{1,0:T(8,128)(2,1)}, s16[144,128]{1,0:T(8,128)(2,1)S(1)}, u32[]{:S(2)}, u32[]{:S(2)}) collective-permute-start(s16[144,128]{1,0:T(8,128)(2,1)} %get-tuple-element.27), channel_id=1, source_target_pairs={{0,4},{4,0},{8,12},{12,8},{16,20},{20,16},{24,28},{28,24},{1,5},{5... | collective-permute-start | bytes 110600 | tf_op jit(solution)/shard_map/ppermute | solution.py:554
  53.4 2.6 %copy-start.3 = (s16[144,128]{1,0:T(8,128)(2,1)}, s16[144,128]{1,0:T(8,128)(2,1)S(1)}, u32[]{:S(2)}) copy-start(s16[144,128]{1,0:T(8,128)(2,1)S(1)} %collective-permute-done.13.refs_2_) | copy-start | bytes 110596
  53.4 2.6 %copy-start.4 = (s16[144,128]{1,0:T(8,128)(2,1)}, s16[144,128]{1,0:T(8,128)(2,1)S(1)}, u32[]{:S(2)}) copy-start(s16[144,128]{1,0:T(8,128)(2,1)S(1)} %collective-permute-done.14.refs_3_) | copy-start | bytes 110596
  (10 other events, 12.3 us)

commit v7 on v6

--- a/solution.py
+++ b/solution.py
@@ -64,42 +64,19 @@
     return jnp.dot(left, right, preferred_element_type=jnp.float32)
 
 
-def partner_of(index, step, count):
-    if count & (count - 1) == 0:
-        return index ^ step, index ^ step
-    return (index + step) % count, (index + count - step) % count
-
-
-def slab_step(turn, core):
-    return CORES * turn + CORES - 1 - core
-
-
-def turn_groups(slab_count):
-    turns = list(reversed(range(slab_count // CORES)))
-    middle = (len(turns) + 1) // 2
-    return [group for group in (turns[:middle], turns[middle:]) if group]
-
-
-def block_places(slab_index, pair_index, slab_count, pair_count):
+def piece_places(pair_index, pair_count):
     chips = pair_count // CORES
     chip = pair_index // CORES
     for core_step in range(CORES):
-        core = (pair_index + core_step) % CORES
         for chip_step in range(chips):
-            source = (chip + chips - chip_step) % chips
-            for turns in turn_groups(slab_count):
-                steps = [slab_step(turn, core) for turn in turns]
-                yield [(source, partner_of(slab_index, step, slab_count)[1]) for step in steps]
+            yield (chip + chips - chip_step) % chips * CORES + (pair_index + core_step) % CORES
 
 
 def force_kernel(sizes, match_ref, centers_ref, *refs):
-    slab_count, pair_count = sizes[3:]
-    block_count = len(turn_groups(slab_count)) * pair_count
-    block_refs = refs[:block_count]
-    constant_refs = refs[block_count : block_count + 6]
-    out_refs = refs[block_count + 6 : block_count + 6 + slab_count]
-    scratch = refs[block_count + 6 + slab_count :]
-    force_body(sizes, match_ref, centers_ref, block_refs, constant_refs, out_refs, *scratch)
+    pair_count = sizes[4]
+    block_refs, constant_refs = refs[:pair_count], refs[pair_count : pair_count + 6]
+    out_ref, scratch = refs[pair_count + 6], refs[pair_count + 7 :]
+    force_body(sizes, match_ref, centers_ref, block_refs, constant_refs, out_ref, *scratch)
 
 
 def force_body(
@@ -108,7 +85,7 @@
     centers_hbm,
     block_refs,
     constant_refs,
-    out_refs,
+    out_ref,
     match_ref,
     centers_ref,
     boxes_ref,
@@ -139,14 +116,9 @@
     slab_index = lax.axis_index("slab")
     pair_index = lax.axis_index("pair")
 
-    sources = [match_hbm, centers_hbm]
+    sources = [match_hbm, centers_hbm, *block_refs]
     targets = [match_ref, centers_ref]
-    block_rows = boxes_ref.shape[2]
-    places = block_places(slab_index, pair_index, slab_count, pair_count)
-    for block_ref, group_places in zip(block_refs, places):
-        for index, place in enumerate(group_places):
-            sources.append(block_ref.at[index * block_rows : (index + 1) * block_rows])
-            targets.append(boxes_ref.at[place])
+    targets += [boxes_ref.at[pair] for pair in piece_places(pair_index, pair_count)]
     copies = []
     for source, target in zip(sources, targets):
         copies.append(pltpu.make_async_copy(source, target, sems.at[len(copies)]))
@@ -177,17 +149,17 @@
         copy.wait()
 
     def spread(index, carry):
-        chip = index // slab_count
+        pair = index // slab_count
         slab = index % slab_count
-        for chunk in range(CORES * own_count * planes // 2):
-            block = boxes_ref[chip, slab, 16 * chunk : 16 * chunk + 16, :].astype(jnp.float32)
+        for chunk in range(own_count * planes // 2):
+            block = boxes_ref[pair, slab, 16 * chunk : 16 * chunk + 16, :].astype(jnp.float32)
             for half in range(2):
-                member, plane = divmod(2 * chunk + half, planes)
-                start = (chip * CORES * own_count + member) * tiles * pitch + REACH + slab * planes + plane
+                own, plane = divmod(2 * chunk + half, planes)
+                start = (pair * own_count + own) * tiles * pitch + REACH + slab * planes + plane
                 fields[pl.ds(start, tiles, stride=pitch), :] = block[8 * half : 8 * half + 8, :]
         return carry
 
-    lax.fori_loop(0, pair_count // CORES * slab_count, spread, 0)
+    lax.fori_loop(0, pair_count * slab_count, spread, 0)
 
     step_rows = 16
     lane = lax.broadcasted_iota(jnp.int32, (step_rows, LANES), 1)
@@ -346,8 +318,7 @@
     lax.fori_loop(0, own_count * side // step_rows, collect, 0)
 
     lane_index = lax.broadcasted_iota(jnp.int32, (tiles, LANES), 1)
-    for step in range(slab_count):
-        slab = partner_of(slab_index, step, slab_count)[0]
+    for slab in range(slab_count):
         exponents = jnp.zeros((tiles, LANES), jnp.float32)
         factors = jnp.zeros((tiles, LANES), jnp.float32)
         codes = []
@@ -361,9 +332,9 @@
             factors = jnp.where(lane_index == chunk, factor, factors)
             if chunk % 2:
                 pair = jnp.concatenate(codes[-2:], axis=0)
-                out_refs[step][tiles * (chunk - 1) : tiles * (chunk + 1), :] = whole_codes(pair)
+                out_ref[slab, tiles * (chunk - 1) : tiles * (chunk + 1), :] = whole_codes(pair)
         header = jnp.concatenate([exponents, factors], axis=0)
-        out_refs[step][tiles * own_count * planes :, :] = whole_codes(header)
+        out_ref[slab, tiles * own_count * planes :, :] = whole_codes(header)
 
 
 def whole_codes(value):
@@ -379,112 +350,43 @@
     return jnp.clip(code, -CODE_LIMIT, CODE_LIMIT), exponent, factor
 
 
-def gather_boxes(blocks, slab_count, pair_count):
-    chips = pair_count // CORES
-    arrived = {}
-    for turns in turn_groups(slab_count):
-        for turn in turns:
-            perm = []
-            for slab in range(slab_count):
-                for pair in range(pair_count):
-                    target = partner_of(slab, slab_step(turn, pair % CORES), slab_count)[0]
-                    perm.append((slab * pair_count + pair, target * pair_count + pair))
-            arrived[turn] = lax.ppermute(blocks[turn], ("slab", "pair"), perm)
-    own = [jnp.concatenate([arrived[t] for t in turns]) for turns in turn_groups(slab_count)]
-    pieces = [own]
-    for step in range(1, chips):
+def gather_boxes(boxes, pair_count):
+    pieces = [boxes]
+    for step in range(1, pair_count // CORES):
         perm = [(i, (i + step * CORES) % pair_count) for i in range(pair_count)]
-        pieces.append([lax.ppermute(block, "pair", perm) for block in own])
-    other = [[swap_cores(block, pair_count) for block in piece] for piece in pieces]
-    return [block for piece in pieces + other for block in piece]
-
-
-def swap_cores(block, pair_count):
-    return lax.ppermute(block, "pair", [(i, i ^ 1) for i in range(pair_count)])
-
-
-def pack_kernel(sizes, *refs):
-    own_count, slab_count = sizes
-    orbital_refs, out_refs, lines = refs[:CORES], refs[CORES:-1], refs[-1]
-    row_count, cells = orbital_refs[0].shape
-    tiles = cells // LANES
-    slab_index = lax.axis_index("slab")
-    core = lax.axis_index("pair") % CORES
-    for side in range(CORES):
-        base = (core ^ side) * tiles * row_count
-        for tile in range(tiles):
-            columns = slice(tile * LANES, (tile + 1) * LANES)
-            rows = pl.ds(pl.multiple_of(base + tile * row_count, 8), row_count)
-            lines[rows, :] = orbital_refs[side][:, columns].astype(jnp.float32)
-    for turn, out_ref in enumerate(out_refs):
-        first = partner_of(slab_index, slab_step(turn, core), slab_count)[0] * own_count
-        for chunk in range(CORES * own_count * tiles // 16):
-            halves = []
-            for half in range(2):
-                member, tile = divmod(16 * chunk + 8 * half, tiles)
-                side, own = divmod(member, own_count)
-                start = (side * tiles + tile) * row_count + first + own
-                halves.append(lines[pl.ds(start, 8, stride=row_count), :])
-            block = jnp.concatenate(halves, axis=0).astype(jnp.bfloat16)
-            out_ref[16 * chunk : 16 * chunk + 16, :] = block
-
-
-def pack(orbitals, other, own_count, slab_count):
-    row_count, cells = orbitals.shape
-    rows = CORES * own_count * cells // LANES
-    vectors = pl.BlockSpec(memory_space=pltpu.VMEM)
-    turns = slab_count // CORES
-    return pl.pallas_call(
-        functools.partial(pack_kernel, (own_count, slab_count)),
-        out_shape=[jax.ShapeDtypeStruct((rows, LANES), jnp.bfloat16)] * turns,
-        in_specs=[vectors] * CORES,
-        out_specs=[vectors] * turns,
-        scratch_shapes=[pltpu.VMEM((CORES * row_count * cells // LANES, LANES), jnp.float32)],
-        compiler_params=pltpu.CompilerParams(vmem_limit_bytes=60 * 1024 * 1024),
-    )(orbitals, other)
-
-
-def unpack_kernel(sizes, *refs):
-    own_count, slab_count, tiles = sizes
-    block_refs, out_ref, blocks, sems = refs[:slab_count], *refs[slab_count:]
-    slab_index = lax.axis_index("slab")
-    copies = []
-    for index in range(slab_count):
-        copies.append(pltpu.make_async_copy(block_refs[index], blocks.at[index], sems.at[index]))
-        copies[-1].start()
-    for index in reversed(range(slab_count)):
-        step = slab_count - 1 - index
-        copies[index].wait()
-        first = partner_of(slab_index, step, slab_count)[1] * own_count
-        row_count = own_count * tiles
-        header = blocks[index, row_count:, :].astype(jnp.int32).astype(jnp.float32)
+        pieces.append(lax.ppermute(boxes, "pair", perm))
+    swap = [(i, i ^ 1) for i in range(pair_count)]
+    return pieces + [lax.ppermute(piece, "pair", swap) for piece in pieces]
+
+
+def unpack_kernel(sizes, blocks_ref, out_ref):
+    own_count, tiles = sizes
+    row_count = own_count * tiles
+    for slab in range(blocks_ref.shape[0]):
+        header = blocks_ref[slab, row_count:, :].astype(jnp.int32).astype(jnp.float32)
         units = jnp.exp2(header[:8, :])
         factors = header[8:, :] * (1.0 / (CODE_LIMIT * FACTOR_UNIT))
         for pair in range(row_count // 16):
-            codes = blocks[index, 16 * pair : 16 * pair + 16, :].astype(jnp.int32).astype(jnp.float32)
+            codes = blocks_ref[slab, 16 * pair : 16 * pair + 16, :].astype(jnp.int32).astype(jnp.float32)
             for half in range(2):
                 chunk = 2 * pair + half
                 own, tile = divmod(8 * chunk, tiles)
-                row = first + own
+                row = slab * own_count + own
                 start = (row // 8 * tiles + tile) * 8 + row % 8
                 value = codes[8 * half : 8 * half + 8, :] * factors[:, chunk : chunk + 1]
                 out_ref[pl.ds(start, 8, stride=8), :] = value * units[:, chunk : chunk + 1]
 
 
 def unpack(blocks, own_count, cells):
-    slab_count = len(blocks)
-    row_count = own_count * slab_count
+    row_count = own_count * blocks.shape[0]
     tiles = cells // LANES
+    vectors = pl.BlockSpec(memory_space=pltpu.VMEM)
     out = pl.pallas_call(
-        functools.partial(unpack_kernel, (own_count, slab_count, tiles)),
+        functools.partial(unpack_kernel, (own_count, tiles)),
         out_shape=jax.ShapeDtypeStruct((row_count * tiles, LANES), jnp.float32),
-        in_specs=[pl.BlockSpec(memory_space=pl.ANY)] * slab_count,
-        out_specs=pl.BlockSpec(memory_space=pltpu.VMEM),
-        scratch_shapes=[
-            pltpu.VMEM((slab_count,) + blocks[0].shape, jnp.int16),
-            pltpu.SemaphoreType.DMA((slab_count,)),
-        ],
-    )(*blocks)
+        in_specs=[vectors],
+        out_specs=vectors,
+    )(blocks)
     return out.reshape(row_count // 8, tiles, 8, LANES).transpose(0, 2, 1, 3).reshape(row_count, cells)
 
 
@@ -492,7 +394,6 @@
     _, rounds, team = match.shape
     own_count = team // pair_count
     rows = own_count * side * side // LANES * (side // slab_count)
-    block_count = slab_count * pair_count // CORES
     tiles = side * side // LANES
     solves = own_count * rounds
     group = min(solves, 8)
@@ -512,13 +413,13 @@
     flops = 2 * solves * side * 3 * 2 * (cells * cells // 2 + cells * group * side)
     return pl.pallas_call(
         functools.partial(force_kernel, sizes),
-        out_shape=[jax.ShapeDtypeStruct((rows + HEADER_ROWS, LANES), jnp.int16)] * slab_count,
+        out_shape=jax.ShapeDtypeStruct((slab_count, rows + HEADER_ROWS, LANES), jnp.int16),
         in_specs=[distant] * 2 + [either] * len(blocks) + [distant] * len(constants),
-        out_specs=[vectors] * slab_count,
+        out_specs=vectors,
         scratch_shapes=[
             pltpu.SMEM(match.shape, jnp.int32),
             pltpu.SMEM(centers.shape, jnp.int32),
-            pltpu.VMEM((pair_count // CORES, slab_count, CORES * rows, LANES), jnp.bfloat16),
+            pltpu.VMEM((pair_count, slab_count, rows, LANES), jnp.bfloat16),
             *[pltpu.VMEM(constant.shape, constant.dtype) for constant in constants],
             pltpu.VMEM((team * tiles * pitch, LANES), jnp.float32),
             pltpu.VMEM((solves * side, cells), jnp.bfloat16),
@@ -526,7 +427,7 @@
             wide,
             pltpu.VMEM((solves * tiles * pitch, LANES), jnp.float32),
             pltpu.VMEM((own_count * tiles * side, LANES), jnp.float32),
-            pltpu.SemaphoreType.DMA((block_count + 2 + len(constants),)),
+            pltpu.SemaphoreType.DMA((pair_count + 2 + len(constants),)),
         ],
         compiler_params=pltpu.CompilerParams(vmem_limit_bytes=60 * 1024 * 1024),
         cost_estimate=pl.CostEstimate(flops=flops, bytes_accessed=8 * 1024 * 1024, transcendentals=0),
@@ -544,15 +445,12 @@
     local_rows, plane_cells = orbitals.shape
     own_count = local_rows // slab_count
     side = round((plane_cells * slab_count) ** (1.0 / 3.0))
-    other = swap_cores(orbitals, pair_count)
-    blocks = pack(orbitals, other, own_count, slab_count)
-    team_blocks = gather_boxes(blocks, slab_count, pair_count)
-    forces = team_forces(matchings, centers.T, team_blocks, side, slab_count, pair_count)
-    received = []
-    for step in reversed(range(1, slab_count)):
-        perm = [(i, partner_of(i, step, slab_count)[0]) for i in range(slab_count)]
-        received.append(lax.ppermute(forces[step], "slab", perm))
-    return unpack(received + [forces[0]], own_count, plane_cells)
+    blocks = orbitals.reshape(slab_count, own_count * plane_cells // LANES, LANES)
+    boxes = lax.all_to_all(blocks, "slab", split_axis=0, concat_axis=0, tiled=True)
+    pieces = gather_boxes(boxes, pair_count)
+    codes = team_forces(matchings, centers.T, pieces, side, slab_count, pair_count)
+    codes = lax.all_to_all(codes, "slab", split_axis=0, concat_axis=0, tiled=True)
+    return unpack(codes, own_count, plane_cells)
 
 
 def solution(mesh):

time: 59.5 us -> 59 us (level)
  blocking collectives: 0 us -> 31.7 us
  starting transfers between devices: 24.2 us -> 1.5 us
  waiting for transfers between devices: 13.2 us -> 6.4 us
  Pallas kernels: 19.8 us -> 17.4 us
    all_to_all x0 -> x2, blocking collectives: none -> 31.7 us  [the longest x1 16 us: shards(): lax.all_to_all(blocks, 'slab', split_axis=0, concat_axis=0, tiled=True)]
    ppermute x18 -> x3, starting transfers between devices: 24.2 us -> 1.5 us  [the longest x1 1.49 us: gather_boxes(): pieces.append(lax.ppermute(boxes, 'pair', perm))]
    ppermute x18 -> x3, waiting for transfers between devices: 13.2 us -> 6.4 us  [the longest x1 4.88 us: gather_boxes(): pieces.append(lax.ppermute(boxes, 'pair', perm))]
    pallas_call x3 -> x2, Pallas kernels: 19.8 us -> 17.4 us  [the longest x1 15.1 us: team_forces(): pl.pallas_call(functools.partial(force_kernel, sizes), out_shape=jax.Shap...]
    unnamed x34 -> x8, local copies, waits for them, and re-layouts: 1.92 us -> 0.7 us
    reshape x0 -> x1, local copies, waits for them, and re-layouts: none -> 1.07 us  [shards(): orbitals.reshape(slab_count, own_count * plane_cells // LANES, LANES)]
  transfers between devices with their start and end apart: 18 -> 3, of which waited for: 8 -> 2; matrix products, arithmetic and copies ran while one was open for 0% -> 0% of each run, Pallas kernels for 0% -> 0%
where the time goes in v7:
time: 59 us; the launch traced here: 58.7 us
  blocking collectives  31.7 us (54%)
  Pallas kernels  17.4 us (29%)
  waiting for transfers between devices  6.4 us (11%)
  local copies, waits for them, and re-layouts  1.77 us (3%)
  starting transfers between devices  1.5 us (3%)
    all_to_all x1, blocking collectives, shards(): lax.all_to_all(blocks, 'slab', split_axis=0, concat_axis=0, tiled=True)  16 us
    all_to_all x1, blocking collectives, shards(): lax.all_to_all(codes, 'slab', split_axis=0, concat_axis=0, tiled=True)  15.7 us
    pallas_call x1, Pallas kernels, team_forces(): pl.pallas_call(functools.partial(force_kernel, sizes), out_shape=jax.Shap...  15.1 us
    ppermute x1, waiting for transfers between devices, gather_boxes(): pieces.append(lax.ppermute(boxes, 'pair', perm))  4.88 us
    pallas_call x1, Pallas kernels, unpack(): pl.pallas_call(functools.partial(unpack_kernel, (own_count, tiles)), out_...  2.25 us
    ppermute x2, waiting for transfers between devices, gather_boxes(): return pieces + [lax.ppermute(piece, 'pair', swap) for piece in pieces]  1.52 us
    ppermute x1, starting transfers between devices, gather_boxes(): pieces.append(lax.ppermute(boxes, 'pair', perm))  1.49 us
  transfers between devices with their start and end apart: 3, of which 2 were waited for; matrix products, arithmetic and copies ran while one was open for 0% of the time, Pallas kernels for 0%

profile of v7, /device:TPU:0, one launch (start us, length us, event | category | flops | bytes accessed | tf_op | source)
XLA Modules:
  0.0 58.7 jit_solution(17055708722811103677)
XLA Ops:
  0.0 1.1 %reshape.9 = bf16[8,128,128]{2,1,0:T(8,128)(2,1)S(1)} reshape(bf16[32,4096]{1,0:T(8,128)(2,1)} %param.9) | data formatting | bytes 524288 | tf_op jit(solution)/shard_map/reshape | solution.py:448
  1.1 16.0 %all_to_all.10.refs_0_ = bf16[8,128,128]{2,1,0:T(8,128)(2,1)S(1)} all-to-all(bf16[8,128,128]{2,1,0:T(8,128)(2,1)S(1)} %reshape.9), channel_id=1, replica_groups=mesh['slab'=8,'pair'=4] {'slab'}, dimensions={0} | all-to-all | bytes 524288 | tf_op jit(solution)/shard_map/all_to_all | solution.py:449
  17.1 0.0 copy-start
  17.1 1.5 %collective-permute-start = (bf16[8,128,128]{2,1,0:T(8,128)(2,1)S(1)}, bf16[8,128,128]{2,1,0:T(8,128)(2,1)S(1)}, u32[]{:S(2)}, u32[]{:S(2)}) collective-permute-start(bf16[8,128,128]{2,1,0:T(8,128)(2,1)S(1)} %all_to_all.10.refs_0_), channel_id=1, source_target_pairs={{0,2},{1,3},{2,0},{3,1},{4,6},{5,7},{6,4},{7,5},{8,10},{9,11},{10,... | collective-permute-start | bytes 786440 | tf_op jit(solution)/shard_map/ppermute | solution.py:357
  18.6 0.0 collective-permute-start.1
  18.6 4.9 %collective-permute-done.refs_1_ = bf16[8,128,128]{2,1,0:T(8,128)(2,1)S(1)} collective-permute-done((bf16[8,128,128]{2,1,0:T(8,128)(2,1)S(1)}, bf16[8,128,128]{2,1,0:T(8,128)(2,1)S(1)}, u32[]{:S(2)}, u32[]{:S(2)}) %collective-permute-start) | collective-permute-done | bytes 262176 | tf_op jit(solution)/shard_map/ppermute | solution.py:357
  23.4 0.0 copy-start.1
  23.4 0.0 collective-permute-start.2
  23.5 0.0 collective-permute-done.1.refs_2_
  23.5 0.0 copy-start.2
  23.5 1.5 %collective-permute-done.2.refs_3_ = bf16[8,128,128]{2,1,0:T(8,128)(2,1)S(1)} collective-permute-done((bf16[8,128,128]{2,1,0:T(8,128)(2,1)S(1)}, bf16[8,128,128]{2,1,0:T(8,128)(2,1)S(1)}, u32[]{:S(2)}, u32[]{:S(2)}) %collective-permute-start.2) | collective-permute-done | bytes 262176 | tf_op jit(solution)/shard_map/ppermute | solution.py:359
  25.0 0.0 copy-start.3
  25.0 0.0 copy-done
  25.0 0.0 copy-done.1
  25.0 0.0 copy-done.2
  25.0 0.7 %copy-done.3 = bf16[8,128,128]{2,1,0:T(8,128)(2,1)} copy-done((bf16[8,128,128]{2,1,0:T(8,128)(2,1)}, bf16[8,128,128]{2,1,0:T(8,128)(2,1)S(1)}, u32[]{:S(2)}) %copy-start.3) | copy-done | bytes 262168
  25.7 15.1 %shard_map.91 = s16[8,144,128]{2,1,0:T(8,128)(2,1)} custom-call(s32[1,4,16]{2,1,0:T(4,128)} %match_ref.1, s32[3,128]{1,0:T(4,128)} %bitcast.6, bf16[8,128,128]{2,1,0:T(8,128)(2,1)} %copy-done, bf16[8,128,128]{2,1,0:T(8,128)(2,1)} %copy-done.1, bf16[8,128,128]{2,1,0:T(8,128)(2,1)} %copy-done.2, bf16[8,128,128]{2,1,0:T(8,128)(2,1)} %copy-done.3, ...), custom_call_target="tpu_custom_call" | custom-call | flops 4831838208 | bytes 8388608 | tf_op jit(solution)/shard_map/pallas_call | solution.py:414
  40.8 15.7 %all_to_all.11.blocks_ref = s16[8,144,128]{2,1,0:T(8,128)(2,1)} all-to-all(s16[8,144,128]{2,1,0:T(8,128)(2,1)} %shard_map.91), channel_id=1, replica_groups=mesh['slab'=8,'pair'=4] {'slab'}, dimensions={0} | all-to-all | bytes 589824 | tf_op jit(solution)/shard_map/all_to_all | solution.py:452
  56.5 2.3 %shard_map.92 = f32[1024,128]{1,0:T(8,128)} custom-call(s16[8,144,128]{2,1,0:T(8,128)(2,1)} %all_to_all.11.blocks_ref), custom_call_target="tpu_custom_call" | custom-call | tf_op jit(solution)/shard_map/pallas_call | solution.py:384
Async XLA Ops:
  17.1 7.9 %copy-start = (bf16[8,128,128]{2,1,0:T(8,128)(2,1)}, bf16[8,128,128]{2,1,0:T(8,128)(2,1)S(1)}, u32[]{:S(2)}) copy-start(bf16[8,128,128]{2,1,0:T(8,128)(2,1)S(1)} %all_to_all.10.refs_0_) | copy-start | bytes 786436
  17.1 6.4 %collective-permute-start = (bf16[8,128,128]{2,1,0:T(8,128)(2,1)S(1)}, bf16[8,128,128]{2,1,0:T(8,128)(2,1)S(1)}, u32[]{:S(2)}, u32[]{:S(2)}) collective-permute-start(bf16[8,128,128]{2,1,0:T(8,128)(2,1)S(1)} %all_to_all.10.refs_0_), channel_id=1, source_target_pairs={{0,2},{1,3},{2,0},{3,1},{4,6},{5,7},{6,4},{7,5},{8,10},{9,11},{10,... | collective-permute-start | bytes 786440 | tf_op jit(solution)/shard_map/ppermute | solution.py:357
  18.6 4.9 %collective-permute-start.1 = (bf16[8,128,128]{2,1,0:T(8,128)(2,1)S(1)}, bf16[8,128,128]{2,1,0:T(8,128)(2,1)S(1)}, u32[]{:S(2)}, u32[]{:S(2)}) collective-permute-start(bf16[8,128,128]{2,1,0:T(8,128)(2,1)S(1)} %all_to_all.10.refs_0_), channel_id=1, source_target_pairs={{0,1},{1,0},{2,3},{3,2},{4,5},{5,4},{6,7},{7,6},{8,9},{9,8},{10,11... | collective-permute-start | bytes 786440 | tf_op jit(solution)/shard_map/ppermute | solution.py:359
  23.4 1.5 %copy-start.1 = (bf16[8,128,128]{2,1,0:T(8,128)(2,1)}, bf16[8,128,128]{2,1,0:T(8,128)(2,1)S(1)}, u32[]{:S(2)}) copy-start(bf16[8,128,128]{2,1,0:T(8,128)(2,1)S(1)} %collective-permute-done.refs_1_) | copy-start | bytes 786436
  23.4 1.5 %collective-permute-start.2 = (bf16[8,128,128]{2,1,0:T(8,128)(2,1)S(1)}, bf16[8,128,128]{2,1,0:T(8,128)(2,1)S(1)}, u32[]{:S(2)}, u32[]{:S(2)}) collective-permute-start(bf16[8,128,128]{2,1,0:T(8,128)(2,1)S(1)} %collective-permute-done.refs_1_), channel_id=1, source_target_pairs={{0,1},{1,0},{2,3},{3,2},{4,5},{5,4},{6,7},{7,6},{8,9},{9,8},{10,11... | collective-permute-start | bytes 786440 | tf_op jit(solution)/shard_map/ppermute | solution.py:359
  23.5 1.5 %copy-start.2 = (bf16[8,128,128]{2,1,0:T(8,128)(2,1)}, bf16[8,128,128]{2,1,0:T(8,128)(2,1)S(1)}, u32[]{:S(2)}) copy-start(bf16[8,128,128]{2,1,0:T(8,128)(2,1)S(1)} %collective-permute-done.1.refs_2_) | copy-start | bytes 786436
  25.0 0.7 %copy-start.3 = (bf16[8,128,128]{2,1,0:T(8,128)(2,1)}, bf16[8,128,128]{2,1,0:T(8,128)(2,1)S(1)}, u32[]{:S(2)}) copy-start(bf16[8,128,128]{2,1,0:T(8,128)(2,1)S(1)} %collective-permute-done.2.refs_3_) | copy-start | bytes 786436

commit v8 on v7

--- a/solution.py
+++ b/solution.py
@@ -64,6 +64,12 @@
     return jnp.dot(left, right, preferred_element_type=jnp.float32)
 
 
+def partner_of(index, step, count):
+    if count & (count - 1) == 0:
+        return index ^ step, index ^ step
+    return (index + step) % count, (index + count - step) % count
+
+
 def piece_places(pair_index, pair_count):
     chips = pair_count // CORES
     chip = pair_index // CORES
@@ -73,10 +79,11 @@
 
 
 def force_kernel(sizes, match_ref, centers_ref, *refs):
-    pair_count = sizes[4]
-    block_refs, constant_refs = refs[:pair_count], refs[pair_count : pair_count + 6]
-    out_ref, scratch = refs[pair_count + 6], refs[pair_count + 7 :]
-    force_body(sizes, match_ref, centers_ref, block_refs, constant_refs, out_ref, *scratch)
+    slab_count, pair_count = sizes[3:]
+    block_refs, refs = refs[:pair_count], refs[pair_count:]
+    constant_refs, refs = refs[:6], refs[6:]
+    out_refs, scratch = refs[:slab_count], refs[slab_count:]
+    force_body(sizes, match_ref, centers_ref, block_refs, constant_refs, out_refs, *scratch)
 
 
 def force_body(
@@ -85,7 +92,7 @@
     centers_hbm,
     block_refs,
     constant_refs,
-    out_ref,
+    out_refs,
     match_ref,
     centers_ref,
     boxes_ref,
@@ -256,14 +263,16 @@
     def along_x(start, columns, source):
         high = source[start : start + group_rows, columns]
         low = source[row_count + start : row_count + start + group_rows, columns]
-        value = dot(mix_ref[...], high)
-        return value[:group_rows] + (value[group_rows:] + dot(mix_ref[:group_rows, :], low))
+        return dot(mix_ref[...], jnp.concatenate([high, low, high], axis=0))
 
     def in_plane(parity, columns, source, high_ref, low_ref):
         inner = slice(parity * half_cells, (parity + 1) * half_cells)
-        value = dot(source[:, inner], high_ref[parity, :, columns])
-        rest = dot(source[:row_count, inner], low_ref[parity, :, columns])
-        return value[:row_count] + (value[row_count:] + rest)
+        high = source[:row_count, inner]
+        low = source[row_count:, inner]
+        basis = high_ref[parity, :, columns]
+        rest = low_ref[parity, :, columns]
+        left = jnp.concatenate([high, low, high], axis=1)
+        return dot(left, jnp.concatenate([basis, basis, rest], axis=0))
 
     for start in range(0, row_count, group_rows):
         for column in range(0, cells, width):
@@ -318,7 +327,8 @@
     lax.fori_loop(0, own_count * side // step_rows, collect, 0)
 
     lane_index = lax.broadcasted_iota(jnp.int32, (tiles, LANES), 1)
-    for slab in range(slab_count):
+    for step in range(slab_count):
+        slab = partner_of(slab_index, step, slab_count)[0]
         exponents = jnp.zeros((tiles, LANES), jnp.float32)
         factors = jnp.zeros((tiles, LANES), jnp.float32)
         codes = []
@@ -332,9 +342,9 @@
             factors = jnp.where(lane_index == chunk, factor, factors)
             if chunk % 2:
                 pair = jnp.concatenate(codes[-2:], axis=0)
-                out_ref[slab, tiles * (chunk - 1) : tiles * (chunk + 1), :] = whole_codes(pair)
+                out_refs[step][tiles * (chunk - 1) : tiles * (chunk + 1), :] = whole_codes(pair)
         header = jnp.concatenate([exponents, factors], axis=0)
-        out_ref[slab, tiles * own_count * planes :, :] = whole_codes(header)
+        out_refs[step][tiles * own_count * planes :, :] = whole_codes(header)
 
 
 def whole_codes(value):
@@ -359,34 +369,47 @@
     return pieces + [lax.ppermute(piece, "pair", swap) for piece in pieces]
 
 
-def unpack_kernel(sizes, blocks_ref, out_ref):
-    own_count, tiles = sizes
-    row_count = own_count * tiles
-    for slab in range(blocks_ref.shape[0]):
-        header = blocks_ref[slab, row_count:, :].astype(jnp.int32).astype(jnp.float32)
+def unpack_kernel(sizes, *refs):
+    own_count, slab_count, tiles = sizes
+    block_refs, out_ref, blocks, sems = refs[:slab_count], *refs[slab_count:]
+    slab_index = lax.axis_index("slab")
+    copies = []
+    for index in range(slab_count):
+        copies.append(pltpu.make_async_copy(block_refs[index], blocks.at[index], sems.at[index]))
+        copies[-1].start()
+    for index in reversed(range(slab_count)):
+        step = slab_count - 1 - index
+        copies[index].wait()
+        first = partner_of(slab_index, step, slab_count)[1] * own_count
+        row_count = own_count * tiles
+        header = blocks[index, row_count:, :].astype(jnp.int32).astype(jnp.float32)
         units = jnp.exp2(header[:8, :])
         factors = header[8:, :] * (1.0 / (CODE_LIMIT * FACTOR_UNIT))
         for pair in range(row_count // 16):
-            codes = blocks_ref[slab, 16 * pair : 16 * pair + 16, :].astype(jnp.int32).astype(jnp.float32)
+            codes = blocks[index, 16 * pair : 16 * pair + 16, :].astype(jnp.int32).astype(jnp.float32)
             for half in range(2):
                 chunk = 2 * pair + half
                 own, tile = divmod(8 * chunk, tiles)
-                row = slab * own_count + own
+                row = first + own
                 start = (row // 8 * tiles + tile) * 8 + row % 8
                 value = codes[8 * half : 8 * half + 8, :] * factors[:, chunk : chunk + 1]
                 out_ref[pl.ds(start, 8, stride=8), :] = value * units[:, chunk : chunk + 1]
 
 
 def unpack(blocks, own_count, cells):
-    row_count = own_count * blocks.shape[0]
+    slab_count = len(blocks)
+    row_count = own_count * slab_count
     tiles = cells // LANES
-    vectors = pl.BlockSpec(memory_space=pltpu.VMEM)
     out = pl.pallas_call(
-        functools.partial(unpack_kernel, (own_count, tiles)),
+        functools.partial(unpack_kernel, (own_count, slab_count, tiles)),
         out_shape=jax.ShapeDtypeStruct((row_count * tiles, LANES), jnp.float32),
-        in_specs=[vectors],
-        out_specs=vectors,
-    )(blocks)
+        in_specs=[pl.BlockSpec(memory_space=pl.ANY)] * slab_count,
+        out_specs=pl.BlockSpec(memory_space=pltpu.VMEM),
+        scratch_shapes=[
+            pltpu.VMEM((slab_count,) + blocks[0].shape, jnp.int16),
+            pltpu.SemaphoreType.DMA((slab_count,)),
+        ],
+    )(*blocks)
     return out.reshape(row_count // 8, tiles, 8, LANES).transpose(0, 2, 1, 3).reshape(row_count, cells)
 
 
@@ -400,7 +423,8 @@
     cells = side * side
     pitch = side + 2 * REACH
     basis = sine_basis(side)
-    mix = np.concatenate(split_constant(np.kron(np.eye(group), basis)), axis=0)
+    mix_high, mix_low = split_constant(np.kron(np.eye(group), basis))
+    mix = np.concatenate([mix_high, mix_high, mix_low], axis=1)
     there = np.stack([np.kron(basis[parity::2, : side // 2].T, basis) for parity in range(2)])
     gain = chebyshev_gain(side).reshape(side, side, side)
     gain = np.concatenate([gain[:, parity::2].reshape(side, -1) for parity in range(2)], axis=1)
@@ -413,9 +437,9 @@
     flops = 2 * solves * side * 3 * 2 * (cells * cells // 2 + cells * group * side)
     return pl.pallas_call(
         functools.partial(force_kernel, sizes),
-        out_shape=jax.ShapeDtypeStruct((slab_count, rows + HEADER_ROWS, LANES), jnp.int16),
+        out_shape=[jax.ShapeDtypeStruct((rows + HEADER_ROWS, LANES), jnp.int16)] * slab_count,
         in_specs=[distant] * 2 + [either] * len(blocks) + [distant] * len(constants),
-        out_specs=vectors,
+        out_specs=[vectors] * slab_count,
         scratch_shapes=[
             pltpu.SMEM(match.shape, jnp.int32),
             pltpu.SMEM(centers.shape, jnp.int32),
@@ -449,8 +473,11 @@
     boxes = lax.all_to_all(blocks, "slab", split_axis=0, concat_axis=0, tiled=True)
     pieces = gather_boxes(boxes, pair_count)
     codes = team_forces(matchings, centers.T, pieces, side, slab_count, pair_count)
-    codes = lax.all_to_all(codes, "slab", split_axis=0, concat_axis=0, tiled=True)
-    return unpack(codes, own_count, plane_cells)
+    received = []
+    for step in reversed(range(1, slab_count)):
+        perm = [(i, partner_of(i, step, slab_count)[0]) for i in range(slab_count)]
+        received.append(lax.ppermute(codes[step], "slab", perm))
+    return unpack(received + [codes[0]], own_count, plane_cells)
 
 
 def solution(mesh):

time: 59 us -> 59.1 us (level)
  blocking collectives: 31.7 us -> 16 us
  starting transfers between devices: 1.5 us -> 12.7 us
  waiting for transfers between devices: 6.4 us -> 9.95 us
    all_to_all x1 -> x0, blocking collectives: 15.7 us -> none  [shards(): lax.all_to_all(codes, 'slab', split_axis=0, concat_axis=0, tiled=True)]
    ppermute x0 -> x7, starting transfers between devices: none -> 11.2 us  [shards(): received.append(lax.ppermute(codes[step], 'slab', perm))]
    ppermute x0 -> x7, waiting for transfers between devices: none -> 3.55 us  [shards(): received.append(lax.ppermute(codes[step], 'slab', perm))]
    unnamed x8 -> x22, local copies, waits for them, and re-layouts: 0.7 us -> 1.28 us
  transfers between devices with their start and end apart: 3 -> 10, of which waited for: 2 -> 6; matrix products, arithmetic and copies ran while one was open for 0% -> 0% of each run, Pallas kernels for 0% -> 0%
where the time goes in v8:
time: 59.1 us; the launch traced here: 58.8 us
  Pallas kernels  17.8 us (30%)
  blocking collectives  16 us (27%)
  starting transfers between devices  12.7 us (21%)
  waiting for transfers between devices  9.95 us (17%)
  local copies, waits for them, and re-layouts  2.36 us (4%)
    all_to_all x1, blocking collectives, shards(): lax.all_to_all(blocks, 'slab', split_axis=0, concat_axis=0, tiled=True)  16 us
    pallas_call x1, Pallas kernels, team_forces(): pl.pallas_call(functools.partial(force_kernel, sizes), out_shape=[jax.Sha...  15 us
    ppermute x7, starting transfers between devices, shards(): received.append(lax.ppermute(codes[step], 'slab', perm))  11.2 us
    ppermute x1, waiting for transfers between devices, gather_boxes(): pieces.append(lax.ppermute(boxes, 'pair', perm))  4.88 us
    ppermute x7, waiting for transfers between devices, shards(): received.append(lax.ppermute(codes[step], 'slab', perm))  3.55 us
    pallas_call x1, Pallas kernels, unpack(): pl.pallas_call(functools.partial(unpack_kernel, (own_count, slab_count, t...  2.74 us
    ppermute x2, waiting for transfers between devices, gather_boxes(): return pieces + [lax.ppermute(piece, 'pair', swap) for piece in pieces]  1.52 us
    ppermute x1, starting transfers between devices, gather_boxes(): pieces.append(lax.ppermute(boxes, 'pair', perm))  1.49 us
  transfers between devices with their start and end apart: 10, of which 6 were waited for; matrix products, arithmetic and copies ran while one was open for 0% of the time, Pallas kernels for 0%

profile of v8, /device:TPU:0, one launch (start us, length us, event | category | flops | bytes accessed | tf_op | source)
XLA Modules:
  0.0 58.8 jit_solution(13668221489494926218)
XLA Ops:
  0.0 1.1 %reshape.9 = bf16[8,128,128]{2,1,0:T(8,128)(2,1)S(1)} reshape(bf16[32,4096]{1,0:T(8,128)(2,1)} %param.9) | data formatting | bytes 524288 | tf_op jit(solution)/shard_map/reshape | solution.py:472
  1.1 16.0 %all_to_all.5.refs_0_ = bf16[8,128,128]{2,1,0:T(8,128)(2,1)S(1)} all-to-all(bf16[8,128,128]{2,1,0:T(8,128)(2,1)S(1)} %reshape.9), channel_id=1, replica_groups=mesh['slab'=8,'pair'=4] {'slab'}, dimensions={0} | all-to-all | bytes 524288 | tf_op jit(solution)/shard_map/all_to_all | solution.py:473
  17.1 1.5 %collective-permute-start = (bf16[8,128,128]{2,1,0:T(8,128)(2,1)S(1)}, bf16[8,128,128]{2,1,0:T(8,128)(2,1)S(1)}, u32[]{:S(2)}, u32[]{:S(2)}) collective-permute-start(bf16[8,128,128]{2,1,0:T(8,128)(2,1)S(1)} %all_to_all.5.refs_0_), channel_id=1, source_target_pairs={{0,2},{1,3},{2,0},{3,1},{4,6},{5,7},{6,4},{7,5},{8,10},{9,11},{10,... | collective-permute-start | bytes 786440 | tf_op jit(solution)/shard_map/ppermute | solution.py:367
  18.6 0.0 collective-permute-start.1
  18.6 4.9 %collective-permute-done.refs_1_ = bf16[8,128,128]{2,1,0:T(8,128)(2,1)S(1)} collective-permute-done((bf16[8,128,128]{2,1,0:T(8,128)(2,1)S(1)}, bf16[8,128,128]{2,1,0:T(8,128)(2,1)S(1)}, u32[]{:S(2)}, u32[]{:S(2)}) %collective-permute-start) | collective-permute-done | bytes 262176 | tf_op jit(solution)/shard_map/ppermute | solution.py:367
  23.4 0.0 collective-permute-start.2
  23.5 1.5 %collective-permute-done.2.refs_3_ = bf16[8,128,128]{2,1,0:T(8,128)(2,1)S(1)} collective-permute-done((bf16[8,128,128]{2,1,0:T(8,128)(2,1)S(1)}, bf16[8,128,128]{2,1,0:T(8,128)(2,1)S(1)}, u32[]{:S(2)}, u32[]{:S(2)}) %collective-permute-start.2) | collective-permute-done | bytes 262176 | tf_op jit(solution)/shard_map/ppermute | solution.py:369
  25.0 0.7 %copy-done.10 = bf16[8,128,128]{2,1,0:T(8,128)(2,1)} copy-done((bf16[8,128,128]{2,1,0:T(8,128)(2,1)}, bf16[8,128,128]{2,1,0:T(8,128)(2,1)S(1)}, u32[]{:S(2)}) %copy-start.10) | copy-done | bytes 262168
  25.7 15.0 %shard_map.91 = (s16[144,128]{1,0:T(8,128)(2,1)}, s16[144,128]{1,0:T(8,128)(2,1)}, s16[144,128]{1,0:T(8,128)(2,1)}, s16[144,128]{1,0:T(8,128)(2,1)}, s16[144,128...) custom-call(s32[1,4,16]{2,1,0:T(4,128)} %match_ref.1, ...), custom_call_target="tpu_custom_call" | custom-call | flops 4831838208 | bytes 8388608 | tf_op jit(solution)/shard_map/pallas_call | solution.py:438
  40.7 3.7 %collective-permute-start.3 = (s16[144,128]{1,0:T(8,128)(2,1)}, s16[144,128]{1,0:T(8,128)(2,1)S(1)}, u32[]{:S(2)}, u32[]{:S(2)}) collective-permute-start(s16[144,128]{1,0:T(8,128)(2,1)} %get-tuple-element.13), channel_id=1, source_target_pairs={{0,28},{4,24},{8,20},{12,16},{16,12},{20,8},{24,4},{28,0},{1,29},{... | collective-permute-start | bytes 110600 | tf_op jit(solution)/shard_map/ppermute | solution.py:479
  44.4 1.0 %collective-permute-start.4 = (s16[144,128]{1,0:T(8,128)(2,1)}, s16[144,128]{1,0:T(8,128)(2,1)S(1)}, u32[]{:S(2)}, u32[]{:S(2)}) collective-permute-start(s16[144,128]{1,0:T(8,128)(2,1)} %get-tuple-element.14), channel_id=1, source_target_pairs={{0,24},{4,28},{8,16},{12,20},{16,8},{20,12},{24,0},{28,4},{1,25},{... | collective-permute-start | bytes 110600 | tf_op jit(solution)/shard_map/ppermute | solution.py:479
  45.5 0.4 collective-permute-start.5
  45.9 2.6 %collective-permute-start.6 = (s16[144,128]{1,0:T(8,128)(2,1)}, s16[144,128]{1,0:T(8,128)(2,1)S(1)}, u32[]{:S(2)}, u32[]{:S(2)}) collective-permute-start(s16[144,128]{1,0:T(8,128)(2,1)} %get-tuple-element.16), channel_id=1, source_target_pairs={{0,16},{4,20},{8,24},{12,28},{16,0},{20,4},{24,8},{28,12},{1,17},{... | collective-permute-start | bytes 110600 | tf_op jit(solution)/shard_map/ppermute | solution.py:479
  48.4 1.3 %collective-permute-start.7 = (s16[144,128]{1,0:T(8,128)(2,1)}, s16[144,128]{1,0:T(8,128)(2,1)S(1)}, u32[]{:S(2)}, u32[]{:S(2)}) collective-permute-start(s16[144,128]{1,0:T(8,128)(2,1)} %get-tuple-element.17), channel_id=1, source_target_pairs={{0,12},{4,8},{8,4},{12,0},{16,28},{20,24},{24,20},{28,16},{1,13},{... | collective-permute-start | bytes 110600 | tf_op jit(solution)/shard_map/ppermute | solution.py:479
  49.7 0.0 collective-permute-done.3.refs_0_
  49.7 1.6 %collective-permute-start.8 = (s16[144,128]{1,0:T(8,128)(2,1)}, s16[144,128]{1,0:T(8,128)(2,1)S(1)}, u32[]{:S(2)}, u32[]{:S(2)}) collective-permute-start(s16[144,128]{1,0:T(8,128)(2,1)} %get-tuple-element.18), channel_id=1, source_target_pairs={{0,8},{4,12},{8,0},{12,4},{16,24},{20,28},{24,16},{28,20},{1,9},{5... | collective-permute-start | bytes 110600 | tf_op jit(solution)/shard_map/ppermute | solution.py:479
  51.3 0.0 collective-permute-done.4.refs_1_
  51.3 0.6 %collective-permute-start.9 = (s16[144,128]{1,0:T(8,128)(2,1)}, s16[144,128]{1,0:T(8,128)(2,1)S(1)}, u32[]{:S(2)}, u32[]{:S(2)}) collective-permute-start(s16[144,128]{1,0:T(8,128)(2,1)} %get-tuple-element.19), channel_id=1, source_target_pairs={{0,4},{4,0},{8,12},{12,8},{16,20},{20,16},{24,28},{28,24},{1,5},{5... | collective-permute-start | bytes 110600 | tf_op jit(solution)/shard_map/ppermute | solution.py:479
  51.9 0.5 collective-permute-done.6.refs_3_
  52.4 1.1 %collective-permute-done.7.refs_4_ = s16[144,128]{1,0:T(8,128)(2,1)S(1)} collective-permute-done((s16[144,128]{1,0:T(8,128)(2,1)}, s16[144,128]{1,0:T(8,128)(2,1)S(1)}, u32[]{:S(2)}, u32[]{:S(2)}) %collective-permute-start.7) | collective-permute-done | bytes 36896 | tf_op jit(solution)/shard_map/ppermute | solution.py:479
  53.5 0.4 collective-permute-done.8.refs_5_
  53.9 1.6 %collective-permute-done.9.refs_6_ = s16[144,128]{1,0:T(8,128)(2,1)S(1)} collective-permute-done((s16[144,128]{1,0:T(8,128)(2,1)}, s16[144,128]{1,0:T(8,128)(2,1)S(1)}, u32[]{:S(2)}, u32[]{:S(2)}) %collective-permute-start.9) | collective-permute-done | bytes 36896 | tf_op jit(solution)/shard_map/ppermute | solution.py:479
  55.5 0.6 copy-done.7
  56.1 2.7 %shard_map.92 = f32[1024,128]{1,0:T(8,128)} custom-call(s16[144,128]{1,0:T(8,128)(2,1)} %copy-done.1, s16[144,128]{1,0:T(8,128)(2,1)} %copy-done.2, s16[144,128]{1,0:T(8,128)(2,1)} %copy-done.3, s16[144,128]{1,0:T(8,128)(2,1)} %copy-done.4, s16[144,128]{1,0:T(8,128)(2,1)} %copy-done.5, s16[144,128]{1,0:T(8,128)(2,1)} %copy-done.6, ...), custom_call_target="tpu_custom_call" | custom-call | tf_op jit(solution)/shard_map/pallas_call | solution.py:403
  (22 shorter events, 0.0 us)
Async XLA Ops:
  17.1 7.9 %copy-start = (bf16[8,128,128]{2,1,0:T(8,128)(2,1)}, bf16[8,128,128]{2,1,0:T(8,128)(2,1)S(1)}, u32[]{:S(2)}) copy-start(bf16[8,128,128]{2,1,0:T(8,128)(2,1)S(1)} %all_to_all.5.refs_0_) | copy-start | bytes 786436
  17.1 6.4 %collective-permute-start = (bf16[8,128,128]{2,1,0:T(8,128)(2,1)S(1)}, bf16[8,128,128]{2,1,0:T(8,128)(2,1)S(1)}, u32[]{:S(2)}, u32[]{:S(2)}) collective-permute-start(bf16[8,128,128]{2,1,0:T(8,128)(2,1)S(1)} %all_to_all.5.refs_0_), channel_id=1, source_target_pairs={{0,2},{1,3},{2,0},{3,1},{4,6},{5,7},{6,4},{7,5},{8,10},{9,11},{10,... | collective-permute-start | bytes 786440 | tf_op jit(solution)/shard_map/ppermute | solution.py:367
  18.6 4.9 %collective-permute-start.1 = (bf16[8,128,128]{2,1,0:T(8,128)(2,1)S(1)}, bf16[8,128,128]{2,1,0:T(8,128)(2,1)S(1)}, u32[]{:S(2)}, u32[]{:S(2)}) collective-permute-start(bf16[8,128,128]{2,1,0:T(8,128)(2,1)S(1)} %all_to_all.5.refs_0_), channel_id=1, source_target_pairs={{0,1},{1,0},{2,3},{3,2},{4,5},{5,4},{6,7},{7,6},{8,9},{9,8},{10,11... | collective-permute-start | bytes 786440 | tf_op jit(solution)/shard_map/ppermute | solution.py:369
  23.4 1.5 %copy-start.8 = (bf16[8,128,128]{2,1,0:T(8,128)(2,1)}, bf16[8,128,128]{2,1,0:T(8,128)(2,1)S(1)}, u32[]{:S(2)}) copy-start(bf16[8,128,128]{2,1,0:T(8,128)(2,1)S(1)} %collective-permute-done.refs_1_) | copy-start | bytes 786436
  23.4 1.5 %collective-permute-start.2 = (bf16[8,128,128]{2,1,0:T(8,128)(2,1)S(1)}, bf16[8,128,128]{2,1,0:T(8,128)(2,1)S(1)}, u32[]{:S(2)}, u32[]{:S(2)}) collective-permute-start(bf16[8,128,128]{2,1,0:T(8,128)(2,1)S(1)} %collective-permute-done.refs_1_), channel_id=1, source_target_pairs={{0,1},{1,0},{2,3},{3,2},{4,5},{5,4},{6,7},{7,6},{8,9},{9,8},{10,11... | collective-permute-start | bytes 786440 | tf_op jit(solution)/shard_map/ppermute | solution.py:369
  23.5 1.5 %copy-start.9 = (bf16[8,128,128]{2,1,0:T(8,128)(2,1)}, bf16[8,128,128]{2,1,0:T(8,128)(2,1)S(1)}, u32[]{:S(2)}) copy-start(bf16[8,128,128]{2,1,0:T(8,128)(2,1)S(1)} %collective-permute-done.1.refs_2_) | copy-start | bytes 786436
  25.0 0.7 %copy-start.10 = (bf16[8,128,128]{2,1,0:T(8,128)(2,1)}, bf16[8,128,128]{2,1,0:T(8,128)(2,1)S(1)}, u32[]{:S(2)}) copy-start(bf16[8,128,128]{2,1,0:T(8,128)(2,1)S(1)} %collective-permute-done.2.refs_3_) | copy-start | bytes 786436
  40.7 9.0 %collective-permute-start.3 = (s16[144,128]{1,0:T(8,128)(2,1)}, s16[144,128]{1,0:T(8,128)(2,1)S(1)}, u32[]{:S(2)}, u32[]{:S(2)}) collective-permute-start(s16[144,128]{1,0:T(8,128)(2,1)} %get-tuple-element.13), channel_id=1, source_target_pairs={{0,28},{4,24},{8,20},{12,16},{16,12},{20,8},{24,4},{28,0},{1,29},{... | collective-permute-start | bytes 110600 | tf_op jit(solution)/shard_map/ppermute | solution.py:479
  44.4 6.9 %collective-permute-start.4 = (s16[144,128]{1,0:T(8,128)(2,1)}, s16[144,128]{1,0:T(8,128)(2,1)S(1)}, u32[]{:S(2)}, u32[]{:S(2)}) collective-permute-start(s16[144,128]{1,0:T(8,128)(2,1)} %get-tuple-element.14), channel_id=1, source_target_pairs={{0,24},{4,28},{8,16},{12,20},{16,8},{20,12},{24,0},{28,4},{1,25},{... | collective-permute-start | bytes 110600 | tf_op jit(solution)/shard_map/ppermute | solution.py:479
  45.5 6.5 %collective-permute-start.5 = (s16[144,128]{1,0:T(8,128)(2,1)}, s16[144,128]{1,0:T(8,128)(2,1)S(1)}, u32[]{:S(2)}, u32[]{:S(2)}) collective-permute-start(s16[144,128]{1,0:T(8,128)(2,1)} %get-tuple-element.15), channel_id=1, source_target_pairs={{0,20},{4,16},{8,28},{12,24},{16,4},{20,0},{24,12},{28,8},{1,21},{... | collective-permute-start | bytes 110600 | tf_op jit(solution)/shard_map/ppermute | solution.py:479
  45.9 6.6 %collective-permute-start.6 = (s16[144,128]{1,0:T(8,128)(2,1)}, s16[144,128]{1,0:T(8,128)(2,1)S(1)}, u32[]{:S(2)}, u32[]{:S(2)}) collective-permute-start(s16[144,128]{1,0:T(8,128)(2,1)} %get-tuple-element.16), channel_id=1, source_target_pairs={{0,16},{4,20},{8,24},{12,28},{16,0},{20,4},{24,8},{28,12},{1,17},{... | collective-permute-start | bytes 110600 | tf_op jit(solution)/shard_map/ppermute | solution.py:479
  48.4 5.1 %collective-permute-start.7 = (s16[144,128]{1,0:T(8,128)(2,1)}, s16[144,128]{1,0:T(8,128)(2,1)S(1)}, u32[]{:S(2)}, u32[]{:S(2)}) collective-permute-start(s16[144,128]{1,0:T(8,128)(2,1)} %get-tuple-element.17), channel_id=1, source_target_pairs={{0,12},{4,8},{8,4},{12,0},{16,28},{20,24},{24,20},{28,16},{1,13},{... | collective-permute-start | bytes 110600 | tf_op jit(solution)/shard_map/ppermute | solution.py:479
  49.7 5.8 %copy-start.1 = (s16[144,128]{1,0:T(8,128)(2,1)}, s16[144,128]{1,0:T(8,128)(2,1)S(1)}, u32[]{:S(2)}) copy-start(s16[144,128]{1,0:T(8,128)(2,1)S(1)} %collective-permute-done.3.refs_0_) | copy-start | bytes 110596
  49.7 4.2 %collective-permute-start.8 = (s16[144,128]{1,0:T(8,128)(2,1)}, s16[144,128]{1,0:T(8,128)(2,1)S(1)}, u32[]{:S(2)}, u32[]{:S(2)}) collective-permute-start(s16[144,128]{1,0:T(8,128)(2,1)} %get-tuple-element.18), channel_id=1, source_target_pairs={{0,8},{4,12},{8,0},{12,4},{16,24},{20,28},{24,16},{28,20},{1,9},{5... | collective-permute-start | bytes 110600 | tf_op jit(solution)/shard_map/ppermute | solution.py:479
  51.3 4.2 %copy-start.2 = (s16[144,128]{1,0:T(8,128)(2,1)}, s16[144,128]{1,0:T(8,128)(2,1)S(1)}, u32[]{:S(2)}) copy-start(s16[144,128]{1,0:T(8,128)(2,1)S(1)} %collective-permute-done.4.refs_1_) | copy-start | bytes 110596
  51.3 4.2 %collective-permute-start.9 = (s16[144,128]{1,0:T(8,128)(2,1)}, s16[144,128]{1,0:T(8,128)(2,1)S(1)}, u32[]{:S(2)}, u32[]{:S(2)}) collective-permute-start(s16[144,128]{1,0:T(8,128)(2,1)} %get-tuple-element.19), channel_id=1, source_target_pairs={{0,4},{4,0},{8,12},{12,8},{16,20},{20,16},{24,28},{28,24},{1,5},{5... | collective-permute-start | bytes 110600 | tf_op jit(solution)/shard_map/ppermute | solution.py:479
  51.9 3.6 %copy-start.3 = (s16[144,128]{1,0:T(8,128)(2,1)}, s16[144,128]{1,0:T(8,128)(2,1)S(1)}, u32[]{:S(2)}) copy-start(s16[144,128]{1,0:T(8,128)(2,1)S(1)} %collective-permute-done.5.refs_2_) | copy-start | bytes 110596
  52.4 3.1 %copy-start.4 = (s16[144,128]{1,0:T(8,128)(2,1)}, s16[144,128]{1,0:T(8,128)(2,1)S(1)}, u32[]{:S(2)}) copy-start(s16[144,128]{1,0:T(8,128)(2,1)S(1)} %collective-permute-done.6.refs_3_) | copy-start | bytes 110596
  53.5 2.0 %copy-start.5 = (s16[144,128]{1,0:T(8,128)(2,1)}, s16[144,128]{1,0:T(8,128)(2,1)S(1)}, u32[]{:S(2)}) copy-start(s16[144,128]{1,0:T(8,128)(2,1)S(1)} %collective-permute-done.7.refs_4_) | copy-start | bytes 110596
  53.9 1.6 %copy-start.6 = (s16[144,128]{1,0:T(8,128)(2,1)}, s16[144,128]{1,0:T(8,128)(2,1)S(1)}, u32[]{:S(2)}) copy-start(s16[144,128]{1,0:T(8,128)(2,1)S(1)} %collective-permute-done.8.refs_5_) | copy-start | bytes 110596
  55.5 0.6 %copy-start.7 = (s16[144,128]{1,0:T(8,128)(2,1)}, s16[144,128]{1,0:T(8,128)(2,1)S(1)}, u32[]{:S(2)}) copy-start(s16[144,128]{1,0:T(8,128)(2,1)S(1)} %collective-permute-done.9.refs_6_) | copy-start | bytes 110596

commit v9 on v8

--- a/solution.py
+++ b/solution.py
@@ -70,51 +70,139 @@
     return (index + step) % count, (index + count - step) % count
 
 
-def piece_places(pair_index, pair_count):
-    chips = pair_count // CORES
-    chip = pair_index // CORES
-    for core_step in range(CORES):
-        for chip_step in range(chips):
-            yield (chip + chips - chip_step) % chips * CORES + (pair_index + core_step) % CORES
-
-
-def force_kernel(sizes, match_ref, centers_ref, *refs):
-    slab_count, pair_count = sizes[3:]
-    block_refs, refs = refs[:pair_count], refs[pair_count:]
-    constant_refs, refs = refs[:6], refs[6:]
-    out_refs, scratch = refs[:slab_count], refs[slab_count:]
-    force_body(sizes, match_ref, centers_ref, block_refs, constant_refs, out_refs, *scratch)
-
-
-def force_body(
-    sizes,
-    match_hbm,
-    centers_hbm,
-    block_refs,
-    constant_refs,
-    out_refs,
-    match_ref,
-    centers_ref,
-    boxes_ref,
-    mix_ref,
-    gain_ref,
-    there_high,
-    there_low,
-    back_high,
-    back_low,
-    fields,
-    partner,
-    first,
-    second,
-    terms,
-    total,
-    sems,
+def pair_geometry(sizes, match_ref, centers_ref, index):
+    _, rounds, own_count, slab_count, _ = sizes
+    slab_index = lax.axis_index("slab")
+    pair_index = lax.axis_index("pair")
+
+    def orbital_of(member):
+        return (member // own_count * slab_count + slab_index) * own_count + member % own_count
+
+    member = pair_index * own_count + index // rounds
+    mate = match_ref[0, index % rounds, member]
+    own_offset = []
+    mate_offset = []
+    distance = 0
+    for axis in range(3):
+        mine = centers_ref[axis, orbital_of(member)]
+        other = centers_ref[axis, orbital_of(mate)]
+        anchor = (mine + other) >> 1
+        own_offset.append(mine - anchor)
+        mate_offset.append(other - anchor)
+        distance = distance + (mine - other) * (mine - other)
+    return member, mate, own_offset, mate_offset, distance <= CUT2
+
+
+def box_shape(sizes):
+    side = sizes[0]
+    return side * side // LANES, LANES // side, side + 2 * REACH
+
+
+def clear_edges(sizes, ref, first, count):
+    side = sizes[0]
+    tiles, _, pitch = box_shape(sizes)
+    zeros = jnp.zeros((REACH, LANES), jnp.float32)
+
+    def clear(index, carry):
+        start = (first * tiles + index) * pitch
+        ref[pl.ds(pl.multiple_of(start, 8), REACH), :] = zeros
+        ref[pl.ds(pl.multiple_of(start + REACH + side, 8), REACH), :] = zeros
+        return carry
+
+    lax.fori_loop(0, count * tiles, clear, 0, unroll=8)
+
+
+def spread(sizes, boxes_ref, fields, pair):
+    side, _, own_count, slab_count, _ = sizes
+    planes = side // slab_count
+    tiles, _, pitch = box_shape(sizes)
+
+    def spread_slab(slab, carry):
+        for chunk in range(own_count * planes // 2):
+            block = boxes_ref[pair, slab, 16 * chunk : 16 * chunk + 16, :].astype(jnp.float32)
+            for half in range(2):
+                own, plane = divmod(2 * chunk + half, planes)
+                start = (pair * own_count + own) * tiles * pitch + REACH + slab * planes + plane
+                fields[pl.ds(start, tiles, stride=pitch), :] = block[8 * half : 8 * half + 8, :]
+        return carry
+
+    lax.fori_loop(0, slab_count, spread_slab, 0)
+
+
+def rolled(sizes, ref, box, row, rows, offset_x, offset_flat):
+    tiles, _, pitch = box_shape(sizes)
+    whole = (offset_flat >> 7) & (tiles - 1)
+    part = offset_flat & (LANES - 1)
+    start = box * tiles * pitch + REACH + row - offset_x
+    moved = []
+    for tile in range(tiles):
+        first_row = start + ((tile - whole) & (tiles - 1)) * pitch
+        moved.append(pltpu.roll(ref[pl.ds(first_row, rows), :], part, axis=1))
+    keep = lax.broadcasted_iota(jnp.int32, (rows, LANES), 1) >= part
+    return [jnp.where(keep, moved[t], moved[(t - 1) % tiles]) for t in range(tiles)]
+
+
+def place_partner(sizes, fields, box, own_offset, offset, active, out_ref, rows):
+    side = sizes[0]
+    tiles, lines, _ = box_shape(sizes)
+    placed = rolled(sizes, fields, box, 0, side, offset[0], offset[1] * side + offset[2])
+    lane = lax.broadcasted_iota(jnp.int32, (1, LANES), 1)
+    lows = [jnp.maximum(jnp.maximum(a, b), 0) for a, b in zip(own_offset, offset)]
+    highs = [side + jnp.minimum(jnp.minimum(a, b), 0) for a, b in zip(own_offset, offset)]
+    point_ok = (lane % side >= lows[2]) & (lane % side < highs[2]) & active
+    for tile in range(tiles):
+        line = lane // side + tile * lines
+        ok = jnp.where(point_ok & (line >= lows[1]) & (line < highs[1]), 1.0, 0.0)
+        out_ref[rows, tile * LANES : (tile + 1) * LANES] = (placed[tile] * ok).astype(jnp.bfloat16)
+
+
+def near_kernel(
+    sizes, match_hbm, centers_hbm, own_hbm, other_hbm, mine_ref, partner_ref, match_ref, centers_ref, boxes_ref, fields, sems
 ):
+    side, rounds, own_count, _, _ = sizes
+    tiles, _, _ = box_shape(sizes)
+    pair_index = lax.axis_index("pair")
+    core = pair_index % CORES
+    first_member = pair_index // CORES * CORES * own_count
+    sources = (match_hbm, centers_hbm, own_hbm, other_hbm)
+    targets = (match_ref, centers_ref, boxes_ref.at[core], boxes_ref.at[1 - core])
+    copies = [pltpu.make_async_copy(s, t, sems.at[i]) for i, (s, t) in enumerate(zip(sources, targets))]
+    for copy in copies:
+        copy.start()
+    clear_edges(sizes, fields, 0, CORES * own_count)
+    for copy in copies:
+        copy.wait()
+    for pair in range(CORES):
+        spread(sizes, boxes_ref, fields, pair)
+
+    def place(index, carry):
+        member, mate, a, b, active = pair_geometry(sizes, match_ref, centers_ref, index)
+        rows = pl.ds(pl.multiple_of(index * side, side), side)
+        placed = rolled(sizes, fields, member - first_member, 0, side, a[0], a[1] * side + a[2])
+        for tile in range(tiles):
+            mine_ref[rows, tile * LANES : (tile + 1) * LANES] = placed[tile].astype(jnp.bfloat16)
+        local = mate - first_member
+
+        @pl.when((local >= 0) & (local < CORES * own_count))
+        def _():
+            place_partner(sizes, fields, local, a, b, active, partner_ref, rows)
+
+        return carry
+
+    lax.fori_loop(0, own_count * rounds, place, 0)
+
+
+def force_kernel(sizes, match_hbm, centers_hbm, mine_hbm, partner_hbm, *refs):
     side, rounds, own_count, slab_count, pair_count = sizes
+    piece_hbm, refs = refs[: pair_count - CORES], refs[pair_count - CORES :]
+    constant_hbm, refs = refs[:6], refs[6:]
+    out_refs, refs = refs[:slab_count], refs[slab_count:]
+    match_ref, centers_ref, mine, partner, boxes_ref, *refs = refs
+    constants, refs = refs[:6], refs[6:]
+    mix_ref, gain_ref, there_high, there_low, back_high, back_low = constants
+    fields, first, second, terms, total, sems = refs
     planes = side // slab_count
-    tiles = side * side // LANES
-    lines = LANES // side
-    pitch = side + 2 * REACH
+    tiles, lines, pitch = box_shape(sizes)
     solves = own_count * rounds
     group = min(solves, 8)
     group_rows = group * side
@@ -122,68 +210,48 @@
     width = 2 * LANES
     slab_index = lax.axis_index("slab")
     pair_index = lax.axis_index("pair")
-
-    sources = [match_hbm, centers_hbm, *block_refs]
-    targets = [match_ref, centers_ref]
-    targets += [boxes_ref.at[pair] for pair in piece_places(pair_index, pair_count)]
-    copies = []
-    for source, target in zip(sources, targets):
-        copies.append(pltpu.make_async_copy(source, target, sems.at[len(copies)]))
-    constants = (mix_ref, gain_ref, there_high, there_low, back_high, back_low)
-    constant_copies = []
-    for index, (source, target) in enumerate(zip(constant_refs, constants)):
-        constant_copies.append(pltpu.make_async_copy(source, target, sems.at[len(copies) + index]))
-    for copy in copies + constant_copies:
+    core = pair_index % CORES
+    chip = pair_index // CORES
+    chips = pair_count // CORES
+    first_member = chip * CORES * own_count
+
+    places = [
+        (chip + chips - step) % chips * CORES + (core + core_step) % CORES
+        for core_step in range(CORES)
+        for step in range(1, chips)
+    ]
+    sources = [match_hbm, centers_hbm, *piece_hbm, mine_hbm, partner_hbm, *constant_hbm]
+    targets = [match_ref, centers_ref, *[boxes_ref.at[pair] for pair in places], mine, partner, *constants]
+    copies = [pltpu.make_async_copy(s, t, sems.at[i]) for i, (s, t) in enumerate(zip(sources, targets))]
+    for copy in copies:
         copy.start()
-
-    zeros = jnp.zeros((REACH, LANES), jnp.float32)
-
-    def clear(index, carry):
-        fields[pl.ds(pl.multiple_of(index * pitch, 8), REACH), :] = zeros
-        fields[pl.ds(pl.multiple_of(index * pitch + REACH + side, 8), REACH), :] = zeros
+    for pair in places:
+        clear_edges(sizes, fields, pair * own_count, own_count)
+    clear_edges(sizes, terms, 0, solves)
+    boxes_count = 2 + len(places)
+    for copy in copies[:boxes_count]:
+        copy.wait()
+    for pair in places:
+        spread(sizes, boxes_ref, fields, pair)
+    for copy in copies[boxes_count : boxes_count + 2]:
+        copy.wait()
+
+    def place(index, carry):
+        _, mate, a, b, active = pair_geometry(sizes, match_ref, centers_ref, index)
+        local = mate - first_member
+
+        @pl.when((local < 0) | (local >= CORES * own_count))
+        def _():
+            rows = pl.ds(pl.multiple_of(index * side, side), side)
+            place_partner(sizes, fields, mate, a, b, active, partner, rows)
+
         return carry
 
-    lax.fori_loop(0, pair_count * own_count * tiles, clear, 0, unroll=8)
-
-    def clear_terms(index, carry):
-        terms[pl.ds(pl.multiple_of(index * pitch, 8), REACH), :] = zeros
-        terms[pl.ds(pl.multiple_of(index * pitch + REACH + side, 8), REACH), :] = zeros
-        return carry
-
-    lax.fori_loop(0, solves * tiles, clear_terms, 0, unroll=8)
-
-    for copy in copies:
-        copy.wait()
-
-    def spread(index, carry):
-        pair = index // slab_count
-        slab = index % slab_count
-        for chunk in range(own_count * planes // 2):
-            block = boxes_ref[pair, slab, 16 * chunk : 16 * chunk + 16, :].astype(jnp.float32)
-            for half in range(2):
-                own, plane = divmod(2 * chunk + half, planes)
-                start = (pair * own_count + own) * tiles * pitch + REACH + slab * planes + plane
-                fields[pl.ds(start, tiles, stride=pitch), :] = block[8 * half : 8 * half + 8, :]
-        return carry
-
-    lax.fori_loop(0, pair_count * slab_count, spread, 0)
-
-    step_rows = 16
-    lane = lax.broadcasted_iota(jnp.int32, (step_rows, LANES), 1)
-    lane_row = lax.broadcasted_iota(jnp.int32, (1, LANES), 1)
-    lane_line = lane_row // side
-    lane_point = lane_row % side
-
-    def rolled(ref, base, row, offset_x, offset_flat):
-        whole = (offset_flat >> 7) & (tiles - 1)
-        part = offset_flat & (LANES - 1)
-        start = base * pitch + REACH + row - offset_x
-        moved = []
-        for tile in range(tiles):
-            first_row = start + ((tile - whole) & (tiles - 1)) * pitch
-            moved.append(pltpu.roll(ref[pl.ds(first_row, step_rows), :], part, axis=1))
-        keep = lane >= part
-        return [jnp.where(keep, moved[t], moved[(t - 1) % tiles]) for t in range(tiles)]
+    lax.fori_loop(0, solves, place, 0)
+
+    row_count = solves * side
+    half_tiles = tiles // 2
+    half_cells = cells // 2
 
     def mirrored(tile):
         line = lax.broadcasted_iota(jnp.int32, tile.shape, 1) // side
@@ -195,30 +263,6 @@
                 result = moved if result is None else jnp.where(line % 2 == index, moved, result)
         return result
 
-    def orbital_of(member):
-        return (member // own_count * slab_count + slab_index) * own_count + member % own_count
-
-    def geometry(index):
-        own = index // rounds
-        turn = index % rounds
-        member = pair_index * own_count + own
-        mate = match_ref[0, turn, member]
-        own_offset = []
-        mate_offset = []
-        distance = 0
-        for axis in range(3):
-            mine = centers_ref[axis, orbital_of(member)]
-            other = centers_ref[axis, orbital_of(mate)]
-            anchor = (mine + other) >> 1
-            own_offset.append(mine - anchor)
-            mate_offset.append(other - anchor)
-            distance = distance + (mine - other) * (mine - other)
-        return own, member, mate, own_offset, mate_offset, distance <= CUT2
-
-    row_count = solves * side
-    half_tiles = tiles // 2
-    half_cells = cells // 2
-
     def store_split(ref, start, count, columns, value):
         high, low = split_pair(value)
         if isinstance(start, int):
@@ -228,36 +272,25 @@
             ref[pl.ds(pl.multiple_of(start, count), count), columns] = high
             ref[pl.ds(pl.multiple_of(row_count + start, count), count), columns] = low
 
-    def densities(step, carry):
-        index = step // (side // step_rows)
-        row = step % (side // step_rows) * step_rows
-        own, member, mate, a, b, active = geometry(index)
-        mine = rolled(fields, member * tiles, row, a[0], a[1] * side + a[2])
-        other = rolled(fields, mate * tiles, row, b[0], b[1] * side + b[2])
-        low_line = jnp.maximum(jnp.maximum(a[1], b[1]), 0)
-        high_line = jnp.where(active, side + jnp.minimum(jnp.minimum(a[1], b[1]), 0), 0)
-        low_point = jnp.maximum(jnp.maximum(a[2], b[2]), 0)
-        high_point = side + jnp.minimum(jnp.minimum(a[2], b[2]), 0)
-        point_ok = (lane_point >= low_point) & (lane_point < high_point)
-        start = step * step_rows
-        rows = pl.ds(pl.multiple_of(start, step_rows), step_rows)
-        density = []
-        for tile in range(tiles):
-            line = lane_line + tile * lines
-            ok = jnp.where(point_ok & (line >= low_line) & (line < high_line), 1.0, 0.0)
-            masked = other[tile] * ok
-            partner[rows, tile * LANES : (tile + 1) * LANES] = masked.astype(jnp.bfloat16)
-            density.append(mine[tile] * masked)
+    def densities(index, carry):
+        start = index * side
+        rows = pl.ds(pl.multiple_of(start, side), side)
+
+        def density(tile):
+            columns = slice(tile * LANES, (tile + 1) * LANES)
+            return mine[rows, columns].astype(jnp.float32) * partner[rows, columns].astype(jnp.float32)
+
         for tile in range(half_tiles):
-            mirror = mirrored(density[tiles - 1 - tile])
-            for parity, value in enumerate((density[tile] + mirror, density[tile] - mirror)):
+            near = density(tile)
+            far = mirrored(density(tiles - 1 - tile))
+            for parity, value in enumerate((near + far, near - far)):
                 column = parity * half_cells + tile * LANES
-                store_split(first, start, step_rows, slice(column, column + LANES), value)
+                store_split(first, start, side, slice(column, column + LANES), value)
         return carry
 
-    lax.fori_loop(0, solves * side // step_rows, densities, 0, unroll=2)
-
-    for copy in constant_copies:
+    lax.fori_loop(0, solves, densities, 0, unroll=2)
+
+    for copy in copies[boxes_count + 2 :]:
         copy.wait()
 
     def along_x(start, columns, source):
@@ -310,14 +343,16 @@
                         row = ((start // side + solve) * tiles + place) * pitch + REACH
                         terms[row : row + side, :] = value[solve * side : (solve + 1) * side, :]
 
+    step_rows = 16
+
     def collect(step, carry):
         own = step // (side // step_rows)
         row = step % (side // step_rows) * step_rows
         sums = None
         for turn in range(rounds):
             index = own * rounds + turn
-            _, _, _, a, _, _ = geometry(index)
-            term = rolled(terms, index * tiles, row, -a[0], -(a[1] * side + a[2]))
+            _, _, a, _, _ = pair_geometry(sizes, match_ref, centers_ref, index)
+            term = rolled(sizes, terms, index, row, step_rows, -a[0], -(a[1] * side + a[2]))
             sums = term if sums is None else [s + t for s, t in zip(sums, term)]
         for tile in range(tiles):
             start = (own * tiles + tile) * side + row
@@ -360,13 +395,16 @@
     return jnp.clip(code, -CODE_LIMIT, CODE_LIMIT), exponent, factor
 
 
-def gather_boxes(boxes, pair_count):
-    pieces = [boxes]
+def swap_cores(block, pair_count):
+    return lax.ppermute(block, "pair", [(i, i ^ 1) for i in range(pair_count)])
+
+
+def gather_chips(boxes, pair_count):
+    pieces = []
     for step in range(1, pair_count // CORES):
         perm = [(i, (i + step * CORES) % pair_count) for i in range(pair_count)]
         pieces.append(lax.ppermute(boxes, "pair", perm))
-    swap = [(i, i ^ 1) for i in range(pair_count)]
-    return pieces + [lax.ppermute(piece, "pair", swap) for piece in pieces]
+    return pieces
 
 
 def unpack_kernel(sizes, *refs):
@@ -409,19 +447,41 @@
             pltpu.VMEM((slab_count,) + blocks[0].shape, jnp.int16),
             pltpu.SemaphoreType.DMA((slab_count,)),
         ],
+        compiler_params=pltpu.CompilerParams(vmem_limit_bytes=8 * 1024 * 1024),
     )(*blocks)
     return out.reshape(row_count // 8, tiles, 8, LANES).transpose(0, 2, 1, 3).reshape(row_count, cells)
 
 
-def team_forces(match, centers, blocks, side, slab_count, pair_count):
-    _, rounds, team = match.shape
-    own_count = team // pair_count
-    rows = own_count * side * side // LANES * (side // slab_count)
-    tiles = side * side // LANES
+def place_near(sizes, match, centers, boxes, other):
+    side, rounds, own_count, slab_count, _ = sizes
+    tiles, _, pitch = box_shape(sizes)
+    placed = (own_count * rounds * side, side * side)
+    either = pl.BlockSpec(memory_space=pl.ANY)
+    vectors = pl.BlockSpec(memory_space=pltpu.VMEM)
+    return pl.pallas_call(
+        functools.partial(near_kernel, sizes),
+        out_shape=[jax.ShapeDtypeStruct(placed, jnp.bfloat16)] * 2,
+        in_specs=[either] * 4,
+        out_specs=[vectors] * 2,
+        scratch_shapes=[
+            pltpu.SMEM(match.shape, jnp.int32),
+            pltpu.SMEM(centers.shape, jnp.int32),
+            pltpu.VMEM((CORES,) + boxes.shape, jnp.bfloat16),
+            pltpu.VMEM((CORES * own_count * tiles * pitch, LANES), jnp.float32),
+            pltpu.SemaphoreType.DMA((4,)),
+        ],
+        compiler_params=pltpu.CompilerParams(vmem_limit_bytes=32 * 1024 * 1024),
+        cost_estimate=pl.CostEstimate(flops=5 * 10**9, bytes_accessed=4 * 1024 * 1024, transcendentals=0),
+    )(match, centers, boxes, other)
+
+
+def team_forces(sizes, match, centers, mine, partner, pieces):
+    side, rounds, own_count, slab_count, pair_count = sizes
+    tiles, _, pitch = box_shape(sizes)
+    _, rows, _ = pieces[0].shape
     solves = own_count * rounds
     group = min(solves, 8)
     cells = side * side
-    pitch = side + 2 * REACH
     basis = sine_basis(side)
     mix_high, mix_low = split_constant(np.kron(np.eye(group), basis))
     mix = np.concatenate([mix_high, mix_high, mix_low], axis=1)
@@ -429,38 +489,34 @@
     gain = chebyshev_gain(side).reshape(side, side, side)
     gain = np.concatenate([gain[:, parity::2].reshape(side, -1) for parity in range(2)], axis=1)
     constants = (mix, gain, *split_constant(there), *split_constant(there.transpose(0, 2, 1)))
-    sizes = (side, rounds, own_count, slab_count, pair_count)
     either = pl.BlockSpec(memory_space=pl.ANY)
     distant = pl.BlockSpec(memory_space=pltpu.HBM)
     vectors = pl.BlockSpec(memory_space=pltpu.VMEM)
     wide = pltpu.VMEM((2 * solves * side, cells), jnp.bfloat16)
     flops = 2 * solves * side * 3 * 2 * (cells * cells // 2 + cells * group * side)
+    inputs = [match, centers, mine, partner, *pieces, *[jnp.asarray(constant) for constant in constants]]
     return pl.pallas_call(
         functools.partial(force_kernel, sizes),
         out_shape=[jax.ShapeDtypeStruct((rows + HEADER_ROWS, LANES), jnp.int16)] * slab_count,
-        in_specs=[distant] * 2 + [either] * len(blocks) + [distant] * len(constants),
+        in_specs=[distant] * 2 + [either] * (len(inputs) - 2 - len(constants)) + [distant] * len(constants),
         out_specs=[vectors] * slab_count,
         scratch_shapes=[
             pltpu.SMEM(match.shape, jnp.int32),
             pltpu.SMEM(centers.shape, jnp.int32),
+            pltpu.VMEM(mine.shape, jnp.bfloat16),
+            pltpu.VMEM(partner.shape, jnp.bfloat16),
             pltpu.VMEM((pair_count, slab_count, rows, LANES), jnp.bfloat16),
             *[pltpu.VMEM(constant.shape, constant.dtype) for constant in constants],
-            pltpu.VMEM((team * tiles * pitch, LANES), jnp.float32),
-            pltpu.VMEM((solves * side, cells), jnp.bfloat16),
+            pltpu.VMEM((own_count * pair_count * tiles * pitch, LANES), jnp.float32),
             wide,
             wide,
             pltpu.VMEM((solves * tiles * pitch, LANES), jnp.float32),
             pltpu.VMEM((own_count * tiles * side, LANES), jnp.float32),
-            pltpu.SemaphoreType.DMA((pair_count + 2 + len(constants),)),
+            pltpu.SemaphoreType.DMA((len(inputs),)),
         ],
         compiler_params=pltpu.CompilerParams(vmem_limit_bytes=60 * 1024 * 1024),
         cost_estimate=pl.CostEstimate(flops=flops, bytes_accessed=8 * 1024 * 1024, transcendentals=0),
-    )(
-        match,
-        centers,
-        *blocks,
-        *[jnp.asarray(constant) for constant in constants],
-    )
+    )(*inputs)
 
 
 def shards(orbitals, centers, matchings):
@@ -471,8 +527,12 @@
     side = round((plane_cells * slab_count) ** (1.0 / 3.0))
     blocks = orbitals.reshape(slab_count, own_count * plane_cells // LANES, LANES)
     boxes = lax.all_to_all(blocks, "slab", split_axis=0, concat_axis=0, tiled=True)
-    pieces = gather_boxes(boxes, pair_count)
-    codes = team_forces(matchings, centers.T, pieces, side, slab_count, pair_count)
+    sizes = (side, matchings.shape[1], own_count, slab_count, pair_count)
+    pieces = gather_chips(boxes, pair_count)
+    mine, partner = place_near(sizes, matchings, centers.T, boxes, swap_cores(boxes, pair_count))
+    pieces, mine, partner = lax.optimization_barrier((pieces, mine, partner))
+    pieces = pieces + [swap_cores(piece, pair_count) for piece in pieces]
+    codes = team_forces(sizes, matchings, centers.T, mine, partner, pieces)
     received = []
     for step in reversed(range(1, slab_count)):
         perm = [(i, partner_of(i, step, slab_count)[0]) for i in range(slab_count)]

time: 59.1 us -> 58.9 us (level)
  waiting for transfers between devices: 9.95 us -> 6.3 us
  local copies, waits for them, and re-layouts: 2.36 us -> 4.54 us
  Pallas kernels: 17.8 us -> 19 us
    pallas_call x0 -> x1, Pallas kernels: none -> 3.89 us  [place_near(): pl.pallas_call(functools.partial(near_kernel, sizes), out_shape=[jax.Shap...]
    ppermute x3, waiting for transfers between devices: 6.4 us -> 2.88 us  [the longest x2 1.57 us: swap_cores(): return lax.ppermute(block, 'pair', [(i, i ^ 1) for i in range(pair_count)])]
    unnamed x22 -> x14, local copies, waits for them, and re-layouts: 1.28 us -> 3.46 us
    pallas_call x1, Pallas kernels: 15 us -> 12.9 us  [team_forces(): pl.pallas_call(functools.partial(force_kernel, sizes), out_shape=[jax.Sha...]
  transfers between devices with their start and end apart: 10 -> 10, of which waited for: 6 -> 5; matrix products, arithmetic and copies ran while one was open for 0% -> 0% of each run, Pallas kernels for 0% -> 7%
where the time goes in v9:
time: 58.9 us; the launch traced here: 58.6 us
  Pallas kernels  19 us (32%)
  blocking collectives  16 us (27%)
  starting transfers between devices  12.7 us (22%)
  waiting for transfers between devices  6.3 us (11%)
  local copies, waits for them, and re-layouts  4.54 us (8%)
    all_to_all x1, blocking collectives, shards(): lax.all_to_all(blocks, 'slab', split_axis=0, concat_axis=0, tiled=True)  16 us
    pallas_call x1, Pallas kernels, team_forces(): pl.pallas_call(functools.partial(force_kernel, sizes), out_shape=[jax.Sha...  12.9 us
    ppermute x7, starting transfers between devices, shards(): received.append(lax.ppermute(codes[step], 'slab', perm))  11.2 us
    pallas_call x1, Pallas kernels, place_near(): pl.pallas_call(functools.partial(near_kernel, sizes), out_shape=[jax.Shap...  3.89 us
    unnamed x14, local copies, waits for them, and re-layouts  3.46 us
    ppermute x7, waiting for transfers between devices, shards(): received.append(lax.ppermute(codes[step], 'slab', perm))  3.42 us
    pallas_call x1, Pallas kernels, unpack(): pl.pallas_call(functools.partial(unpack_kernel, (own_count, slab_count, t...  2.2 us
    ppermute x2, waiting for transfers between devices, swap_cores(): return lax.ppermute(block, 'pair', [(i, i ^ 1) for i in range(pair_count)])  1.57 us
  transfers between devices with their start and end apart: 10, of which 5 were waited for; matrix products, arithmetic and copies ran while one was open for 0% of the time, Pallas kernels for 7%

profile of v9, /device:TPU:0, one launch (start us, length us, event | category | flops | bytes accessed | tf_op | source)
XLA Modules:
  0.0 58.6 jit_solution(5054909258537339199)
XLA Ops:
  0.0 1.1 %reshape.9 = bf16[8,128,128]{2,1,0:T(8,128)(2,1)S(1)} reshape(bf16[32,4096]{1,0:T(8,128)(2,1)} %param.9) | data formatting | bytes 524288 | tf_op jit(solution)/shard_map/reshape | solution.py:528
  1.1 0.0 copy-start.1
  1.1 0.0 copy-start.2
  1.1 16.0 %all_to_all.5.own_hbm = bf16[8,128,128]{2,1,0:T(8,128)(2,1)S(1)} all-to-all(bf16[8,128,128]{2,1,0:T(8,128)(2,1)S(1)} %reshape.9), channel_id=1, replica_groups=mesh['slab'=8,'pair'=4] {'slab'}, dimensions={0} | all-to-all | bytes 524288 | tf_op jit(solution)/shard_map/all_to_all | solution.py:529
  17.1 0.0 collective-permute-start.1
  17.1 1.5 %collective-permute-start = (bf16[8,128,128]{2,1,0:T(8,128)(2,1)S(1)}, bf16[8,128,128]{2,1,0:T(8,128)(2,1)S(1)}, u32[]{:S(2)}, u32[]{:S(2)}) collective-permute-start(bf16[8,128,128]{2,1,0:T(8,128)(2,1)S(1)} %all_to_all.5.own_hbm), channel_id=1, source_target_pairs={{0,2},{1,3},{2,0},{3,1},{4,6},{5,7},{6,4},{7,5},{8,10},{9,11},{10,... | collective-permute-start | bytes 786440 | tf_op jit(solution)/shard_map/ppermute | solution.py:406
  18.6 0.0 collective-permute-done.1.other_hbm
  18.6 3.9 %shard_map.91 = (bf16[512,1024]{1,0:T(8,128)(2,1)S(1)}, bf16[512,1024]{1,0:T(8,128)(2,1)S(1)}) custom-call(s32[1,4,16]{2,1,0:T(4,128)S(1)} %copy-done.1, s32[3,128]{1,0:T(4,128)S(1)} %bitcast.7, bf16[8,128,128]{2,1,0:T(8,128)(2,1)S(1)} %all_to_all.5.own_hbm, bf16[8,128,128]{2,1,0:T(8,128)(2,1)S(1)} %collective-permute-done.1.other_hbm), custom_call_target="tpu_custom_call" | custom-call | flops 5000000000 | bytes 4194304 | tf_op jit(solution)/shard_map/pallas_call | solution.py:461
  22.5 1.0 %copy-done.3 = bf16[512,1024]{1,0:T(8,128)(2,1)} copy-done((bf16[512,1024]{1,0:T(8,128)(2,1)}, bf16[512,1024]{1,0:T(8,128)(2,1)S(1)}, u32[]{:S(2)}) %copy-start.3) | copy-done | bytes 1048600
  23.5 1.0 %copy-done.4 = bf16[512,1024]{1,0:T(8,128)(2,1)} copy-done((bf16[512,1024]{1,0:T(8,128)(2,1)}, bf16[512,1024]{1,0:T(8,128)(2,1)S(1)}, u32[]{:S(2)}) %copy-start.4) | copy-done | bytes 1048600
  24.5 1.3 %collective-permute-done.refs_0_ = bf16[8,128,128]{2,1,0:T(8,128)(2,1)S(1)} collective-permute-done((bf16[8,128,128]{2,1,0:T(8,128)(2,1)S(1)}, bf16[8,128,128]{2,1,0:T(8,128)(2,1)S(1)}, u32[]{:S(2)}, u32[]{:S(2)}) %collective-permute-start) | collective-permute-done | bytes 262176 | tf_op jit(solution)/shard_map/ppermute | solution.py:406
  25.8 1.5 %collective-permute-done.2.refs_1_ = bf16[8,128,128]{2,1,0:T(8,128)(2,1)S(1)} collective-permute-done((bf16[8,128,128]{2,1,0:T(8,128)(2,1)S(1)}, bf16[8,128,128]{2,1,0:T(8,128)(2,1)S(1)}, u32[]{:S(2)}, u32[]{:S(2)}) %collective-permute-start.2) | collective-permute-done | bytes 262176 | tf_op jit(solution)/shard_map/ppermute | solution.py:399
  27.4 0.7 %copy-done.6 = bf16[8,128,128]{2,1,0:T(8,128)(2,1)} copy-done((bf16[8,128,128]{2,1,0:T(8,128)(2,1)}, bf16[8,128,128]{2,1,0:T(8,128)(2,1)S(1)}, u32[]{:S(2)}) %copy-start.6) | copy-done | bytes 262168
  28.1 12.9 %shard_map.92 = (s16[144,128]{1,0:T(8,128)(2,1)}, s16[144,128]{1,0:T(8,128)(2,1)}, s16[144,128]{1,0:T(8,128)(2,1)}, s16[144,128]{1,0:T(8,128)(2,1)}, s16[144,128...) custom-call(s32[1,4,16]{2,1,0:T(4,128)} %match_hbm.3, ...), custom_call_target="tpu_custom_call" | custom-call | flops 4831838208 | bytes 8388608 | tf_op jit(solution)/shard_map/pallas_call | solution.py:498
  41.0 2.1 %collective-permute-start.3 = (s16[144,128]{1,0:T(8,128)(2,1)}, s16[144,128]{1,0:T(8,128)(2,1)S(1)}, u32[]{:S(2)}, u32[]{:S(2)}) collective-permute-start(s16[144,128]{1,0:T(8,128)(2,1)} %get-tuple-element.23), channel_id=1, source_target_pairs={{0,28},{4,24},{8,20},{12,16},{16,12},{20,8},{24,4},{28,0},{1,29},{... | collective-permute-start | bytes 110600 | tf_op jit(solution)/shard_map/ppermute | solution.py:539
  43.1 2.5 %collective-permute-start.4 = (s16[144,128]{1,0:T(8,128)(2,1)}, s16[144,128]{1,0:T(8,128)(2,1)S(1)}, u32[]{:S(2)}, u32[]{:S(2)}) collective-permute-start(s16[144,128]{1,0:T(8,128)(2,1)} %get-tuple-element.24), channel_id=1, source_target_pairs={{0,24},{4,28},{8,16},{12,20},{16,8},{20,12},{24,0},{28,4},{1,25},{... | collective-permute-start | bytes 110600 | tf_op jit(solution)/shard_map/ppermute | solution.py:539
  45.6 3.1 %collective-permute-start.6 = (s16[144,128]{1,0:T(8,128)(2,1)}, s16[144,128]{1,0:T(8,128)(2,1)S(1)}, u32[]{:S(2)}, u32[]{:S(2)}) collective-permute-start(s16[144,128]{1,0:T(8,128)(2,1)} %get-tuple-element.26), channel_id=1, source_target_pairs={{0,16},{4,20},{8,24},{12,28},{16,0},{20,4},{24,8},{28,12},{1,17},{... | collective-permute-start | bytes 110600 | tf_op jit(solution)/shard_map/ppermute | solution.py:539
  48.7 2.7 %collective-permute-start.8 = (s16[144,128]{1,0:T(8,128)(2,1)}, s16[144,128]{1,0:T(8,128)(2,1)S(1)}, u32[]{:S(2)}, u32[]{:S(2)}) collective-permute-start(s16[144,128]{1,0:T(8,128)(2,1)} %get-tuple-element.28), channel_id=1, source_target_pairs={{0,8},{4,12},{8,0},{12,4},{16,24},{20,28},{24,16},{28,20},{1,9},{5... | collective-permute-start | bytes 110600 | tf_op jit(solution)/shard_map/ppermute | solution.py:539
  51.4 0.8 %collective-permute-start.9 = (s16[144,128]{1,0:T(8,128)(2,1)}, s16[144,128]{1,0:T(8,128)(2,1)S(1)}, u32[]{:S(2)}, u32[]{:S(2)}) collective-permute-start(s16[144,128]{1,0:T(8,128)(2,1)} %get-tuple-element.29), channel_id=1, source_target_pairs={{0,4},{4,0},{8,12},{12,8},{16,20},{20,16},{24,28},{28,24},{1,5},{5... | collective-permute-start | bytes 110600 | tf_op jit(solution)/shard_map/ppermute | solution.py:539
  52.2 1.6 %collective-permute-done.7.refs_4_ = s16[144,128]{1,0:T(8,128)(2,1)S(1)} collective-permute-done((s16[144,128]{1,0:T(8,128)(2,1)}, s16[144,128]{1,0:T(8,128)(2,1)S(1)}, u32[]{:S(2)}, u32[]{:S(2)}) %collective-permute-start.7) | collective-permute-done | bytes 36896 | tf_op jit(solution)/shard_map/ppermute | solution.py:539
  53.7 0.2 collective-permute-done.8.refs_5_
  53.9 1.6 %collective-permute-done.9.refs_6_ = s16[144,128]{1,0:T(8,128)(2,1)S(1)} collective-permute-done((s16[144,128]{1,0:T(8,128)(2,1)}, s16[144,128]{1,0:T(8,128)(2,1)S(1)}, u32[]{:S(2)}, u32[]{:S(2)}) %collective-permute-start.9) | collective-permute-done | bytes 36896 | tf_op jit(solution)/shard_map/ppermute | solution.py:539
  55.6 0.8 %copy-done = s16[144,128]{1,0:T(8,128)(2,1)S(1)} copy-done((s16[144,128]{1,0:T(8,128)(2,1)S(1)}, s16[144,128]{1,0:T(8,128)(2,1)}, u32[]{:S(2)}) %copy-start) | copy-done | bytes 36888
  56.3 2.2 %shard_map.93 = f32[1024,128]{1,0:T(8,128)} custom-call(s16[144,128]{1,0:T(8,128)(2,1)S(1)} %collective-permute-done.3.refs_0_, s16[144,128]{1,0:T(8,128)(2,1)S(1)} %collective-permute-done.4.refs_1_, s16[144,128]{1,0:T(8,128)(2,1)S(1)} %collective-permute-done.5.refs_2_, s16[144,128]{1,0:T(8,128)(2,1)S(1)} %collective-permute-done.6.refs_3_, ...), custom_call_target="tpu_custom_call" | custom-call | tf_op jit(solution)/shard_map/pallas_call | solution.py:441
  (15 shorter events, 0.0 us)
Async XLA Ops:
  1.1 17.6 %copy-start.1 = (s32[1,4,16]{2,1,0:T(4,128)S(1)}, s32[1,4,16]{2,1,0:T(4,128)}, u32[]{:S(2)}) copy-start(s32[1,4,16]{2,1,0:T(4,128)} %match_hbm.3) | copy-start | bytes 772
  1.1 17.6 %copy-start.2 = (s32[128,3]{0,1:T(4,128)S(1)}, s32[128,3]{0,1:T(4,128)}, u32[]{:S(2)}) copy-start(s32[128,3]{0,1:T(4,128)} %param.10) | copy-start | bytes 4612
  17.1 1.5 %collective-permute-start.1 = (bf16[8,128,128]{2,1,0:T(8,128)(2,1)S(1)}, bf16[8,128,128]{2,1,0:T(8,128)(2,1)S(1)}, u32[]{:S(2)}, u32[]{:S(2)}) collective-permute-start(bf16[8,128,128]{2,1,0:T(8,128)(2,1)S(1)} %all_to_all.5.own_hbm), channel_id=1, source_target_pairs={{0,1},{1,0},{2,3},{3,2},{4,5},{5,4},{6,7},{7,6},{8,9},{9,8},{10,11... | collective-permute-start | bytes 786440 | tf_op jit(solution)/shard_map/ppermute | solution.py:399
  17.1 8.7 %collective-permute-start = (bf16[8,128,128]{2,1,0:T(8,128)(2,1)S(1)}, bf16[8,128,128]{2,1,0:T(8,128)(2,1)S(1)}, u32[]{:S(2)}, u32[]{:S(2)}) collective-permute-start(bf16[8,128,128]{2,1,0:T(8,128)(2,1)S(1)} %all_to_all.5.own_hbm), channel_id=1, source_target_pairs={{0,2},{1,3},{2,0},{3,1},{4,6},{5,7},{6,4},{7,5},{8,10},{9,11},{10,... | collective-permute-start | bytes 786440 | tf_op jit(solution)/shard_map/ppermute | solution.py:406
  22.5 1.0 %copy-start.3 = (bf16[512,1024]{1,0:T(8,128)(2,1)}, bf16[512,1024]{1,0:T(8,128)(2,1)S(1)}, u32[]{:S(2)}) copy-start(bf16[512,1024]{1,0:T(8,128)(2,1)S(1)} %get-tuple-element.20.mine_hbm) | copy-start | bytes 3145732
  23.5 1.0 %copy-start.4 = (bf16[512,1024]{1,0:T(8,128)(2,1)}, bf16[512,1024]{1,0:T(8,128)(2,1)S(1)}, u32[]{:S(2)}) copy-start(bf16[512,1024]{1,0:T(8,128)(2,1)S(1)} %get-tuple-element.21.partner_hbm) | copy-start | bytes 3145732
  25.8 1.5 %copy-start.5 = (bf16[8,128,128]{2,1,0:T(8,128)(2,1)}, bf16[8,128,128]{2,1,0:T(8,128)(2,1)S(1)}, u32[]{:S(2)}) copy-start(bf16[8,128,128]{2,1,0:T(8,128)(2,1)S(1)} %collective-permute-done.refs_0_) | copy-start | bytes 786436
  25.8 1.5 %collective-permute-start.2 = (bf16[8,128,128]{2,1,0:T(8,128)(2,1)S(1)}, bf16[8,128,128]{2,1,0:T(8,128)(2,1)S(1)}, u32[]{:S(2)}, u32[]{:S(2)}) collective-permute-start(bf16[8,128,128]{2,1,0:T(8,128)(2,1)S(1)} %collective-permute-done.refs_0_), channel_id=1, source_target_pairs={{0,1},{1,0},{2,3},{3,2},{4,5},{5,4},{6,7},{7,6},{8,9},{9,8},{10,11... | collective-permute-start | bytes 786440 | tf_op jit(solution)/shard_map/ppermute | solution.py:399
  27.4 0.7 %copy-start.6 = (bf16[8,128,128]{2,1,0:T(8,128)(2,1)}, bf16[8,128,128]{2,1,0:T(8,128)(2,1)S(1)}, u32[]{:S(2)}) copy-start(bf16[8,128,128]{2,1,0:T(8,128)(2,1)S(1)} %collective-permute-done.2.refs_1_) | copy-start | bytes 786436
  41.0 7.7 %collective-permute-start.3 = (s16[144,128]{1,0:T(8,128)(2,1)}, s16[144,128]{1,0:T(8,128)(2,1)S(1)}, u32[]{:S(2)}, u32[]{:S(2)}) collective-permute-start(s16[144,128]{1,0:T(8,128)(2,1)} %get-tuple-element.23), channel_id=1, source_target_pairs={{0,28},{4,24},{8,20},{12,16},{16,12},{20,8},{24,4},{28,0},{1,29},{... | collective-permute-start | bytes 110600 | tf_op jit(solution)/shard_map/ppermute | solution.py:539
  43.1 8.4 %collective-permute-start.4 = (s16[144,128]{1,0:T(8,128)(2,1)}, s16[144,128]{1,0:T(8,128)(2,1)S(1)}, u32[]{:S(2)}, u32[]{:S(2)}) collective-permute-start(s16[144,128]{1,0:T(8,128)(2,1)} %get-tuple-element.24), channel_id=1, source_target_pairs={{0,24},{4,28},{8,16},{12,20},{16,8},{20,12},{24,0},{28,4},{1,25},{... | collective-permute-start | bytes 110600 | tf_op jit(solution)/shard_map/ppermute | solution.py:539
  45.6 6.6 %collective-permute-start.5 = (s16[144,128]{1,0:T(8,128)(2,1)}, s16[144,128]{1,0:T(8,128)(2,1)S(1)}, u32[]{:S(2)}, u32[]{:S(2)}) collective-permute-start(s16[144,128]{1,0:T(8,128)(2,1)} %get-tuple-element.25), channel_id=1, source_target_pairs={{0,20},{4,16},{8,28},{12,24},{16,4},{20,0},{24,12},{28,8},{1,21},{... | collective-permute-start | bytes 110600 | tf_op jit(solution)/shard_map/ppermute | solution.py:539
  45.6 6.6 %collective-permute-start.6 = (s16[144,128]{1,0:T(8,128)(2,1)}, s16[144,128]{1,0:T(8,128)(2,1)S(1)}, u32[]{:S(2)}, u32[]{:S(2)}) collective-permute-start(s16[144,128]{1,0:T(8,128)(2,1)} %get-tuple-element.26), channel_id=1, source_target_pairs={{0,16},{4,20},{8,24},{12,28},{16,0},{20,4},{24,8},{28,12},{1,17},{... | collective-permute-start | bytes 110600 | tf_op jit(solution)/shard_map/ppermute | solution.py:539
  48.7 5.1 %collective-permute-start.7 = (s16[144,128]{1,0:T(8,128)(2,1)}, s16[144,128]{1,0:T(8,128)(2,1)S(1)}, u32[]{:S(2)}, u32[]{:S(2)}) collective-permute-start(s16[144,128]{1,0:T(8,128)(2,1)} %get-tuple-element.27), channel_id=1, source_target_pairs={{0,12},{4,8},{8,4},{12,0},{16,28},{20,24},{24,20},{28,16},{1,13},{... | collective-permute-start | bytes 110600 | tf_op jit(solution)/shard_map/ppermute | solution.py:539
  48.7 5.3 %collective-permute-start.8 = (s16[144,128]{1,0:T(8,128)(2,1)}, s16[144,128]{1,0:T(8,128)(2,1)S(1)}, u32[]{:S(2)}, u32[]{:S(2)}) collective-permute-start(s16[144,128]{1,0:T(8,128)(2,1)} %get-tuple-element.28), channel_id=1, source_target_pairs={{0,8},{4,12},{8,0},{12,4},{16,24},{20,28},{24,16},{28,20},{1,9},{5... | collective-permute-start | bytes 110600 | tf_op jit(solution)/shard_map/ppermute | solution.py:539
  51.4 4.2 %collective-permute-start.9 = (s16[144,128]{1,0:T(8,128)(2,1)}, s16[144,128]{1,0:T(8,128)(2,1)S(1)}, u32[]{:S(2)}, u32[]{:S(2)}) collective-permute-start(s16[144,128]{1,0:T(8,128)(2,1)} %get-tuple-element.29), channel_id=1, source_target_pairs={{0,4},{4,0},{8,12},{12,8},{16,20},{20,16},{24,28},{28,24},{1,5},{5... | collective-permute-start | bytes 110600 | tf_op jit(solution)/shard_map/ppermute | solution.py:539
  55.6 0.8 %copy-start = (s16[144,128]{1,0:T(8,128)(2,1)S(1)}, s16[144,128]{1,0:T(8,128)(2,1)}, u32[]{:S(2)}) copy-start(s16[144,128]{1,0:T(8,128)(2,1)} %get-tuple-element.30.refs_7_) | copy-start | bytes 110596

commit v10 on v9

--- a/solution.py
+++ b/solution.py
@@ -290,8 +290,8 @@
 
     lax.fori_loop(0, solves, densities, 0, unroll=2)
 
-    for copy in copies[boxes_count + 2 :]:
-        copy.wait()
+    mix_copy, gain_copy, *matrix_copies = copies[boxes_count + 2 :]
+    mix_copy.wait()
 
     def along_x(start, columns, source):
         high = source[start : start + group_rows, columns]
@@ -312,6 +312,8 @@
             columns = slice(column, column + width)
             store_split(second, start, group_rows, columns, along_x(start, columns, first))
 
+    for copy in (gain_copy, *matrix_copies[:2]):
+        copy.wait()
     for parity in range(2):
         for column in range(0, half_cells, width):
             columns = slice(column, column + width)
@@ -321,6 +323,8 @@
             value = (value.reshape(solves, side, width) * gain[None]).reshape(row_count, width)
             store_split(first, 0, row_count, columns, value)
 
+    for copy in matrix_copies[2:]:
+        copy.wait()
     for parity in range(2):
         for column in range(0, half_cells, width):
             value = in_plane(parity, slice(column, column + width), first, back_high, back_low)
@@ -470,7 +474,7 @@
             pltpu.VMEM((CORES * own_count * tiles * pitch, LANES), jnp.float32),
             pltpu.SemaphoreType.DMA((4,)),
         ],
-        compiler_params=pltpu.CompilerParams(vmem_limit_bytes=32 * 1024 * 1024),
+        compiler_params=pltpu.CompilerParams(vmem_limit_bytes=60 * 1024 * 1024),
         cost_estimate=pl.CostEstimate(flops=5 * 10**9, bytes_accessed=4 * 1024 * 1024, transcendentals=0),
     )(match, centers, boxes, other)
 

time: 58.9 us -> 59.7 us (1.014)
  Pallas kernels: 19 us -> 21.1 us
  local copies, waits for them, and re-layouts: 4.54 us -> 3.28 us
    pallas_call x1, Pallas kernels: 3.89 us -> 5.56 us  [place_near(): pl.pallas_call(functools.partial(near_kernel, sizes), out_shape=[jax.Shap...]
    unnamed x14 -> x10, local copies, waits for them, and re-layouts: 3.46 us -> 2.2 us
  transfers between devices with their start and end apart: 10 -> 10, of which waited for: 5 -> 6; matrix products, arithmetic and copies ran while one was open for 0% -> 0% of each run, Pallas kernels for 7% -> 9%
where the time goes in v10:
time: 59.7 us; the launch traced here: 59.4 us
  Pallas kernels  21.1 us (35%)
  blocking collectives  16 us (27%)
  starting transfers between devices  12.7 us (21%)
  waiting for transfers between devices  6.33 us (11%)
  local copies, waits for them, and re-layouts  3.28 us (5%)
    all_to_all x1, blocking collectives, shards(): lax.all_to_all(blocks, 'slab', split_axis=0, concat_axis=0, tiled=True)  16 us
    pallas_call x1, Pallas kernels, team_forces(): pl.pallas_call(functools.partial(force_kernel, sizes), out_shape=[jax.Sha...  13.3 us
    ppermute x7, starting transfers between devices, shards(): received.append(lax.ppermute(codes[step], 'slab', perm))  11.2 us
    pallas_call x1, Pallas kernels, place_near(): pl.pallas_call(functools.partial(near_kernel, sizes), out_shape=[jax.Shap...  5.56 us
    ppermute x7, waiting for transfers between devices, shards(): received.append(lax.ppermute(codes[step], 'slab', perm))  3.85 us
    unnamed x10, local copies, waits for them, and re-layouts  2.2 us
    pallas_call x1, Pallas kernels, unpack(): pl.pallas_call(functools.partial(unpack_kernel, (own_count, slab_count, t...  2.2 us
    ppermute x2, waiting for transfers between devices, swap_cores(): return lax.ppermute(block, 'pair', [(i, i ^ 1) for i in range(pair_count)])  1.57 us
  transfers between devices with their start and end apart: 10, of which 6 were waited for; matrix products, arithmetic and copies ran while one was open for 0% of the time, Pallas kernels for 9%

profile of v10, /device:TPU:0, one launch (start us, length us, event | category | flops | bytes accessed | tf_op | source)
XLA Modules:
  0.0 59.4 jit_solution(13031281712363937058)
XLA Ops:
  0.0 1.1 %reshape.9 = bf16[8,128,128]{2,1,0:T(8,128)(2,1)S(1)} reshape(bf16[32,4096]{1,0:T(8,128)(2,1)} %param.9) | data formatting | bytes 524288 | tf_op jit(solution)/shard_map/reshape | solution.py:532
  1.1 16.0 %all_to_all.5.own_hbm = bf16[8,128,128]{2,1,0:T(8,128)(2,1)S(1)} all-to-all(bf16[8,128,128]{2,1,0:T(8,128)(2,1)S(1)} %reshape.9), channel_id=1, replica_groups=mesh['slab'=8,'pair'=4] {'slab'}, dimensions={0} | all-to-all | bytes 524288 | tf_op jit(solution)/shard_map/all_to_all | solution.py:533
  17.1 0.0 collective-permute-start.1
  17.1 1.5 %collective-permute-start = (bf16[8,128,128]{2,1,0:T(8,128)(2,1)S(1)}, bf16[8,128,128]{2,1,0:T(8,128)(2,1)S(1)}, u32[]{:S(2)}, u32[]{:S(2)}) collective-permute-start(bf16[8,128,128]{2,1,0:T(8,128)(2,1)S(1)} %all_to_all.5.own_hbm), channel_id=1, source_target_pairs={{0,2},{1,3},{2,0},{3,1},{4,6},{5,7},{6,4},{7,5},{8,10},{9,11},{10,... | collective-permute-start | bytes 786440 | tf_op jit(solution)/shard_map/ppermute | solution.py:410
  18.6 0.0 collective-permute-done.1.other_hbm
  18.6 0.7 %copy-done.4 = bf16[8,128,128]{2,1,0:T(8,128)(2,1)} copy-done((bf16[8,128,128]{2,1,0:T(8,128)(2,1)}, bf16[8,128,128]{2,1,0:T(8,128)(2,1)S(1)}, u32[]{:S(2)}) %copy-start.4) | copy-done | bytes 262168
  19.3 5.6 %shard_map.91 = (bf16[512,1024]{1,0:T(8,128)(2,1)}, bf16[512,1024]{1,0:T(8,128)(2,1)}) custom-call(s32[1,4,16]{2,1,0:T(4,128)} %match_hbm.3, s32[3,128]{1,0:T(4,128)} %bitcast.6, bf16[8,128,128]{2,1,0:T(8,128)(2,1)} %copy-done.1, bf16[8,128,128]{2,1,0:T(8,128)(2,1)} %copy-done.4), custom_call_target="tpu_custom_call" | custom-call | flops 5000000000 | bytes 4194304 | tf_op jit(solution)/shard_map/pallas_call | solution.py:465
  24.9 0.9 %collective-permute-done.refs_0_ = bf16[8,128,128]{2,1,0:T(8,128)(2,1)S(1)} collective-permute-done((bf16[8,128,128]{2,1,0:T(8,128)(2,1)S(1)}, bf16[8,128,128]{2,1,0:T(8,128)(2,1)S(1)}, u32[]{:S(2)}, u32[]{:S(2)}) %collective-permute-start) | collective-permute-done | bytes 262176 | tf_op jit(solution)/shard_map/ppermute | solution.py:410
  25.8 1.5 %collective-permute-done.2.refs_1_ = bf16[8,128,128]{2,1,0:T(8,128)(2,1)S(1)} collective-permute-done((bf16[8,128,128]{2,1,0:T(8,128)(2,1)S(1)}, bf16[8,128,128]{2,1,0:T(8,128)(2,1)S(1)}, u32[]{:S(2)}, u32[]{:S(2)}) %collective-permute-start.2) | collective-permute-done | bytes 262176 | tf_op jit(solution)/shard_map/ppermute | solution.py:403
  27.3 0.7 %copy-done.3 = bf16[8,128,128]{2,1,0:T(8,128)(2,1)} copy-done((bf16[8,128,128]{2,1,0:T(8,128)(2,1)}, bf16[8,128,128]{2,1,0:T(8,128)(2,1)S(1)}, u32[]{:S(2)}) %copy-start.3) | copy-done | bytes 262168
  28.1 13.3 %shard_map.92 = (s16[144,128]{1,0:T(8,128)(2,1)}, s16[144,128]{1,0:T(8,128)(2,1)}, s16[144,128]{1,0:T(8,128)(2,1)}, s16[144,128]{1,0:T(8,128)(2,1)}, s16[144,128...) custom-call(s32[1,4,16]{2,1,0:T(4,128)} %match_hbm.3, ...), custom_call_target="tpu_custom_call" | custom-call | flops 4831838208 | bytes 8388608 | tf_op jit(solution)/shard_map/pallas_call | solution.py:502
  41.4 2.0 %collective-permute-start.3 = (s16[144,128]{1,0:T(8,128)(2,1)}, s16[144,128]{1,0:T(8,128)(2,1)S(1)}, u32[]{:S(2)}, u32[]{:S(2)}) collective-permute-start(s16[144,128]{1,0:T(8,128)(2,1)} %get-tuple-element.23), channel_id=1, source_target_pairs={{0,28},{4,24},{8,20},{12,16},{16,12},{20,8},{24,4},{28,0},{1,29},{... | collective-permute-start | bytes 110600 | tf_op jit(solution)/shard_map/ppermute | solution.py:543
  43.4 3.0 %collective-permute-start.4 = (s16[144,128]{1,0:T(8,128)(2,1)}, s16[144,128]{1,0:T(8,128)(2,1)S(1)}, u32[]{:S(2)}, u32[]{:S(2)}) collective-permute-start(s16[144,128]{1,0:T(8,128)(2,1)} %get-tuple-element.24), channel_id=1, source_target_pairs={{0,24},{4,28},{8,16},{12,20},{16,8},{20,12},{24,0},{28,4},{1,25},{... | collective-permute-start | bytes 110600 | tf_op jit(solution)/shard_map/ppermute | solution.py:543
  46.4 0.0 collective-permute-start.5
  46.4 2.7 %collective-permute-start.6 = (s16[144,128]{1,0:T(8,128)(2,1)}, s16[144,128]{1,0:T(8,128)(2,1)S(1)}, u32[]{:S(2)}, u32[]{:S(2)}) collective-permute-start(s16[144,128]{1,0:T(8,128)(2,1)} %get-tuple-element.26), channel_id=1, source_target_pairs={{0,16},{4,20},{8,24},{12,28},{16,0},{20,4},{24,8},{28,12},{1,17},{... | collective-permute-start | bytes 110600 | tf_op jit(solution)/shard_map/ppermute | solution.py:543
  49.1 3.2 %collective-permute-start.8 = (s16[144,128]{1,0:T(8,128)(2,1)}, s16[144,128]{1,0:T(8,128)(2,1)S(1)}, u32[]{:S(2)}, u32[]{:S(2)}) collective-permute-start(s16[144,128]{1,0:T(8,128)(2,1)} %get-tuple-element.28), channel_id=1, source_target_pairs={{0,8},{4,12},{8,0},{12,4},{16,24},{20,28},{24,16},{28,20},{1,9},{5... | collective-permute-start | bytes 110600 | tf_op jit(solution)/shard_map/ppermute | solution.py:543
  52.3 0.3 collective-permute-start.9
  52.6 0.1 collective-permute-done.5.refs_2_
  52.7 0.0 collective-permute-done.6.refs_3_
  52.7 1.5 %collective-permute-done.7.refs_4_ = s16[144,128]{1,0:T(8,128)(2,1)S(1)} collective-permute-done((s16[144,128]{1,0:T(8,128)(2,1)}, s16[144,128]{1,0:T(8,128)(2,1)S(1)}, u32[]{:S(2)}, u32[]{:S(2)}) %collective-permute-start.7) | collective-permute-done | bytes 36896 | tf_op jit(solution)/shard_map/ppermute | solution.py:543
  54.2 0.6 %collective-permute-done.8.refs_5_ = s16[144,128]{1,0:T(8,128)(2,1)S(1)} collective-permute-done((s16[144,128]{1,0:T(8,128)(2,1)}, s16[144,128]{1,0:T(8,128)(2,1)S(1)}, u32[]{:S(2)}, u32[]{:S(2)}) %collective-permute-start.8) | collective-permute-done | bytes 36896 | tf_op jit(solution)/shard_map/ppermute | solution.py:543
  54.8 1.6 %collective-permute-done.9.refs_6_ = s16[144,128]{1,0:T(8,128)(2,1)S(1)} collective-permute-done((s16[144,128]{1,0:T(8,128)(2,1)}, s16[144,128]{1,0:T(8,128)(2,1)S(1)}, u32[]{:S(2)}, u32[]{:S(2)}) %collective-permute-start.9) | collective-permute-done | bytes 36896 | tf_op jit(solution)/shard_map/ppermute | solution.py:543
  56.5 0.8 %copy-done = s16[144,128]{1,0:T(8,128)(2,1)S(1)} copy-done((s16[144,128]{1,0:T(8,128)(2,1)S(1)}, s16[144,128]{1,0:T(8,128)(2,1)}, u32[]{:S(2)}) %copy-start) | copy-done | bytes 36888
  57.2 2.2 %shard_map.93 = f32[1024,128]{1,0:T(8,128)} custom-call(s16[144,128]{1,0:T(8,128)(2,1)S(1)} %collective-permute-done.3.refs_0_, s16[144,128]{1,0:T(8,128)(2,1)S(1)} %collective-permute-done.4.refs_1_, s16[144,128]{1,0:T(8,128)(2,1)S(1)} %collective-permute-done.5.refs_2_, s16[144,128]{1,0:T(8,128)(2,1)S(1)} %collective-permute-done.6.refs_3_, ...), custom_call_target="tpu_custom_call" | custom-call | tf_op jit(solution)/shard_map/pallas_call | solution.py:445
  (11 shorter events, 0.0 us)
Async XLA Ops:
  17.1 1.5 %copy-start.1 = (bf16[8,128,128]{2,1,0:T(8,128)(2,1)}, bf16[8,128,128]{2,1,0:T(8,128)(2,1)S(1)}, u32[]{:S(2)}) copy-start(bf16[8,128,128]{2,1,0:T(8,128)(2,1)S(1)} %all_to_all.5.own_hbm) | copy-start | bytes 786436
  17.1 1.5 %collective-permute-start.1 = (bf16[8,128,128]{2,1,0:T(8,128)(2,1)S(1)}, bf16[8,128,128]{2,1,0:T(8,128)(2,1)S(1)}, u32[]{:S(2)}, u32[]{:S(2)}) collective-permute-start(bf16[8,128,128]{2,1,0:T(8,128)(2,1)S(1)} %all_to_all.5.own_hbm), channel_id=1, source_target_pairs={{0,1},{1,0},{2,3},{3,2},{4,5},{5,4},{6,7},{7,6},{8,9},{9,8},{10,11... | collective-permute-start | bytes 786440 | tf_op jit(solution)/shard_map/ppermute | solution.py:403
  17.1 8.7 %collective-permute-start = (bf16[8,128,128]{2,1,0:T(8,128)(2,1)S(1)}, bf16[8,128,128]{2,1,0:T(8,128)(2,1)S(1)}, u32[]{:S(2)}, u32[]{:S(2)}) collective-permute-start(bf16[8,128,128]{2,1,0:T(8,128)(2,1)S(1)} %all_to_all.5.own_hbm), channel_id=1, source_target_pairs={{0,2},{1,3},{2,0},{3,1},{4,6},{5,7},{6,4},{7,5},{8,10},{9,11},{10,... | collective-permute-start | bytes 786440 | tf_op jit(solution)/shard_map/ppermute | solution.py:410
  18.6 0.7 %copy-start.4 = (bf16[8,128,128]{2,1,0:T(8,128)(2,1)}, bf16[8,128,128]{2,1,0:T(8,128)(2,1)S(1)}, u32[]{:S(2)}) copy-start(bf16[8,128,128]{2,1,0:T(8,128)(2,1)S(1)} %collective-permute-done.1.other_hbm) | copy-start | bytes 786436
  25.8 1.5 %copy-start.2 = (bf16[8,128,128]{2,1,0:T(8,128)(2,1)}, bf16[8,128,128]{2,1,0:T(8,128)(2,1)S(1)}, u32[]{:S(2)}) copy-start(bf16[8,128,128]{2,1,0:T(8,128)(2,1)S(1)} %collective-permute-done.refs_0_) | copy-start | bytes 786436
  25.8 1.5 %collective-permute-start.2 = (bf16[8,128,128]{2,1,0:T(8,128)(2,1)S(1)}, bf16[8,128,128]{2,1,0:T(8,128)(2,1)S(1)}, u32[]{:S(2)}, u32[]{:S(2)}) collective-permute-start(bf16[8,128,128]{2,1,0:T(8,128)(2,1)S(1)} %collective-permute-done.refs_0_), channel_id=1, source_target_pairs={{0,1},{1,0},{2,3},{3,2},{4,5},{5,4},{6,7},{7,6},{8,9},{9,8},{10,11... | collective-permute-start | bytes 786440 | tf_op jit(solution)/shard_map/ppermute | solution.py:403
  27.3 0.7 %copy-start.3 = (bf16[8,128,128]{2,1,0:T(8,128)(2,1)}, bf16[8,128,128]{2,1,0:T(8,128)(2,1)S(1)}, u32[]{:S(2)}) copy-start(bf16[8,128,128]{2,1,0:T(8,128)(2,1)S(1)} %collective-permute-done.2.refs_1_) | copy-start | bytes 786436
  41.4 7.7 %collective-permute-start.3 = (s16[144,128]{1,0:T(8,128)(2,1)}, s16[144,128]{1,0:T(8,128)(2,1)S(1)}, u32[]{:S(2)}, u32[]{:S(2)}) collective-permute-start(s16[144,128]{1,0:T(8,128)(2,1)} %get-tuple-element.23), channel_id=1, source_target_pairs={{0,28},{4,24},{8,20},{12,16},{16,12},{20,8},{24,4},{28,0},{1,29},{... | collective-permute-start | bytes 110600 | tf_op jit(solution)/shard_map/ppermute | solution.py:543
  43.4 8.9 %collective-permute-start.4 = (s16[144,128]{1,0:T(8,128)(2,1)}, s16[144,128]{1,0:T(8,128)(2,1)S(1)}, u32[]{:S(2)}, u32[]{:S(2)}) collective-permute-start(s16[144,128]{1,0:T(8,128)(2,1)} %get-tuple-element.24), channel_id=1, source_target_pairs={{0,24},{4,28},{8,16},{12,20},{16,8},{20,12},{24,0},{28,4},{1,25},{... | collective-permute-start | bytes 110600 | tf_op jit(solution)/shard_map/ppermute | solution.py:543
  46.4 6.2 %collective-permute-start.5 = (s16[144,128]{1,0:T(8,128)(2,1)}, s16[144,128]{1,0:T(8,128)(2,1)S(1)}, u32[]{:S(2)}, u32[]{:S(2)}) collective-permute-start(s16[144,128]{1,0:T(8,128)(2,1)} %get-tuple-element.25), channel_id=1, source_target_pairs={{0,20},{4,16},{8,28},{12,24},{16,4},{20,0},{24,12},{28,8},{1,21},{... | collective-permute-start | bytes 110600 | tf_op jit(solution)/shard_map/ppermute | solution.py:543
  46.4 6.2 %collective-permute-start.6 = (s16[144,128]{1,0:T(8,128)(2,1)}, s16[144,128]{1,0:T(8,128)(2,1)S(1)}, u32[]{:S(2)}, u32[]{:S(2)}) collective-permute-start(s16[144,128]{1,0:T(8,128)(2,1)} %get-tuple-element.26), channel_id=1, source_target_pairs={{0,16},{4,20},{8,24},{12,28},{16,0},{20,4},{24,8},{28,12},{1,17},{... | collective-permute-start | bytes 110600 | tf_op jit(solution)/shard_map/ppermute | solution.py:543
  49.1 5.1 %collective-permute-start.7 = (s16[144,128]{1,0:T(8,128)(2,1)}, s16[144,128]{1,0:T(8,128)(2,1)S(1)}, u32[]{:S(2)}, u32[]{:S(2)}) collective-permute-start(s16[144,128]{1,0:T(8,128)(2,1)} %get-tuple-element.27), channel_id=1, source_target_pairs={{0,12},{4,8},{8,4},{12,0},{16,28},{20,24},{24,20},{28,16},{1,13},{... | collective-permute-start | bytes 110600 | tf_op jit(solution)/shard_map/ppermute | solution.py:543
  49.1 5.7 %collective-permute-start.8 = (s16[144,128]{1,0:T(8,128)(2,1)}, s16[144,128]{1,0:T(8,128)(2,1)S(1)}, u32[]{:S(2)}, u32[]{:S(2)}) collective-permute-start(s16[144,128]{1,0:T(8,128)(2,1)} %get-tuple-element.28), channel_id=1, source_target_pairs={{0,8},{4,12},{8,0},{12,4},{16,24},{20,28},{24,16},{28,20},{1,9},{5... | collective-permute-start | bytes 110600 | tf_op jit(solution)/shard_map/ppermute | solution.py:543
  52.3 4.2 %collective-permute-start.9 = (s16[144,128]{1,0:T(8,128)(2,1)}, s16[144,128]{1,0:T(8,128)(2,1)S(1)}, u32[]{:S(2)}, u32[]{:S(2)}) collective-permute-start(s16[144,128]{1,0:T(8,128)(2,1)} %get-tuple-element.29), channel_id=1, source_target_pairs={{0,4},{4,0},{8,12},{12,8},{16,20},{20,16},{24,28},{28,24},{1,5},{5... | collective-permute-start | bytes 110600 | tf_op jit(solution)/shard_map/ppermute | solution.py:543
  56.4 0.8 %copy-start = (s16[144,128]{1,0:T(8,128)(2,1)S(1)}, s16[144,128]{1,0:T(8,128)(2,1)}, u32[]{:S(2)}) copy-start(s16[144,128]{1,0:T(8,128)(2,1)} %get-tuple-element.30.refs_7_) | copy-start | bytes 110596

commit v11 on v10

--- a/solution.py
+++ b/solution.py
@@ -156,24 +156,21 @@
         out_ref[rows, tile * LANES : (tile + 1) * LANES] = (placed[tile] * ok).astype(jnp.bfloat16)
 
 
-def near_kernel(
-    sizes, match_hbm, centers_hbm, own_hbm, other_hbm, mine_ref, partner_ref, match_ref, centers_ref, boxes_ref, fields, sems
+def own_kernel(
+    sizes, match_hbm, centers_hbm, own_hbm, mine_ref, partner_ref, match_ref, centers_ref, boxes_ref, fields, sems
 ):
     side, rounds, own_count, _, _ = sizes
     tiles, _, _ = box_shape(sizes)
-    pair_index = lax.axis_index("pair")
-    core = pair_index % CORES
-    first_member = pair_index // CORES * CORES * own_count
-    sources = (match_hbm, centers_hbm, own_hbm, other_hbm)
-    targets = (match_ref, centers_ref, boxes_ref.at[core], boxes_ref.at[1 - core])
+    first_member = lax.axis_index("pair") * own_count
+    sources = (match_hbm, centers_hbm, own_hbm)
+    targets = (match_ref, centers_ref, boxes_ref.at[0])
     copies = [pltpu.make_async_copy(s, t, sems.at[i]) for i, (s, t) in enumerate(zip(sources, targets))]
     for copy in copies:
         copy.start()
-    clear_edges(sizes, fields, 0, CORES * own_count)
+    clear_edges(sizes, fields, 0, own_count)
     for copy in copies:
         copy.wait()
-    for pair in range(CORES):
-        spread(sizes, boxes_ref, fields, pair)
+    spread(sizes, boxes_ref, fields, 0)
 
     def place(index, carry):
         member, mate, a, b, active = pair_geometry(sizes, match_ref, centers_ref, index)
@@ -183,7 +180,7 @@
             mine_ref[rows, tile * LANES : (tile + 1) * LANES] = placed[tile].astype(jnp.bfloat16)
         local = mate - first_member
 
-        @pl.when((local >= 0) & (local < CORES * own_count))
+        @pl.when((local >= 0) & (local < own_count))
         def _():
             place_partner(sizes, fields, local, a, b, active, partner_ref, rows)
 
@@ -194,7 +191,7 @@
 
 def force_kernel(sizes, match_hbm, centers_hbm, mine_hbm, partner_hbm, *refs):
     side, rounds, own_count, slab_count, pair_count = sizes
-    piece_hbm, refs = refs[: pair_count - CORES], refs[pair_count - CORES :]
+    piece_hbm, refs = refs[: pair_count - 1], refs[pair_count - 1 :]
     constant_hbm, refs = refs[:6], refs[6:]
     out_refs, refs = refs[:slab_count], refs[slab_count:]
     match_ref, centers_ref, mine, partner, boxes_ref, *refs = refs
@@ -207,19 +204,20 @@
     group = min(solves, 8)
     group_rows = group * side
     cells = tiles * LANES
-    width = 2 * LANES
+    width = cells // 2
     slab_index = lax.axis_index("slab")
     pair_index = lax.axis_index("pair")
     core = pair_index % CORES
     chip = pair_index // CORES
     chips = pair_count // CORES
-    first_member = chip * CORES * own_count
+    first_member = pair_index * own_count
 
     places = [
         (chip + chips - step) % chips * CORES + (core + core_step) % CORES
         for core_step in range(CORES)
-        for step in range(1, chips)
+        for step in range(chips)
     ]
+    places = places[1:]
     sources = [match_hbm, centers_hbm, *piece_hbm, mine_hbm, partner_hbm, *constant_hbm]
     targets = [match_ref, centers_ref, *[boxes_ref.at[pair] for pair in places], mine, partner, *constants]
     copies = [pltpu.make_async_copy(s, t, sems.at[i]) for i, (s, t) in enumerate(zip(sources, targets))]
@@ -240,7 +238,7 @@
         _, mate, a, b, active = pair_geometry(sizes, match_ref, centers_ref, index)
         local = mate - first_member
 
-        @pl.when((local < 0) | (local >= CORES * own_count))
+        @pl.when((local < 0) | (local >= own_count))
         def _():
             rows = pl.ds(pl.multiple_of(index * side, side), side)
             place_partner(sizes, fields, mate, a, b, active, partner, rows)
@@ -308,9 +306,8 @@
         return dot(left, jnp.concatenate([basis, basis, rest], axis=0))
 
     for start in range(0, row_count, group_rows):
-        for column in range(0, cells, width):
-            columns = slice(column, column + width)
-            store_split(second, start, group_rows, columns, along_x(start, columns, first))
+        columns = slice(0, cells)
+        store_split(second, start, group_rows, columns, along_x(start, columns, first))
 
     for copy in (gain_copy, *matrix_copies[:2]):
         copy.wait()
@@ -456,27 +453,27 @@
     return out.reshape(row_count // 8, tiles, 8, LANES).transpose(0, 2, 1, 3).reshape(row_count, cells)
 
 
-def place_near(sizes, match, centers, boxes, other):
+def place_own(sizes, match, centers, boxes):
     side, rounds, own_count, slab_count, _ = sizes
     tiles, _, pitch = box_shape(sizes)
     placed = (own_count * rounds * side, side * side)
     either = pl.BlockSpec(memory_space=pl.ANY)
     vectors = pl.BlockSpec(memory_space=pltpu.VMEM)
     return pl.pallas_call(
-        functools.partial(near_kernel, sizes),
+        functools.partial(own_kernel, sizes),
         out_shape=[jax.ShapeDtypeStruct(placed, jnp.bfloat16)] * 2,
-        in_specs=[either] * 4,
+        in_specs=[either] * 3,
         out_specs=[vectors] * 2,
         scratch_shapes=[
             pltpu.SMEM(match.shape, jnp.int32),
             pltpu.SMEM(centers.shape, jnp.int32),
-            pltpu.VMEM((CORES,) + boxes.shape, jnp.bfloat16),
-            pltpu.VMEM((CORES * own_count * tiles * pitch, LANES), jnp.float32),
-            pltpu.SemaphoreType.DMA((4,)),
+            pltpu.VMEM((1,) + boxes.shape, jnp.bfloat16),
+            pltpu.VMEM((own_count * tiles * pitch, LANES), jnp.float32),
+            pltpu.SemaphoreType.DMA((3,)),
         ],
         compiler_params=pltpu.CompilerParams(vmem_limit_bytes=60 * 1024 * 1024),
         cost_estimate=pl.CostEstimate(flops=5 * 10**9, bytes_accessed=4 * 1024 * 1024, transcendentals=0),
-    )(match, centers, boxes, other)
+    )(match, centers, boxes)
 
 
 def team_forces(sizes, match, centers, mine, partner, pieces):
@@ -533,9 +530,11 @@
     boxes = lax.all_to_all(blocks, "slab", split_axis=0, concat_axis=0, tiled=True)
     sizes = (side, matchings.shape[1], own_count, slab_count, pair_count)
     pieces = gather_chips(boxes, pair_count)
-    mine, partner = place_near(sizes, matchings, centers.T, boxes, swap_cores(boxes, pair_count))
+    mine, partner = place_own(sizes, matchings, centers.T, boxes)
+    boxes, mine, partner = lax.optimization_barrier((boxes, mine, partner))
+    swapped = [swap_cores(boxes, pair_count)]
     pieces, mine, partner = lax.optimization_barrier((pieces, mine, partner))
-    pieces = pieces + [swap_cores(piece, pair_count) for piece in pieces]
+    pieces = pieces + swapped + [swap_cores(piece, pair_count) for piece in pieces]
     codes = team_forces(sizes, matchings, centers.T, mine, partner, pieces)
     received = []
     for step in reversed(range(1, slab_count)):

time: 59.7 us -> 58.6 us (0.982)
  waiting for transfers between devices: 6.33 us -> 4.97 us
    ppermute x1, waiting for transfers between devices: 0.9 us -> 0.01 us  [gather_chips(): pieces.append(lax.ppermute(boxes, 'pair', perm))]
where the time goes in v11:
time: 58.6 us; the launch traced here: 58.3 us
  Pallas kernels  21 us (36%)
  blocking collectives  16 us (27%)
  starting transfers between devices  13.2 us (23%)
  waiting for transfers between devices  4.97 us (8%)
  local copies, waits for them, and re-layouts  3.1 us (5%)
    all_to_all x1, blocking collectives, shards(): lax.all_to_all(blocks, 'slab', split_axis=0, concat_axis=0, tiled=True)  16 us
    pallas_call x1, Pallas kernels, team_forces(): pl.pallas_call(functools.partial(force_kernel, sizes), out_shape=[jax.Sha...  13.6 us
    ppermute x7, starting transfers between devices, shards(): received.append(lax.ppermute(codes[step], 'slab', perm))  11.2 us
    pallas_call x1, Pallas kernels, place_own(): pl.pallas_call(functools.partial(own_kernel, sizes), out_shape=[jax.Shape...  5.16 us
    ppermute x7, waiting for transfers between devices, shards(): received.append(lax.ppermute(codes[step], 'slab', perm))  3.58 us
    pallas_call x1, Pallas kernels, unpack(): pl.pallas_call(functools.partial(unpack_kernel, (own_count, slab_count, t...  2.2 us
    unnamed x10, local copies, waits for them, and re-layouts  2.03 us
    ppermute x1, starting transfers between devices, gather_chips(): pieces.append(lax.ppermute(boxes, 'pair', perm))  1.49 us
  transfers between devices with their start and end apart: 10, of which 6 were waited for; matrix products, arithmetic and copies ran while one was open for 0% of the time, Pallas kernels for 9%

profile of v11, /device:TPU:0, one launch (start us, length us, event | category | flops | bytes accessed | tf_op | source)
XLA Modules:
  0.0 58.3 jit_solution(14835723243175843313)
XLA Ops:
  0.0 1.1 %reshape.9 = bf16[8,128,128]{2,1,0:T(8,128)(2,1)S(1)} reshape(bf16[32,4096]{1,0:T(8,128)(2,1)} %param.9) | data formatting | bytes 524288 | tf_op jit(solution)/shard_map/reshape | solution.py:529
  1.1 16.0 %all_to_all.5.own_hbm = bf16[8,128,128]{2,1,0:T(8,128)(2,1)S(1)} all-to-all(bf16[8,128,128]{2,1,0:T(8,128)(2,1)S(1)} %reshape.9), channel_id=1, replica_groups=mesh['slab'=8,'pair'=4] {'slab'}, dimensions={0} | all-to-all | bytes 524288 | tf_op jit(solution)/shard_map/all_to_all | solution.py:530
  17.1 1.5 %collective-permute-start = (bf16[8,128,128]{2,1,0:T(8,128)(2,1)S(1)}, bf16[8,128,128]{2,1,0:T(8,128)(2,1)S(1)}, u32[]{:S(2)}, u32[]{:S(2)}) collective-permute-start(bf16[8,128,128]{2,1,0:T(8,128)(2,1)S(1)} %all_to_all.5.own_hbm), channel_id=1, source_target_pairs={{0,2},{1,3},{2,0},{3,1},{4,6},{5,7},{6,4},{7,5},{8,10},{9,11},{10,... | collective-permute-start | bytes 786440 | tf_op jit(solution)/shard_map/ppermute | solution.py:407
  18.6 5.2 %shard_map.91 = (bf16[512,1024]{1,0:T(8,128)(2,1)}, bf16[512,1024]{1,0:T(8,128)(2,1)}) custom-call(s32[1,4,16]{2,1,0:T(4,128)} %match_hbm.3, s32[3,128]{1,0:T(4,128)} %bitcast.6, bf16[8,128,128]{2,1,0:T(8,128)(2,1)} %copy-done.1), custom_call_target="tpu_custom_call" | custom-call | flops 5000000000 | bytes 4194304 | tf_op jit(solution)/shard_map/pallas_call | solution.py:462
  23.7 0.1 collective-permute-start.1
  23.8 0.5 collective-permute-start.2
  24.3 1.2 %collective-permute-done.1.refs_1_ = bf16[8,128,128]{2,1,0:T(8,128)(2,1)S(1)} collective-permute-done((bf16[8,128,128]{2,1,0:T(8,128)(2,1)}, bf16[8,128,128]{2,1,0:T(8,128)(2,1)S(1)}, u32[]{:S(2)}, u32[]{:S(2)}) %collective-permute-start.1) | collective-permute-done | bytes 262176 | tf_op jit(solution)/shard_map/ppermute | solution.py:400
  25.6 0.2 collective-permute-done.2.refs_2_
  25.7 0.5 copy-done.3
  26.3 0.7 %copy-done.4 = bf16[8,128,128]{2,1,0:T(8,128)(2,1)} copy-done((bf16[8,128,128]{2,1,0:T(8,128)(2,1)}, bf16[8,128,128]{2,1,0:T(8,128)(2,1)S(1)}, u32[]{:S(2)}) %copy-start.4) | copy-done | bytes 262168
  27.0 13.6 %shard_map.92 = (s16[144,128]{1,0:T(8,128)(2,1)}, s16[144,128]{1,0:T(8,128)(2,1)}, s16[144,128]{1,0:T(8,128)(2,1)}, s16[144,128]{1,0:T(8,128)(2,1)}, s16[144,128...) custom-call(s32[1,4,16]{2,1,0:T(4,128)} %match_hbm.3, ...), custom_call_target="tpu_custom_call" | custom-call | flops 4831838208 | bytes 8388608 | tf_op jit(solution)/shard_map/pallas_call | solution.py:499
  40.6 2.9 %collective-permute-start.3 = (s16[144,128]{1,0:T(8,128)(2,1)}, s16[144,128]{1,0:T(8,128)(2,1)S(1)}, u32[]{:S(2)}, u32[]{:S(2)}) collective-permute-start(s16[144,128]{1,0:T(8,128)(2,1)} %get-tuple-element.29), channel_id=1, source_target_pairs={{0,28},{4,24},{8,20},{12,16},{16,12},{20,8},{24,4},{28,0},{1,29},{... | collective-permute-start | bytes 110600 | tf_op jit(solution)/shard_map/ppermute | solution.py:542
  43.4 1.9 %collective-permute-start.4 = (s16[144,128]{1,0:T(8,128)(2,1)}, s16[144,128]{1,0:T(8,128)(2,1)S(1)}, u32[]{:S(2)}, u32[]{:S(2)}) collective-permute-start(s16[144,128]{1,0:T(8,128)(2,1)} %get-tuple-element.30), channel_id=1, source_target_pairs={{0,24},{4,28},{8,16},{12,20},{16,8},{20,12},{24,0},{28,4},{1,25},{... | collective-permute-start | bytes 110600 | tf_op jit(solution)/shard_map/ppermute | solution.py:542
  45.3 3.0 %collective-permute-start.6 = (s16[144,128]{1,0:T(8,128)(2,1)}, s16[144,128]{1,0:T(8,128)(2,1)S(1)}, u32[]{:S(2)}, u32[]{:S(2)}) collective-permute-start(s16[144,128]{1,0:T(8,128)(2,1)} %get-tuple-element.32), channel_id=1, source_target_pairs={{0,16},{4,20},{8,24},{12,28},{16,0},{20,4},{24,8},{28,12},{1,17},{... | collective-permute-start | bytes 110600 | tf_op jit(solution)/shard_map/ppermute | solution.py:542
  48.3 0.4 collective-permute-start.7
  48.7 0.0 collective-permute-done.3.refs_0_
  48.7 2.5 %collective-permute-start.8 = (s16[144,128]{1,0:T(8,128)(2,1)}, s16[144,128]{1,0:T(8,128)(2,1)S(1)}, u32[]{:S(2)}, u32[]{:S(2)}) collective-permute-start(s16[144,128]{1,0:T(8,128)(2,1)} %get-tuple-element.34), channel_id=1, source_target_pairs={{0,8},{4,12},{8,0},{12,4},{16,24},{20,28},{24,16},{28,20},{1,9},{5... | collective-permute-start | bytes 110600 | tf_op jit(solution)/shard_map/ppermute | solution.py:542
  51.2 0.6 %collective-permute-start.9 = (s16[144,128]{1,0:T(8,128)(2,1)}, s16[144,128]{1,0:T(8,128)(2,1)S(1)}, u32[]{:S(2)}, u32[]{:S(2)}) collective-permute-start(s16[144,128]{1,0:T(8,128)(2,1)} %get-tuple-element.35), channel_id=1, source_target_pairs={{0,4},{4,0},{8,12},{12,8},{16,20},{20,16},{24,28},{28,24},{1,5},{5... | collective-permute-start | bytes 110600 | tf_op jit(solution)/shard_map/ppermute | solution.py:542
  51.8 0.4 collective-permute-done.6.refs_3_
  52.2 1.2 %collective-permute-done.7.refs_4_ = s16[144,128]{1,0:T(8,128)(2,1)S(1)} collective-permute-done((s16[144,128]{1,0:T(8,128)(2,1)}, s16[144,128]{1,0:T(8,128)(2,1)S(1)}, u32[]{:S(2)}, u32[]{:S(2)}) %collective-permute-start.7) | collective-permute-done | bytes 36896 | tf_op jit(solution)/shard_map/ppermute | solution.py:542
  53.4 0.3 collective-permute-done.8.refs_5_
  53.7 1.6 %collective-permute-done.9.refs_6_ = s16[144,128]{1,0:T(8,128)(2,1)S(1)} collective-permute-done((s16[144,128]{1,0:T(8,128)(2,1)}, s16[144,128]{1,0:T(8,128)(2,1)S(1)}, u32[]{:S(2)}, u32[]{:S(2)}) %collective-permute-start.9) | collective-permute-done | bytes 36896 | tf_op jit(solution)/shard_map/ppermute | solution.py:542
  55.4 0.8 %copy-done = s16[144,128]{1,0:T(8,128)(2,1)S(1)} copy-done((s16[144,128]{1,0:T(8,128)(2,1)S(1)}, s16[144,128]{1,0:T(8,128)(2,1)}, u32[]{:S(2)}) %copy-start) | copy-done | bytes 36888
  56.1 2.2 %shard_map.93 = f32[1024,128]{1,0:T(8,128)} custom-call(s16[144,128]{1,0:T(8,128)(2,1)S(1)} %collective-permute-done.3.refs_0_, s16[144,128]{1,0:T(8,128)(2,1)S(1)} %collective-permute-done.4.refs_1_, s16[144,128]{1,0:T(8,128)(2,1)S(1)} %collective-permute-done.5.refs_2_, s16[144,128]{1,0:T(8,128)(2,1)S(1)} %collective-permute-done.6.refs_3_, ...), custom_call_target="tpu_custom_call" | custom-call | tf_op jit(solution)/shard_map/pallas_call | solution.py:442
  (11 shorter events, 0.0 us)
Async XLA Ops:
  17.1 1.5 %copy-start.1 = (bf16[8,128,128]{2,1,0:T(8,128)(2,1)}, bf16[8,128,128]{2,1,0:T(8,128)(2,1)S(1)}, u32[]{:S(2)}) copy-start(bf16[8,128,128]{2,1,0:T(8,128)(2,1)S(1)} %all_to_all.5.own_hbm) | copy-start | bytes 786436
  17.1 6.7 %collective-permute-start = (bf16[8,128,128]{2,1,0:T(8,128)(2,1)S(1)}, bf16[8,128,128]{2,1,0:T(8,128)(2,1)S(1)}, u32[]{:S(2)}, u32[]{:S(2)}) collective-permute-start(bf16[8,128,128]{2,1,0:T(8,128)(2,1)S(1)} %all_to_all.5.own_hbm), channel_id=1, source_target_pairs={{0,2},{1,3},{2,0},{3,1},{4,6},{5,7},{6,4},{7,5},{8,10},{9,11},{10,... | collective-permute-start | bytes 786440 | tf_op jit(solution)/shard_map/ppermute | solution.py:407
  23.7 1.8 %collective-permute-start.1 = (bf16[8,128,128]{2,1,0:T(8,128)(2,1)}, bf16[8,128,128]{2,1,0:T(8,128)(2,1)S(1)}, u32[]{:S(2)}, u32[]{:S(2)}) collective-permute-start(bf16[8,128,128]{2,1,0:T(8,128)(2,1)} %copy-done.1), channel_id=1, source_target_pairs={{0,1},{1,0},{2,3},{3,2},{4,5},{5,4},{6,7},{7,6},{8,9},{9,8},{10,11... | collective-permute-start | bytes 786440 | tf_op jit(solution)/shard_map/ppermute | solution.py:400
  23.8 1.9 %copy-start.2 = (bf16[8,128,128]{2,1,0:T(8,128)(2,1)}, bf16[8,128,128]{2,1,0:T(8,128)(2,1)S(1)}, u32[]{:S(2)}) copy-start(bf16[8,128,128]{2,1,0:T(8,128)(2,1)S(1)} %collective-permute-done.refs_0_) | copy-start | bytes 786436
  23.8 1.9 %collective-permute-start.2 = (bf16[8,128,128]{2,1,0:T(8,128)(2,1)S(1)}, bf16[8,128,128]{2,1,0:T(8,128)(2,1)S(1)}, u32[]{:S(2)}, u32[]{:S(2)}) collective-permute-start(bf16[8,128,128]{2,1,0:T(8,128)(2,1)S(1)} %collective-permute-done.refs_0_), channel_id=1, source_target_pairs={{0,1},{1,0},{2,3},{3,2},{4,5},{5,4},{6,7},{7,6},{8,9},{9,8},{10,11... | collective-permute-start | bytes 786440 | tf_op jit(solution)/shard_map/ppermute | solution.py:400
  25.6 0.7 %copy-start.3 = (bf16[8,128,128]{2,1,0:T(8,128)(2,1)}, bf16[8,128,128]{2,1,0:T(8,128)(2,1)S(1)}, u32[]{:S(2)}) copy-start(bf16[8,128,128]{2,1,0:T(8,128)(2,1)S(1)} %collective-permute-done.1.refs_1_) | copy-start | bytes 786436
  26.3 0.7 %copy-start.4 = (bf16[8,128,128]{2,1,0:T(8,128)(2,1)}, bf16[8,128,128]{2,1,0:T(8,128)(2,1)S(1)}, u32[]{:S(2)}) copy-start(bf16[8,128,128]{2,1,0:T(8,128)(2,1)S(1)} %collective-permute-done.2.refs_2_) | copy-start | bytes 786436
  40.6 8.1 %collective-permute-start.3 = (s16[144,128]{1,0:T(8,128)(2,1)}, s16[144,128]{1,0:T(8,128)(2,1)S(1)}, u32[]{:S(2)}, u32[]{:S(2)}) collective-permute-start(s16[144,128]{1,0:T(8,128)(2,1)} %get-tuple-element.29), channel_id=1, source_target_pairs={{0,28},{4,24},{8,20},{12,16},{16,12},{20,8},{24,4},{28,0},{1,29},{... | collective-permute-start | bytes 110600 | tf_op jit(solution)/shard_map/ppermute | solution.py:542
  43.4 7.8 %collective-permute-start.4 = (s16[144,128]{1,0:T(8,128)(2,1)}, s16[144,128]{1,0:T(8,128)(2,1)S(1)}, u32[]{:S(2)}, u32[]{:S(2)}) collective-permute-start(s16[144,128]{1,0:T(8,128)(2,1)} %get-tuple-element.30), channel_id=1, source_target_pairs={{0,24},{4,28},{8,16},{12,20},{16,8},{20,12},{24,0},{28,4},{1,25},{... | collective-permute-start | bytes 110600 | tf_op jit(solution)/shard_map/ppermute | solution.py:542
  45.3 6.5 %collective-permute-start.5 = (s16[144,128]{1,0:T(8,128)(2,1)}, s16[144,128]{1,0:T(8,128)(2,1)S(1)}, u32[]{:S(2)}, u32[]{:S(2)}) collective-permute-start(s16[144,128]{1,0:T(8,128)(2,1)} %get-tuple-element.31), channel_id=1, source_target_pairs={{0,20},{4,16},{8,28},{12,24},{16,4},{20,0},{24,12},{28,8},{1,21},{... | collective-permute-start | bytes 110600 | tf_op jit(solution)/shard_map/ppermute | solution.py:542
  45.3 6.9 %collective-permute-start.6 = (s16[144,128]{1,0:T(8,128)(2,1)}, s16[144,128]{1,0:T(8,128)(2,1)S(1)}, u32[]{:S(2)}, u32[]{:S(2)}) collective-permute-start(s16[144,128]{1,0:T(8,128)(2,1)} %get-tuple-element.32), channel_id=1, source_target_pairs={{0,16},{4,20},{8,24},{12,28},{16,0},{20,4},{24,8},{28,12},{1,17},{... | collective-permute-start | bytes 110600 | tf_op jit(solution)/shard_map/ppermute | solution.py:542
  48.3 5.2 %collective-permute-start.7 = (s16[144,128]{1,0:T(8,128)(2,1)}, s16[144,128]{1,0:T(8,128)(2,1)S(1)}, u32[]{:S(2)}, u32[]{:S(2)}) collective-permute-start(s16[144,128]{1,0:T(8,128)(2,1)} %get-tuple-element.33), channel_id=1, source_target_pairs={{0,12},{4,8},{8,4},{12,0},{16,28},{20,24},{24,20},{28,16},{1,13},{... | collective-permute-start | bytes 110600 | tf_op jit(solution)/shard_map/ppermute | solution.py:542
  48.7 5.0 %collective-permute-start.8 = (s16[144,128]{1,0:T(8,128)(2,1)}, s16[144,128]{1,0:T(8,128)(2,1)S(1)}, u32[]{:S(2)}, u32[]{:S(2)}) collective-permute-start(s16[144,128]{1,0:T(8,128)(2,1)} %get-tuple-element.34), channel_id=1, source_target_pairs={{0,8},{4,12},{8,0},{12,4},{16,24},{20,28},{24,16},{28,20},{1,9},{5... | collective-permute-start | bytes 110600 | tf_op jit(solution)/shard_map/ppermute | solution.py:542
  51.2 4.2 %collective-permute-start.9 = (s16[144,128]{1,0:T(8,128)(2,1)}, s16[144,128]{1,0:T(8,128)(2,1)S(1)}, u32[]{:S(2)}, u32[]{:S(2)}) collective-permute-start(s16[144,128]{1,0:T(8,128)(2,1)} %get-tuple-element.35), channel_id=1, source_target_pairs={{0,4},{4,0},{8,12},{12,8},{16,20},{20,16},{24,28},{28,24},{1,5},{5... | collective-permute-start | bytes 110600 | tf_op jit(solution)/shard_map/ppermute | solution.py:542
  55.4 0.8 %copy-start = (s16[144,128]{1,0:T(8,128)(2,1)S(1)}, s16[144,128]{1,0:T(8,128)(2,1)}, u32[]{:S(2)}) copy-start(s16[144,128]{1,0:T(8,128)(2,1)} %get-tuple-element.36.refs_7_) | copy-start | bytes 110596

commit v12 on v11

--- a/solution.py
+++ b/solution.py
@@ -126,7 +126,7 @@
                 fields[pl.ds(start, tiles, stride=pitch), :] = block[8 * half : 8 * half + 8, :]
         return carry
 
-    lax.fori_loop(0, slab_count, spread_slab, 0)
+    lax.fori_loop(0, slab_count, spread_slab, 0, unroll=4)
 
 
 def rolled(sizes, ref, box, row, rows, offset_x, offset_flat):
@@ -263,16 +263,12 @@
 
     def store_split(ref, start, count, columns, value):
         high, low = split_pair(value)
-        if isinstance(start, int):
-            ref[start : start + count, columns] = high
-            ref[row_count + start : row_count + start + count, columns] = low
-        else:
-            ref[pl.ds(pl.multiple_of(start, count), count), columns] = high
-            ref[pl.ds(pl.multiple_of(row_count + start, count), count), columns] = low
-
-    def densities(index, carry):
+        ref[start : start + count, columns] = high
+        ref[row_count + start : row_count + start + count, columns] = low
+
+    def densities(index):
         start = index * side
-        rows = pl.ds(pl.multiple_of(start, side), side)
+        rows = slice(start, start + side)
 
         def density(tile):
             columns = slice(tile * LANES, (tile + 1) * LANES)
@@ -284,9 +280,6 @@
             for parity, value in enumerate((near + far, near - far)):
                 column = parity * half_cells + tile * LANES
                 store_split(first, start, side, slice(column, column + LANES), value)
-        return carry
-
-    lax.fori_loop(0, solves, densities, 0, unroll=2)
 
     mix_copy, gain_copy, *matrix_copies = copies[boxes_count + 2 :]
     mix_copy.wait()
@@ -306,6 +299,8 @@
         return dot(left, jnp.concatenate([basis, basis, rest], axis=0))
 
     for start in range(0, row_count, group_rows):
+        for index in range(start // side, (start + group_rows) // side):
+            densities(index)
         columns = slice(0, cells)
         store_split(second, start, group_rows, columns, along_x(start, columns, first))
 
@@ -360,7 +355,7 @@
             total[pl.ds(pl.multiple_of(start, step_rows), step_rows), :] = sums[tile]
         return carry
 
-    lax.fori_loop(0, own_count * side // step_rows, collect, 0)
+    lax.fori_loop(0, own_count * side // step_rows, collect, 0, unroll=2)
 
     lane_index = lax.broadcasted_iota(jnp.int32, (tiles, LANES), 1)
     for step in range(slab_count):

time: 58.6 us -> 57.5 us (0.981)
  Pallas kernels: 21 us -> 19.9 us
    pallas_call x1, Pallas kernels: 13.6 us -> 12.8 us  [team_forces(): pl.pallas_call(functools.partial(force_kernel, sizes), out_shape=[jax.Sha...]
  transfers between devices with their start and end apart: 10 -> 10, of which waited for: 6 -> 5; matrix products, arithmetic and copies ran while one was open for 0% -> 0% of each run, Pallas kernels for 9% -> 9%
where the time goes in v12:
time: 57.5 us; the launch traced here: 57.3 us
  Pallas kernels  19.9 us (35%)
  blocking collectives  16 us (28%)
  starting transfers between devices  13.2 us (23%)
  waiting for transfers between devices  4.96 us (9%)
  local copies, waits for them, and re-layouts  3.1 us (5%)
    all_to_all x1, blocking collectives, shards(): lax.all_to_all(blocks, 'slab', split_axis=0, concat_axis=0, tiled=True)  16 us
    pallas_call x1, Pallas kernels, team_forces(): pl.pallas_call(functools.partial(force_kernel, sizes), out_shape=[jax.Sha...  12.8 us
    ppermute x7, starting transfers between devices, shards(): received.append(lax.ppermute(codes[step], 'slab', perm))  11.2 us
    pallas_call x1, Pallas kernels, place_own(): pl.pallas_call(functools.partial(own_kernel, sizes), out_shape=[jax.Shape...  4.93 us
    ppermute x7, waiting for transfers between devices, shards(): received.append(lax.ppermute(codes[step], 'slab', perm))  3.57 us
    pallas_call x1, Pallas kernels, unpack(): pl.pallas_call(functools.partial(unpack_kernel, (own_count, slab_count, t...  2.2 us
    unnamed x10, local copies, waits for them, and re-layouts  2.03 us
    ppermute x1, starting transfers between devices, gather_chips(): pieces.append(lax.ppermute(boxes, 'pair', perm))  1.49 us
  transfers between devices with their start and end apart: 10, of which 5 were waited for; matrix products, arithmetic and copies ran while one was open for 0% of the time, Pallas kernels for 9%

profile of v12, /device:TPU:0, one launch (start us, length us, event | category | flops | bytes accessed | tf_op | source)
XLA Modules:
  0.0 57.3 jit_solution(11880515770630750308)
XLA Ops:
  0.0 1.1 %reshape.9 = bf16[8,128,128]{2,1,0:T(8,128)(2,1)S(1)} reshape(bf16[32,4096]{1,0:T(8,128)(2,1)} %param.9) | data formatting | bytes 524288 | tf_op jit(solution)/shard_map/reshape | solution.py:524
  1.1 16.0 %all_to_all.5.own_hbm = bf16[8,128,128]{2,1,0:T(8,128)(2,1)S(1)} all-to-all(bf16[8,128,128]{2,1,0:T(8,128)(2,1)S(1)} %reshape.9), channel_id=1, replica_groups=mesh['slab'=8,'pair'=4] {'slab'}, dimensions={0} | all-to-all | bytes 524288 | tf_op jit(solution)/shard_map/all_to_all | solution.py:525
  17.1 1.5 %collective-permute-start = (bf16[8,128,128]{2,1,0:T(8,128)(2,1)S(1)}, bf16[8,128,128]{2,1,0:T(8,128)(2,1)S(1)}, u32[]{:S(2)}, u32[]{:S(2)}) collective-permute-start(bf16[8,128,128]{2,1,0:T(8,128)(2,1)S(1)} %all_to_all.5.own_hbm), channel_id=1, source_target_pairs={{0,2},{1,3},{2,0},{3,1},{4,6},{5,7},{6,4},{7,5},{8,10},{9,11},{10,... | collective-permute-start | bytes 786440 | tf_op jit(solution)/shard_map/ppermute | solution.py:402
  18.6 4.9 %shard_map.91 = (bf16[512,1024]{1,0:T(8,128)(2,1)}, bf16[512,1024]{1,0:T(8,128)(2,1)}) custom-call(s32[1,4,16]{2,1,0:T(4,128)} %match_hbm.3, s32[3,128]{1,0:T(4,128)} %bitcast.6, bf16[8,128,128]{2,1,0:T(8,128)(2,1)} %copy-done.1), custom_call_target="tpu_custom_call" | custom-call | flops 5000000000 | bytes 4194304 | tf_op jit(solution)/shard_map/pallas_call | solution.py:457
  23.5 0.1 collective-permute-start.1
  23.6 0.5 collective-permute-start.2
  24.1 1.2 %collective-permute-done.1.refs_1_ = bf16[8,128,128]{2,1,0:T(8,128)(2,1)S(1)} collective-permute-done((bf16[8,128,128]{2,1,0:T(8,128)(2,1)}, bf16[8,128,128]{2,1,0:T(8,128)(2,1)S(1)}, u32[]{:S(2)}, u32[]{:S(2)}) %collective-permute-start.1) | collective-permute-done | bytes 262176 | tf_op jit(solution)/shard_map/ppermute | solution.py:395
  25.3 0.2 collective-permute-done.2.refs_2_
  25.5 0.5 copy-done.3
  26.0 0.7 %copy-done.4 = bf16[8,128,128]{2,1,0:T(8,128)(2,1)} copy-done((bf16[8,128,128]{2,1,0:T(8,128)(2,1)}, bf16[8,128,128]{2,1,0:T(8,128)(2,1)S(1)}, u32[]{:S(2)}) %copy-start.4) | copy-done | bytes 262168
  26.7 12.8 %shard_map.92 = (s16[144,128]{1,0:T(8,128)(2,1)}, s16[144,128]{1,0:T(8,128)(2,1)}, s16[144,128]{1,0:T(8,128)(2,1)}, s16[144,128]{1,0:T(8,128)(2,1)}, s16[144,128...) custom-call(s32[1,4,16]{2,1,0:T(4,128)} %match_hbm.3, ...), custom_call_target="tpu_custom_call" | custom-call | flops 4831838208 | bytes 8388608 | tf_op jit(solution)/shard_map/pallas_call | solution.py:494
  39.5 2.8 %collective-permute-start.3 = (s16[144,128]{1,0:T(8,128)(2,1)}, s16[144,128]{1,0:T(8,128)(2,1)S(1)}, u32[]{:S(2)}, u32[]{:S(2)}) collective-permute-start(s16[144,128]{1,0:T(8,128)(2,1)} %get-tuple-element.29), channel_id=1, source_target_pairs={{0,28},{4,24},{8,20},{12,16},{16,12},{20,8},{24,4},{28,0},{1,29},{... | collective-permute-start | bytes 110600 | tf_op jit(solution)/shard_map/ppermute | solution.py:537
  42.4 1.9 %collective-permute-start.4 = (s16[144,128]{1,0:T(8,128)(2,1)}, s16[144,128]{1,0:T(8,128)(2,1)S(1)}, u32[]{:S(2)}, u32[]{:S(2)}) collective-permute-start(s16[144,128]{1,0:T(8,128)(2,1)} %get-tuple-element.30), channel_id=1, source_target_pairs={{0,24},{4,28},{8,16},{12,20},{16,8},{20,12},{24,0},{28,4},{1,25},{... | collective-permute-start | bytes 110600 | tf_op jit(solution)/shard_map/ppermute | solution.py:537
  44.3 3.0 %collective-permute-start.6 = (s16[144,128]{1,0:T(8,128)(2,1)}, s16[144,128]{1,0:T(8,128)(2,1)S(1)}, u32[]{:S(2)}, u32[]{:S(2)}) collective-permute-start(s16[144,128]{1,0:T(8,128)(2,1)} %get-tuple-element.32), channel_id=1, source_target_pairs={{0,16},{4,20},{8,24},{12,28},{16,0},{20,4},{24,8},{28,12},{1,17},{... | collective-permute-start | bytes 110600 | tf_op jit(solution)/shard_map/ppermute | solution.py:537
  47.2 0.4 collective-permute-start.7
  47.6 2.5 %collective-permute-start.8 = (s16[144,128]{1,0:T(8,128)(2,1)}, s16[144,128]{1,0:T(8,128)(2,1)S(1)}, u32[]{:S(2)}, u32[]{:S(2)}) collective-permute-start(s16[144,128]{1,0:T(8,128)(2,1)} %get-tuple-element.34), channel_id=1, source_target_pairs={{0,8},{4,12},{8,0},{12,4},{16,24},{20,28},{24,16},{28,20},{1,9},{5... | collective-permute-start | bytes 110600 | tf_op jit(solution)/shard_map/ppermute | solution.py:537
  50.1 0.6 %collective-permute-start.9 = (s16[144,128]{1,0:T(8,128)(2,1)}, s16[144,128]{1,0:T(8,128)(2,1)S(1)}, u32[]{:S(2)}, u32[]{:S(2)}) collective-permute-start(s16[144,128]{1,0:T(8,128)(2,1)} %get-tuple-element.35), channel_id=1, source_target_pairs={{0,4},{4,0},{8,12},{12,8},{16,20},{20,16},{24,28},{28,24},{1,5},{5... | collective-permute-start | bytes 110600 | tf_op jit(solution)/shard_map/ppermute | solution.py:537
  50.7 0.0 collective-permute-done.5.refs_2_
  50.7 0.0 collective-permute-done.6.refs_3_
  50.7 1.6 %collective-permute-done.7.refs_4_ = s16[144,128]{1,0:T(8,128)(2,1)S(1)} collective-permute-done((s16[144,128]{1,0:T(8,128)(2,1)}, s16[144,128]{1,0:T(8,128)(2,1)S(1)}, u32[]{:S(2)}, u32[]{:S(2)}) %collective-permute-start.7) | collective-permute-done | bytes 36896 | tf_op jit(solution)/shard_map/ppermute | solution.py:537
  52.3 0.4 collective-permute-done.8.refs_5_
  52.7 1.6 %collective-permute-done.9.refs_6_ = s16[144,128]{1,0:T(8,128)(2,1)S(1)} collective-permute-done((s16[144,128]{1,0:T(8,128)(2,1)}, s16[144,128]{1,0:T(8,128)(2,1)S(1)}, u32[]{:S(2)}, u32[]{:S(2)}) %collective-permute-start.9) | collective-permute-done | bytes 36896 | tf_op jit(solution)/shard_map/ppermute | solution.py:537
  54.3 0.8 %copy-done = s16[144,128]{1,0:T(8,128)(2,1)S(1)} copy-done((s16[144,128]{1,0:T(8,128)(2,1)S(1)}, s16[144,128]{1,0:T(8,128)(2,1)}, u32[]{:S(2)}) %copy-start) | copy-done | bytes 36888
  55.1 2.2 %shard_map.93 = f32[1024,128]{1,0:T(8,128)} custom-call(s16[144,128]{1,0:T(8,128)(2,1)S(1)} %collective-permute-done.3.refs_0_, s16[144,128]{1,0:T(8,128)(2,1)S(1)} %collective-permute-done.4.refs_1_, s16[144,128]{1,0:T(8,128)(2,1)S(1)} %collective-permute-done.5.refs_2_, s16[144,128]{1,0:T(8,128)(2,1)S(1)} %collective-permute-done.6.refs_3_, ...), custom_call_target="tpu_custom_call" | custom-call | tf_op jit(solution)/shard_map/pallas_call | solution.py:437
  (11 shorter events, 0.0 us)
Async XLA Ops:
  17.1 1.5 %copy-start.1 = (bf16[8,128,128]{2,1,0:T(8,128)(2,1)}, bf16[8,128,128]{2,1,0:T(8,128)(2,1)S(1)}, u32[]{:S(2)}) copy-start(bf16[8,128,128]{2,1,0:T(8,128)(2,1)S(1)} %all_to_all.5.own_hbm) | copy-start | bytes 786436
  17.1 6.5 %collective-permute-start = (bf16[8,128,128]{2,1,0:T(8,128)(2,1)S(1)}, bf16[8,128,128]{2,1,0:T(8,128)(2,1)S(1)}, u32[]{:S(2)}, u32[]{:S(2)}) collective-permute-start(bf16[8,128,128]{2,1,0:T(8,128)(2,1)S(1)} %all_to_all.5.own_hbm), channel_id=1, source_target_pairs={{0,2},{1,3},{2,0},{3,1},{4,6},{5,7},{6,4},{7,5},{8,10},{9,11},{10,... | collective-permute-start | bytes 786440 | tf_op jit(solution)/shard_map/ppermute | solution.py:402
  23.5 1.8 %collective-permute-start.1 = (bf16[8,128,128]{2,1,0:T(8,128)(2,1)}, bf16[8,128,128]{2,1,0:T(8,128)(2,1)S(1)}, u32[]{:S(2)}, u32[]{:S(2)}) collective-permute-start(bf16[8,128,128]{2,1,0:T(8,128)(2,1)} %copy-done.1), channel_id=1, source_target_pairs={{0,1},{1,0},{2,3},{3,2},{4,5},{5,4},{6,7},{7,6},{8,9},{9,8},{10,11... | collective-permute-start | bytes 786440 | tf_op jit(solution)/shard_map/ppermute | solution.py:395
  23.6 1.9 %copy-start.2 = (bf16[8,128,128]{2,1,0:T(8,128)(2,1)}, bf16[8,128,128]{2,1,0:T(8,128)(2,1)S(1)}, u32[]{:S(2)}) copy-start(bf16[8,128,128]{2,1,0:T(8,128)(2,1)S(1)} %collective-permute-done.refs_0_) | copy-start | bytes 786436
  23.6 1.9 %collective-permute-start.2 = (bf16[8,128,128]{2,1,0:T(8,128)(2,1)S(1)}, bf16[8,128,128]{2,1,0:T(8,128)(2,1)S(1)}, u32[]{:S(2)}, u32[]{:S(2)}) collective-permute-start(bf16[8,128,128]{2,1,0:T(8,128)(2,1)S(1)} %collective-permute-done.refs_0_), channel_id=1, source_target_pairs={{0,1},{1,0},{2,3},{3,2},{4,5},{5,4},{6,7},{7,6},{8,9},{9,8},{10,11... | collective-permute-start | bytes 786440 | tf_op jit(solution)/shard_map/ppermute | solution.py:395
  25.3 0.7 %copy-start.3 = (bf16[8,128,128]{2,1,0:T(8,128)(2,1)}, bf16[8,128,128]{2,1,0:T(8,128)(2,1)S(1)}, u32[]{:S(2)}) copy-start(bf16[8,128,128]{2,1,0:T(8,128)(2,1)S(1)} %collective-permute-done.1.refs_1_) | copy-start | bytes 786436
  26.0 0.7 %copy-start.4 = (bf16[8,128,128]{2,1,0:T(8,128)(2,1)}, bf16[8,128,128]{2,1,0:T(8,128)(2,1)S(1)}, u32[]{:S(2)}) copy-start(bf16[8,128,128]{2,1,0:T(8,128)(2,1)S(1)} %collective-permute-done.2.refs_2_) | copy-start | bytes 786436
  39.5 8.1 %collective-permute-start.3 = (s16[144,128]{1,0:T(8,128)(2,1)}, s16[144,128]{1,0:T(8,128)(2,1)S(1)}, u32[]{:S(2)}, u32[]{:S(2)}) collective-permute-start(s16[144,128]{1,0:T(8,128)(2,1)} %get-tuple-element.29), channel_id=1, source_target_pairs={{0,28},{4,24},{8,20},{12,16},{16,12},{20,8},{24,4},{28,0},{1,29},{... | collective-permute-start | bytes 110600 | tf_op jit(solution)/shard_map/ppermute | solution.py:537
  42.4 7.8 %collective-permute-start.4 = (s16[144,128]{1,0:T(8,128)(2,1)}, s16[144,128]{1,0:T(8,128)(2,1)S(1)}, u32[]{:S(2)}, u32[]{:S(2)}) collective-permute-start(s16[144,128]{1,0:T(8,128)(2,1)} %get-tuple-element.30), channel_id=1, source_target_pairs={{0,24},{4,28},{8,16},{12,20},{16,8},{20,12},{24,0},{28,4},{1,25},{... | collective-permute-start | bytes 110600 | tf_op jit(solution)/shard_map/ppermute | solution.py:537
  44.3 6.5 %collective-permute-start.5 = (s16[144,128]{1,0:T(8,128)(2,1)}, s16[144,128]{1,0:T(8,128)(2,1)S(1)}, u32[]{:S(2)}, u32[]{:S(2)}) collective-permute-start(s16[144,128]{1,0:T(8,128)(2,1)} %get-tuple-element.31), channel_id=1, source_target_pairs={{0,20},{4,16},{8,28},{12,24},{16,4},{20,0},{24,12},{28,8},{1,21},{... | collective-permute-start | bytes 110600 | tf_op jit(solution)/shard_map/ppermute | solution.py:537
  44.3 6.5 %collective-permute-start.6 = (s16[144,128]{1,0:T(8,128)(2,1)}, s16[144,128]{1,0:T(8,128)(2,1)S(1)}, u32[]{:S(2)}, u32[]{:S(2)}) collective-permute-start(s16[144,128]{1,0:T(8,128)(2,1)} %get-tuple-element.32), channel_id=1, source_target_pairs={{0,16},{4,20},{8,24},{12,28},{16,0},{20,4},{24,8},{28,12},{1,17},{... | collective-permute-start | bytes 110600 | tf_op jit(solution)/shard_map/ppermute | solution.py:537
  47.2 5.1 %collective-permute-start.7 = (s16[144,128]{1,0:T(8,128)(2,1)}, s16[144,128]{1,0:T(8,128)(2,1)S(1)}, u32[]{:S(2)}, u32[]{:S(2)}) collective-permute-start(s16[144,128]{1,0:T(8,128)(2,1)} %get-tuple-element.33), channel_id=1, source_target_pairs={{0,12},{4,8},{8,4},{12,0},{16,28},{20,24},{24,20},{28,16},{1,13},{... | collective-permute-start | bytes 110600 | tf_op jit(solution)/shard_map/ppermute | solution.py:537
  47.6 5.0 %collective-permute-start.8 = (s16[144,128]{1,0:T(8,128)(2,1)}, s16[144,128]{1,0:T(8,128)(2,1)S(1)}, u32[]{:S(2)}, u32[]{:S(2)}) collective-permute-start(s16[144,128]{1,0:T(8,128)(2,1)} %get-tuple-element.34), channel_id=1, source_target_pairs={{0,8},{4,12},{8,0},{12,4},{16,24},{20,28},{24,16},{28,20},{1,9},{5... | collective-permute-start | bytes 110600 | tf_op jit(solution)/shard_map/ppermute | solution.py:537
  50.1 4.2 %collective-permute-start.9 = (s16[144,128]{1,0:T(8,128)(2,1)}, s16[144,128]{1,0:T(8,128)(2,1)S(1)}, u32[]{:S(2)}, u32[]{:S(2)}) collective-permute-start(s16[144,128]{1,0:T(8,128)(2,1)} %get-tuple-element.35), channel_id=1, source_target_pairs={{0,4},{4,0},{8,12},{12,8},{16,20},{20,16},{24,28},{28,24},{1,5},{5... | collective-permute-start | bytes 110600 | tf_op jit(solution)/shard_map/ppermute | solution.py:537
  54.3 0.8 %copy-start = (s16[144,128]{1,0:T(8,128)(2,1)S(1)}, s16[144,128]{1,0:T(8,128)(2,1)}, u32[]{:S(2)}) copy-start(s16[144,128]{1,0:T(8,128)(2,1)} %get-tuple-element.36.refs_7_) | copy-start | bytes 110596

commit v13 on v12

--- a/solution.py
+++ b/solution.py
@@ -142,7 +142,7 @@
     return [jnp.where(keep, moved[t], moved[(t - 1) % tiles]) for t in range(tiles)]
 
 
-def place_partner(sizes, fields, box, own_offset, offset, active, out_ref, rows):
+def place_partner(sizes, fields, box, own_offset, offset, active):
     side = sizes[0]
     tiles, lines, _ = box_shape(sizes)
     placed = rolled(sizes, fields, box, 0, side, offset[0], offset[1] * side + offset[2])
@@ -150,10 +150,12 @@
     lows = [jnp.maximum(jnp.maximum(a, b), 0) for a, b in zip(own_offset, offset)]
     highs = [side + jnp.minimum(jnp.minimum(a, b), 0) for a, b in zip(own_offset, offset)]
     point_ok = (lane % side >= lows[2]) & (lane % side < highs[2]) & active
+    result = []
     for tile in range(tiles):
         line = lane // side + tile * lines
         ok = jnp.where(point_ok & (line >= lows[1]) & (line < highs[1]), 1.0, 0.0)
-        out_ref[rows, tile * LANES : (tile + 1) * LANES] = (placed[tile] * ok).astype(jnp.bfloat16)
+        result.append(placed[tile] * ok)
+    return result
 
 
 def own_kernel(
@@ -182,7 +184,9 @@
 
         @pl.when((local >= 0) & (local < own_count))
         def _():
-            place_partner(sizes, fields, local, a, b, active, partner_ref, rows)
+            placed = place_partner(sizes, fields, local, a, b, active)
+            for tile in range(tiles):
+                partner_ref[rows, tile * LANES : (tile + 1) * LANES] = placed[tile].astype(jnp.bfloat16)
 
         return carry
 
@@ -197,7 +201,7 @@
     match_ref, centers_ref, mine, partner, boxes_ref, *refs = refs
     constants, refs = refs[:6], refs[6:]
     mix_ref, gain_ref, there_high, there_low, back_high, back_low = constants
-    fields, first, second, terms, total, sems = refs
+    fields, first, second, *terms, total, sems = refs
     planes = side // slab_count
     tiles, lines, pitch = box_shape(sizes)
     solves = own_count * rounds
@@ -225,7 +229,8 @@
         copy.start()
     for pair in places:
         clear_edges(sizes, fields, pair * own_count, own_count)
-    clear_edges(sizes, terms, 0, solves)
+    for ref in terms:
+        clear_edges(sizes, ref, 0, group)
     boxes_count = 2 + len(places)
     for copy in copies[:boxes_count]:
         copy.wait()
@@ -233,19 +238,6 @@
         spread(sizes, boxes_ref, fields, pair)
     for copy in copies[boxes_count : boxes_count + 2]:
         copy.wait()
-
-    def place(index, carry):
-        _, mate, a, b, active = pair_geometry(sizes, match_ref, centers_ref, index)
-        local = mate - first_member
-
-        @pl.when((local < 0) | (local >= own_count))
-        def _():
-            rows = pl.ds(pl.multiple_of(index * side, side), side)
-            place_partner(sizes, fields, mate, a, b, active, partner, rows)
-
-        return carry
-
-    lax.fori_loop(0, solves, place, 0)
 
     row_count = solves * side
     half_tiles = tiles // 2
@@ -269,15 +261,18 @@
     def densities(index):
         start = index * side
         rows = slice(start, start + side)
-
-        def density(tile):
+        _, mate, a, b, active = pair_geometry(sizes, match_ref, centers_ref, index)
+        is_own = (mate >= first_member) & (mate < first_member + own_count)
+        placed = place_partner(sizes, fields, mate, a, b, active)
+        density = []
+        for tile in range(tiles):
             columns = slice(tile * LANES, (tile + 1) * LANES)
-            return mine[rows, columns].astype(jnp.float32) * partner[rows, columns].astype(jnp.float32)
-
+            chosen = jnp.where(is_own, partner[rows, columns].astype(jnp.float32), placed[tile])
+            partner[rows, columns] = chosen.astype(jnp.bfloat16)
+            density.append(mine[rows, columns].astype(jnp.float32) * chosen)
         for tile in range(half_tiles):
-            near = density(tile)
-            far = mirrored(density(tiles - 1 - tile))
-            for parity, value in enumerate((near + far, near - far)):
+            far = mirrored(density[tiles - 1 - tile])
+            for parity, value in enumerate((density[tile] + far, density[tile] - far)):
                 column = parity * half_cells + tile * LANES
                 store_split(first, start, side, slice(column, column + LANES), value)
 
@@ -336,26 +331,26 @@
                     columns = slice(place * LANES, (place + 1) * LANES)
                     value = value * partner[start : start + group_rows, columns].astype(jnp.float32)
                     for solve in range(group):
-                        row = ((start // side + solve) * tiles + place) * pitch + REACH
-                        terms[row : row + side, :] = value[solve * side : (solve + 1) * side, :]
+                        row = (solve * tiles + place) * pitch + REACH
+                        terms[start // group_rows][row : row + side, :] = value[solve * side : (solve + 1) * side, :]
 
     step_rows = 16
 
-    def collect(step, carry):
-        own = step // (side // step_rows)
-        row = step % (side // step_rows) * step_rows
+    def collect(own, row):
         sums = None
         for turn in range(rounds):
             index = own * rounds + turn
             _, _, a, _, _ = pair_geometry(sizes, match_ref, centers_ref, index)
-            term = rolled(sizes, terms, index, row, step_rows, -a[0], -(a[1] * side + a[2]))
+            ref = terms[index // group]
+            term = rolled(sizes, ref, index % group, row, step_rows, -a[0], -(a[1] * side + a[2]))
             sums = term if sums is None else [s + t for s, t in zip(sums, term)]
         for tile in range(tiles):
             start = (own * tiles + tile) * side + row
-            total[pl.ds(pl.multiple_of(start, step_rows), step_rows), :] = sums[tile]
-        return carry
-
-    lax.fori_loop(0, own_count * side // step_rows, collect, 0, unroll=2)
+            total[start : start + step_rows, :] = sums[tile]
+
+    for own in range(own_count):
+        for row in range(0, side, step_rows):
+            collect(own, row)
 
     lane_index = lax.broadcasted_iota(jnp.int32, (tiles, LANES), 1)
     for step in range(slab_count):
@@ -506,7 +501,7 @@
             pltpu.VMEM((own_count * pair_count * tiles * pitch, LANES), jnp.float32),
             wide,
             wide,
-            pltpu.VMEM((solves * tiles * pitch, LANES), jnp.float32),
+            *[pltpu.VMEM((group * tiles * pitch, LANES), jnp.float32)] * (solves // group),
             pltpu.VMEM((own_count * tiles * side, LANES), jnp.float32),
             pltpu.SemaphoreType.DMA((len(inputs),)),
         ],

time: 57.5 us -> 55.5 us (0.965)
  Pallas kernels: 19.9 us -> 17.8 us
    pallas_call x1, Pallas kernels: 12.8 us -> 10.8 us  [team_forces(): pl.pallas_call(functools.partial(force_kernel, sizes), out_shape=[jax.Sha...]
  transfers between devices with their start and end apart: 10 -> 10, of which waited for: 5 -> 7; matrix products, arithmetic and copies ran while one was open for 0% -> 0% of each run, Pallas kernels for 9% -> 9%
where the time goes in v13:
time: 55.5 us
  Pallas kernels  17.8 us (32%)
  blocking collectives  16 us (29%)
  starting transfers between devices  13.2 us (24%)
  waiting for transfers between devices  5.39 us (10%)
  local copies, waits for them, and re-layouts  3.1 us (6%)
    all_to_all x1, blocking collectives, shards(): lax.all_to_all(blocks, 'slab', split_axis=0, concat_axis=0, tiled=True)  16 us
    ppermute x7, starting transfers between devices, shards(): received.append(lax.ppermute(codes[step], 'slab', perm))  11.2 us
    pallas_call x1, Pallas kernels, team_forces(): pl.pallas_call(functools.partial(force_kernel, sizes), out_shape=[jax.Sha...  10.8 us
    pallas_call x1, Pallas kernels, place_own(): pl.pallas_call(functools.partial(own_kernel, sizes), out_shape=[jax.Shape...  4.73 us
    ppermute x7, waiting for transfers between devices, shards(): received.append(lax.ppermute(codes[step], 'slab', perm))  3.94 us
    pallas_call x1, Pallas kernels, unpack(): pl.pallas_call(functools.partial(unpack_kernel, (own_count, slab_count, t...  2.2 us
    unnamed x10, local copies, waits for them, and re-layouts  2.03 us
    ppermute x1, starting transfers between devices, gather_chips(): pieces.append(lax.ppermute(boxes, 'pair', perm))  1.49 us
  transfers between devices with their start and end apart: 10, of which 7 were waited for; matrix products, arithmetic and copies ran while one was open for 0% of the time, Pallas kernels for 9%

profile of v13, /device:TPU:0, one launch (start us, length us, event | category | flops | bytes accessed | tf_op | source)
XLA Modules:
  0.0 55.5 jit_solution(9840963220751804161)
XLA Ops:
  0.0 1.1 %reshape.9 = bf16[8,128,128]{2,1,0:T(8,128)(2,1)S(1)} reshape(bf16[32,4096]{1,0:T(8,128)(2,1)} %param.9) | data formatting | bytes 524288 | tf_op jit(solution)/shard_map/reshape | solution.py:519
  1.1 16.0 %all_to_all.5.own_hbm = bf16[8,128,128]{2,1,0:T(8,128)(2,1)S(1)} all-to-all(bf16[8,128,128]{2,1,0:T(8,128)(2,1)S(1)} %reshape.9), channel_id=1, replica_groups=mesh['slab'=8,'pair'=4] {'slab'}, dimensions={0} | all-to-all | bytes 524288 | tf_op jit(solution)/shard_map/all_to_all | solution.py:520
  17.1 1.5 %collective-permute-start = (bf16[8,128,128]{2,1,0:T(8,128)(2,1)S(1)}, bf16[8,128,128]{2,1,0:T(8,128)(2,1)S(1)}, u32[]{:S(2)}, u32[]{:S(2)}) collective-permute-start(bf16[8,128,128]{2,1,0:T(8,128)(2,1)S(1)} %all_to_all.5.own_hbm), channel_id=1, source_target_pairs={{0,2},{1,3},{2,0},{3,1},{4,6},{5,7},{6,4},{7,5},{8,10},{9,11},{10,... | collective-permute-start | bytes 786440 | tf_op jit(solution)/shard_map/ppermute | solution.py:397
  18.6 4.7 %shard_map.91 = (bf16[512,1024]{1,0:T(8,128)(2,1)}, bf16[512,1024]{1,0:T(8,128)(2,1)}) custom-call(s32[1,4,16]{2,1,0:T(4,128)} %match_hbm.3, s32[3,128]{1,0:T(4,128)} %bitcast.6, bf16[8,128,128]{2,1,0:T(8,128)(2,1)} %copy-done.1), custom_call_target="tpu_custom_call" | custom-call | flops 5000000000 | bytes 4194304 | tf_op jit(solution)/shard_map/pallas_call | solution.py:452
  23.3 0.1 collective-permute-start.1
  23.4 0.1 collective-permute-done.refs_0_
  23.4 0.4 collective-permute-start.2
  23.9 1.2 %collective-permute-done.1.refs_1_ = bf16[8,128,128]{2,1,0:T(8,128)(2,1)S(1)} collective-permute-done((bf16[8,128,128]{2,1,0:T(8,128)(2,1)}, bf16[8,128,128]{2,1,0:T(8,128)(2,1)S(1)}, u32[]{:S(2)}, u32[]{:S(2)}) %collective-permute-start.1) | collective-permute-done | bytes 262176 | tf_op jit(solution)/shard_map/ppermute | solution.py:390
  25.1 0.2 collective-permute-done.2.refs_2_
  25.3 0.5 copy-done.3
  25.8 0.7 %copy-done.4 = bf16[8,128,128]{2,1,0:T(8,128)(2,1)} copy-done((bf16[8,128,128]{2,1,0:T(8,128)(2,1)}, bf16[8,128,128]{2,1,0:T(8,128)(2,1)S(1)}, u32[]{:S(2)}) %copy-start.4) | copy-done | bytes 262168
  26.5 10.8 %shard_map.92 = (s16[144,128]{1,0:T(8,128)(2,1)}, s16[144,128]{1,0:T(8,128)(2,1)}, s16[144,128]{1,0:T(8,128)(2,1)}, s16[144,128]{1,0:T(8,128)(2,1)}, s16[144,128...) custom-call(s32[1,4,16]{2,1,0:T(4,128)} %match_hbm.3, ...), custom_call_target="tpu_custom_call" | custom-call | flops 4831838208 | bytes 8388608 | tf_op jit(solution)/shard_map/pallas_call | solution.py:489
  37.4 2.9 %collective-permute-start.3 = (s16[144,128]{1,0:T(8,128)(2,1)}, s16[144,128]{1,0:T(8,128)(2,1)S(1)}, u32[]{:S(2)}, u32[]{:S(2)}) collective-permute-start(s16[144,128]{1,0:T(8,128)(2,1)} %get-tuple-element.29), channel_id=1, source_target_pairs={{0,28},{4,24},{8,20},{12,16},{16,12},{20,8},{24,4},{28,0},{1,29},{... | collective-permute-start | bytes 110600 | tf_op jit(solution)/shard_map/ppermute | solution.py:532
  40.2 2.3 %collective-permute-start.4 = (s16[144,128]{1,0:T(8,128)(2,1)}, s16[144,128]{1,0:T(8,128)(2,1)S(1)}, u32[]{:S(2)}, u32[]{:S(2)}) collective-permute-start(s16[144,128]{1,0:T(8,128)(2,1)} %get-tuple-element.30), channel_id=1, source_target_pairs={{0,24},{4,28},{8,16},{12,20},{16,8},{20,12},{24,0},{28,4},{1,25},{... | collective-permute-start | bytes 110600 | tf_op jit(solution)/shard_map/ppermute | solution.py:532
  42.5 2.6 %collective-permute-start.6 = (s16[144,128]{1,0:T(8,128)(2,1)}, s16[144,128]{1,0:T(8,128)(2,1)S(1)}, u32[]{:S(2)}, u32[]{:S(2)}) collective-permute-start(s16[144,128]{1,0:T(8,128)(2,1)} %get-tuple-element.32), channel_id=1, source_target_pairs={{0,16},{4,20},{8,24},{12,28},{16,0},{20,4},{24,8},{28,12},{1,17},{... | collective-permute-start | bytes 110600 | tf_op jit(solution)/shard_map/ppermute | solution.py:532
  45.1 0.4 collective-permute-start.7
  45.5 2.8 %collective-permute-start.8 = (s16[144,128]{1,0:T(8,128)(2,1)}, s16[144,128]{1,0:T(8,128)(2,1)S(1)}, u32[]{:S(2)}, u32[]{:S(2)}) collective-permute-start(s16[144,128]{1,0:T(8,128)(2,1)} %get-tuple-element.34), channel_id=1, source_target_pairs={{0,8},{4,12},{8,0},{12,4},{16,24},{20,28},{24,16},{28,20},{1,9},{5... | collective-permute-start | bytes 110600 | tf_op jit(solution)/shard_map/ppermute | solution.py:532
  48.4 0.2 collective-permute-start.9
  48.6 0.3 collective-permute-done.5.refs_2_
  48.9 1.4 %collective-permute-done.7.refs_4_ = s16[144,128]{1,0:T(8,128)(2,1)S(1)} collective-permute-done((s16[144,128]{1,0:T(8,128)(2,1)}, s16[144,128]{1,0:T(8,128)(2,1)S(1)}, u32[]{:S(2)}, u32[]{:S(2)}) %collective-permute-start.7) | collective-permute-done | bytes 36896 | tf_op jit(solution)/shard_map/ppermute | solution.py:532
  50.3 0.6 %collective-permute-done.8.refs_5_ = s16[144,128]{1,0:T(8,128)(2,1)S(1)} collective-permute-done((s16[144,128]{1,0:T(8,128)(2,1)}, s16[144,128]{1,0:T(8,128)(2,1)S(1)}, u32[]{:S(2)}, u32[]{:S(2)}) %collective-permute-start.8) | collective-permute-done | bytes 36896 | tf_op jit(solution)/shard_map/ppermute | solution.py:532
  50.9 1.6 %collective-permute-done.9.refs_6_ = s16[144,128]{1,0:T(8,128)(2,1)S(1)} collective-permute-done((s16[144,128]{1,0:T(8,128)(2,1)}, s16[144,128]{1,0:T(8,128)(2,1)S(1)}, u32[]{:S(2)}, u32[]{:S(2)}) %collective-permute-start.9) | collective-permute-done | bytes 36896 | tf_op jit(solution)/shard_map/ppermute | solution.py:532
  52.5 0.8 %copy-done = s16[144,128]{1,0:T(8,128)(2,1)S(1)} copy-done((s16[144,128]{1,0:T(8,128)(2,1)S(1)}, s16[144,128]{1,0:T(8,128)(2,1)}, u32[]{:S(2)}) %copy-start) | copy-done | bytes 36888
  53.3 2.2 %shard_map.93 = f32[1024,128]{1,0:T(8,128)} custom-call(s16[144,128]{1,0:T(8,128)(2,1)S(1)} %collective-permute-done.3.refs_0_, s16[144,128]{1,0:T(8,128)(2,1)S(1)} %collective-permute-done.4.refs_1_, s16[144,128]{1,0:T(8,128)(2,1)S(1)} %collective-permute-done.5.refs_2_, s16[144,128]{1,0:T(8,128)(2,1)S(1)} %collective-permute-done.6.refs_3_, ...), custom_call_target="tpu_custom_call" | custom-call | tf_op jit(solution)/shard_map/pallas_call | solution.py:432
  (11 shorter events, 0.0 us)
Async XLA Ops:
  17.1 1.5 %copy-start.1 = (bf16[8,128,128]{2,1,0:T(8,128)(2,1)}, bf16[8,128,128]{2,1,0:T(8,128)(2,1)S(1)}, u32[]{:S(2)}) copy-start(bf16[8,128,128]{2,1,0:T(8,128)(2,1)S(1)} %all_to_all.5.own_hbm) | copy-start | bytes 786436
  17.1 6.4 %collective-permute-start = (bf16[8,128,128]{2,1,0:T(8,128)(2,1)S(1)}, bf16[8,128,128]{2,1,0:T(8,128)(2,1)S(1)}, u32[]{:S(2)}, u32[]{:S(2)}) collective-permute-start(bf16[8,128,128]{2,1,0:T(8,128)(2,1)S(1)} %all_to_all.5.own_hbm), channel_id=1, source_target_pairs={{0,2},{1,3},{2,0},{3,1},{4,6},{5,7},{6,4},{7,5},{8,10},{9,11},{10,... | collective-permute-start | bytes 786440 | tf_op jit(solution)/shard_map/ppermute | solution.py:397
  23.3 1.8 %collective-permute-start.1 = (bf16[8,128,128]{2,1,0:T(8,128)(2,1)}, bf16[8,128,128]{2,1,0:T(8,128)(2,1)S(1)}, u32[]{:S(2)}, u32[]{:S(2)}) collective-permute-start(bf16[8,128,128]{2,1,0:T(8,128)(2,1)} %copy-done.1), channel_id=1, source_target_pairs={{0,1},{1,0},{2,3},{3,2},{4,5},{5,4},{6,7},{7,6},{8,9},{9,8},{10,11... | collective-permute-start | bytes 786440 | tf_op jit(solution)/shard_map/ppermute | solution.py:390
  23.4 1.8 %copy-start.2 = (bf16[8,128,128]{2,1,0:T(8,128)(2,1)}, bf16[8,128,128]{2,1,0:T(8,128)(2,1)S(1)}, u32[]{:S(2)}) copy-start(bf16[8,128,128]{2,1,0:T(8,128)(2,1)S(1)} %collective-permute-done.refs_0_) | copy-start | bytes 786436
  23.4 1.8 %collective-permute-start.2 = (bf16[8,128,128]{2,1,0:T(8,128)(2,1)S(1)}, bf16[8,128,128]{2,1,0:T(8,128)(2,1)S(1)}, u32[]{:S(2)}, u32[]{:S(2)}) collective-permute-start(bf16[8,128,128]{2,1,0:T(8,128)(2,1)S(1)} %collective-permute-done.refs_0_), channel_id=1, source_target_pairs={{0,1},{1,0},{2,3},{3,2},{4,5},{5,4},{6,7},{7,6},{8,9},{9,8},{10,11... | collective-permute-start | bytes 786440 | tf_op jit(solution)/shard_map/ppermute | solution.py:390
  25.1 0.7 %copy-start.3 = (bf16[8,128,128]{2,1,0:T(8,128)(2,1)}, bf16[8,128,128]{2,1,0:T(8,128)(2,1)S(1)}, u32[]{:S(2)}) copy-start(bf16[8,128,128]{2,1,0:T(8,128)(2,1)S(1)} %collective-permute-done.1.refs_1_) | copy-start | bytes 786436
  25.8 0.7 %copy-start.4 = (bf16[8,128,128]{2,1,0:T(8,128)(2,1)}, bf16[8,128,128]{2,1,0:T(8,128)(2,1)S(1)}, u32[]{:S(2)}) copy-start(bf16[8,128,128]{2,1,0:T(8,128)(2,1)S(1)} %collective-permute-done.2.refs_2_) | copy-start | bytes 786436
  37.4 8.2 %collective-permute-start.3 = (s16[144,128]{1,0:T(8,128)(2,1)}, s16[144,128]{1,0:T(8,128)(2,1)S(1)}, u32[]{:S(2)}, u32[]{:S(2)}) collective-permute-start(s16[144,128]{1,0:T(8,128)(2,1)} %get-tuple-element.29), channel_id=1, source_target_pairs={{0,28},{4,24},{8,20},{12,16},{16,12},{20,8},{24,4},{28,0},{1,29},{... | collective-permute-start | bytes 110600 | tf_op jit(solution)/shard_map/ppermute | solution.py:532
  40.2 8.1 %collective-permute-start.4 = (s16[144,128]{1,0:T(8,128)(2,1)}, s16[144,128]{1,0:T(8,128)(2,1)S(1)}, u32[]{:S(2)}, u32[]{:S(2)}) collective-permute-start(s16[144,128]{1,0:T(8,128)(2,1)} %get-tuple-element.30), channel_id=1, source_target_pairs={{0,24},{4,28},{8,16},{12,20},{16,8},{20,12},{24,0},{28,4},{1,25},{... | collective-permute-start | bytes 110600 | tf_op jit(solution)/shard_map/ppermute | solution.py:532
  42.5 6.4 %collective-permute-start.5 = (s16[144,128]{1,0:T(8,128)(2,1)}, s16[144,128]{1,0:T(8,128)(2,1)S(1)}, u32[]{:S(2)}, u32[]{:S(2)}) collective-permute-start(s16[144,128]{1,0:T(8,128)(2,1)} %get-tuple-element.31), channel_id=1, source_target_pairs={{0,20},{4,16},{8,28},{12,24},{16,4},{20,0},{24,12},{28,8},{1,21},{... | collective-permute-start | bytes 110600 | tf_op jit(solution)/shard_map/ppermute | solution.py:532
  42.5 6.4 %collective-permute-start.6 = (s16[144,128]{1,0:T(8,128)(2,1)}, s16[144,128]{1,0:T(8,128)(2,1)S(1)}, u32[]{:S(2)}, u32[]{:S(2)}) collective-permute-start(s16[144,128]{1,0:T(8,128)(2,1)} %get-tuple-element.32), channel_id=1, source_target_pairs={{0,16},{4,20},{8,24},{12,28},{16,0},{20,4},{24,8},{28,12},{1,17},{... | collective-permute-start | bytes 110600 | tf_op jit(solution)/shard_map/ppermute | solution.py:532
  45.1 5.2 %collective-permute-start.7 = (s16[144,128]{1,0:T(8,128)(2,1)}, s16[144,128]{1,0:T(8,128)(2,1)S(1)}, u32[]{:S(2)}, u32[]{:S(2)}) collective-permute-start(s16[144,128]{1,0:T(8,128)(2,1)} %get-tuple-element.33), channel_id=1, source_target_pairs={{0,12},{4,8},{8,4},{12,0},{16,28},{20,24},{24,20},{28,16},{1,13},{... | collective-permute-start | bytes 110600 | tf_op jit(solution)/shard_map/ppermute | solution.py:532
  45.5 5.4 %collective-permute-start.8 = (s16[144,128]{1,0:T(8,128)(2,1)}, s16[144,128]{1,0:T(8,128)(2,1)S(1)}, u32[]{:S(2)}, u32[]{:S(2)}) collective-permute-start(s16[144,128]{1,0:T(8,128)(2,1)} %get-tuple-element.34), channel_id=1, source_target_pairs={{0,8},{4,12},{8,0},{12,4},{16,24},{20,28},{24,16},{28,20},{1,9},{5... | collective-permute-start | bytes 110600 | tf_op jit(solution)/shard_map/ppermute | solution.py:532
  48.4 4.2 %collective-permute-start.9 = (s16[144,128]{1,0:T(8,128)(2,1)}, s16[144,128]{1,0:T(8,128)(2,1)S(1)}, u32[]{:S(2)}, u32[]{:S(2)}) collective-permute-start(s16[144,128]{1,0:T(8,128)(2,1)} %get-tuple-element.35), channel_id=1, source_target_pairs={{0,4},{4,0},{8,12},{12,8},{16,20},{20,16},{24,28},{28,24},{1,5},{5... | collective-permute-start | bytes 110600 | tf_op jit(solution)/shard_map/ppermute | solution.py:532
  52.5 0.8 %copy-start = (s16[144,128]{1,0:T(8,128)(2,1)S(1)}, s16[144,128]{1,0:T(8,128)(2,1)}, u32[]{:S(2)}) copy-start(s16[144,128]{1,0:T(8,128)(2,1)} %get-tuple-element.36.refs_7_) | copy-start | bytes 110596

commit v14 on v13

--- a/solution.py
+++ b/solution.py
@@ -112,21 +112,36 @@
     lax.fori_loop(0, count * tiles, clear, 0, unroll=8)
 
 
+def turned(tiles):
+    row = lax.broadcasted_iota(jnp.int32, (8, LANES), 0)
+    tiles = list(tiles)
+    for distance in (4, 2, 1):
+        low = (row & distance) == 0
+        for index in range(8):
+            if index & distance == 0:
+                first, second = tiles[index], tiles[index + distance]
+                tiles[index] = jnp.where(low, first, pltpu.roll(second, distance, axis=0))
+                tiles[index + distance] = jnp.where(low, pltpu.roll(first, 8 - distance, axis=0), second)
+    return tiles
+
+
 def spread(sizes, boxes_ref, fields, pair):
     side, _, own_count, slab_count, _ = sizes
     planes = side // slab_count
     tiles, _, pitch = box_shape(sizes)
-
-    def spread_slab(slab, carry):
-        for chunk in range(own_count * planes // 2):
-            block = boxes_ref[pair, slab, 16 * chunk : 16 * chunk + 16, :].astype(jnp.float32)
-            for half in range(2):
-                own, plane = divmod(2 * chunk + half, planes)
-                start = (pair * own_count + own) * tiles * pitch + REACH + slab * planes + plane
-                fields[pl.ds(start, tiles, stride=pitch), :] = block[8 * half : 8 * half + 8, :]
-        return carry
-
-    lax.fori_loop(0, slab_count, spread_slab, 0, unroll=4)
+    for group in range(side // 8):
+        halves = {}
+        for slab in range(8 * group // planes, (8 * group + 7) // planes + 1):
+            for chunk in range(own_count * planes // 2):
+                block = boxes_ref[pair, slab, 16 * chunk : 16 * chunk + 16, :].astype(jnp.float32)
+                for half in range(2):
+                    own, plane = divmod(2 * chunk + half, planes)
+                    halves[own, slab * planes + plane] = block[8 * half : 8 * half + 8, :]
+        for own in range(own_count):
+            rows = turned([halves[own, 8 * group + index] for index in range(8)])
+            for tile in range(tiles):
+                start = ((pair * own_count + own) * tiles + tile) * pitch + REACH + 8 * group
+                fields[pl.ds(pl.multiple_of(start, 8), 8), :] = rows[tile]
 
 
 def rolled(sizes, ref, box, row, rows, offset_x, offset_flat):
@@ -201,7 +216,7 @@
     match_ref, centers_ref, mine, partner, boxes_ref, *refs = refs
     constants, refs = refs[:6], refs[6:]
     mix_ref, gain_ref, there_high, there_low, back_high, back_low = constants
-    fields, first, second, *terms, total, sems = refs
+    fields, first, second, *terms, all_codes, sems = refs
     planes = side // slab_count
     tiles, lines, pitch = box_shape(sizes)
     solves = own_count * rounds
@@ -344,33 +359,30 @@
             ref = terms[index // group]
             term = rolled(sizes, ref, index % group, row, step_rows, -a[0], -(a[1] * side + a[2]))
             sums = term if sums is None else [s + t for s, t in zip(sums, term)]
-        for tile in range(tiles):
-            start = (own * tiles + tile) * side + row
-            total[start : start + step_rows, :] = sums[tile]
-
+        return sums
+
+    lane_index = lax.broadcasted_iota(jnp.int32, (tiles, LANES), 1)
+    exponents = [jnp.zeros((tiles, LANES), jnp.float32)] * slab_count
+    factors = [jnp.zeros((tiles, LANES), jnp.float32)] * slab_count
+    codes = {}
     for own in range(own_count):
         for row in range(0, side, step_rows):
-            collect(own, row)
-
-    lane_index = lax.broadcasted_iota(jnp.int32, (tiles, LANES), 1)
+            sums = collect(own, row)
+            for half in range(0, step_rows, 8):
+                for index, value in enumerate(turned([tile[half : half + 8, :] for tile in sums])):
+                    slab, plane = divmod(row + half + index, planes)
+                    chunk = own * planes + plane
+                    codes[slab, chunk], exponent, factor = encode(value)
+                    exponents[slab] = jnp.where(lane_index == chunk, exponent, exponents[slab])
+                    factors[slab] = jnp.where(lane_index == chunk, factor, factors[slab])
+                    if chunk % 2:
+                        pair = jnp.concatenate([codes[slab, chunk - 1], codes[slab, chunk]], axis=0)
+                        all_codes[slab, tiles * (chunk - 1) : tiles * (chunk + 1), :] = whole_codes(pair)
+    for slab in range(slab_count):
+        header = jnp.concatenate([exponents[slab], factors[slab]], axis=0)
+        all_codes[slab, tiles * own_count * planes :, :] = whole_codes(header)
     for step in range(slab_count):
-        slab = partner_of(slab_index, step, slab_count)[0]
-        exponents = jnp.zeros((tiles, LANES), jnp.float32)
-        factors = jnp.zeros((tiles, LANES), jnp.float32)
-        codes = []
-        for chunk in range(own_count * planes):
-            own, plane = divmod(chunk, planes)
-            start = own * tiles * side + slab * planes + plane
-            value = total[pl.ds(start, tiles, stride=side), :]
-            code, exponent, factor = encode(value)
-            codes.append(code)
-            exponents = jnp.where(lane_index == chunk, exponent, exponents)
-            factors = jnp.where(lane_index == chunk, factor, factors)
-            if chunk % 2:
-                pair = jnp.concatenate(codes[-2:], axis=0)
-                out_refs[step][tiles * (chunk - 1) : tiles * (chunk + 1), :] = whole_codes(pair)
-        header = jnp.concatenate([exponents, factors], axis=0)
-        out_refs[step][tiles * own_count * planes :, :] = whole_codes(header)
+        out_refs[step][...] = all_codes[partner_of(slab_index, step, slab_count)[0]]
 
 
 def whole_codes(value):
@@ -404,25 +416,31 @@
     slab_index = lax.axis_index("slab")
     copies = []
     for index in range(slab_count):
-        copies.append(pltpu.make_async_copy(block_refs[index], blocks.at[index], sems.at[index]))
+        slab = partner_of(slab_index, slab_count - 1 - index, slab_count)[1]
+        copies.append(pltpu.make_async_copy(block_refs[index], blocks.at[slab], sems.at[index]))
         copies[-1].start()
-    for index in reversed(range(slab_count)):
-        step = slab_count - 1 - index
-        copies[index].wait()
-        first = partner_of(slab_index, step, slab_count)[1] * own_count
-        row_count = own_count * tiles
-        header = blocks[index, row_count:, :].astype(jnp.int32).astype(jnp.float32)
+    for copy in copies:
+        copy.wait()
+    row_count = own_count * tiles
+    values = {}
+    for slab in range(slab_count):
+        header = blocks[slab, row_count:, :].astype(jnp.int32).astype(jnp.float32)
         units = jnp.exp2(header[:8, :])
         factors = header[8:, :] * (1.0 / (CODE_LIMIT * FACTOR_UNIT))
         for pair in range(row_count // 16):
-            codes = blocks[index, 16 * pair : 16 * pair + 16, :].astype(jnp.int32).astype(jnp.float32)
+            codes = blocks[slab, 16 * pair : 16 * pair + 16, :].astype(jnp.int32).astype(jnp.float32)
             for half in range(2):
                 chunk = 2 * pair + half
-                own, tile = divmod(8 * chunk, tiles)
-                row = first + own
-                start = (row // 8 * tiles + tile) * 8 + row % 8
+                own, plane = divmod(8 * chunk, tiles)
                 value = codes[8 * half : 8 * half + 8, :] * factors[:, chunk : chunk + 1]
-                out_ref[pl.ds(start, 8, stride=8), :] = value * units[:, chunk : chunk + 1]
+                values[slab * own_count + own, plane // 8] = value * units[:, chunk : chunk + 1]
+        if (slab + 1) * own_count % 8 == 0:
+            band = (slab + 1) * own_count // 8 - 1
+            for plane in range(tiles // 8):
+                rows = turned([values[8 * band + index, plane] for index in range(8)])
+                for tile in range(8):
+                    start = (band * tiles + 8 * plane + tile) * 8
+                    out_ref[start : start + 8, :] = rows[tile]
 
 
 def unpack(blocks, own_count, cells):
@@ -502,7 +520,7 @@
             wide,
             wide,
             *[pltpu.VMEM((group * tiles * pitch, LANES), jnp.float32)] * (solves // group),
-            pltpu.VMEM((own_count * tiles * side, LANES), jnp.float32),
+            pltpu.VMEM((slab_count, rows + HEADER_ROWS, LANES), jnp.int16),
             pltpu.SemaphoreType.DMA((len(inputs),)),
         ],
         compiler_params=pltpu.CompilerParams(vmem_limit_bytes=60 * 1024 * 1024),

time: 55.5 us -> 54.9 us (0.989)
  waiting for transfers between devices: 5.39 us -> 4.37 us
    ppermute x7, waiting for transfers between devices: 3.94 us -> 2.97 us  [shards(): received.append(lax.ppermute(codes[step], 'slab', perm))]
  transfers between devices with their start and end apart: 10 -> 10, of which waited for: 7 -> 4; matrix products, arithmetic and copies ran while one was open for 0% -> 0% of each run, Pallas kernels for 9% -> 9%
where the time goes in v14:
time: 54.9 us; the launch traced here: 54.4 us
  Pallas kernels  17.6 us (32%)
  blocking collectives  16 us (29%)
  starting transfers between devices  13.2 us (24%)
  waiting for transfers between devices  4.37 us (8%)
  local copies, waits for them, and re-layouts  3.1 us (6%)
    all_to_all x1, blocking collectives, shards(): lax.all_to_all(blocks, 'slab', split_axis=0, concat_axis=0, tiled=True)  16 us
    ppermute x7, starting transfers between devices, shards(): received.append(lax.ppermute(codes[step], 'slab', perm))  11.2 us
    pallas_call x1, Pallas kernels, team_forces(): pl.pallas_call(functools.partial(force_kernel, sizes), out_shape=[jax.Sha...  10.8 us
    pallas_call x1, Pallas kernels, place_own(): pl.pallas_call(functools.partial(own_kernel, sizes), out_shape=[jax.Shape...  5.1 us
    ppermute x7, waiting for transfers between devices, shards(): received.append(lax.ppermute(codes[step], 'slab', perm))  2.97 us
    unnamed x10, local copies, waits for them, and re-layouts  2.03 us
    pallas_call x1, Pallas kernels, unpack(): pl.pallas_call(functools.partial(unpack_kernel, (own_count, slab_count, t...  1.74 us
    ppermute x1, starting transfers between devices, gather_chips(): pieces.append(lax.ppermute(boxes, 'pair', perm))  1.49 us
  transfers between devices with their start and end apart: 10, of which 4 were waited for; matrix products, arithmetic and copies ran while one was open for 0% of the time, Pallas kernels for 9%

profile of v14, /device:TPU:0, one launch (start us, length us, event | category | flops | bytes accessed | tf_op | source)
XLA Modules:
  0.0 54.4 jit_solution(2538495228903625390)
XLA Ops:
  0.0 1.1 %reshape.9 = bf16[8,128,128]{2,1,0:T(8,128)(2,1)S(1)} reshape(bf16[32,4096]{1,0:T(8,128)(2,1)} %param.9) | data formatting | bytes 524288 | tf_op jit(solution)/shard_map/reshape | solution.py:537
  1.1 16.0 %all_to_all.5.own_hbm = bf16[8,128,128]{2,1,0:T(8,128)(2,1)S(1)} all-to-all(bf16[8,128,128]{2,1,0:T(8,128)(2,1)S(1)} %reshape.9), channel_id=1, replica_groups=mesh['slab'=8,'pair'=4] {'slab'}, dimensions={0} | all-to-all | bytes 524288 | tf_op jit(solution)/shard_map/all_to_all | solution.py:538
  17.1 1.5 %collective-permute-start = (bf16[8,128,128]{2,1,0:T(8,128)(2,1)S(1)}, bf16[8,128,128]{2,1,0:T(8,128)(2,1)S(1)}, u32[]{:S(2)}, u32[]{:S(2)}) collective-permute-start(bf16[8,128,128]{2,1,0:T(8,128)(2,1)S(1)} %all_to_all.5.own_hbm), channel_id=1, source_target_pairs={{0,2},{1,3},{2,0},{3,1},{4,6},{5,7},{6,4},{7,5},{8,10},{9,11},{10,... | collective-permute-start | bytes 786440 | tf_op jit(solution)/shard_map/ppermute | solution.py:409
  18.6 5.1 %shard_map.91 = (bf16[512,1024]{1,0:T(8,128)(2,1)}, bf16[512,1024]{1,0:T(8,128)(2,1)}) custom-call(s32[1,4,16]{2,1,0:T(4,128)} %match_hbm.3, s32[3,128]{1,0:T(4,128)} %bitcast.6, bf16[8,128,128]{2,1,0:T(8,128)(2,1)} %copy-done.1), custom_call_target="tpu_custom_call" | custom-call | flops 5000000000 | bytes 4194304 | tf_op jit(solution)/shard_map/pallas_call | solution.py:470
  23.7 0.1 collective-permute-start.1
  23.8 0.0 collective-permute-done.refs_0_
  23.8 0.5 collective-permute-start.2
  24.3 1.2 %collective-permute-done.1.refs_1_ = bf16[8,128,128]{2,1,0:T(8,128)(2,1)S(1)} collective-permute-done((bf16[8,128,128]{2,1,0:T(8,128)(2,1)}, bf16[8,128,128]{2,1,0:T(8,128)(2,1)S(1)}, u32[]{:S(2)}, u32[]{:S(2)}) %collective-permute-start.1) | collective-permute-done | bytes 262176 | tf_op jit(solution)/shard_map/ppermute | solution.py:402
  25.5 0.2 collective-permute-done.2.refs_2_
  25.7 0.5 copy-done.3
  26.2 0.7 %copy-done.4 = bf16[8,128,128]{2,1,0:T(8,128)(2,1)} copy-done((bf16[8,128,128]{2,1,0:T(8,128)(2,1)}, bf16[8,128,128]{2,1,0:T(8,128)(2,1)S(1)}, u32[]{:S(2)}) %copy-start.4) | copy-done | bytes 262168
  26.9 10.8 %shard_map.92 = (s16[144,128]{1,0:T(8,128)(2,1)}, s16[144,128]{1,0:T(8,128)(2,1)}, s16[144,128]{1,0:T(8,128)(2,1)}, s16[144,128]{1,0:T(8,128)(2,1)}, s16[144,128...) custom-call(s32[1,4,16]{2,1,0:T(4,128)} %match_hbm.3, ...), custom_call_target="tpu_custom_call" | custom-call | flops 4831838208 | bytes 8388608 | tf_op jit(solution)/shard_map/pallas_call | solution.py:507
  37.7 2.5 %collective-permute-start.3 = (s16[144,128]{1,0:T(8,128)(2,1)}, s16[144,128]{1,0:T(8,128)(2,1)S(1)}, u32[]{:S(2)}, u32[]{:S(2)}) collective-permute-start(s16[144,128]{1,0:T(8,128)(2,1)} %get-tuple-element.29), channel_id=1, source_target_pairs={{0,28},{4,24},{8,20},{12,16},{16,12},{20,8},{24,4},{28,0},{1,29},{... | collective-permute-start | bytes 110600 | tf_op jit(solution)/shard_map/ppermute | solution.py:550
  40.2 1.6 %collective-permute-start.4 = (s16[144,128]{1,0:T(8,128)(2,1)}, s16[144,128]{1,0:T(8,128)(2,1)S(1)}, u32[]{:S(2)}, u32[]{:S(2)}) collective-permute-start(s16[144,128]{1,0:T(8,128)(2,1)} %get-tuple-element.30), channel_id=1, source_target_pairs={{0,24},{4,28},{8,16},{12,20},{16,8},{20,12},{24,0},{28,4},{1,25},{... | collective-permute-start | bytes 110600 | tf_op jit(solution)/shard_map/ppermute | solution.py:550
  41.8 3.6 %collective-permute-start.6 = (s16[144,128]{1,0:T(8,128)(2,1)}, s16[144,128]{1,0:T(8,128)(2,1)S(1)}, u32[]{:S(2)}, u32[]{:S(2)}) collective-permute-start(s16[144,128]{1,0:T(8,128)(2,1)} %get-tuple-element.32), channel_id=1, source_target_pairs={{0,16},{4,20},{8,24},{12,28},{16,0},{20,4},{24,8},{28,12},{1,17},{... | collective-permute-start | bytes 110600 | tf_op jit(solution)/shard_map/ppermute | solution.py:550
  45.4 0.1 collective-permute-start.7
  45.5 0.0 collective-permute-done.3.refs_0_
  45.5 2.2 %collective-permute-start.8 = (s16[144,128]{1,0:T(8,128)(2,1)}, s16[144,128]{1,0:T(8,128)(2,1)S(1)}, u32[]{:S(2)}, u32[]{:S(2)}) collective-permute-start(s16[144,128]{1,0:T(8,128)(2,1)} %get-tuple-element.34), channel_id=1, source_target_pairs={{0,8},{4,12},{8,0},{12,4},{16,24},{20,28},{24,16},{28,20},{1,9},{5... | collective-permute-start | bytes 110600 | tf_op jit(solution)/shard_map/ppermute | solution.py:550
  47.7 1.2 %collective-permute-start.9 = (s16[144,128]{1,0:T(8,128)(2,1)}, s16[144,128]{1,0:T(8,128)(2,1)S(1)}, u32[]{:S(2)}, u32[]{:S(2)}) collective-permute-start(s16[144,128]{1,0:T(8,128)(2,1)} %get-tuple-element.35), channel_id=1, source_target_pairs={{0,4},{4,0},{8,12},{12,8},{16,20},{20,16},{24,28},{28,24},{1,5},{5... | collective-permute-start | bytes 110600 | tf_op jit(solution)/shard_map/ppermute | solution.py:550
  48.9 0.0 collective-permute-done.6.refs_3_
  48.9 1.5 %collective-permute-done.7.refs_4_ = s16[144,128]{1,0:T(8,128)(2,1)S(1)} collective-permute-done((s16[144,128]{1,0:T(8,128)(2,1)}, s16[144,128]{1,0:T(8,128)(2,1)S(1)}, u32[]{:S(2)}, u32[]{:S(2)}) %collective-permute-start.7) | collective-permute-done | bytes 36896 | tf_op jit(solution)/shard_map/ppermute | solution.py:550
  50.5 1.4 %collective-permute-done.9.refs_6_ = s16[144,128]{1,0:T(8,128)(2,1)S(1)} collective-permute-done((s16[144,128]{1,0:T(8,128)(2,1)}, s16[144,128]{1,0:T(8,128)(2,1)S(1)}, u32[]{:S(2)}, u32[]{:S(2)}) %collective-permute-start.9) | collective-permute-done | bytes 36896 | tf_op jit(solution)/shard_map/ppermute | solution.py:550
  51.8 0.8 %copy-done = s16[144,128]{1,0:T(8,128)(2,1)S(1)} copy-done((s16[144,128]{1,0:T(8,128)(2,1)S(1)}, s16[144,128]{1,0:T(8,128)(2,1)}, u32[]{:S(2)}) %copy-start) | copy-done | bytes 36888
  52.6 1.7 %shard_map.93 = f32[1024,128]{1,0:T(8,128)} custom-call(s16[144,128]{1,0:T(8,128)(2,1)S(1)} %collective-permute-done.3.refs_0_, s16[144,128]{1,0:T(8,128)(2,1)S(1)} %collective-permute-done.4.refs_1_, s16[144,128]{1,0:T(8,128)(2,1)S(1)} %collective-permute-done.5.refs_2_, s16[144,128]{1,0:T(8,128)(2,1)S(1)} %collective-permute-done.6.refs_3_, ...), custom_call_target="tpu_custom_call" | custom-call | tf_op jit(solution)/shard_map/pallas_call | solution.py:450
  (11 shorter events, 0.0 us)
Async XLA Ops:
  17.1 1.5 %copy-start.1 = (bf16[8,128,128]{2,1,0:T(8,128)(2,1)}, bf16[8,128,128]{2,1,0:T(8,128)(2,1)S(1)}, u32[]{:S(2)}) copy-start(bf16[8,128,128]{2,1,0:T(8,128)(2,1)S(1)} %all_to_all.5.own_hbm) | copy-start | bytes 786436
  17.1 6.7 %collective-permute-start = (bf16[8,128,128]{2,1,0:T(8,128)(2,1)S(1)}, bf16[8,128,128]{2,1,0:T(8,128)(2,1)S(1)}, u32[]{:S(2)}, u32[]{:S(2)}) collective-permute-start(bf16[8,128,128]{2,1,0:T(8,128)(2,1)S(1)} %all_to_all.5.own_hbm), channel_id=1, source_target_pairs={{0,2},{1,3},{2,0},{3,1},{4,6},{5,7},{6,4},{7,5},{8,10},{9,11},{10,... | collective-permute-start | bytes 786440 | tf_op jit(solution)/shard_map/ppermute | solution.py:409
  23.7 1.8 %collective-permute-start.1 = (bf16[8,128,128]{2,1,0:T(8,128)(2,1)}, bf16[8,128,128]{2,1,0:T(8,128)(2,1)S(1)}, u32[]{:S(2)}, u32[]{:S(2)}) collective-permute-start(bf16[8,128,128]{2,1,0:T(8,128)(2,1)} %copy-done.1), channel_id=1, source_target_pairs={{0,1},{1,0},{2,3},{3,2},{4,5},{5,4},{6,7},{7,6},{8,9},{9,8},{10,11... | collective-permute-start | bytes 786440 | tf_op jit(solution)/shard_map/ppermute | solution.py:402
  23.8 1.9 %copy-start.2 = (bf16[8,128,128]{2,1,0:T(8,128)(2,1)}, bf16[8,128,128]{2,1,0:T(8,128)(2,1)S(1)}, u32[]{:S(2)}) copy-start(bf16[8,128,128]{2,1,0:T(8,128)(2,1)S(1)} %collective-permute-done.refs_0_) | copy-start | bytes 786436
  23.8 1.9 %collective-permute-start.2 = (bf16[8,128,128]{2,1,0:T(8,128)(2,1)S(1)}, bf16[8,128,128]{2,1,0:T(8,128)(2,1)S(1)}, u32[]{:S(2)}, u32[]{:S(2)}) collective-permute-start(bf16[8,128,128]{2,1,0:T(8,128)(2,1)S(1)} %collective-permute-done.refs_0_), channel_id=1, source_target_pairs={{0,1},{1,0},{2,3},{3,2},{4,5},{5,4},{6,7},{7,6},{8,9},{9,8},{10,11... | collective-permute-start | bytes 786440 | tf_op jit(solution)/shard_map/ppermute | solution.py:402
  25.5 0.7 %copy-start.3 = (bf16[8,128,128]{2,1,0:T(8,128)(2,1)}, bf16[8,128,128]{2,1,0:T(8,128)(2,1)S(1)}, u32[]{:S(2)}) copy-start(bf16[8,128,128]{2,1,0:T(8,128)(2,1)S(1)} %collective-permute-done.1.refs_1_) | copy-start | bytes 786436
  26.2 0.7 %copy-start.4 = (bf16[8,128,128]{2,1,0:T(8,128)(2,1)}, bf16[8,128,128]{2,1,0:T(8,128)(2,1)S(1)}, u32[]{:S(2)}) copy-start(bf16[8,128,128]{2,1,0:T(8,128)(2,1)S(1)} %collective-permute-done.2.refs_2_) | copy-start | bytes 786436
  37.7 7.8 %collective-permute-start.3 = (s16[144,128]{1,0:T(8,128)(2,1)}, s16[144,128]{1,0:T(8,128)(2,1)S(1)}, u32[]{:S(2)}, u32[]{:S(2)}) collective-permute-start(s16[144,128]{1,0:T(8,128)(2,1)} %get-tuple-element.29), channel_id=1, source_target_pairs={{0,28},{4,24},{8,20},{12,16},{16,12},{20,8},{24,4},{28,0},{1,29},{... | collective-permute-start | bytes 110600 | tf_op jit(solution)/shard_map/ppermute | solution.py:550
  40.2 7.5 %collective-permute-start.4 = (s16[144,128]{1,0:T(8,128)(2,1)}, s16[144,128]{1,0:T(8,128)(2,1)S(1)}, u32[]{:S(2)}, u32[]{:S(2)}) collective-permute-start(s16[144,128]{1,0:T(8,128)(2,1)} %get-tuple-element.30), channel_id=1, source_target_pairs={{0,24},{4,28},{8,16},{12,20},{16,8},{20,12},{24,0},{28,4},{1,25},{... | collective-permute-start | bytes 110600 | tf_op jit(solution)/shard_map/ppermute | solution.py:550
  41.8 7.1 %collective-permute-start.5 = (s16[144,128]{1,0:T(8,128)(2,1)}, s16[144,128]{1,0:T(8,128)(2,1)S(1)}, u32[]{:S(2)}, u32[]{:S(2)}) collective-permute-start(s16[144,128]{1,0:T(8,128)(2,1)} %get-tuple-element.31), channel_id=1, source_target_pairs={{0,20},{4,16},{8,28},{12,24},{16,4},{20,0},{24,12},{28,8},{1,21},{... | collective-permute-start | bytes 110600 | tf_op jit(solution)/shard_map/ppermute | solution.py:550
  41.8 7.1 %collective-permute-start.6 = (s16[144,128]{1,0:T(8,128)(2,1)}, s16[144,128]{1,0:T(8,128)(2,1)S(1)}, u32[]{:S(2)}, u32[]{:S(2)}) collective-permute-start(s16[144,128]{1,0:T(8,128)(2,1)} %get-tuple-element.32), channel_id=1, source_target_pairs={{0,16},{4,20},{8,24},{12,28},{16,0},{20,4},{24,8},{28,12},{1,17},{... | collective-permute-start | bytes 110600 | tf_op jit(solution)/shard_map/ppermute | solution.py:550
  45.4 5.1 %collective-permute-start.7 = (s16[144,128]{1,0:T(8,128)(2,1)}, s16[144,128]{1,0:T(8,128)(2,1)S(1)}, u32[]{:S(2)}, u32[]{:S(2)}) collective-permute-start(s16[144,128]{1,0:T(8,128)(2,1)} %get-tuple-element.33), channel_id=1, source_target_pairs={{0,12},{4,8},{8,4},{12,0},{16,28},{20,24},{24,20},{28,16},{1,13},{... | collective-permute-start | bytes 110600 | tf_op jit(solution)/shard_map/ppermute | solution.py:550
  45.5 5.0 %collective-permute-start.8 = (s16[144,128]{1,0:T(8,128)(2,1)}, s16[144,128]{1,0:T(8,128)(2,1)S(1)}, u32[]{:S(2)}, u32[]{:S(2)}) collective-permute-start(s16[144,128]{1,0:T(8,128)(2,1)} %get-tuple-element.34), channel_id=1, source_target_pairs={{0,8},{4,12},{8,0},{12,4},{16,24},{20,28},{24,16},{28,20},{1,9},{5... | collective-permute-start | bytes 110600 | tf_op jit(solution)/shard_map/ppermute | solution.py:550
  47.7 4.2 %collective-permute-start.9 = (s16[144,128]{1,0:T(8,128)(2,1)}, s16[144,128]{1,0:T(8,128)(2,1)S(1)}, u32[]{:S(2)}, u32[]{:S(2)}) collective-permute-start(s16[144,128]{1,0:T(8,128)(2,1)} %get-tuple-element.35), channel_id=1, source_target_pairs={{0,4},{4,0},{8,12},{12,8},{16,20},{20,16},{24,28},{28,24},{1,5},{5... | collective-permute-start | bytes 110600 | tf_op jit(solution)/shard_map/ppermute | solution.py:550
  51.8 0.8 %copy-start = (s16[144,128]{1,0:T(8,128)(2,1)S(1)}, s16[144,128]{1,0:T(8,128)(2,1)}, u32[]{:S(2)}) copy-start(s16[144,128]{1,0:T(8,128)(2,1)} %get-tuple-element.36.refs_7_) | copy-start | bytes 110596

commit v15 on v14

--- a/solution.py
+++ b/solution.py
@@ -2,7 +2,6 @@
 
 import jax
 import jax.numpy as jnp
-import ml_dtypes
 import numpy as np
 from jax import lax
 from jax.experimental import pallas as pl
@@ -22,12 +21,6 @@
 LOWEST_EXPONENT = -120.0
 TINY = 1e-37
 HEADER_ROWS = 16
-
-
-def split_constant(matrix):
-    high = matrix.astype(ml_dtypes.bfloat16)
-    low = (matrix - high.astype(np.float64)).astype(ml_dtypes.bfloat16)
-    return high, low
 
 
 def sine_basis(side):
@@ -174,7 +167,7 @@
 
 
 def own_kernel(
-    sizes, match_hbm, centers_hbm, own_hbm, mine_ref, partner_ref, match_ref, centers_ref, boxes_ref, fields, sems
+    sizes, match_hbm, centers_hbm, own_hbm, mine_ref, match_ref, centers_ref, boxes_ref, fields, sems
 ):
     side, rounds, own_count, _, _ = sizes
     tiles, _, _ = box_shape(sizes)
@@ -190,32 +183,25 @@
     spread(sizes, boxes_ref, fields, 0)
 
     def place(index, carry):
-        member, mate, a, b, active = pair_geometry(sizes, match_ref, centers_ref, index)
+        member, _, a, _, _ = pair_geometry(sizes, match_ref, centers_ref, index)
         rows = pl.ds(pl.multiple_of(index * side, side), side)
         placed = rolled(sizes, fields, member - first_member, 0, side, a[0], a[1] * side + a[2])
         for tile in range(tiles):
             mine_ref[rows, tile * LANES : (tile + 1) * LANES] = placed[tile].astype(jnp.bfloat16)
-        local = mate - first_member
-
-        @pl.when((local >= 0) & (local < own_count))
-        def _():
-            placed = place_partner(sizes, fields, local, a, b, active)
-            for tile in range(tiles):
-                partner_ref[rows, tile * LANES : (tile + 1) * LANES] = placed[tile].astype(jnp.bfloat16)
-
         return carry
 
     lax.fori_loop(0, own_count * rounds, place, 0)
 
 
-def force_kernel(sizes, match_hbm, centers_hbm, mine_hbm, partner_hbm, *refs):
+def force_kernel(sizes, match_hbm, centers_hbm, mine_hbm, *refs):
     side, rounds, own_count, slab_count, pair_count = sizes
-    piece_hbm, refs = refs[: pair_count - 1], refs[pair_count - 1 :]
-    constant_hbm, refs = refs[:6], refs[6:]
+    piece_hbm, refs = refs[:pair_count], refs[pair_count:]
+    constant_hbm, refs = refs[:3], refs[3:]
     out_refs, refs = refs[:slab_count], refs[slab_count:]
     match_ref, centers_ref, mine, partner, boxes_ref, *refs = refs
-    constants, refs = refs[:6], refs[6:]
-    mix_ref, gain_ref, there_high, there_low, back_high, back_low = constants
+    constants, refs = refs[:3], refs[3:]
+    basis_ref, line_ref, gain_ref = constants
+    mix_ref, there_high, there_low, back_high, back_low, *refs = refs
     fields, first, second, *terms, all_codes, sems = refs
     planes = side // slab_count
     tiles, lines, pitch = box_shape(sizes)
@@ -229,16 +215,14 @@
     core = pair_index % CORES
     chip = pair_index // CORES
     chips = pair_count // CORES
-    first_member = pair_index * own_count
 
     places = [
         (chip + chips - step) % chips * CORES + (core + core_step) % CORES
         for core_step in range(CORES)
         for step in range(chips)
     ]
-    places = places[1:]
-    sources = [match_hbm, centers_hbm, *piece_hbm, mine_hbm, partner_hbm, *constant_hbm]
-    targets = [match_ref, centers_ref, *[boxes_ref.at[pair] for pair in places], mine, partner, *constants]
+    sources = [match_hbm, centers_hbm, *constant_hbm, *piece_hbm, mine_hbm]
+    targets = [match_ref, centers_ref, *constants, *[boxes_ref.at[pair] for pair in places], mine]
     copies = [pltpu.make_async_copy(s, t, sems.at[i]) for i, (s, t) in enumerate(zip(sources, targets))]
     for copy in copies:
         copy.start()
@@ -246,13 +230,32 @@
         clear_edges(sizes, fields, pair * own_count, own_count)
     for ref in terms:
         clear_edges(sizes, ref, 0, group)
-    boxes_count = 2 + len(places)
-    for copy in copies[:boxes_count]:
+    for copy in copies[:5]:
+        copy.wait()
+
+    def make_matrices(first_line, high_ref, low_ref):
+        count = side // 2
+        for parity in range(2):
+            for index in range(count):
+                line = first_line + parity * count + index
+                rows = slice(index * side, (index + 1) * side)
+                value = basis_ref[...] * line_ref[line : line + 1, :]
+                high_ref[parity, rows, :], low_ref[parity, rows, :] = split_pair(value)
+
+    block = lax.broadcasted_iota(jnp.int32, (side, group_rows), 1) // side
+    for index in range(group):
+        rows = slice(index * side, (index + 1) * side)
+        value = jnp.where(block == index, basis_ref[:, :group_rows], 0.0)
+        high, low = split_pair(value)
+        for part, piece in enumerate((high, high, low)):
+            mix_ref[rows, part * group_rows : (part + 1) * group_rows] = piece
+    make_matrices(0, there_high, there_low)
+
+    for copy in copies[5:-1]:
         copy.wait()
     for pair in places:
         spread(sizes, boxes_ref, fields, pair)
-    for copy in copies[boxes_count : boxes_count + 2]:
-        copy.wait()
+    copies[-1].wait()
 
     row_count = solves * side
     half_tiles = tiles // 2
@@ -277,22 +280,17 @@
         start = index * side
         rows = slice(start, start + side)
         _, mate, a, b, active = pair_geometry(sizes, match_ref, centers_ref, index)
-        is_own = (mate >= first_member) & (mate < first_member + own_count)
         placed = place_partner(sizes, fields, mate, a, b, active)
         density = []
         for tile in range(tiles):
             columns = slice(tile * LANES, (tile + 1) * LANES)
-            chosen = jnp.where(is_own, partner[rows, columns].astype(jnp.float32), placed[tile])
-            partner[rows, columns] = chosen.astype(jnp.bfloat16)
-            density.append(mine[rows, columns].astype(jnp.float32) * chosen)
+            partner[rows, columns] = placed[tile].astype(jnp.bfloat16)
+            density.append(mine[rows, columns].astype(jnp.float32) * placed[tile])
         for tile in range(half_tiles):
             far = mirrored(density[tiles - 1 - tile])
             for parity, value in enumerate((density[tile] + far, density[tile] - far)):
                 column = parity * half_cells + tile * LANES
                 store_split(first, start, side, slice(column, column + LANES), value)
-
-    mix_copy, gain_copy, *matrix_copies = copies[boxes_count + 2 :]
-    mix_copy.wait()
 
     def along_x(start, columns, source):
         high = source[start : start + group_rows, columns]
@@ -314,8 +312,7 @@
         columns = slice(0, cells)
         store_split(second, start, group_rows, columns, along_x(start, columns, first))
 
-    for copy in (gain_copy, *matrix_copies[:2]):
-        copy.wait()
+    make_matrices(side, back_high, back_low)
     for parity in range(2):
         for column in range(0, half_cells, width):
             columns = slice(column, column + width)
@@ -325,8 +322,6 @@
             value = (value.reshape(solves, side, width) * gain[None]).reshape(row_count, width)
             store_split(first, 0, row_count, columns, value)
 
-    for copy in matrix_copies[2:]:
-        copy.wait()
     for parity in range(2):
         for column in range(0, half_cells, width):
             value = in_plane(parity, slice(column, column + width), first, back_high, back_low)
@@ -469,9 +464,9 @@
     vectors = pl.BlockSpec(memory_space=pltpu.VMEM)
     return pl.pallas_call(
         functools.partial(own_kernel, sizes),
-        out_shape=[jax.ShapeDtypeStruct(placed, jnp.bfloat16)] * 2,
+        out_shape=jax.ShapeDtypeStruct(placed, jnp.bfloat16),
         in_specs=[either] * 3,
-        out_specs=[vectors] * 2,
+        out_specs=vectors,
         scratch_shapes=[
             pltpu.SMEM(match.shape, jnp.int32),
             pltpu.SMEM(centers.shape, jnp.int32),
@@ -484,7 +479,7 @@
     )(match, centers, boxes)
 
 
-def team_forces(sizes, match, centers, mine, partner, pieces):
+def team_forces(sizes, match, centers, mine, pieces):
     side, rounds, own_count, slab_count, pair_count = sizes
     tiles, _, pitch = box_shape(sizes)
     _, rows, _ = pieces[0].shape
@@ -492,18 +487,19 @@
     group = min(solves, 8)
     cells = side * side
     basis = sine_basis(side)
-    mix_high, mix_low = split_constant(np.kron(np.eye(group), basis))
-    mix = np.concatenate([mix_high, mix_high, mix_low], axis=1)
-    there = np.stack([np.kron(basis[parity::2, : side // 2].T, basis) for parity in range(2)])
+    halves = [basis[parity::2, : side // 2].T for parity in range(2)]
+    lines = np.concatenate(halves + [half.T for half in halves])
+    lines = np.repeat(lines, side, axis=1).astype(np.float32)
+    tile = np.tile(basis, (1, side // 2)).astype(np.float32)
     gain = chebyshev_gain(side).reshape(side, side, side)
     gain = np.concatenate([gain[:, parity::2].reshape(side, -1) for parity in range(2)], axis=1)
-    constants = (mix, gain, *split_constant(there), *split_constant(there.transpose(0, 2, 1)))
+    constants = (tile, lines, gain)
     either = pl.BlockSpec(memory_space=pl.ANY)
     distant = pl.BlockSpec(memory_space=pltpu.HBM)
     vectors = pl.BlockSpec(memory_space=pltpu.VMEM)
     wide = pltpu.VMEM((2 * solves * side, cells), jnp.bfloat16)
     flops = 2 * solves * side * 3 * 2 * (cells * cells // 2 + cells * group * side)
-    inputs = [match, centers, mine, partner, *pieces, *[jnp.asarray(constant) for constant in constants]]
+    inputs = [match, centers, mine, *pieces, *[jnp.asarray(constant) for constant in constants]]
     return pl.pallas_call(
         functools.partial(force_kernel, sizes),
         out_shape=[jax.ShapeDtypeStruct((rows + HEADER_ROWS, LANES), jnp.int16)] * slab_count,
@@ -513,9 +509,11 @@
             pltpu.SMEM(match.shape, jnp.int32),
             pltpu.SMEM(centers.shape, jnp.int32),
             pltpu.VMEM(mine.shape, jnp.bfloat16),
-            pltpu.VMEM(partner.shape, jnp.bfloat16),
+            pltpu.VMEM(mine.shape, jnp.bfloat16),
             pltpu.VMEM((pair_count, slab_count, rows, LANES), jnp.bfloat16),
             *[pltpu.VMEM(constant.shape, constant.dtype) for constant in constants],
+            pltpu.VMEM((group * side, 3 * group * side), jnp.bfloat16),
+            *[pltpu.VMEM((2, cells // 2, cells // 2), jnp.bfloat16)] * 4,
             pltpu.VMEM((own_count * pair_count * tiles * pitch, LANES), jnp.float32),
             wide,
             wide,
@@ -538,12 +536,12 @@
     boxes = lax.all_to_all(blocks, "slab", split_axis=0, concat_axis=0, tiled=True)
     sizes = (side, matchings.shape[1], own_count, slab_count, pair_count)
     pieces = gather_chips(boxes, pair_count)
-    mine, partner = place_own(sizes, matchings, centers.T, boxes)
-    boxes, mine, partner = lax.optimization_barrier((boxes, mine, partner))
+    mine = place_own(sizes, matchings, centers.T, boxes)
+    boxes, mine = lax.optimization_barrier((boxes, mine))
     swapped = [swap_cores(boxes, pair_count)]
-    pieces, mine, partner = lax.optimization_barrier((pieces, mine, partner))
-    pieces = pieces + swapped + [swap_cores(piece, pair_count) for piece in pieces]
-    codes = team_forces(sizes, matchings, centers.T, mine, partner, pieces)
+    pieces, mine = lax.optimization_barrier((pieces, mine))
+    swapped += [swap_cores(piece, pair_count) for piece in pieces]
+    codes = team_forces(sizes, matchings, centers.T, mine, [boxes] + pieces + swapped)
     received = []
     for step in reversed(range(1, slab_count)):
         perm = [(i, partner_of(i, step, slab_count)[0]) for i in range(slab_count)]

time: 54.9 us -> 53.8 us (0.980)
  Pallas kernels: 17.6 us -> 16.1 us
  waiting for transfers between devices: 4.37 us -> 5.84 us
    pallas_call x1, Pallas kernels: 5.1 us -> 4.05 us  [place_own(): pl.pallas_call(functools.partial(own_kernel, sizes), out_shape=jax.ShapeD...]
    ppermute x1, waiting for transfers between devices: 0.01 us -> 0.74 us  [gather_chips(): pieces.append(lax.ppermute(boxes, 'pair', perm))]
    ppermute x7, waiting for transfers between devices: 2.97 us -> 3.56 us  [shards(): received.append(lax.ppermute(codes[step], 'slab', perm))]
  transfers between devices with their start and end apart: 10 -> 10, of which waited for: 4 -> 7; matrix products, arithmetic and copies ran while one was open for 0% -> 0% of each run, Pallas kernels for 9% -> 8%
where the time goes in v15:
time: 53.8 us; the launch traced here: 53.5 us
  Pallas kernels  16.1 us (30%)
  blocking collectives  16 us (30%)
  starting transfers between devices  12.8 us (24%)
  waiting for transfers between devices  5.84 us (11%)
  local copies, waits for them, and re-layouts  2.71 us (5%)
    all_to_all x1, blocking collectives, shards(): lax.all_to_all(blocks, 'slab', split_axis=0, concat_axis=0, tiled=True)  16 us
    ppermute x7, starting transfers between devices, shards(): received.append(lax.ppermute(codes[step], 'slab', perm))  11.2 us
    pallas_call x1, Pallas kernels, team_forces(): pl.pallas_call(functools.partial(force_kernel, sizes), out_shape=[jax.Sha...  10.3 us
    pallas_call x1, Pallas kernels, place_own(): pl.pallas_call(functools.partial(own_kernel, sizes), out_shape=jax.ShapeD...  4.05 us
    ppermute x7, waiting for transfers between devices, shards(): received.append(lax.ppermute(codes[step], 'slab', perm))  3.56 us
    pallas_call x1, Pallas kernels, unpack(): pl.pallas_call(functools.partial(unpack_kernel, (own_count, slab_count, t...  1.74 us
    unnamed x10, local copies, waits for them, and re-layouts  1.64 us
    ppermute x2, waiting for transfers between devices, swap_cores(): return lax.ppermute(block, 'pair', [(i, i ^ 1) for i in range(pair_count)])  1.53 us
  transfers between devices with their start and end apart: 10, of which 7 were waited for; matrix products, arithmetic and copies ran while one was open for 0% of the time, Pallas kernels for 8%

profile of v15, /device:TPU:0, one launch (start us, length us, event | category | flops | bytes accessed | tf_op | source)
XLA Modules:
  0.0 53.5 jit_solution(3908204738835314183)
XLA Ops:
  0.0 1.1 %reshape.9 = bf16[8,128,128]{2,1,0:T(8,128)(2,1)S(1)} reshape(bf16[32,4096]{1,0:T(8,128)(2,1)} %param.6) | data formatting | bytes 524288 | tf_op jit(solution)/shard_map/reshape | solution.py:535
  1.1 16.0 %all_to_all.5.own_hbm.refs_0_ = bf16[8,128,128]{2,1,0:T(8,128)(2,1)S(1)} all-to-all(bf16[8,128,128]{2,1,0:T(8,128)(2,1)S(1)} %reshape.9), channel_id=1, replica_groups=mesh['slab'=8,'pair'=4] {'slab'}, dimensions={0} | all-to-all | bytes 524288 | tf_op jit(solution)/shard_map/all_to_all | solution.py:536
  17.1 1.5 %collective-permute-start = (bf16[8,128,128]{2,1,0:T(8,128)(2,1)S(1)}, bf16[8,128,128]{2,1,0:T(8,128)(2,1)S(1)}, u32[]{:S(2)}, u32[]{:S(2)}) collective-permute-start(bf16[8,128,128]{2,1,0:T(8,128)(2,1)S(1)} %all_to_all.5.own_hbm.refs_0_), channel_id=1, source_target_pairs={{0,2},{1,3},{2,0},{3,1},{4,6},{5,7},{6,4},{7,5},{8,10},{9,11},{10,... | collective-permute-start | bytes 786440 | tf_op jit(solution)/shard_map/ppermute | solution.py:404
  18.6 4.0 %shard_map.64.mine_hbm = bf16[512,1024]{1,0:T(8,128)(2,1)} custom-call(s32[1,4,16]{2,1,0:T(4,128)} %match_hbm.3, s32[3,128]{1,0:T(4,128)} %bitcast.6, bf16[8,128,128]{2,1,0:T(8,128)(2,1)} %copy-done.1), custom_call_target="tpu_custom_call" | custom-call | flops 5000000000 | bytes 4194304 | tf_op jit(solution)/shard_map/pallas_call | solution.py:465
  22.6 0.1 collective-permute-start.1
  22.7 0.7 %collective-permute-done.refs_1_ = bf16[8,128,128]{2,1,0:T(8,128)(2,1)S(1)} collective-permute-done((bf16[8,128,128]{2,1,0:T(8,128)(2,1)S(1)}, bf16[8,128,128]{2,1,0:T(8,128)(2,1)S(1)}, u32[]{:S(2)}, u32[]{:S(2)}) %collective-permute-start) | collective-permute-done | bytes 262176 | tf_op jit(solution)/shard_map/ppermute | solution.py:404
  23.5 1.0 %collective-permute-done.1.refs_2_ = bf16[8,128,128]{2,1,0:T(8,128)(2,1)S(1)} collective-permute-done((bf16[8,128,128]{2,1,0:T(8,128)(2,1)}, bf16[8,128,128]{2,1,0:T(8,128)(2,1)S(1)}, u32[]{:S(2)}, u32[]{:S(2)}) %collective-permute-start.1) | collective-permute-done | bytes 262176 | tf_op jit(solution)/shard_map/ppermute | solution.py:397
  24.4 0.5 %collective-permute-done.2.refs_3_ = bf16[8,128,128]{2,1,0:T(8,128)(2,1)S(1)} collective-permute-done((bf16[8,128,128]{2,1,0:T(8,128)(2,1)S(1)}, bf16[8,128,128]{2,1,0:T(8,128)(2,1)S(1)}, u32[]{:S(2)}, u32[]{:S(2)}) %collective-permute-start.2) | collective-permute-done | bytes 262176 | tf_op jit(solution)/shard_map/ppermute | solution.py:397
  25.0 0.1 copy-done.3
  25.1 0.7 %copy-done.4 = bf16[8,128,128]{2,1,0:T(8,128)(2,1)} copy-done((bf16[8,128,128]{2,1,0:T(8,128)(2,1)}, bf16[8,128,128]{2,1,0:T(8,128)(2,1)S(1)}, u32[]{:S(2)}) %copy-start.4) | copy-done | bytes 262168
  25.9 10.3 %shard_map.65 = (s16[144,128]{1,0:T(8,128)(2,1)}, s16[144,128]{1,0:T(8,128)(2,1)}, s16[144,128]{1,0:T(8,128)(2,1)}, s16[144,128]{1,0:T(8,128)(2,1)}, s16[144,128...) custom-call(s32[1,4,16]{2,1,0:T(4,128)} %match_hbm.3, ...), custom_call_target="tpu_custom_call" | custom-call | flops 4831838208 | bytes 8388608 | tf_op jit(solution)/shard_map/pallas_call | solution.py:503
  36.2 3.5 %collective-permute-start.3 = (s16[144,128]{1,0:T(8,128)(2,1)}, s16[144,128]{1,0:T(8,128)(2,1)S(1)}, u32[]{:S(2)}, u32[]{:S(2)}) collective-permute-start(s16[144,128]{1,0:T(8,128)(2,1)} %get-tuple-element.21), channel_id=1, source_target_pairs={{0,28},{4,24},{8,20},{12,16},{16,12},{20,8},{24,4},{28,0},{1,29},{... | collective-permute-start | bytes 110600 | tf_op jit(solution)/shard_map/ppermute | solution.py:548
  39.7 1.2 %collective-permute-start.4 = (s16[144,128]{1,0:T(8,128)(2,1)}, s16[144,128]{1,0:T(8,128)(2,1)S(1)}, u32[]{:S(2)}, u32[]{:S(2)}) collective-permute-start(s16[144,128]{1,0:T(8,128)(2,1)} %get-tuple-element.22), channel_id=1, source_target_pairs={{0,24},{4,28},{8,16},{12,20},{16,8},{20,12},{24,0},{28,4},{1,25},{... | collective-permute-start | bytes 110600 | tf_op jit(solution)/shard_map/ppermute | solution.py:548
  40.9 0.3 collective-permute-start.5
  41.2 2.7 %collective-permute-start.6 = (s16[144,128]{1,0:T(8,128)(2,1)}, s16[144,128]{1,0:T(8,128)(2,1)S(1)}, u32[]{:S(2)}, u32[]{:S(2)}) collective-permute-start(s16[144,128]{1,0:T(8,128)(2,1)} %get-tuple-element.24), channel_id=1, source_target_pairs={{0,16},{4,20},{8,24},{12,28},{16,0},{20,4},{24,8},{28,12},{1,17},{... | collective-permute-start | bytes 110600 | tf_op jit(solution)/shard_map/ppermute | solution.py:548
  43.9 1.1 %collective-permute-start.7 = (s16[144,128]{1,0:T(8,128)(2,1)}, s16[144,128]{1,0:T(8,128)(2,1)S(1)}, u32[]{:S(2)}, u32[]{:S(2)}) collective-permute-start(s16[144,128]{1,0:T(8,128)(2,1)} %get-tuple-element.25), channel_id=1, source_target_pairs={{0,12},{4,8},{8,4},{12,0},{16,28},{20,24},{24,20},{28,16},{1,13},{... | collective-permute-start | bytes 110600 | tf_op jit(solution)/shard_map/ppermute | solution.py:548
  45.0 1.8 %collective-permute-start.8 = (s16[144,128]{1,0:T(8,128)(2,1)}, s16[144,128]{1,0:T(8,128)(2,1)S(1)}, u32[]{:S(2)}, u32[]{:S(2)}) collective-permute-start(s16[144,128]{1,0:T(8,128)(2,1)} %get-tuple-element.26), channel_id=1, source_target_pairs={{0,8},{4,12},{8,0},{12,4},{16,24},{20,28},{24,16},{28,20},{1,9},{5... | collective-permute-start | bytes 110600 | tf_op jit(solution)/shard_map/ppermute | solution.py:548
  46.8 0.6 %collective-permute-start.9 = (s16[144,128]{1,0:T(8,128)(2,1)}, s16[144,128]{1,0:T(8,128)(2,1)S(1)}, u32[]{:S(2)}, u32[]{:S(2)}) collective-permute-start(s16[144,128]{1,0:T(8,128)(2,1)} %get-tuple-element.27), channel_id=1, source_target_pairs={{0,4},{4,0},{8,12},{12,8},{16,20},{20,16},{24,28},{28,24},{1,5},{5... | collective-permute-start | bytes 110600 | tf_op jit(solution)/shard_map/ppermute | solution.py:548
  47.4 0.5 collective-permute-done.6.refs_3_
  47.9 1.1 %collective-permute-done.7.refs_4_ = s16[144,128]{1,0:T(8,128)(2,1)S(1)} collective-permute-done((s16[144,128]{1,0:T(8,128)(2,1)}, s16[144,128]{1,0:T(8,128)(2,1)S(1)}, u32[]{:S(2)}, u32[]{:S(2)}) %collective-permute-start.7) | collective-permute-done | bytes 36896 | tf_op jit(solution)/shard_map/ppermute | solution.py:548
  49.0 0.4 collective-permute-done.8.refs_5_
  49.3 1.6 %collective-permute-done.9.refs_6_ = s16[144,128]{1,0:T(8,128)(2,1)S(1)} collective-permute-done((s16[144,128]{1,0:T(8,128)(2,1)}, s16[144,128]{1,0:T(8,128)(2,1)S(1)}, u32[]{:S(2)}, u32[]{:S(2)}) %collective-permute-start.9) | collective-permute-done | bytes 36896 | tf_op jit(solution)/shard_map/ppermute | solution.py:548
  51.0 0.8 %copy-done = s16[144,128]{1,0:T(8,128)(2,1)S(1)} copy-done((s16[144,128]{1,0:T(8,128)(2,1)S(1)}, s16[144,128]{1,0:T(8,128)(2,1)}, u32[]{:S(2)}) %copy-start) | copy-done | bytes 36888
  51.7 1.7 %shard_map.66 = f32[1024,128]{1,0:T(8,128)} custom-call(s16[144,128]{1,0:T(8,128)(2,1)S(1)} %collective-permute-done.3.refs_0_, s16[144,128]{1,0:T(8,128)(2,1)S(1)} %collective-permute-done.4.refs_1_, s16[144,128]{1,0:T(8,128)(2,1)S(1)} %collective-permute-done.5.refs_2_, s16[144,128]{1,0:T(8,128)(2,1)S(1)} %collective-permute-done.6.refs_3_, ...), custom_call_target="tpu_custom_call" | custom-call | tf_op jit(solution)/shard_map/pallas_call | solution.py:445
  (11 shorter events, 0.0 us)
Async XLA Ops:
  17.1 1.5 %copy-start.1 = (bf16[8,128,128]{2,1,0:T(8,128)(2,1)}, bf16[8,128,128]{2,1,0:T(8,128)(2,1)S(1)}, u32[]{:S(2)}) copy-start(bf16[8,128,128]{2,1,0:T(8,128)(2,1)S(1)} %all_to_all.5.own_hbm.refs_0_) | copy-start | bytes 786436
  17.1 6.4 %collective-permute-start = (bf16[8,128,128]{2,1,0:T(8,128)(2,1)S(1)}, bf16[8,128,128]{2,1,0:T(8,128)(2,1)S(1)}, u32[]{:S(2)}, u32[]{:S(2)}) collective-permute-start(bf16[8,128,128]{2,1,0:T(8,128)(2,1)S(1)} %all_to_all.5.own_hbm.refs_0_), channel_id=1, source_target_pairs={{0,2},{1,3},{2,0},{3,1},{4,6},{5,7},{6,4},{7,5},{8,10},{9,11},{10,... | collective-permute-start | bytes 786440 | tf_op jit(solution)/shard_map/ppermute | solution.py:404
  22.6 1.8 %collective-permute-start.1 = (bf16[8,128,128]{2,1,0:T(8,128)(2,1)}, bf16[8,128,128]{2,1,0:T(8,128)(2,1)S(1)}, u32[]{:S(2)}, u32[]{:S(2)}) collective-permute-start(bf16[8,128,128]{2,1,0:T(8,128)(2,1)} %copy-done.1), channel_id=1, source_target_pairs={{0,1},{1,0},{2,3},{3,2},{4,5},{5,4},{6,7},{7,6},{8,9},{9,8},{10,11... | collective-permute-start | bytes 786440 | tf_op jit(solution)/shard_map/ppermute | solution.py:397
  23.4 1.5 %copy-start.2 = (bf16[8,128,128]{2,1,0:T(8,128)(2,1)}, bf16[8,128,128]{2,1,0:T(8,128)(2,1)S(1)}, u32[]{:S(2)}) copy-start(bf16[8,128,128]{2,1,0:T(8,128)(2,1)S(1)} %collective-permute-done.refs_1_) | copy-start | bytes 786436
  23.4 1.5 %collective-permute-start.2 = (bf16[8,128,128]{2,1,0:T(8,128)(2,1)S(1)}, bf16[8,128,128]{2,1,0:T(8,128)(2,1)S(1)}, u32[]{:S(2)}, u32[]{:S(2)}) collective-permute-start(bf16[8,128,128]{2,1,0:T(8,128)(2,1)S(1)} %collective-permute-done.refs_1_), channel_id=1, source_target_pairs={{0,1},{1,0},{2,3},{3,2},{4,5},{5,4},{6,7},{7,6},{8,9},{9,8},{10,11... | collective-permute-start | bytes 786440 | tf_op jit(solution)/shard_map/ppermute | solution.py:397
  24.4 0.7 %copy-start.3 = (bf16[8,128,128]{2,1,0:T(8,128)(2,1)}, bf16[8,128,128]{2,1,0:T(8,128)(2,1)S(1)}, u32[]{:S(2)}) copy-start(bf16[8,128,128]{2,1,0:T(8,128)(2,1)S(1)} %collective-permute-done.1.refs_2_) | copy-start | bytes 786436
  25.1 0.7 %copy-start.4 = (bf16[8,128,128]{2,1,0:T(8,128)(2,1)}, bf16[8,128,128]{2,1,0:T(8,128)(2,1)S(1)}, u32[]{:S(2)}) copy-start(bf16[8,128,128]{2,1,0:T(8,128)(2,1)S(1)} %collective-permute-done.2.refs_3_) | copy-start | bytes 786436
  36.2 8.8 %collective-permute-start.3 = (s16[144,128]{1,0:T(8,128)(2,1)}, s16[144,128]{1,0:T(8,128)(2,1)S(1)}, u32[]{:S(2)}, u32[]{:S(2)}) collective-permute-start(s16[144,128]{1,0:T(8,128)(2,1)} %get-tuple-element.21), channel_id=1, source_target_pairs={{0,28},{4,24},{8,20},{12,16},{16,12},{20,8},{24,4},{28,0},{1,29},{... | collective-permute-start | bytes 110600 | tf_op jit(solution)/shard_map/ppermute | solution.py:548
  39.7 7.0 %collective-permute-start.4 = (s16[144,128]{1,0:T(8,128)(2,1)}, s16[144,128]{1,0:T(8,128)(2,1)S(1)}, u32[]{:S(2)}, u32[]{:S(2)}) collective-permute-start(s16[144,128]{1,0:T(8,128)(2,1)} %get-tuple-element.22), channel_id=1, source_target_pairs={{0,24},{4,28},{8,16},{12,20},{16,8},{20,12},{24,0},{28,4},{1,25},{... | collective-permute-start | bytes 110600 | tf_op jit(solution)/shard_map/ppermute | solution.py:548
  40.9 6.5 %collective-permute-start.5 = (s16[144,128]{1,0:T(8,128)(2,1)}, s16[144,128]{1,0:T(8,128)(2,1)S(1)}, u32[]{:S(2)}, u32[]{:S(2)}) collective-permute-start(s16[144,128]{1,0:T(8,128)(2,1)} %get-tuple-element.23), channel_id=1, source_target_pairs={{0,20},{4,16},{8,28},{12,24},{16,4},{20,0},{24,12},{28,8},{1,21},{... | collective-permute-start | bytes 110600 | tf_op jit(solution)/shard_map/ppermute | solution.py:548
  41.2 6.7 %collective-permute-start.6 = (s16[144,128]{1,0:T(8,128)(2,1)}, s16[144,128]{1,0:T(8,128)(2,1)S(1)}, u32[]{:S(2)}, u32[]{:S(2)}) collective-permute-start(s16[144,128]{1,0:T(8,128)(2,1)} %get-tuple-element.24), channel_id=1, source_target_pairs={{0,16},{4,20},{8,24},{12,28},{16,0},{20,4},{24,8},{28,12},{1,17},{... | collective-permute-start | bytes 110600 | tf_op jit(solution)/shard_map/ppermute | solution.py:548
  43.9 5.1 %collective-permute-start.7 = (s16[144,128]{1,0:T(8,128)(2,1)}, s16[144,128]{1,0:T(8,128)(2,1)S(1)}, u32[]{:S(2)}, u32[]{:S(2)}) collective-permute-start(s16[144,128]{1,0:T(8,128)(2,1)} %get-tuple-element.25), channel_id=1, source_target_pairs={{0,12},{4,8},{8,4},{12,0},{16,28},{20,24},{24,20},{28,16},{1,13},{... | collective-permute-start | bytes 110600 | tf_op jit(solution)/shard_map/ppermute | solution.py:548
  45.0 4.3 %collective-permute-start.8 = (s16[144,128]{1,0:T(8,128)(2,1)}, s16[144,128]{1,0:T(8,128)(2,1)S(1)}, u32[]{:S(2)}, u32[]{:S(2)}) collective-permute-start(s16[144,128]{1,0:T(8,128)(2,1)} %get-tuple-element.26), channel_id=1, source_target_pairs={{0,8},{4,12},{8,0},{12,4},{16,24},{20,28},{24,16},{28,20},{1,9},{5... | collective-permute-start | bytes 110600 | tf_op jit(solution)/shard_map/ppermute | solution.py:548
  46.8 4.2 %collective-permute-start.9 = (s16[144,128]{1,0:T(8,128)(2,1)}, s16[144,128]{1,0:T(8,128)(2,1)S(1)}, u32[]{:S(2)}, u32[]{:S(2)}) collective-permute-start(s16[144,128]{1,0:T(8,128)(2,1)} %get-tuple-element.27), channel_id=1, source_target_pairs={{0,4},{4,0},{8,12},{12,8},{16,20},{20,16},{24,28},{28,24},{1,5},{5... | collective-permute-start | bytes 110600 | tf_op jit(solution)/shard_map/ppermute | solution.py:548
  51.0 0.8 %copy-start = (s16[144,128]{1,0:T(8,128)(2,1)S(1)}, s16[144,128]{1,0:T(8,128)(2,1)}, u32[]{:S(2)}) copy-start(s16[144,128]{1,0:T(8,128)(2,1)} %get-tuple-element.28.refs_7_) | copy-start | bytes 110596

commit v16 on v15

--- a/solution.py
+++ b/solution.py
@@ -21,6 +21,7 @@
 LOWEST_EXPONENT = -120.0
 TINY = 1e-37
 HEADER_ROWS = 16
+ENTRIES = 8
 
 
 def sine_basis(side):
@@ -166,14 +167,15 @@
     return result
 
 
-def own_kernel(
-    sizes, match_hbm, centers_hbm, own_hbm, mine_ref, match_ref, centers_ref, boxes_ref, fields, sems
-):
+def own_kernel(sizes, match_hbm, centers_hbm, own_hbm, *refs):
+    constant_hbm, refs = refs[:3], refs[3:]
+    mine_ref, table_ref, *constant_refs = refs[:5]
+    match_ref, centers_ref, boxes_ref, fields, sems = refs[5:]
     side, rounds, own_count, _, _ = sizes
     tiles, _, _ = box_shape(sizes)
     first_member = lax.axis_index("pair") * own_count
-    sources = (match_hbm, centers_hbm, own_hbm)
-    targets = (match_ref, centers_ref, boxes_ref.at[0])
+    sources = (match_hbm, centers_hbm, own_hbm, *constant_hbm)
+    targets = (match_ref, centers_ref, boxes_ref.at[0], *constant_refs)
     copies = [pltpu.make_async_copy(s, t, sems.at[i]) for i, (s, t) in enumerate(zip(sources, targets))]
     for copy in copies:
         copy.start()
@@ -183,7 +185,9 @@
     spread(sizes, boxes_ref, fields, 0)
 
     def place(index, carry):
-        member, _, a, _, _ = pair_geometry(sizes, match_ref, centers_ref, index)
+        member, mate, a, b, active = pair_geometry(sizes, match_ref, centers_ref, index)
+        for place, entry in enumerate((mate, *a, *b, jnp.where(active, 1, 0))):
+            table_ref[index * ENTRIES + place] = entry
         rows = pl.ds(pl.multiple_of(index * side, side), side)
         placed = rolled(sizes, fields, member - first_member, 0, side, a[0], a[1] * side + a[2])
         for tile in range(tiles):
@@ -193,12 +197,12 @@
     lax.fori_loop(0, own_count * rounds, place, 0)
 
 
-def force_kernel(sizes, match_hbm, centers_hbm, mine_hbm, *refs):
+def force_kernel(sizes, mine_hbm, table_hbm, *refs):
     side, rounds, own_count, slab_count, pair_count = sizes
     piece_hbm, refs = refs[:pair_count], refs[pair_count:]
     constant_hbm, refs = refs[:3], refs[3:]
     out_refs, refs = refs[:slab_count], refs[slab_count:]
-    match_ref, centers_ref, mine, partner, boxes_ref, *refs = refs
+    table_ref, mine, partner, boxes_ref, *refs = refs
     constants, refs = refs[:3], refs[3:]
     basis_ref, line_ref, gain_ref = constants
     mix_ref, there_high, there_low, back_high, back_low, *refs = refs
@@ -221,8 +225,8 @@
         for core_step in range(CORES)
         for step in range(chips)
     ]
-    sources = [match_hbm, centers_hbm, *constant_hbm, *piece_hbm, mine_hbm]
-    targets = [match_ref, centers_ref, *constants, *[boxes_ref.at[pair] for pair in places], mine]
+    sources = [table_hbm, *constant_hbm, *piece_hbm, mine_hbm]
+    targets = [table_ref, *constants, *[boxes_ref.at[pair] for pair in places], mine]
     copies = [pltpu.make_async_copy(s, t, sems.at[i]) for i, (s, t) in enumerate(zip(sources, targets))]
     for copy in copies:
         copy.start()
@@ -230,7 +234,7 @@
         clear_edges(sizes, fields, pair * own_count, own_count)
     for ref in terms:
         clear_edges(sizes, ref, 0, group)
-    for copy in copies[:5]:
+    for copy in copies[:4]:
         copy.wait()
 
     def make_matrices(first_line, high_ref, low_ref):
@@ -251,7 +255,7 @@
             mix_ref[rows, part * group_rows : (part + 1) * group_rows] = piece
     make_matrices(0, there_high, there_low)
 
-    for copy in copies[5:-1]:
+    for copy in copies[4:-1]:
         copy.wait()
     for pair in places:
         spread(sizes, boxes_ref, fields, pair)
@@ -279,8 +283,8 @@
     def densities(index):
         start = index * side
         rows = slice(start, start + side)
-        _, mate, a, b, active = pair_geometry(sizes, match_ref, centers_ref, index)
-        placed = place_partner(sizes, fields, mate, a, b, active)
+        mate, *offsets, active = [table_ref[index * ENTRIES + place] for place in range(ENTRIES)]
+        placed = place_partner(sizes, fields, mate, offsets[:3], offsets[3:], active == 1)
         density = []
         for tile in range(tiles):
             columns = slice(tile * LANES, (tile + 1) * LANES)
@@ -350,7 +354,7 @@
         sums = None
         for turn in range(rounds):
             index = own * rounds + turn
-            _, _, a, _, _ = pair_geometry(sizes, match_ref, centers_ref, index)
+            a = [table_ref[index * ENTRIES + 1 + axis] for axis in range(3)]
             ref = terms[index // group]
             term = rolled(sizes, ref, index % group, row, step_rows, -a[0], -(a[1] * side + a[2]))
             sums = term if sums is None else [s + t for s, t in zip(sums, term)]
@@ -456,36 +460,7 @@
     return out.reshape(row_count // 8, tiles, 8, LANES).transpose(0, 2, 1, 3).reshape(row_count, cells)
 
 
-def place_own(sizes, match, centers, boxes):
-    side, rounds, own_count, slab_count, _ = sizes
-    tiles, _, pitch = box_shape(sizes)
-    placed = (own_count * rounds * side, side * side)
-    either = pl.BlockSpec(memory_space=pl.ANY)
-    vectors = pl.BlockSpec(memory_space=pltpu.VMEM)
-    return pl.pallas_call(
-        functools.partial(own_kernel, sizes),
-        out_shape=jax.ShapeDtypeStruct(placed, jnp.bfloat16),
-        in_specs=[either] * 3,
-        out_specs=vectors,
-        scratch_shapes=[
-            pltpu.SMEM(match.shape, jnp.int32),
-            pltpu.SMEM(centers.shape, jnp.int32),
-            pltpu.VMEM((1,) + boxes.shape, jnp.bfloat16),
-            pltpu.VMEM((own_count * tiles * pitch, LANES), jnp.float32),
-            pltpu.SemaphoreType.DMA((3,)),
-        ],
-        compiler_params=pltpu.CompilerParams(vmem_limit_bytes=60 * 1024 * 1024),
-        cost_estimate=pl.CostEstimate(flops=5 * 10**9, bytes_accessed=4 * 1024 * 1024, transcendentals=0),
-    )(match, centers, boxes)
-
-
-def team_forces(sizes, match, centers, mine, pieces):
-    side, rounds, own_count, slab_count, pair_count = sizes
-    tiles, _, pitch = box_shape(sizes)
-    _, rows, _ = pieces[0].shape
-    solves = own_count * rounds
-    group = min(solves, 8)
-    cells = side * side
+def kernel_constants(side):
     basis = sine_basis(side)
     halves = [basis[parity::2, : side // 2].T for parity in range(2)]
     lines = np.concatenate(halves + [half.T for half in halves])
@@ -493,21 +468,57 @@
     tile = np.tile(basis, (1, side // 2)).astype(np.float32)
     gain = chebyshev_gain(side).reshape(side, side, side)
     gain = np.concatenate([gain[:, parity::2].reshape(side, -1) for parity in range(2)], axis=1)
-    constants = (tile, lines, gain)
+    return [jnp.asarray(constant) for constant in (tile, lines, gain)]
+
+
+def place_own(sizes, match, centers, boxes):
+    side, rounds, own_count, slab_count, _ = sizes
+    tiles, _, pitch = box_shape(sizes)
+    solves = own_count * rounds
+    constants = kernel_constants(side)
+    inputs = [match, centers, boxes, *constants]
     either = pl.BlockSpec(memory_space=pl.ANY)
-    distant = pl.BlockSpec(memory_space=pltpu.HBM)
+    vectors = pl.BlockSpec(memory_space=pltpu.VMEM)
+    return pl.pallas_call(
+        functools.partial(own_kernel, sizes),
+        out_shape=[
+            jax.ShapeDtypeStruct((solves * side, side * side), jnp.bfloat16),
+            jax.ShapeDtypeStruct((solves * ENTRIES,), jnp.int32),
+            *[jax.ShapeDtypeStruct(constant.shape, constant.dtype) for constant in constants],
+        ],
+        in_specs=[either] * len(inputs),
+        out_specs=[vectors, pl.BlockSpec(memory_space=pltpu.SMEM)] + [vectors] * len(constants),
+        scratch_shapes=[
+            pltpu.SMEM(match.shape, jnp.int32),
+            pltpu.SMEM(centers.shape, jnp.int32),
+            pltpu.VMEM((1,) + boxes.shape, jnp.bfloat16),
+            pltpu.VMEM((own_count * tiles * pitch, LANES), jnp.float32),
+            pltpu.SemaphoreType.DMA((len(inputs),)),
+        ],
+        compiler_params=pltpu.CompilerParams(vmem_limit_bytes=32 * 1024 * 1024),
+        cost_estimate=pl.CostEstimate(flops=5 * 10**9, bytes_accessed=4 * 1024 * 1024, transcendentals=0),
+    )(*inputs)
+
+
+def team_forces(sizes, mine, table, constants, pieces):
+    side, rounds, own_count, slab_count, pair_count = sizes
+    tiles, _, pitch = box_shape(sizes)
+    _, rows, _ = pieces[0].shape
+    solves = own_count * rounds
+    group = min(solves, 8)
+    cells = side * side
+    either = pl.BlockSpec(memory_space=pl.ANY)
     vectors = pl.BlockSpec(memory_space=pltpu.VMEM)
     wide = pltpu.VMEM((2 * solves * side, cells), jnp.bfloat16)
     flops = 2 * solves * side * 3 * 2 * (cells * cells // 2 + cells * group * side)
-    inputs = [match, centers, mine, *pieces, *[jnp.asarray(constant) for constant in constants]]
+    inputs = [mine, table, *pieces, *constants]
     return pl.pallas_call(
         functools.partial(force_kernel, sizes),
         out_shape=[jax.ShapeDtypeStruct((rows + HEADER_ROWS, LANES), jnp.int16)] * slab_count,
-        in_specs=[distant] * 2 + [either] * (len(inputs) - 2 - len(constants)) + [distant] * len(constants),
+        in_specs=[either] * len(inputs),
         out_specs=[vectors] * slab_count,
         scratch_shapes=[
-            pltpu.SMEM(match.shape, jnp.int32),
-            pltpu.SMEM(centers.shape, jnp.int32),
+            pltpu.SMEM(table.shape, jnp.int32),
             pltpu.VMEM(mine.shape, jnp.bfloat16),
             pltpu.VMEM(mine.shape, jnp.bfloat16),
             pltpu.VMEM((pair_count, slab_count, rows, LANES), jnp.bfloat16),
@@ -521,7 +532,7 @@
             pltpu.VMEM((slab_count, rows + HEADER_ROWS, LANES), jnp.int16),
             pltpu.SemaphoreType.DMA((len(inputs),)),
         ],
-        compiler_params=pltpu.CompilerParams(vmem_limit_bytes=60 * 1024 * 1024),
+        compiler_params=pltpu.CompilerParams(vmem_limit_bytes=32 * 1024 * 1024),
         cost_estimate=pl.CostEstimate(flops=flops, bytes_accessed=8 * 1024 * 1024, transcendentals=0),
     )(*inputs)
 
@@ -536,12 +547,12 @@
     boxes = lax.all_to_all(blocks, "slab", split_axis=0, concat_axis=0, tiled=True)
     sizes = (side, matchings.shape[1], own_count, slab_count, pair_count)
     pieces = gather_chips(boxes, pair_count)
-    mine = place_own(sizes, matchings, centers.T, boxes)
+    mine, table, *constants = place_own(sizes, matchings, centers.T, boxes)
     boxes, mine = lax.optimization_barrier((boxes, mine))
     swapped = [swap_cores(boxes, pair_count)]
     pieces, mine = lax.optimization_barrier((pieces, mine))
     swapped += [swap_cores(piece, pair_count) for piece in pieces]
-    codes = team_forces(sizes, matchings, centers.T, mine, [boxes] + pieces + swapped)
+    codes = team_forces(sizes, mine, table, constants, [boxes] + pieces + swapped)
     received = []
     for step in reversed(range(1, slab_count)):
         perm = [(i, partner_of(i, step, slab_count)[0]) for i in range(slab_count)]

time: 53.8 us -> 50.7 us (0.942)
  Pallas kernels: 16.1 us -> 14.1 us
  local copies, waits for them, and re-layouts: 2.71 us -> 1.11 us
    unnamed x10, local copies, waits for them, and re-layouts: 1.64 us -> 0.03 us
    pallas_call x1, Pallas kernels: 10.3 us -> 9.04 us  [team_forces(): pl.pallas_call(functools.partial(force_kernel, sizes), out_shape=[jax.Sha...]
    pallas_call x1, Pallas kernels: 4.05 us -> 3.34 us  [place_own(): pl.pallas_call(functools.partial(own_kernel, sizes), out_shape=[jax.Shape...]
    ppermute x1, waiting for transfers between devices: 0.74 us -> 1.43 us  [gather_chips(): pieces.append(lax.ppermute(boxes, 'pair', perm))]
  transfers between devices with their start and end apart: 10 -> 10, of which waited for: 7 -> 7; matrix products, arithmetic and copies ran while one was open for 0% -> 0% of each run, Pallas kernels for 8% -> 7%
where the time goes in v16:
time: 50.7 us; the launch traced here: 50.5 us
  blocking collectives  16.1 us (32%)
  Pallas kernels  14.1 us (28%)
  starting transfers between devices  12.8 us (25%)
  waiting for transfers between devices  6.31 us (12%)
  local copies, waits for them, and re-layouts  1.11 us (2%)
    all_to_all x1, blocking collectives, shards(): lax.all_to_all(blocks, 'slab', split_axis=0, concat_axis=0, tiled=True)  16.1 us
    ppermute x7, starting transfers between devices, shards(): received.append(lax.ppermute(codes[step], 'slab', perm))  11.2 us
    pallas_call x1, Pallas kernels, team_forces(): pl.pallas_call(functools.partial(force_kernel, sizes), out_shape=[jax.Sha...  9.04 us
    ppermute x7, waiting for transfers between devices, shards(): received.append(lax.ppermute(codes[step], 'slab', perm))  3.35 us
    pallas_call x1, Pallas kernels, place_own(): pl.pallas_call(functools.partial(own_kernel, sizes), out_shape=[jax.Shape...  3.34 us
    pallas_call x1, Pallas kernels, unpack(): pl.pallas_call(functools.partial(unpack_kernel, (own_count, slab_count, t...  1.74 us
    ppermute x2, waiting for transfers between devices, swap_cores(): return lax.ppermute(block, 'pair', [(i, i ^ 1) for i in range(pair_count)])  1.53 us
    ppermute x1, starting transfers between devices, gather_chips(): pieces.append(lax.ppermute(boxes, 'pair', perm))  1.49 us
  transfers between devices with their start and end apart: 10, of which 7 were waited for; matrix products, arithmetic and copies ran while one was open for 0% of the time, Pallas kernels for 7%

profile of v16, /device:TPU:0, one launch (start us, length us, event | category | flops | bytes accessed | tf_op | source)
XLA Modules:
  0.0 50.5 jit_solution(16898311336840181949)
XLA Ops:
  0.0 1.1 %reshape.9 = bf16[8,128,128]{2,1,0:T(8,128)(2,1)S(1)} reshape(bf16[32,4096]{1,0:T(8,128)(2,1)} %param.6) | data formatting | bytes 524288 | tf_op jit(solution)/shard_map/reshape | solution.py:546
  1.1 0.0 copy-start.2
  1.1 0.0 copy-start.3
  1.1 0.0 copy-start.4
  1.1 16.1 %all_to_all.5.own_hbm.refs_0_ = bf16[8,128,128]{2,1,0:T(8,128)(2,1)S(1)} all-to-all(bf16[8,128,128]{2,1,0:T(8,128)(2,1)S(1)} %reshape.9), channel_id=1, replica_groups=mesh['slab'=8,'pair'=4] {'slab'}, dimensions={0} | all-to-all | bytes 524288 | tf_op jit(solution)/shard_map/all_to_all | solution.py:547
  17.3 1.5 %collective-permute-start = (bf16[8,128,128]{2,1,0:T(8,128)(2,1)S(1)}, bf16[8,128,128]{2,1,0:T(8,128)(2,1)S(1)}, u32[]{:S(2)}, u32[]{:S(2)}) collective-permute-start(bf16[8,128,128]{2,1,0:T(8,128)(2,1)S(1)} %all_to_all.5.own_hbm.refs_0_), channel_id=1, source_target_pairs={{0,2},{1,3},{2,0},{3,1},{4,6},{5,7},{6,4},{7,5},{8,10},{9,11},{10,... | collective-permute-start | bytes 786440 | tf_op jit(solution)/shard_map/ppermute | solution.py:408
  18.8 3.3 %shard_map.64 = (bf16[512,1024]{1,0:T(8,128)(2,1)S(1)}, s32[128]{0:T(128)S(1)}, f32[32,512]{1,0:T(8,128)S(1)}, f32[64,512]{1,0:T(8,128)S(1)}, f32[32,1024]{1,0:T(8,128)S(1)}) custom-call(s32[1,4,16]{2,1,0:T(4,128)S(1)} %copy-done, s32[3,128]{1,0:T(4,128)S(1)} %bitcast.6, bf16[8,128,128]{2,1,0:T(8,128)(2,1)S(1)} %all_to_all.5.own_hbm.refs_0_, ...), custom_call_target="tpu_custom_call" | custom-call | flops 5000000000 | bytes 4194304 | tf_op jit(solution)/shard_map/pallas_call | solution.py:482
  22.1 0.1 collective-permute-start.1
  22.2 1.4 %collective-permute-done.refs_1_ = bf16[8,128,128]{2,1,0:T(8,128)(2,1)S(1)} collective-permute-done((bf16[8,128,128]{2,1,0:T(8,128)(2,1)S(1)}, bf16[8,128,128]{2,1,0:T(8,128)(2,1)S(1)}, u32[]{:S(2)}, u32[]{:S(2)}) %collective-permute-start) | collective-permute-done | bytes 262176 | tf_op jit(solution)/shard_map/ppermute | solution.py:408
  23.6 0.1 collective-permute-done.1.refs_2_
  23.7 1.4 %collective-permute-done.2.refs_3_ = bf16[8,128,128]{2,1,0:T(8,128)(2,1)S(1)} collective-permute-done((bf16[8,128,128]{2,1,0:T(8,128)(2,1)S(1)}, bf16[8,128,128]{2,1,0:T(8,128)(2,1)S(1)}, u32[]{:S(2)}, u32[]{:S(2)}) %collective-permute-start.2) | collective-permute-done | bytes 262176 | tf_op jit(solution)/shard_map/ppermute | solution.py:401
  25.2 9.0 %shard_map.65 = (s16[144,128]{1,0:T(8,128)(2,1)S(1)}, s16[144,128]{1,0:T(8,128)(2,1)S(1)}, s16[144,128]{1,0:T(8,128)(2,1)S(1)}, s16[144,128]{1,0:T(8,128)(2,1)S(...) custom-call(bf16[512,1024]{1,0:T(8,128)(2,1)S(1)} %get-tuple-element, ...), custom_call_target="tpu_custom_call" | custom-call | flops 4831838208 | bytes 8388608 | tf_op jit(solution)/shard_map/pallas_call | solution.py:515
  34.2 3.7 %collective-permute-start.3 = (s16[144,128]{1,0:T(8,128)(2,1)S(1)}, s16[144,128]{1,0:T(8,128)(2,1)S(1)}, u32[]{:S(2)}, u32[]{:S(2)}) collective-permute-start(s16[144,128]{1,0:T(8,128)(2,1)S(1)} %get-tuple-element.31), channel_id=1, source_target_pairs={{0,28},{4,24},{8,20},{12,16},{16,12},{20,8},{24,4},{28,0},{1,29},{... | collective-permute-start | bytes 110600 | tf_op jit(solution)/shard_map/ppermute | solution.py:559
  37.9 1.0 %collective-permute-start.4 = (s16[144,128]{1,0:T(8,128)(2,1)S(1)}, s16[144,128]{1,0:T(8,128)(2,1)S(1)}, u32[]{:S(2)}, u32[]{:S(2)}) collective-permute-start(s16[144,128]{1,0:T(8,128)(2,1)S(1)} %get-tuple-element.32), channel_id=1, source_target_pairs={{0,24},{4,28},{8,16},{12,20},{16,8},{20,12},{24,0},{28,4},{1,25},{... | collective-permute-start | bytes 110600 | tf_op jit(solution)/shard_map/ppermute | solution.py:559
  39.0 0.4 collective-permute-start.5
  39.4 2.6 %collective-permute-start.6 = (s16[144,128]{1,0:T(8,128)(2,1)S(1)}, s16[144,128]{1,0:T(8,128)(2,1)S(1)}, u32[]{:S(2)}, u32[]{:S(2)}) collective-permute-start(s16[144,128]{1,0:T(8,128)(2,1)S(1)} %get-tuple-element.34), channel_id=1, source_target_pairs={{0,16},{4,20},{8,24},{12,28},{16,0},{20,4},{24,8},{28,12},{1,17},{... | collective-permute-start | bytes 110600 | tf_op jit(solution)/shard_map/ppermute | solution.py:559
  41.9 1.3 %collective-permute-start.7 = (s16[144,128]{1,0:T(8,128)(2,1)S(1)}, s16[144,128]{1,0:T(8,128)(2,1)S(1)}, u32[]{:S(2)}, u32[]{:S(2)}) collective-permute-start(s16[144,128]{1,0:T(8,128)(2,1)S(1)} %get-tuple-element.35), channel_id=1, source_target_pairs={{0,12},{4,8},{8,4},{12,0},{16,28},{20,24},{24,20},{28,16},{1,13},{... | collective-permute-start | bytes 110600 | tf_op jit(solution)/shard_map/ppermute | solution.py:559
  43.2 1.6 %collective-permute-start.8 = (s16[144,128]{1,0:T(8,128)(2,1)S(1)}, s16[144,128]{1,0:T(8,128)(2,1)S(1)}, u32[]{:S(2)}, u32[]{:S(2)}) collective-permute-start(s16[144,128]{1,0:T(8,128)(2,1)S(1)} %get-tuple-element.36), channel_id=1, source_target_pairs={{0,8},{4,12},{8,0},{12,4},{16,24},{20,28},{24,16},{28,20},{1,9},{5... | collective-permute-start | bytes 110600 | tf_op jit(solution)/shard_map/ppermute | solution.py:559
  44.8 0.6 %collective-permute-start.9 = (s16[144,128]{1,0:T(8,128)(2,1)S(1)}, s16[144,128]{1,0:T(8,128)(2,1)S(1)}, u32[]{:S(2)}, u32[]{:S(2)}) collective-permute-start(s16[144,128]{1,0:T(8,128)(2,1)S(1)} %get-tuple-element.37), channel_id=1, source_target_pairs={{0,4},{4,0},{8,12},{12,8},{16,20},{20,16},{24,28},{28,24},{1,5},{5... | collective-permute-start | bytes 110600 | tf_op jit(solution)/shard_map/ppermute | solution.py:559
  45.4 0.3 collective-permute-done.6.refs_3_
  45.7 1.1 %collective-permute-done.7.refs_4_ = s16[144,128]{1,0:T(8,128)(2,1)S(1)} collective-permute-done((s16[144,128]{1,0:T(8,128)(2,1)S(1)}, s16[144,128]{1,0:T(8,128)(2,1)S(1)}, u32[]{:S(2)}, u32[]{:S(2)}) %collective-permute-start.7) | collective-permute-done | bytes 36896 | tf_op jit(solution)/shard_map/ppermute | solution.py:559
  46.8 0.4 collective-permute-done.8.refs_5_
  47.2 1.6 %collective-permute-done.9.refs_6_ = s16[144,128]{1,0:T(8,128)(2,1)S(1)} collective-permute-done((s16[144,128]{1,0:T(8,128)(2,1)S(1)}, s16[144,128]{1,0:T(8,128)(2,1)S(1)}, u32[]{:S(2)}, u32[]{:S(2)}) %collective-permute-start.9) | collective-permute-done | bytes 36896 | tf_op jit(solution)/shard_map/ppermute | solution.py:559
  48.8 1.7 %shard_map.66 = f32[1024,128]{1,0:T(8,128)} custom-call(s16[144,128]{1,0:T(8,128)(2,1)S(1)} %collective-permute-done.3.refs_0_, s16[144,128]{1,0:T(8,128)(2,1)S(1)} %collective-permute-done.4.refs_1_, s16[144,128]{1,0:T(8,128)(2,1)S(1)} %collective-permute-done.5.refs_2_, s16[144,128]{1,0:T(8,128)(2,1)S(1)} %collective-permute-done.6.refs_3_, ...), custom_call_target="tpu_custom_call" | custom-call | tf_op jit(solution)/shard_map/pallas_call | solution.py:449
  (11 shorter events, 0.0 us)
Async XLA Ops:
  1.1 17.7 %copy-start = (s32[1,4,16]{2,1,0:T(4,128)S(1)}, s32[1,4,16]{2,1,0:T(4,128)}, u32[]{:S(2)}) copy-start(s32[1,4,16]{2,1,0:T(4,128)} %match_hbm.1) | copy-start | bytes 772
  1.1 17.7 %copy-start.1 = (s32[128,3]{0,1:T(4,128)S(1)}, s32[128,3]{0,1:T(4,128)}, u32[]{:S(2)}) copy-start(s32[128,3]{0,1:T(4,128)} %param.7) | copy-start | bytes 4612
  1.1 17.7 %copy-start.2 = (f32[32,1024]{1,0:T(8,128)S(1)}, f32[32,1024]{1,0:T(8,128)}, u32[]{:S(2)}) copy-start(f32[32,1024]{1,0:T(8,128)} %constant.8.clone.refs_2_) | copy-start | bytes 393220
  1.1 17.7 %copy-start.3 = (f32[64,512]{1,0:T(8,128)S(1)}, f32[64,512]{1,0:T(8,128)}, u32[]{:S(2)}) copy-start(f32[64,512]{1,0:T(8,128)} %constant.7.clone.refs_1_) | copy-start | bytes 393220
  1.1 17.6 %copy-start.4 = (f32[32,512]{1,0:T(8,128)S(1)}, f32[32,512]{1,0:T(8,128)}, u32[]{:S(2)}) copy-start(f32[32,512]{1,0:T(8,128)} %constant.6.clone.refs_0_) | copy-start | bytes 196612
  17.3 6.4 %collective-permute-start = (bf16[8,128,128]{2,1,0:T(8,128)(2,1)S(1)}, bf16[8,128,128]{2,1,0:T(8,128)(2,1)S(1)}, u32[]{:S(2)}, u32[]{:S(2)}) collective-permute-start(bf16[8,128,128]{2,1,0:T(8,128)(2,1)S(1)} %all_to_all.5.own_hbm.refs_0_), channel_id=1, source_target_pairs={{0,2},{1,3},{2,0},{3,1},{4,6},{5,7},{6,4},{7,5},{8,10},{9,11},{10,... | collective-permute-start | bytes 786440 | tf_op jit(solution)/shard_map/ppermute | solution.py:408
  22.1 1.6 %collective-permute-start.1 = (bf16[8,128,128]{2,1,0:T(8,128)(2,1)S(1)}, bf16[8,128,128]{2,1,0:T(8,128)(2,1)S(1)}, u32[]{:S(2)}, u32[]{:S(2)}) collective-permute-start(bf16[8,128,128]{2,1,0:T(8,128)(2,1)S(1)} %all_to_all.5.own_hbm.refs_0_), channel_id=1, source_target_pairs={{0,1},{1,0},{2,3},{3,2},{4,5},{5,4},{6,7},{7,6},{8,9},{9,8},{10,11... | collective-permute-start | bytes 786440 | tf_op jit(solution)/shard_map/ppermute | solution.py:401
  23.6 1.5 %collective-permute-start.2 = (bf16[8,128,128]{2,1,0:T(8,128)(2,1)S(1)}, bf16[8,128,128]{2,1,0:T(8,128)(2,1)S(1)}, u32[]{:S(2)}, u32[]{:S(2)}) collective-permute-start(bf16[8,128,128]{2,1,0:T(8,128)(2,1)S(1)} %collective-permute-done.refs_1_), channel_id=1, source_target_pairs={{0,1},{1,0},{2,3},{3,2},{4,5},{5,4},{6,7},{7,6},{8,9},{9,8},{10,11... | collective-permute-start | bytes 786440 | tf_op jit(solution)/shard_map/ppermute | solution.py:401
  34.2 9.0 %collective-permute-start.3 = (s16[144,128]{1,0:T(8,128)(2,1)S(1)}, s16[144,128]{1,0:T(8,128)(2,1)S(1)}, u32[]{:S(2)}, u32[]{:S(2)}) collective-permute-start(s16[144,128]{1,0:T(8,128)(2,1)S(1)} %get-tuple-element.31), channel_id=1, source_target_pairs={{0,28},{4,24},{8,20},{12,16},{16,12},{20,8},{24,4},{28,0},{1,29},{... | collective-permute-start | bytes 110600 | tf_op jit(solution)/shard_map/ppermute | solution.py:559
  37.9 6.9 %collective-permute-start.4 = (s16[144,128]{1,0:T(8,128)(2,1)S(1)}, s16[144,128]{1,0:T(8,128)(2,1)S(1)}, u32[]{:S(2)}, u32[]{:S(2)}) collective-permute-start(s16[144,128]{1,0:T(8,128)(2,1)S(1)} %get-tuple-element.32), channel_id=1, source_target_pairs={{0,24},{4,28},{8,16},{12,20},{16,8},{20,12},{24,0},{28,4},{1,25},{... | collective-permute-start | bytes 110600 | tf_op jit(solution)/shard_map/ppermute | solution.py:559
  39.0 6.5 %collective-permute-start.5 = (s16[144,128]{1,0:T(8,128)(2,1)S(1)}, s16[144,128]{1,0:T(8,128)(2,1)S(1)}, u32[]{:S(2)}, u32[]{:S(2)}) collective-permute-start(s16[144,128]{1,0:T(8,128)(2,1)S(1)} %get-tuple-element.33), channel_id=1, source_target_pairs={{0,20},{4,16},{8,28},{12,24},{16,4},{20,0},{24,12},{28,8},{1,21},{... | collective-permute-start | bytes 110600 | tf_op jit(solution)/shard_map/ppermute | solution.py:559
  39.4 6.4 %collective-permute-start.6 = (s16[144,128]{1,0:T(8,128)(2,1)S(1)}, s16[144,128]{1,0:T(8,128)(2,1)S(1)}, u32[]{:S(2)}, u32[]{:S(2)}) collective-permute-start(s16[144,128]{1,0:T(8,128)(2,1)S(1)} %get-tuple-element.34), channel_id=1, source_target_pairs={{0,16},{4,20},{8,24},{12,28},{16,0},{20,4},{24,8},{28,12},{1,17},{... | collective-permute-start | bytes 110600 | tf_op jit(solution)/shard_map/ppermute | solution.py:559
  41.9 4.9 %collective-permute-start.7 = (s16[144,128]{1,0:T(8,128)(2,1)S(1)}, s16[144,128]{1,0:T(8,128)(2,1)S(1)}, u32[]{:S(2)}, u32[]{:S(2)}) collective-permute-start(s16[144,128]{1,0:T(8,128)(2,1)S(1)} %get-tuple-element.35), channel_id=1, source_target_pairs={{0,12},{4,8},{8,4},{12,0},{16,28},{20,24},{24,20},{28,16},{1,13},{... | collective-permute-start | bytes 110600 | tf_op jit(solution)/shard_map/ppermute | solution.py:559
  43.2 4.0 %collective-permute-start.8 = (s16[144,128]{1,0:T(8,128)(2,1)S(1)}, s16[144,128]{1,0:T(8,128)(2,1)S(1)}, u32[]{:S(2)}, u32[]{:S(2)}) collective-permute-start(s16[144,128]{1,0:T(8,128)(2,1)S(1)} %get-tuple-element.36), channel_id=1, source_target_pairs={{0,8},{4,12},{8,0},{12,4},{16,24},{20,28},{24,16},{28,20},{1,9},{5... | collective-permute-start | bytes 110600 | tf_op jit(solution)/shard_map/ppermute | solution.py:559
  44.8 4.0 %collective-permute-start.9 = (s16[144,128]{1,0:T(8,128)(2,1)S(1)}, s16[144,128]{1,0:T(8,128)(2,1)S(1)}, u32[]{:S(2)}, u32[]{:S(2)}) collective-permute-start(s16[144,128]{1,0:T(8,128)(2,1)S(1)} %get-tuple-element.37), channel_id=1, source_target_pairs={{0,4},{4,0},{8,12},{12,8},{16,20},{20,16},{24,28},{28,24},{1,5},{5... | collective-permute-start | bytes 110600 | tf_op jit(solution)/shard_map/ppermute | solution.py:559

commit v17 on v16

--- a/solution.py
+++ b/solution.py
@@ -58,12 +58,6 @@
     return jnp.dot(left, right, preferred_element_type=jnp.float32)
 
 
-def partner_of(index, step, count):
-    if count & (count - 1) == 0:
-        return index ^ step, index ^ step
-    return (index + step) % count, (index + count - step) % count
-
-
 def pair_geometry(sizes, match_ref, centers_ref, index):
     _, rounds, own_count, slab_count, _ = sizes
     slab_index = lax.axis_index("slab")
@@ -201,12 +195,12 @@
     side, rounds, own_count, slab_count, pair_count = sizes
     piece_hbm, refs = refs[:pair_count], refs[pair_count:]
     constant_hbm, refs = refs[:3], refs[3:]
-    out_refs, refs = refs[:slab_count], refs[slab_count:]
+    all_codes, refs = refs[0], refs[1:]
     table_ref, mine, partner, boxes_ref, *refs = refs
     constants, refs = refs[:3], refs[3:]
     basis_ref, line_ref, gain_ref = constants
     mix_ref, there_high, there_low, back_high, back_low, *refs = refs
-    fields, first, second, *terms, all_codes, sems = refs
+    fields, first, second, *terms, sems = refs
     planes = side // slab_count
     tiles, lines, pitch = box_shape(sizes)
     solves = own_count * rounds
@@ -214,7 +208,6 @@
     group_rows = group * side
     cells = tiles * LANES
     width = cells // 2
-    slab_index = lax.axis_index("slab")
     pair_index = lax.axis_index("pair")
     core = pair_index % CORES
     chip = pair_index // CORES
@@ -380,8 +373,6 @@
     for slab in range(slab_count):
         header = jnp.concatenate([exponents[slab], factors[slab]], axis=0)
         all_codes[slab, tiles * own_count * planes :, :] = whole_codes(header)
-    for step in range(slab_count):
-        out_refs[step][...] = all_codes[partner_of(slab_index, step, slab_count)[0]]
 
 
 def whole_codes(value):
@@ -411,18 +402,14 @@
 
 def unpack_kernel(sizes, *refs):
     own_count, slab_count, tiles = sizes
-    block_refs, out_ref, blocks, sems = refs[:slab_count], *refs[slab_count:]
-    slab_index = lax.axis_index("slab")
-    copies = []
-    for index in range(slab_count):
-        slab = partner_of(slab_index, slab_count - 1 - index, slab_count)[1]
-        copies.append(pltpu.make_async_copy(block_refs[index], blocks.at[slab], sems.at[index]))
-        copies[-1].start()
+    blocks_hbm, out_ref, blocks, sems = refs
+    copies = [pltpu.make_async_copy(blocks_hbm.at[slab], blocks.at[slab], sems.at[slab]) for slab in range(slab_count)]
     for copy in copies:
-        copy.wait()
+        copy.start()
     row_count = own_count * tiles
     values = {}
     for slab in range(slab_count):
+        copies[slab].wait()
         header = blocks[slab, row_count:, :].astype(jnp.int32).astype(jnp.float32)
         units = jnp.exp2(header[:8, :])
         factors = header[8:, :] * (1.0 / (CODE_LIMIT * FACTOR_UNIT))
@@ -443,20 +430,20 @@
 
 
 def unpack(blocks, own_count, cells):
-    slab_count = len(blocks)
+    slab_count = blocks.shape[0]
     row_count = own_count * slab_count
     tiles = cells // LANES
     out = pl.pallas_call(
         functools.partial(unpack_kernel, (own_count, slab_count, tiles)),
         out_shape=jax.ShapeDtypeStruct((row_count * tiles, LANES), jnp.float32),
-        in_specs=[pl.BlockSpec(memory_space=pl.ANY)] * slab_count,
+        in_specs=[pl.BlockSpec(memory_space=pl.ANY)],
         out_specs=pl.BlockSpec(memory_space=pltpu.VMEM),
         scratch_shapes=[
-            pltpu.VMEM((slab_count,) + blocks[0].shape, jnp.int16),
+            pltpu.VMEM(blocks.shape, jnp.int16),
             pltpu.SemaphoreType.DMA((slab_count,)),
         ],
         compiler_params=pltpu.CompilerParams(vmem_limit_bytes=8 * 1024 * 1024),
-    )(*blocks)
+    )(blocks)
     return out.reshape(row_count // 8, tiles, 8, LANES).transpose(0, 2, 1, 3).reshape(row_count, cells)
 
 
@@ -514,9 +501,9 @@
     inputs = [mine, table, *pieces, *constants]
     return pl.pallas_call(
         functools.partial(force_kernel, sizes),
-        out_shape=[jax.ShapeDtypeStruct((rows + HEADER_ROWS, LANES), jnp.int16)] * slab_count,
+        out_shape=jax.ShapeDtypeStruct((slab_count, rows + HEADER_ROWS, LANES), jnp.int16),
         in_specs=[either] * len(inputs),
-        out_specs=[vectors] * slab_count,
+        out_specs=vectors,
         scratch_shapes=[
             pltpu.SMEM(table.shape, jnp.int32),
             pltpu.VMEM(mine.shape, jnp.bfloat16),
@@ -529,7 +516,6 @@
             wide,
             wide,
             *[pltpu.VMEM((group * tiles * pitch, LANES), jnp.float32)] * (solves // group),
-            pltpu.VMEM((slab_count, rows + HEADER_ROWS, LANES), jnp.int16),
             pltpu.SemaphoreType.DMA((len(inputs),)),
         ],
         compiler_params=pltpu.CompilerParams(vmem_limit_bytes=32 * 1024 * 1024),
@@ -553,11 +539,8 @@
     pieces, mine = lax.optimization_barrier((pieces, mine))
     swapped += [swap_cores(piece, pair_count) for piece in pieces]
     codes = team_forces(sizes, mine, table, constants, [boxes] + pieces + swapped)
-    received = []
-    for step in reversed(range(1, slab_count)):
-        perm = [(i, partner_of(i, step, slab_count)[0]) for i in range(slab_count)]
-        received.append(lax.ppermute(codes[step], "slab", perm))
-    return unpack(received + [codes[0]], own_count, plane_cells)
+    codes = lax.all_to_all(codes, "slab", split_axis=0, concat_axis=0, tiled=True)
+    return unpack(codes, own_count, plane_cells)
 
 
 def solution(mesh):

time: 50.7 us -> 52 us (1.026)
  blocking collectives: 16.1 us -> 31.5 us
  starting transfers between devices: 12.8 us -> 1.56 us
  waiting for transfers between devices: 6.31 us -> 2.97 us
    all_to_all x0 -> x1, blocking collectives: none -> 15.3 us  [shards(): lax.all_to_all(codes, 'slab', split_axis=0, concat_axis=0, tiled=True)]
    ppermute x7 -> x0, starting transfers between devices: 11.2 us -> none  [shards(): received.append(lax.ppermute(codes[step], 'slab', perm))]
    ppermute x7 -> x0, waiting for transfers between devices: 3.35 us -> none  [shards(): received.append(lax.ppermute(codes[step], 'slab', perm))]
  transfers between devices with their start and end apart: 10 -> 3, of which waited for: 7 -> 3; matrix products, arithmetic and copies ran while one was open for 0% -> 0% of each run, Pallas kernels for 7% -> 6%
where the time goes in v17:
time: 52 us; the launch traced here: 51.8 us
  blocking collectives  31.5 us (61%)
  Pallas kernels  14.6 us (28%)
  waiting for transfers between devices  2.97 us (6%)
  starting transfers between devices  1.56 us (3%)
  local copies, waits for them, and re-layouts  1.11 us (2%)
    all_to_all x1, blocking collectives, shards(): lax.all_to_all(blocks, 'slab', split_axis=0, concat_axis=0, tiled=True)  16.1 us
    all_to_all x1, blocking collectives, shards(): lax.all_to_all(codes, 'slab', split_axis=0, concat_axis=0, tiled=True)  15.3 us
    pallas_call x1, Pallas kernels, team_forces(): pl.pallas_call(functools.partial(force_kernel, sizes), out_shape=jax.Shap...  9.02 us
    pallas_call x1, Pallas kernels, place_own(): pl.pallas_call(functools.partial(own_kernel, sizes), out_shape=[jax.Shape...  3.34 us
    pallas_call x1, Pallas kernels, unpack(): pl.pallas_call(functools.partial(unpack_kernel, (own_count, slab_count, t...  2.23 us
    ppermute x2, waiting for transfers between devices, swap_cores(): return lax.ppermute(block, 'pair', [(i, i ^ 1) for i in range(pair_count)])  1.53 us
    ppermute x1, starting transfers between devices, gather_chips(): pieces.append(lax.ppermute(boxes, 'pair', perm))  1.49 us
    ppermute x1, waiting for transfers between devices, gather_chips(): pieces.append(lax.ppermute(boxes, 'pair', perm))  1.43 us
  transfers between devices with their start and end apart: 3, of which 3 were waited for; matrix products, arithmetic and copies ran while one was open for 0% of the time, Pallas kernels for 6%

profile of v17, /device:TPU:0, one launch (start us, length us, event | category | flops | bytes accessed | tf_op | source)
XLA Modules:
  0.0 51.8 jit_solution(10355146281517653029)
XLA Ops:
  0.0 1.1 %reshape.9 = bf16[8,128,128]{2,1,0:T(8,128)(2,1)S(1)} reshape(bf16[32,4096]{1,0:T(8,128)(2,1)} %param.6) | data formatting | bytes 524288 | tf_op jit(solution)/shard_map/reshape | solution.py:532
  1.1 0.0 copy-start
  1.1 0.0 copy-start.1
  1.1 0.0 copy-start.2
  1.1 0.0 copy-start.3
  1.1 0.0 copy-start.4
  1.1 16.1 %all_to_all.10.own_hbm.refs_0_ = bf16[8,128,128]{2,1,0:T(8,128)(2,1)S(1)} all-to-all(bf16[8,128,128]{2,1,0:T(8,128)(2,1)S(1)} %reshape.9), channel_id=1, replica_groups=mesh['slab'=8,'pair'=4] {'slab'}, dimensions={0} | all-to-all | bytes 524288 | tf_op jit(solution)/shard_map/all_to_all | solution.py:533
  17.3 1.5 %collective-permute-start = (bf16[8,128,128]{2,1,0:T(8,128)(2,1)S(1)}, bf16[8,128,128]{2,1,0:T(8,128)(2,1)S(1)}, u32[]{:S(2)}, u32[]{:S(2)}) collective-permute-start(bf16[8,128,128]{2,1,0:T(8,128)(2,1)S(1)} %all_to_all.10.own_hbm.refs_0_), channel_id=1, source_target_pairs={{0,2},{1,3},{2,0},{3,1},{4,6},{5,7},{6,4},{7,5},{8,10},{9,11},{10,... | collective-permute-start | bytes 786440 | tf_op jit(solution)/shard_map/ppermute | solution.py:399
  18.8 0.0 copy-done
  18.8 0.0 copy-done.1
  18.8 0.0 copy-done.2
  18.8 0.0 copy-done.3
  18.8 0.0 copy-done.4
  18.8 3.3 %shard_map.64 = (bf16[512,1024]{1,0:T(8,128)(2,1)S(1)}, s32[128]{0:T(128)S(1)}, f32[32,512]{1,0:T(8,128)S(1)}, f32[64,512]{1,0:T(8,128)S(1)}, f32[32,1024]{1,0:T(8,128)S(1)}) custom-call(s32[1,4,16]{2,1,0:T(4,128)S(1)} %copy-done, s32[3,128]{1,0:T(4,128)S(1)} %bitcast.6, bf16[8,128,128]{2,1,0:T(8,128)(2,1)S(1)} %all_to_all.10.own_hbm.refs_0_, ...), custom_call_target="tpu_custom_call" | custom-call | flops 5000000000 | bytes 4194304 | tf_op jit(solution)/shard_map/pallas_call | solution.py:469
  22.1 0.1 collective-permute-start.1
  22.2 1.4 %collective-permute-done.refs_1_ = bf16[8,128,128]{2,1,0:T(8,128)(2,1)S(1)} collective-permute-done((bf16[8,128,128]{2,1,0:T(8,128)(2,1)S(1)}, bf16[8,128,128]{2,1,0:T(8,128)(2,1)S(1)}, u32[]{:S(2)}, u32[]{:S(2)}) %collective-permute-start) | collective-permute-done | bytes 262176 | tf_op jit(solution)/shard_map/ppermute | solution.py:399
  23.6 0.0 collective-permute-start.2
  23.6 0.1 collective-permute-done.1.refs_2_
  23.7 1.4 %collective-permute-done.2.refs_3_ = bf16[8,128,128]{2,1,0:T(8,128)(2,1)S(1)} collective-permute-done((bf16[8,128,128]{2,1,0:T(8,128)(2,1)S(1)}, bf16[8,128,128]{2,1,0:T(8,128)(2,1)S(1)}, u32[]{:S(2)}, u32[]{:S(2)}) %collective-permute-start.2) | collective-permute-done | bytes 262176 | tf_op jit(solution)/shard_map/ppermute | solution.py:392
  25.2 9.0 %shard_map.65 = s16[8,144,128]{2,1,0:T(8,128)(2,1)S(1)} custom-call(bf16[512,1024]{1,0:T(8,128)(2,1)S(1)} %get-tuple-element.16.mine_hbm, s32[128]{0:T(128)S(1)} %get-tuple-element.17.table_hbm, bf16[8,128,128]{2,1,0:T(8,128)(2,1)S(1)} %all_to_all.10.own_hbm.refs_0_, bf16[8,128,128]{2,1,0:T(8,128)(2,1)S(1)} %collective-permute-done.refs_1_, ...), custom_call_target="tpu_custom_call" | custom-call | flops 4831838208 | bytes 8388608 | tf_op jit(solution)/shard_map/pallas_call | solution.py:502
  34.2 15.3 %all_to_all.11.refs_0_ = s16[8,144,128]{2,1,0:T(8,128)(2,1)S(1)} all-to-all(s16[8,144,128]{2,1,0:T(8,128)(2,1)S(1)} %shard_map.65), channel_id=1, replica_groups=mesh['slab'=8,'pair'=4] {'slab'}, dimensions={0} | all-to-all | bytes 589824 | tf_op jit(solution)/shard_map/all_to_all | solution.py:542
  49.6 2.2 %shard_map.66 = f32[1024,128]{1,0:T(8,128)} custom-call(s16[8,144,128]{2,1,0:T(8,128)(2,1)S(1)} %all_to_all.11.refs_0_), custom_call_target="tpu_custom_call" | custom-call | tf_op jit(solution)/shard_map/pallas_call | solution.py:436
Async XLA Ops:
  1.1 17.7 %copy-start = (s32[1,4,16]{2,1,0:T(4,128)S(1)}, s32[1,4,16]{2,1,0:T(4,128)}, u32[]{:S(2)}) copy-start(s32[1,4,16]{2,1,0:T(4,128)} %match_hbm.1) | copy-start | bytes 772
  1.1 17.7 %copy-start.1 = (s32[128,3]{0,1:T(4,128)S(1)}, s32[128,3]{0,1:T(4,128)}, u32[]{:S(2)}) copy-start(s32[128,3]{0,1:T(4,128)} %param.7) | copy-start | bytes 4612
  1.1 17.7 %copy-start.2 = (f32[32,1024]{1,0:T(8,128)S(1)}, f32[32,1024]{1,0:T(8,128)}, u32[]{:S(2)}) copy-start(f32[32,1024]{1,0:T(8,128)} %constant.8.clone.refs_2_) | copy-start | bytes 393220
  1.1 17.7 %copy-start.3 = (f32[64,512]{1,0:T(8,128)S(1)}, f32[64,512]{1,0:T(8,128)}, u32[]{:S(2)}) copy-start(f32[64,512]{1,0:T(8,128)} %constant.7.clone.refs_1_) | copy-start | bytes 393220
  1.1 17.6 %copy-start.4 = (f32[32,512]{1,0:T(8,128)S(1)}, f32[32,512]{1,0:T(8,128)}, u32[]{:S(2)}) copy-start(f32[32,512]{1,0:T(8,128)} %constant.6.clone.refs_0_) | copy-start | bytes 196612
  17.3 6.4 %collective-permute-start = (bf16[8,128,128]{2,1,0:T(8,128)(2,1)S(1)}, bf16[8,128,128]{2,1,0:T(8,128)(2,1)S(1)}, u32[]{:S(2)}, u32[]{:S(2)}) collective-permute-start(bf16[8,128,128]{2,1,0:T(8,128)(2,1)S(1)} %all_to_all.10.own_hbm.refs_0_), channel_id=1, source_target_pairs={{0,2},{1,3},{2,0},{3,1},{4,6},{5,7},{6,4},{7,5},{8,10},{9,11},{10,... | collective-permute-start | bytes 786440 | tf_op jit(solution)/shard_map/ppermute | solution.py:399
  22.1 1.6 %collective-permute-start.1 = (bf16[8,128,128]{2,1,0:T(8,128)(2,1)S(1)}, bf16[8,128,128]{2,1,0:T(8,128)(2,1)S(1)}, u32[]{:S(2)}, u32[]{:S(2)}) collective-permute-start(bf16[8,128,128]{2,1,0:T(8,128)(2,1)S(1)} %all_to_all.10.own_hbm.refs_0_), channel_id=1, source_target_pairs={{0,1},{1,0},{2,3},{3,2},{4,5},{5,4},{6,7},{7,6},{8,9},{9,8},{10,11... | collective-permute-start | bytes 786440 | tf_op jit(solution)/shard_map/ppermute | solution.py:392
  23.6 1.5 %collective-permute-start.2 = (bf16[8,128,128]{2,1,0:T(8,128)(2,1)S(1)}, bf16[8,128,128]{2,1,0:T(8,128)(2,1)S(1)}, u32[]{:S(2)}, u32[]{:S(2)}) collective-permute-start(bf16[8,128,128]{2,1,0:T(8,128)(2,1)S(1)} %collective-permute-done.refs_1_), channel_id=1, source_target_pairs={{0,1},{1,0},{2,3},{3,2},{4,5},{5,4},{6,7},{7,6},{8,9},{9,8},{10,11... | collective-permute-start | bytes 786440 | tf_op jit(solution)/shard_map/ppermute | solution.py:392

commit v18 on v16

--- a/solution.py
+++ b/solution.py
@@ -167,20 +167,47 @@
     return result
 
 
+def make_matrices(basis_ref, line_ref, first_line, high_ref, low_ref):
+    side = basis_ref.shape[0]
+    count = side // 2
+    for parity in range(2):
+        for index in range(count):
+            line = first_line + parity * count + index
+            rows = slice(index * side, (index + 1) * side)
+            value = basis_ref[...] * line_ref[line : line + 1, :]
+            high_ref[parity, rows, :], low_ref[parity, rows, :] = split_pair(value)
+
+
+def make_mix(basis_ref, mix_ref):
+    side = basis_ref.shape[0]
+    width = mix_ref.shape[0]
+    block = lax.broadcasted_iota(jnp.int32, (side, width), 1) // side
+    for index in range(width // side):
+        rows = slice(index * side, (index + 1) * side)
+        high, low = split_pair(jnp.where(block == index, basis_ref[:, :width], 0.0))
+        for part, piece in enumerate((high, high, low)):
+            mix_ref[rows, part * width : (part + 1) * width] = piece
+
+
 def own_kernel(sizes, match_hbm, centers_hbm, own_hbm, *refs):
     constant_hbm, refs = refs[:3], refs[3:]
-    mine_ref, table_ref, *constant_refs = refs[:5]
-    match_ref, centers_ref, boxes_ref, fields, sems = refs[5:]
+    mine_ref, table_ref, mix_ref, gain_ref, there_high, there_low, back_high, back_low = refs[:8]
+    match_ref, centers_ref, boxes_ref, basis_ref, line_ref, fields, sems = refs[8:]
     side, rounds, own_count, _, _ = sizes
     tiles, _, _ = box_shape(sizes)
     first_member = lax.axis_index("pair") * own_count
-    sources = (match_hbm, centers_hbm, own_hbm, *constant_hbm)
-    targets = (match_ref, centers_ref, boxes_ref.at[0], *constant_refs)
+    sources = (*constant_hbm, match_hbm, centers_hbm, own_hbm)
+    targets = (basis_ref, line_ref, gain_ref, match_ref, centers_ref, boxes_ref.at[0])
     copies = [pltpu.make_async_copy(s, t, sems.at[i]) for i, (s, t) in enumerate(zip(sources, targets))]
     for copy in copies:
         copy.start()
     clear_edges(sizes, fields, 0, own_count)
-    for copy in copies:
+    for copy in copies[:2]:
+        copy.wait()
+    make_mix(basis_ref, mix_ref)
+    make_matrices(basis_ref, line_ref, 0, there_high, there_low)
+    make_matrices(basis_ref, line_ref, side, back_high, back_low)
+    for copy in copies[2:]:
         copy.wait()
     spread(sizes, boxes_ref, fields, 0)
 
@@ -200,12 +227,11 @@
 def force_kernel(sizes, mine_hbm, table_hbm, *refs):
     side, rounds, own_count, slab_count, pair_count = sizes
     piece_hbm, refs = refs[:pair_count], refs[pair_count:]
-    constant_hbm, refs = refs[:3], refs[3:]
+    constant_hbm, refs = refs[:6], refs[6:]
     out_refs, refs = refs[:slab_count], refs[slab_count:]
     table_ref, mine, partner, boxes_ref, *refs = refs
-    constants, refs = refs[:3], refs[3:]
-    basis_ref, line_ref, gain_ref = constants
-    mix_ref, there_high, there_low, back_high, back_low, *refs = refs
+    constants, refs = refs[:6], refs[6:]
+    mix_ref, gain_ref, there_high, there_low, back_high, back_low = constants
     fields, first, second, *terms, all_codes, sems = refs
     planes = side // slab_count
     tiles, lines, pitch = box_shape(sizes)
@@ -225,8 +251,8 @@
         for core_step in range(CORES)
         for step in range(chips)
     ]
-    sources = [table_hbm, *constant_hbm, *piece_hbm, mine_hbm]
-    targets = [table_ref, *constants, *[boxes_ref.at[pair] for pair in places], mine]
+    sources = [table_hbm, *piece_hbm, mine_hbm, *constant_hbm]
+    targets = [table_ref, *[boxes_ref.at[pair] for pair in places], mine, *constants]
     copies = [pltpu.make_async_copy(s, t, sems.at[i]) for i, (s, t) in enumerate(zip(sources, targets))]
     for copy in copies:
         copy.start()
@@ -234,32 +260,13 @@
         clear_edges(sizes, fields, pair * own_count, own_count)
     for ref in terms:
         clear_edges(sizes, ref, 0, group)
-    for copy in copies[:4]:
-        copy.wait()
-
-    def make_matrices(first_line, high_ref, low_ref):
-        count = side // 2
-        for parity in range(2):
-            for index in range(count):
-                line = first_line + parity * count + index
-                rows = slice(index * side, (index + 1) * side)
-                value = basis_ref[...] * line_ref[line : line + 1, :]
-                high_ref[parity, rows, :], low_ref[parity, rows, :] = split_pair(value)
-
-    block = lax.broadcasted_iota(jnp.int32, (side, group_rows), 1) // side
-    for index in range(group):
-        rows = slice(index * side, (index + 1) * side)
-        value = jnp.where(block == index, basis_ref[:, :group_rows], 0.0)
-        high, low = split_pair(value)
-        for part, piece in enumerate((high, high, low)):
-            mix_ref[rows, part * group_rows : (part + 1) * group_rows] = piece
-    make_matrices(0, there_high, there_low)
-
-    for copy in copies[4:-1]:
+    table_copy, *piece_copies, mine_copy, mix_copy, gain_copy = copies[: pair_count + 4]
+    there_copies, back_copies = copies[pair_count + 4 : pair_count + 6], copies[pair_count + 6 :]
+    for copy in (table_copy, *piece_copies):
         copy.wait()
     for pair in places:
         spread(sizes, boxes_ref, fields, pair)
-    copies[-1].wait()
+    mine_copy.wait()
 
     row_count = solves * side
     half_tiles = tiles // 2
@@ -310,13 +317,15 @@
         left = jnp.concatenate([high, low, high], axis=1)
         return dot(left, jnp.concatenate([basis, basis, rest], axis=0))
 
+    mix_copy.wait()
     for start in range(0, row_count, group_rows):
         for index in range(start // side, (start + group_rows) // side):
             densities(index)
         columns = slice(0, cells)
         store_split(second, start, group_rows, columns, along_x(start, columns, first))
 
-    make_matrices(side, back_high, back_low)
+    for copy in (gain_copy, *there_copies):
+        copy.wait()
     for parity in range(2):
         for column in range(0, half_cells, width):
             columns = slice(column, column + width)
@@ -326,6 +335,8 @@
             value = (value.reshape(solves, side, width) * gain[None]).reshape(row_count, width)
             store_split(first, 0, row_count, columns, value)
 
+    for copy in back_copies:
+        copy.wait()
     for parity in range(2):
         for column in range(0, half_cells, width):
             value = in_plane(parity, slice(column, column + width), first, back_high, back_low)
@@ -476,6 +487,9 @@
     tiles, _, pitch = box_shape(sizes)
     solves = own_count * rounds
     constants = kernel_constants(side)
+    group_rows = min(solves, 8) * side
+    half_cells = side * side // 2
+    matrix = jax.ShapeDtypeStruct((2, half_cells, half_cells), jnp.bfloat16)
     inputs = [match, centers, boxes, *constants]
     either = pl.BlockSpec(memory_space=pl.ANY)
     vectors = pl.BlockSpec(memory_space=pltpu.VMEM)
@@ -484,14 +498,18 @@
         out_shape=[
             jax.ShapeDtypeStruct((solves * side, side * side), jnp.bfloat16),
             jax.ShapeDtypeStruct((solves * ENTRIES,), jnp.int32),
-            *[jax.ShapeDtypeStruct(constant.shape, constant.dtype) for constant in constants],
+            jax.ShapeDtypeStruct((group_rows, 3 * group_rows), jnp.bfloat16),
+            jax.ShapeDtypeStruct(constants[2].shape, jnp.float32),
+            *[matrix] * 4,
         ],
         in_specs=[either] * len(inputs),
-        out_specs=[vectors, pl.BlockSpec(memory_space=pltpu.SMEM)] + [vectors] * len(constants),
+        out_specs=[vectors, pl.BlockSpec(memory_space=pltpu.SMEM)] + [vectors] * 6,
         scratch_shapes=[
             pltpu.SMEM(match.shape, jnp.int32),
             pltpu.SMEM(centers.shape, jnp.int32),
             pltpu.VMEM((1,) + boxes.shape, jnp.bfloat16),
+            pltpu.VMEM(constants[0].shape, jnp.float32),
+            pltpu.VMEM(constants[1].shape, jnp.float32),
             pltpu.VMEM((own_count * tiles * pitch, LANES), jnp.float32),
             pltpu.SemaphoreType.DMA((len(inputs),)),
         ],
@@ -523,8 +541,6 @@
             pltpu.VMEM(mine.shape, jnp.bfloat16),
             pltpu.VMEM((pair_count, slab_count, rows, LANES), jnp.bfloat16),
             *[pltpu.VMEM(constant.shape, constant.dtype) for constant in constants],
-            pltpu.VMEM((group * side, 3 * group * side), jnp.bfloat16),
-            *[pltpu.VMEM((2, cells // 2, cells // 2), jnp.bfloat16)] * 4,
             pltpu.VMEM((own_count * pair_count * tiles * pitch, LANES), jnp.float32),
             wide,
             wide,

time: 50.7 us -> 51 us (level)
  Pallas kernels: 14.1 us -> 15 us
  waiting for transfers between devices: 6.31 us -> 5.74 us
    pallas_call x1, Pallas kernels: 3.34 us -> 3.91 us  [place_own(): pl.pallas_call(functools.partial(own_kernel, sizes), out_shape=[jax.Shape...]
    ppermute x1, waiting for transfers between devices: 1.43 us -> 0.86 us  [gather_chips(): pieces.append(lax.ppermute(boxes, 'pair', perm))]
  transfers between devices with their start and end apart: 10 -> 10, of which waited for: 7 -> 7; matrix products, arithmetic and copies ran while one was open for 0% -> 0% of each run, Pallas kernels for 7% -> 8%
where the time goes in v18:
time: 51 us; the launch traced here: 50.8 us
  blocking collectives  16.1 us (32%)
  Pallas kernels  15 us (29%)
  starting transfers between devices  12.8 us (25%)
  waiting for transfers between devices  5.74 us (11%)
  local copies, waits for them, and re-layouts  1.11 us (2%)
    all_to_all x1, blocking collectives, shards(): lax.all_to_all(blocks, 'slab', split_axis=0, concat_axis=0, tiled=True)  16.1 us
    ppermute x7, starting transfers between devices, shards(): received.append(lax.ppermute(codes[step], 'slab', perm))  11.2 us
    pallas_call x1, Pallas kernels, team_forces(): pl.pallas_call(functools.partial(force_kernel, sizes), out_shape=[jax.Sha...  9.36 us
    pallas_call x1, Pallas kernels, place_own(): pl.pallas_call(functools.partial(own_kernel, sizes), out_shape=[jax.Shape...  3.91 us
    ppermute x7, waiting for transfers between devices, shards(): received.append(lax.ppermute(codes[step], 'slab', perm))  3.35 us
    pallas_call x1, Pallas kernels, unpack(): pl.pallas_call(functools.partial(unpack_kernel, (own_count, slab_count, t...  1.74 us
    ppermute x2, waiting for transfers between devices, swap_cores(): return lax.ppermute(block, 'pair', [(i, i ^ 1) for i in range(pair_count)])  1.53 us
    ppermute x1, starting transfers between devices, gather_chips(): pieces.append(lax.ppermute(boxes, 'pair', perm))  1.49 us
  transfers between devices with their start and end apart: 10, of which 7 were waited for; matrix products, arithmetic and copies ran while one was open for 0% of the time, Pallas kernels for 8%

profile of v18, /device:TPU:0, one launch (start us, length us, event | category | flops | bytes accessed | tf_op | source)
XLA Modules:
  0.0 50.8 jit_solution(13174826585163915591)
XLA Ops:
  0.0 1.1 %reshape.9 = bf16[8,128,128]{2,1,0:T(8,128)(2,1)S(1)} reshape(bf16[32,4096]{1,0:T(8,128)(2,1)} %param.6) | data formatting | bytes 524288 | tf_op jit(solution)/shard_map/reshape | solution.py:562
  1.1 0.0 copy-start.2
  1.1 0.0 copy-start.3
  1.1 0.0 copy-start.4
  1.1 16.1 %all_to_all.5.own_hbm.refs_0_ = bf16[8,128,128]{2,1,0:T(8,128)(2,1)S(1)} all-to-all(bf16[8,128,128]{2,1,0:T(8,128)(2,1)S(1)} %reshape.9), channel_id=1, replica_groups=mesh['slab'=8,'pair'=4] {'slab'}, dimensions={0} | all-to-all | bytes 524288 | tf_op jit(solution)/shard_map/all_to_all | solution.py:563
  17.3 1.5 %collective-permute-start = (bf16[8,128,128]{2,1,0:T(8,128)(2,1)S(1)}, bf16[8,128,128]{2,1,0:T(8,128)(2,1)S(1)}, u32[]{:S(2)}, u32[]{:S(2)}) collective-permute-start(bf16[8,128,128]{2,1,0:T(8,128)(2,1)S(1)} %all_to_all.5.own_hbm.refs_0_), channel_id=1, source_target_pairs={{0,2},{1,3},{2,0},{3,1},{4,6},{5,7},{6,4},{7,5},{8,10},{9,11},{10,... | collective-permute-start | bytes 786440 | tf_op jit(solution)/shard_map/ppermute | solution.py:419
  18.8 3.9 %shard_map.64 = (bf16[512,1024]{1,0:T(8,128)(2,1)S(1)}, s32[128]{0:T(128)S(1)}, bf16[256,768]{1,0:T(8,128)(2,1)S(1)}, f32[32,1024]{1,0:T(8,128)S(1)}, bf16[2,512...) custom-call(s32[1,4,16]{2,1,0:T(4,128)S(1)} %copy-done, ...), custom_call_target="tpu_custom_call" | custom-call | flops 5000000000 | bytes 4194304 | tf_op jit(solution)/shard_map/pallas_call | solution.py:496
  22.7 0.1 collective-permute-start.1
  22.8 0.9 %collective-permute-done.refs_1_ = bf16[8,128,128]{2,1,0:T(8,128)(2,1)S(1)} collective-permute-done((bf16[8,128,128]{2,1,0:T(8,128)(2,1)S(1)}, bf16[8,128,128]{2,1,0:T(8,128)(2,1)S(1)}, u32[]{:S(2)}, u32[]{:S(2)}) %collective-permute-start) | collective-permute-done | bytes 262176 | tf_op jit(solution)/shard_map/ppermute | solution.py:419
  23.6 0.7 %collective-permute-done.1.refs_2_ = bf16[8,128,128]{2,1,0:T(8,128)(2,1)S(1)} collective-permute-done((bf16[8,128,128]{2,1,0:T(8,128)(2,1)S(1)}, bf16[8,128,128]{2,1,0:T(8,128)(2,1)S(1)}, u32[]{:S(2)}, u32[]{:S(2)}) %collective-permute-start.1) | collective-permute-done | bytes 262176 | tf_op jit(solution)/shard_map/ppermute | solution.py:412
  24.3 0.9 %collective-permute-done.2.refs_3_ = bf16[8,128,128]{2,1,0:T(8,128)(2,1)S(1)} collective-permute-done((bf16[8,128,128]{2,1,0:T(8,128)(2,1)S(1)}, bf16[8,128,128]{2,1,0:T(8,128)(2,1)S(1)}, u32[]{:S(2)}, u32[]{:S(2)}) %collective-permute-start.2) | collective-permute-done | bytes 262176 | tf_op jit(solution)/shard_map/ppermute | solution.py:412
  25.2 9.4 %shard_map.65 = (s16[144,128]{1,0:T(8,128)(2,1)S(1)}, s16[144,128]{1,0:T(8,128)(2,1)S(1)}, s16[144,128]{1,0:T(8,128)(2,1)S(1)}, s16[144,128]{1,0:T(8,128)(2,1)S(...) custom-call(bf16[512,1024]{1,0:T(8,128)(2,1)S(1)} %get-tuple-element, ...), custom_call_target="tpu_custom_call" | custom-call | flops 4831838208 | bytes 8388608 | tf_op jit(solution)/shard_map/pallas_call | solution.py:533
  34.5 3.7 %collective-permute-start.3 = (s16[144,128]{1,0:T(8,128)(2,1)S(1)}, s16[144,128]{1,0:T(8,128)(2,1)S(1)}, u32[]{:S(2)}, u32[]{:S(2)}) collective-permute-start(s16[144,128]{1,0:T(8,128)(2,1)S(1)} %get-tuple-element.37), channel_id=1, source_target_pairs={{0,28},{4,24},{8,20},{12,16},{16,12},{20,8},{24,4},{28,0},{1,29},{... | collective-permute-start | bytes 110600 | tf_op jit(solution)/shard_map/ppermute | solution.py:575
  38.2 1.0 %collective-permute-start.4 = (s16[144,128]{1,0:T(8,128)(2,1)S(1)}, s16[144,128]{1,0:T(8,128)(2,1)S(1)}, u32[]{:S(2)}, u32[]{:S(2)}) collective-permute-start(s16[144,128]{1,0:T(8,128)(2,1)S(1)} %get-tuple-element.38), channel_id=1, source_target_pairs={{0,24},{4,28},{8,16},{12,20},{16,8},{20,12},{24,0},{28,4},{1,25},{... | collective-permute-start | bytes 110600 | tf_op jit(solution)/shard_map/ppermute | solution.py:575
  39.3 0.4 collective-permute-start.5
  39.7 2.6 %collective-permute-start.6 = (s16[144,128]{1,0:T(8,128)(2,1)S(1)}, s16[144,128]{1,0:T(8,128)(2,1)S(1)}, u32[]{:S(2)}, u32[]{:S(2)}) collective-permute-start(s16[144,128]{1,0:T(8,128)(2,1)S(1)} %get-tuple-element.40), channel_id=1, source_target_pairs={{0,16},{4,20},{8,24},{12,28},{16,0},{20,4},{24,8},{28,12},{1,17},{... | collective-permute-start | bytes 110600 | tf_op jit(solution)/shard_map/ppermute | solution.py:575
  42.3 1.3 %collective-permute-start.7 = (s16[144,128]{1,0:T(8,128)(2,1)S(1)}, s16[144,128]{1,0:T(8,128)(2,1)S(1)}, u32[]{:S(2)}, u32[]{:S(2)}) collective-permute-start(s16[144,128]{1,0:T(8,128)(2,1)S(1)} %get-tuple-element.41), channel_id=1, source_target_pairs={{0,12},{4,8},{8,4},{12,0},{16,28},{20,24},{24,20},{28,16},{1,13},{... | collective-permute-start | bytes 110600 | tf_op jit(solution)/shard_map/ppermute | solution.py:575
  43.5 1.6 %collective-permute-start.8 = (s16[144,128]{1,0:T(8,128)(2,1)S(1)}, s16[144,128]{1,0:T(8,128)(2,1)S(1)}, u32[]{:S(2)}, u32[]{:S(2)}) collective-permute-start(s16[144,128]{1,0:T(8,128)(2,1)S(1)} %get-tuple-element.42), channel_id=1, source_target_pairs={{0,8},{4,12},{8,0},{12,4},{16,24},{20,28},{24,16},{28,20},{1,9},{5... | collective-permute-start | bytes 110600 | tf_op jit(solution)/shard_map/ppermute | solution.py:575
  45.1 0.6 %collective-permute-start.9 = (s16[144,128]{1,0:T(8,128)(2,1)S(1)}, s16[144,128]{1,0:T(8,128)(2,1)S(1)}, u32[]{:S(2)}, u32[]{:S(2)}) collective-permute-start(s16[144,128]{1,0:T(8,128)(2,1)S(1)} %get-tuple-element.43), channel_id=1, source_target_pairs={{0,4},{4,0},{8,12},{12,8},{16,20},{20,16},{24,28},{28,24},{1,5},{5... | collective-permute-start | bytes 110600 | tf_op jit(solution)/shard_map/ppermute | solution.py:575
  45.8 0.3 collective-permute-done.6.refs_3_
  46.0 1.1 %collective-permute-done.7.refs_4_ = s16[144,128]{1,0:T(8,128)(2,1)S(1)} collective-permute-done((s16[144,128]{1,0:T(8,128)(2,1)S(1)}, s16[144,128]{1,0:T(8,128)(2,1)S(1)}, u32[]{:S(2)}, u32[]{:S(2)}) %collective-permute-start.7) | collective-permute-done | bytes 36896 | tf_op jit(solution)/shard_map/ppermute | solution.py:575
  47.1 0.4 collective-permute-done.8.refs_5_
  47.5 1.6 %collective-permute-done.9.refs_6_ = s16[144,128]{1,0:T(8,128)(2,1)S(1)} collective-permute-done((s16[144,128]{1,0:T(8,128)(2,1)S(1)}, s16[144,128]{1,0:T(8,128)(2,1)S(1)}, u32[]{:S(2)}, u32[]{:S(2)}) %collective-permute-start.9) | collective-permute-done | bytes 36896 | tf_op jit(solution)/shard_map/ppermute | solution.py:575
  49.1 1.7 %shard_map.66 = f32[1024,128]{1,0:T(8,128)} custom-call(s16[144,128]{1,0:T(8,128)(2,1)S(1)} %collective-permute-done.3.refs_0_, s16[144,128]{1,0:T(8,128)(2,1)S(1)} %collective-permute-done.4.refs_1_, s16[144,128]{1,0:T(8,128)(2,1)S(1)} %collective-permute-done.5.refs_2_, s16[144,128]{1,0:T(8,128)(2,1)S(1)} %collective-permute-done.6.refs_3_, ...), custom_call_target="tpu_custom_call" | custom-call | tf_op jit(solution)/shard_map/pallas_call | solution.py:460
  (11 shorter events, 0.0 us)
Async XLA Ops:
  1.1 17.7 %copy-start = (s32[1,4,16]{2,1,0:T(4,128)S(1)}, s32[1,4,16]{2,1,0:T(4,128)}, u32[]{:S(2)}) copy-start(s32[1,4,16]{2,1,0:T(4,128)} %match_hbm.1) | copy-start | bytes 772
  1.1 17.7 %copy-start.1 = (s32[128,3]{0,1:T(4,128)S(1)}, s32[128,3]{0,1:T(4,128)}, u32[]{:S(2)}) copy-start(s32[128,3]{0,1:T(4,128)} %param.7) | copy-start | bytes 4612
  1.1 17.7 %copy-start.2 = (f32[32,1024]{1,0:T(8,128)S(1)}, f32[32,1024]{1,0:T(8,128)}, u32[]{:S(2)}) copy-start(f32[32,1024]{1,0:T(8,128)} %constant.8.clone.refs_2_) | copy-start | bytes 393220
  1.1 17.7 %copy-start.3 = (f32[64,512]{1,0:T(8,128)S(1)}, f32[64,512]{1,0:T(8,128)}, u32[]{:S(2)}) copy-start(f32[64,512]{1,0:T(8,128)} %constant.7.clone.refs_1_) | copy-start | bytes 393220
  1.1 17.6 %copy-start.4 = (f32[32,512]{1,0:T(8,128)S(1)}, f32[32,512]{1,0:T(8,128)}, u32[]{:S(2)}) copy-start(f32[32,512]{1,0:T(8,128)} %constant.6.clone.refs_0_) | copy-start | bytes 196612
  17.3 6.4 %collective-permute-start = (bf16[8,128,128]{2,1,0:T(8,128)(2,1)S(1)}, bf16[8,128,128]{2,1,0:T(8,128)(2,1)S(1)}, u32[]{:S(2)}, u32[]{:S(2)}) collective-permute-start(bf16[8,128,128]{2,1,0:T(8,128)(2,1)S(1)} %all_to_all.5.own_hbm.refs_0_), channel_id=1, source_target_pairs={{0,2},{1,3},{2,0},{3,1},{4,6},{5,7},{6,4},{7,5},{8,10},{9,11},{10,... | collective-permute-start | bytes 786440 | tf_op jit(solution)/shard_map/ppermute | solution.py:419
  22.7 1.6 %collective-permute-start.1 = (bf16[8,128,128]{2,1,0:T(8,128)(2,1)S(1)}, bf16[8,128,128]{2,1,0:T(8,128)(2,1)S(1)}, u32[]{:S(2)}, u32[]{:S(2)}) collective-permute-start(bf16[8,128,128]{2,1,0:T(8,128)(2,1)S(1)} %all_to_all.5.own_hbm.refs_0_), channel_id=1, source_target_pairs={{0,1},{1,0},{2,3},{3,2},{4,5},{5,4},{6,7},{7,6},{8,9},{9,8},{10,11... | collective-permute-start | bytes 786440 | tf_op jit(solution)/shard_map/ppermute | solution.py:412
  23.6 1.5 %collective-permute-start.2 = (bf16[8,128,128]{2,1,0:T(8,128)(2,1)S(1)}, bf16[8,128,128]{2,1,0:T(8,128)(2,1)S(1)}, u32[]{:S(2)}, u32[]{:S(2)}) collective-permute-start(bf16[8,128,128]{2,1,0:T(8,128)(2,1)S(1)} %collective-permute-done.refs_1_), channel_id=1, source_target_pairs={{0,1},{1,0},{2,3},{3,2},{4,5},{5,4},{6,7},{7,6},{8,9},{9,8},{10,11... | collective-permute-start | bytes 786440 | tf_op jit(solution)/shard_map/ppermute | solution.py:412
  34.5 9.0 %collective-permute-start.3 = (s16[144,128]{1,0:T(8,128)(2,1)S(1)}, s16[144,128]{1,0:T(8,128)(2,1)S(1)}, u32[]{:S(2)}, u32[]{:S(2)}) collective-permute-start(s16[144,128]{1,0:T(8,128)(2,1)S(1)} %get-tuple-element.37), channel_id=1, source_target_pairs={{0,28},{4,24},{8,20},{12,16},{16,12},{20,8},{24,4},{28,0},{1,29},{... | collective-permute-start | bytes 110600 | tf_op jit(solution)/shard_map/ppermute | solution.py:575
  38.2 6.9 %collective-permute-start.4 = (s16[144,128]{1,0:T(8,128)(2,1)S(1)}, s16[144,128]{1,0:T(8,128)(2,1)S(1)}, u32[]{:S(2)}, u32[]{:S(2)}) collective-permute-start(s16[144,128]{1,0:T(8,128)(2,1)S(1)} %get-tuple-element.38), channel_id=1, source_target_pairs={{0,24},{4,28},{8,16},{12,20},{16,8},{20,12},{24,0},{28,4},{1,25},{... | collective-permute-start | bytes 110600 | tf_op jit(solution)/shard_map/ppermute | solution.py:575
  39.3 6.5 %collective-permute-start.5 = (s16[144,128]{1,0:T(8,128)(2,1)S(1)}, s16[144,128]{1,0:T(8,128)(2,1)S(1)}, u32[]{:S(2)}, u32[]{:S(2)}) collective-permute-start(s16[144,128]{1,0:T(8,128)(2,1)S(1)} %get-tuple-element.39), channel_id=1, source_target_pairs={{0,20},{4,16},{8,28},{12,24},{16,4},{20,0},{24,12},{28,8},{1,21},{... | collective-permute-start | bytes 110600 | tf_op jit(solution)/shard_map/ppermute | solution.py:575
  39.7 6.4 %collective-permute-start.6 = (s16[144,128]{1,0:T(8,128)(2,1)S(1)}, s16[144,128]{1,0:T(8,128)(2,1)S(1)}, u32[]{:S(2)}, u32[]{:S(2)}) collective-permute-start(s16[144,128]{1,0:T(8,128)(2,1)S(1)} %get-tuple-element.40), channel_id=1, source_target_pairs={{0,16},{4,20},{8,24},{12,28},{16,0},{20,4},{24,8},{28,12},{1,17},{... | collective-permute-start | bytes 110600 | tf_op jit(solution)/shard_map/ppermute | solution.py:575
  42.3 4.9 %collective-permute-start.7 = (s16[144,128]{1,0:T(8,128)(2,1)S(1)}, s16[144,128]{1,0:T(8,128)(2,1)S(1)}, u32[]{:S(2)}, u32[]{:S(2)}) collective-permute-start(s16[144,128]{1,0:T(8,128)(2,1)S(1)} %get-tuple-element.41), channel_id=1, source_target_pairs={{0,12},{4,8},{8,4},{12,0},{16,28},{20,24},{24,20},{28,16},{1,13},{... | collective-permute-start | bytes 110600 | tf_op jit(solution)/shard_map/ppermute | solution.py:575
  43.5 4.0 %collective-permute-start.8 = (s16[144,128]{1,0:T(8,128)(2,1)S(1)}, s16[144,128]{1,0:T(8,128)(2,1)S(1)}, u32[]{:S(2)}, u32[]{:S(2)}) collective-permute-start(s16[144,128]{1,0:T(8,128)(2,1)S(1)} %get-tuple-element.42), channel_id=1, source_target_pairs={{0,8},{4,12},{8,0},{12,4},{16,24},{20,28},{24,16},{28,20},{1,9},{5... | collective-permute-start | bytes 110600 | tf_op jit(solution)/shard_map/ppermute | solution.py:575
  45.1 4.0 %collective-permute-start.9 = (s16[144,128]{1,0:T(8,128)(2,1)S(1)}, s16[144,128]{1,0:T(8,128)(2,1)S(1)}, u32[]{:S(2)}, u32[]{:S(2)}) collective-permute-start(s16[144,128]{1,0:T(8,128)(2,1)S(1)} %get-tuple-element.43), channel_id=1, source_target_pairs={{0,4},{4,0},{8,12},{12,8},{16,20},{20,16},{24,28},{28,24},{1,5},{5... | collective-permute-start | bytes 110600 | tf_op jit(solution)/shard_map/ppermute | solution.py:575

commit v19 on v16

--- a/solution.py
+++ b/solution.py
@@ -380,8 +380,13 @@
     for slab in range(slab_count):
         header = jnp.concatenate([exponents[slab], factors[slab]], axis=0)
         all_codes[slab, tiles * own_count * planes :, :] = whole_codes(header)
+    copies = []
     for step in range(slab_count):
-        out_refs[step][...] = all_codes[partner_of(slab_index, step, slab_count)[0]]
+        slab = partner_of(slab_index, step, slab_count)[0]
+        copies.append(pltpu.make_async_copy(all_codes.at[slab], out_refs[step], sems.at[step]))
+        copies[-1].start()
+    for copy in copies:
+        copy.wait()
 
 
 def whole_codes(value):
@@ -411,7 +416,7 @@
 
 def unpack_kernel(sizes, *refs):
     own_count, slab_count, tiles = sizes
-    block_refs, out_ref, blocks, sems = refs[:slab_count], *refs[slab_count:]
+    block_refs, out_hbm, blocks, out_ref, sems, out_sems = refs[:slab_count], *refs[slab_count:]
     slab_index = lax.axis_index("slab")
     copies = []
     for index in range(slab_count):
@@ -422,6 +427,7 @@
         copy.wait()
     row_count = own_count * tiles
     values = {}
+    copies = []
     for slab in range(slab_count):
         header = blocks[slab, row_count:, :].astype(jnp.int32).astype(jnp.float32)
         units = jnp.exp2(header[:8, :])
@@ -440,6 +446,11 @@
                 for tile in range(8):
                     start = (band * tiles + 8 * plane + tile) * 8
                     out_ref[start : start + 8, :] = rows[tile]
+            rows = slice(band * tiles * 8, (band + 1) * tiles * 8)
+            copies.append(pltpu.make_async_copy(out_ref.at[rows], out_hbm.at[rows], out_sems.at[band]))
+            copies[-1].start()
+    for copy in copies:
+        copy.wait()
 
 
 def unpack(blocks, own_count, cells):
@@ -450,10 +461,12 @@
         functools.partial(unpack_kernel, (own_count, slab_count, tiles)),
         out_shape=jax.ShapeDtypeStruct((row_count * tiles, LANES), jnp.float32),
         in_specs=[pl.BlockSpec(memory_space=pl.ANY)] * slab_count,
-        out_specs=pl.BlockSpec(memory_space=pltpu.VMEM),
+        out_specs=pl.BlockSpec(memory_space=pl.ANY),
         scratch_shapes=[
             pltpu.VMEM((slab_count,) + blocks[0].shape, jnp.int16),
+            pltpu.VMEM((row_count * tiles, LANES), jnp.float32),
             pltpu.SemaphoreType.DMA((slab_count,)),
+            pltpu.SemaphoreType.DMA((row_count // 8,)),
         ],
         compiler_params=pltpu.CompilerParams(vmem_limit_bytes=8 * 1024 * 1024),
     )(*blocks)
@@ -508,7 +521,6 @@
     group = min(solves, 8)
     cells = side * side
     either = pl.BlockSpec(memory_space=pl.ANY)
-    vectors = pl.BlockSpec(memory_space=pltpu.VMEM)
     wide = pltpu.VMEM((2 * solves * side, cells), jnp.bfloat16)
     flops = 2 * solves * side * 3 * 2 * (cells * cells // 2 + cells * group * side)
     inputs = [mine, table, *pieces, *constants]
@@ -516,7 +528,7 @@
         functools.partial(force_kernel, sizes),
         out_shape=[jax.ShapeDtypeStruct((rows + HEADER_ROWS, LANES), jnp.int16)] * slab_count,
         in_specs=[either] * len(inputs),
-        out_specs=[vectors] * slab_count,
+        out_specs=[either] * slab_count,
         scratch_shapes=[
             pltpu.SMEM(table.shape, jnp.int32),
             pltpu.VMEM(mine.shape, jnp.bfloat16),
@@ -530,7 +542,7 @@
             wide,
             *[pltpu.VMEM((group * tiles * pitch, LANES), jnp.float32)] * (solves // group),
             pltpu.VMEM((slab_count, rows + HEADER_ROWS, LANES), jnp.int16),
-            pltpu.SemaphoreType.DMA((len(inputs),)),
+            pltpu.SemaphoreType.DMA((max(len(inputs), slab_count),)),
         ],
         compiler_params=pltpu.CompilerParams(vmem_limit_bytes=32 * 1024 * 1024),
         cost_estimate=pl.CostEstimate(flops=flops, bytes_accessed=8 * 1024 * 1024, transcendentals=0),

time: 50.7 us -> 51.1 us (level)
  no operation moved by 1% of the time
where the time goes in v19:
time: 51.1 us; the launch traced here: 50.9 us
  blocking collectives  16.1 us (32%)
  Pallas kernels  14.5 us (28%)
  starting transfers between devices  12.8 us (25%)
  waiting for transfers between devices  6.3 us (12%)
  local copies, waits for them, and re-layouts  1.11 us (2%)
    all_to_all x1, blocking collectives, shards(): lax.all_to_all(blocks, 'slab', split_axis=0, concat_axis=0, tiled=True)  16.1 us
    ppermute x7, starting transfers between devices, shards(): received.append(lax.ppermute(codes[step], 'slab', perm))  11.2 us
    pallas_call x1, Pallas kernels, team_forces(): pl.pallas_call(functools.partial(force_kernel, sizes), out_shape=[jax.Sha...  9.51 us
    pallas_call x1, Pallas kernels, place_own(): pl.pallas_call(functools.partial(own_kernel, sizes), out_shape=[jax.Shape...  3.34 us
    ppermute x7, waiting for transfers between devices, shards(): received.append(lax.ppermute(codes[step], 'slab', perm))  3.33 us
    pallas_call x1, Pallas kernels, unpack(): pl.pallas_call(functools.partial(unpack_kernel, (own_count, slab_count, t...  1.64 us
    ppermute x2, waiting for transfers between devices, swap_cores(): return lax.ppermute(block, 'pair', [(i, i ^ 1) for i in range(pair_count)])  1.53 us
    ppermute x1, starting transfers between devices, gather_chips(): pieces.append(lax.ppermute(boxes, 'pair', perm))  1.49 us
  transfers between devices with their start and end apart: 10, of which 7 were waited for; matrix products, arithmetic and copies ran while one was open for 0% of the time, Pallas kernels for 7%

profile of v19, /device:TPU:0, one launch (start us, length us, event | category | flops | bytes accessed | tf_op | source)
XLA Modules:
  0.0 50.9 jit_solution(6092724433071223887)
XLA Ops:
  0.0 1.1 %reshape.9 = bf16[8,128,128]{2,1,0:T(8,128)(2,1)S(1)} reshape(bf16[32,4096]{1,0:T(8,128)(2,1)} %param.6) | data formatting | bytes 524288 | tf_op jit(solution)/shard_map/reshape | solution.py:558
  1.1 0.0 copy-start.2
  1.1 0.0 copy-start.3
  1.1 0.0 copy-start.4
  1.1 16.1 %all_to_all.5.own_hbm.refs_0_ = bf16[8,128,128]{2,1,0:T(8,128)(2,1)S(1)} all-to-all(bf16[8,128,128]{2,1,0:T(8,128)(2,1)S(1)} %reshape.9), channel_id=1, replica_groups=mesh['slab'=8,'pair'=4] {'slab'}, dimensions={0} | all-to-all | bytes 524288 | tf_op jit(solution)/shard_map/all_to_all | solution.py:559
  17.3 1.5 %collective-permute-start = (bf16[8,128,128]{2,1,0:T(8,128)(2,1)S(1)}, bf16[8,128,128]{2,1,0:T(8,128)(2,1)S(1)}, u32[]{:S(2)}, u32[]{:S(2)}) collective-permute-start(bf16[8,128,128]{2,1,0:T(8,128)(2,1)S(1)} %all_to_all.5.own_hbm.refs_0_), channel_id=1, source_target_pairs={{0,2},{1,3},{2,0},{3,1},{4,6},{5,7},{6,4},{7,5},{8,10},{9,11},{10,... | collective-permute-start | bytes 786440 | tf_op jit(solution)/shard_map/ppermute | solution.py:413
  18.8 3.3 %shard_map.64 = (bf16[512,1024]{1,0:T(8,128)(2,1)S(1)}, s32[128]{0:T(128)S(1)}, f32[32,512]{1,0:T(8,128)S(1)}, f32[64,512]{1,0:T(8,128)S(1)}, f32[32,1024]{1,0:T(8,128)S(1)}) custom-call(s32[1,4,16]{2,1,0:T(4,128)S(1)} %copy-done, s32[3,128]{1,0:T(4,128)S(1)} %bitcast.6, bf16[8,128,128]{2,1,0:T(8,128)(2,1)S(1)} %all_to_all.5.own_hbm.refs_0_, ...), custom_call_target="tpu_custom_call" | custom-call | flops 5000000000 | bytes 4194304 | tf_op jit(solution)/shard_map/pallas_call | solution.py:495
  22.1 0.1 collective-permute-start.1
  22.2 1.4 %collective-permute-done.refs_1_ = bf16[8,128,128]{2,1,0:T(8,128)(2,1)S(1)} collective-permute-done((bf16[8,128,128]{2,1,0:T(8,128)(2,1)S(1)}, bf16[8,128,128]{2,1,0:T(8,128)(2,1)S(1)}, u32[]{:S(2)}, u32[]{:S(2)}) %collective-permute-start) | collective-permute-done | bytes 262176 | tf_op jit(solution)/shard_map/ppermute | solution.py:413
  23.6 0.1 collective-permute-done.1.refs_2_
  23.7 1.4 %collective-permute-done.2.refs_3_ = bf16[8,128,128]{2,1,0:T(8,128)(2,1)S(1)} collective-permute-done((bf16[8,128,128]{2,1,0:T(8,128)(2,1)S(1)}, bf16[8,128,128]{2,1,0:T(8,128)(2,1)S(1)}, u32[]{:S(2)}, u32[]{:S(2)}) %collective-permute-start.2) | collective-permute-done | bytes 262176 | tf_op jit(solution)/shard_map/ppermute | solution.py:406
  25.2 9.5 %shard_map.65 = (s16[144,128]{1,0:T(8,128)(2,1)S(1)}, s16[144,128]{1,0:T(8,128)(2,1)S(1)}, s16[144,128]{1,0:T(8,128)(2,1)S(1)}, s16[144,128]{1,0:T(8,128)(2,1)S(...) custom-call(bf16[512,1024]{1,0:T(8,128)(2,1)S(1)} %get-tuple-element, ...), custom_call_target="tpu_custom_call" | custom-call | flops 4831838208 | bytes 8388608 | tf_op jit(solution)/shard_map/pallas_call | solution.py:527
  34.7 3.7 %collective-permute-start.3 = (s16[144,128]{1,0:T(8,128)(2,1)S(1)}, s16[144,128]{1,0:T(8,128)(2,1)S(1)}, u32[]{:S(2)}, u32[]{:S(2)}) collective-permute-start(s16[144,128]{1,0:T(8,128)(2,1)S(1)} %get-tuple-element.31), channel_id=1, source_target_pairs={{0,28},{4,24},{8,20},{12,16},{16,12},{20,8},{24,4},{28,0},{1,29},{... | collective-permute-start | bytes 110600 | tf_op jit(solution)/shard_map/ppermute | solution.py:571
  38.4 1.0 %collective-permute-start.4 = (s16[144,128]{1,0:T(8,128)(2,1)S(1)}, s16[144,128]{1,0:T(8,128)(2,1)S(1)}, u32[]{:S(2)}, u32[]{:S(2)}) collective-permute-start(s16[144,128]{1,0:T(8,128)(2,1)S(1)} %get-tuple-element.32), channel_id=1, source_target_pairs={{0,24},{4,28},{8,16},{12,20},{16,8},{20,12},{24,0},{28,4},{1,25},{... | collective-permute-start | bytes 110600 | tf_op jit(solution)/shard_map/ppermute | solution.py:571
  39.4 0.4 collective-permute-start.5
  39.8 2.6 %collective-permute-start.6 = (s16[144,128]{1,0:T(8,128)(2,1)S(1)}, s16[144,128]{1,0:T(8,128)(2,1)S(1)}, u32[]{:S(2)}, u32[]{:S(2)}) collective-permute-start(s16[144,128]{1,0:T(8,128)(2,1)S(1)} %get-tuple-element.34), channel_id=1, source_target_pairs={{0,16},{4,20},{8,24},{12,28},{16,0},{20,4},{24,8},{28,12},{1,17},{... | collective-permute-start | bytes 110600 | tf_op jit(solution)/shard_map/ppermute | solution.py:571
  42.4 1.3 %collective-permute-start.7 = (s16[144,128]{1,0:T(8,128)(2,1)S(1)}, s16[144,128]{1,0:T(8,128)(2,1)S(1)}, u32[]{:S(2)}, u32[]{:S(2)}) collective-permute-start(s16[144,128]{1,0:T(8,128)(2,1)S(1)} %get-tuple-element.35), channel_id=1, source_target_pairs={{0,12},{4,8},{8,4},{12,0},{16,28},{20,24},{24,20},{28,16},{1,13},{... | collective-permute-start | bytes 110600 | tf_op jit(solution)/shard_map/ppermute | solution.py:571
  43.7 1.6 %collective-permute-start.8 = (s16[144,128]{1,0:T(8,128)(2,1)S(1)}, s16[144,128]{1,0:T(8,128)(2,1)S(1)}, u32[]{:S(2)}, u32[]{:S(2)}) collective-permute-start(s16[144,128]{1,0:T(8,128)(2,1)S(1)} %get-tuple-element.36), channel_id=1, source_target_pairs={{0,8},{4,12},{8,0},{12,4},{16,24},{20,28},{24,16},{28,20},{1,9},{5... | collective-permute-start | bytes 110600 | tf_op jit(solution)/shard_map/ppermute | solution.py:571
  45.3 0.6 %collective-permute-start.9 = (s16[144,128]{1,0:T(8,128)(2,1)S(1)}, s16[144,128]{1,0:T(8,128)(2,1)S(1)}, u32[]{:S(2)}, u32[]{:S(2)}) collective-permute-start(s16[144,128]{1,0:T(8,128)(2,1)S(1)} %get-tuple-element.37), channel_id=1, source_target_pairs={{0,4},{4,0},{8,12},{12,8},{16,20},{20,16},{24,28},{28,24},{1,5},{5... | collective-permute-start | bytes 110600 | tf_op jit(solution)/shard_map/ppermute | solution.py:571
  45.9 0.3 collective-permute-done.6.refs_3_
  46.2 1.1 %collective-permute-done.7.refs_4_ = s16[144,128]{1,0:T(8,128)(2,1)S(1)} collective-permute-done((s16[144,128]{1,0:T(8,128)(2,1)S(1)}, s16[144,128]{1,0:T(8,128)(2,1)S(1)}, u32[]{:S(2)}, u32[]{:S(2)}) %collective-permute-start.7) | collective-permute-done | bytes 36896 | tf_op jit(solution)/shard_map/ppermute | solution.py:571
  47.3 0.4 collective-permute-done.8.refs_5_
  47.6 1.6 %collective-permute-done.9.refs_6_ = s16[144,128]{1,0:T(8,128)(2,1)S(1)} collective-permute-done((s16[144,128]{1,0:T(8,128)(2,1)S(1)}, s16[144,128]{1,0:T(8,128)(2,1)S(1)}, u32[]{:S(2)}, u32[]{:S(2)}) %collective-permute-start.9) | collective-permute-done | bytes 36896 | tf_op jit(solution)/shard_map/ppermute | solution.py:571
  49.2 1.6 %shard_map.66 = f32[1024,128]{1,0:T(8,128)} custom-call(s16[144,128]{1,0:T(8,128)(2,1)S(1)} %collective-permute-done.3.refs_0_, s16[144,128]{1,0:T(8,128)(2,1)S(1)} %collective-permute-done.4.refs_1_, s16[144,128]{1,0:T(8,128)(2,1)S(1)} %collective-permute-done.5.refs_2_, s16[144,128]{1,0:T(8,128)(2,1)S(1)} %collective-permute-done.6.refs_3_, ...), custom_call_target="tpu_custom_call" | custom-call | tf_op jit(solution)/shard_map/pallas_call | solution.py:460
  (11 shorter events, 0.0 us)
Async XLA Ops:
  1.1 17.7 %copy-start = (s32[1,4,16]{2,1,0:T(4,128)S(1)}, s32[1,4,16]{2,1,0:T(4,128)}, u32[]{:S(2)}) copy-start(s32[1,4,16]{2,1,0:T(4,128)} %match_hbm.1) | copy-start | bytes 772
  1.1 17.7 %copy-start.1 = (s32[128,3]{0,1:T(4,128)S(1)}, s32[128,3]{0,1:T(4,128)}, u32[]{:S(2)}) copy-start(s32[128,3]{0,1:T(4,128)} %param.7) | copy-start | bytes 4612
  1.1 17.7 %copy-start.2 = (f32[32,1024]{1,0:T(8,128)S(1)}, f32[32,1024]{1,0:T(8,128)}, u32[]{:S(2)}) copy-start(f32[32,1024]{1,0:T(8,128)} %constant.8.clone.refs_2_) | copy-start | bytes 393220
  1.1 17.7 %copy-start.3 = (f32[64,512]{1,0:T(8,128)S(1)}, f32[64,512]{1,0:T(8,128)}, u32[]{:S(2)}) copy-start(f32[64,512]{1,0:T(8,128)} %constant.7.clone.refs_1_) | copy-start | bytes 393220
  1.1 17.6 %copy-start.4 = (f32[32,512]{1,0:T(8,128)S(1)}, f32[32,512]{1,0:T(8,128)}, u32[]{:S(2)}) copy-start(f32[32,512]{1,0:T(8,128)} %constant.6.clone.refs_0_) | copy-start | bytes 196612
  17.3 6.4 %collective-permute-start = (bf16[8,128,128]{2,1,0:T(8,128)(2,1)S(1)}, bf16[8,128,128]{2,1,0:T(8,128)(2,1)S(1)}, u32[]{:S(2)}, u32[]{:S(2)}) collective-permute-start(bf16[8,128,128]{2,1,0:T(8,128)(2,1)S(1)} %all_to_all.5.own_hbm.refs_0_), channel_id=1, source_target_pairs={{0,2},{1,3},{2,0},{3,1},{4,6},{5,7},{6,4},{7,5},{8,10},{9,11},{10,... | collective-permute-start | bytes 786440 | tf_op jit(solution)/shard_map/ppermute | solution.py:413
  22.1 1.6 %collective-permute-start.1 = (bf16[8,128,128]{2,1,0:T(8,128)(2,1)S(1)}, bf16[8,128,128]{2,1,0:T(8,128)(2,1)S(1)}, u32[]{:S(2)}, u32[]{:S(2)}) collective-permute-start(bf16[8,128,128]{2,1,0:T(8,128)(2,1)S(1)} %all_to_all.5.own_hbm.refs_0_), channel_id=1, source_target_pairs={{0,1},{1,0},{2,3},{3,2},{4,5},{5,4},{6,7},{7,6},{8,9},{9,8},{10,11... | collective-permute-start | bytes 786440 | tf_op jit(solution)/shard_map/ppermute | solution.py:406
  23.6 1.5 %collective-permute-start.2 = (bf16[8,128,128]{2,1,0:T(8,128)(2,1)S(1)}, bf16[8,128,128]{2,1,0:T(8,128)(2,1)S(1)}, u32[]{:S(2)}, u32[]{:S(2)}) collective-permute-start(bf16[8,128,128]{2,1,0:T(8,128)(2,1)S(1)} %collective-permute-done.refs_1_), channel_id=1, source_target_pairs={{0,1},{1,0},{2,3},{3,2},{4,5},{5,4},{6,7},{7,6},{8,9},{9,8},{10,11... | collective-permute-start | bytes 786440 | tf_op jit(solution)/shard_map/ppermute | solution.py:406
  34.7 9.0 %collective-permute-start.3 = (s16[144,128]{1,0:T(8,128)(2,1)S(1)}, s16[144,128]{1,0:T(8,128)(2,1)S(1)}, u32[]{:S(2)}, u32[]{:S(2)}) collective-permute-start(s16[144,128]{1,0:T(8,128)(2,1)S(1)} %get-tuple-element.31), channel_id=1, source_target_pairs={{0,28},{4,24},{8,20},{12,16},{16,12},{20,8},{24,4},{28,0},{1,29},{... | collective-permute-start | bytes 110600 | tf_op jit(solution)/shard_map/ppermute | solution.py:571
  38.4 6.9 %collective-permute-start.4 = (s16[144,128]{1,0:T(8,128)(2,1)S(1)}, s16[144,128]{1,0:T(8,128)(2,1)S(1)}, u32[]{:S(2)}, u32[]{:S(2)}) collective-permute-start(s16[144,128]{1,0:T(8,128)(2,1)S(1)} %get-tuple-element.32), channel_id=1, source_target_pairs={{0,24},{4,28},{8,16},{12,20},{16,8},{20,12},{24,0},{28,4},{1,25},{... | collective-permute-start | bytes 110600 | tf_op jit(solution)/shard_map/ppermute | solution.py:571
  39.4 6.5 %collective-permute-start.5 = (s16[144,128]{1,0:T(8,128)(2,1)S(1)}, s16[144,128]{1,0:T(8,128)(2,1)S(1)}, u32[]{:S(2)}, u32[]{:S(2)}) collective-permute-start(s16[144,128]{1,0:T(8,128)(2,1)S(1)} %get-tuple-element.33), channel_id=1, source_target_pairs={{0,20},{4,16},{8,28},{12,24},{16,4},{20,0},{24,12},{28,8},{1,21},{... | collective-permute-start | bytes 110600 | tf_op jit(solution)/shard_map/ppermute | solution.py:571
  39.8 6.3 %collective-permute-start.6 = (s16[144,128]{1,0:T(8,128)(2,1)S(1)}, s16[144,128]{1,0:T(8,128)(2,1)S(1)}, u32[]{:S(2)}, u32[]{:S(2)}) collective-permute-start(s16[144,128]{1,0:T(8,128)(2,1)S(1)} %get-tuple-element.34), channel_id=1, source_target_pairs={{0,16},{4,20},{8,24},{12,28},{16,0},{20,4},{24,8},{28,12},{1,17},{... | collective-permute-start | bytes 110600 | tf_op jit(solution)/shard_map/ppermute | solution.py:571
  42.4 4.9 %collective-permute-start.7 = (s16[144,128]{1,0:T(8,128)(2,1)S(1)}, s16[144,128]{1,0:T(8,128)(2,1)S(1)}, u32[]{:S(2)}, u32[]{:S(2)}) collective-permute-start(s16[144,128]{1,0:T(8,128)(2,1)S(1)} %get-tuple-element.35), channel_id=1, source_target_pairs={{0,12},{4,8},{8,4},{12,0},{16,28},{20,24},{24,20},{28,16},{1,13},{... | collective-permute-start | bytes 110600 | tf_op jit(solution)/shard_map/ppermute | solution.py:571
  43.7 4.0 %collective-permute-start.8 = (s16[144,128]{1,0:T(8,128)(2,1)S(1)}, s16[144,128]{1,0:T(8,128)(2,1)S(1)}, u32[]{:S(2)}, u32[]{:S(2)}) collective-permute-start(s16[144,128]{1,0:T(8,128)(2,1)S(1)} %get-tuple-element.36), channel_id=1, source_target_pairs={{0,8},{4,12},{8,0},{12,4},{16,24},{20,28},{24,16},{28,20},{1,9},{5... | collective-permute-start | bytes 110600 | tf_op jit(solution)/shard_map/ppermute | solution.py:571
  45.3 4.0 %collective-permute-start.9 = (s16[144,128]{1,0:T(8,128)(2,1)S(1)}, s16[144,128]{1,0:T(8,128)(2,1)S(1)}, u32[]{:S(2)}, u32[]{:S(2)}) collective-permute-start(s16[144,128]{1,0:T(8,128)(2,1)S(1)} %get-tuple-element.37), channel_id=1, source_target_pairs={{0,4},{4,0},{8,12},{12,8},{16,20},{20,16},{24,28},{28,24},{1,5},{5... | collective-permute-start | bytes 110600 | tf_op jit(solution)/shard_map/ppermute | solution.py:571

commit v20 on v18

--- a/solution.py
+++ b/solution.py
@@ -127,7 +127,7 @@
         halves = {}
         for slab in range(8 * group // planes, (8 * group + 7) // planes + 1):
             for chunk in range(own_count * planes // 2):
-                block = boxes_ref[pair, slab, 16 * chunk : 16 * chunk + 16, :].astype(jnp.float32)
+                block = boxes_ref[slab, 16 * chunk : 16 * chunk + 16, :].astype(jnp.float32)
                 for half in range(2):
                     own, plane = divmod(2 * chunk + half, planes)
                     halves[own, slab * planes + plane] = block[8 * half : 8 * half + 8, :]
@@ -189,25 +189,23 @@
             mix_ref[rows, part * width : (part + 1) * width] = piece
 
 
-def own_kernel(sizes, match_hbm, centers_hbm, own_hbm, *refs):
-    constant_hbm, refs = refs[:3], refs[3:]
+def own_kernel(sizes, match_hbm, centers_hbm, boxes_ref, *refs):
+    basis_ref, line_ref, gain_hbm, *refs = refs
     mine_ref, table_ref, mix_ref, gain_ref, there_high, there_low, back_high, back_low = refs[:8]
-    match_ref, centers_ref, boxes_ref, basis_ref, line_ref, fields, sems = refs[8:]
+    match_ref, centers_ref, fields, sems = refs[8:]
     side, rounds, own_count, _, _ = sizes
     tiles, _, _ = box_shape(sizes)
     first_member = lax.axis_index("pair") * own_count
-    sources = (*constant_hbm, match_hbm, centers_hbm, own_hbm)
-    targets = (basis_ref, line_ref, gain_ref, match_ref, centers_ref, boxes_ref.at[0])
+    sources = (gain_hbm, match_hbm, centers_hbm)
+    targets = (gain_ref, match_ref, centers_ref)
     copies = [pltpu.make_async_copy(s, t, sems.at[i]) for i, (s, t) in enumerate(zip(sources, targets))]
     for copy in copies:
         copy.start()
     clear_edges(sizes, fields, 0, own_count)
-    for copy in copies[:2]:
-        copy.wait()
     make_mix(basis_ref, mix_ref)
     make_matrices(basis_ref, line_ref, 0, there_high, there_low)
     make_matrices(basis_ref, line_ref, side, back_high, back_low)
-    for copy in copies[2:]:
+    for copy in copies:
         copy.wait()
     spread(sizes, boxes_ref, fields, 0)
 
@@ -224,14 +222,13 @@
     lax.fori_loop(0, own_count * rounds, place, 0)
 
 
-def force_kernel(sizes, mine_hbm, table_hbm, *refs):
+def force_kernel(sizes, mine, table_hbm, *refs):
     side, rounds, own_count, slab_count, pair_count = sizes
-    piece_hbm, refs = refs[:pair_count], refs[pair_count:]
-    constant_hbm, refs = refs[:6], refs[6:]
-    out_refs, refs = refs[:slab_count], refs[slab_count:]
-    table_ref, mine, partner, boxes_ref, *refs = refs
+    piece_refs, refs = refs[:pair_count], refs[pair_count:]
     constants, refs = refs[:6], refs[6:]
     mix_ref, gain_ref, there_high, there_low, back_high, back_low = constants
+    out_refs, refs = refs[:slab_count], refs[slab_count:]
+    table_ref, partner, *refs = refs
     fields, first, second, *terms, all_codes, sems = refs
     planes = side // slab_count
     tiles, lines, pitch = box_shape(sizes)
@@ -251,22 +248,15 @@
         for core_step in range(CORES)
         for step in range(chips)
     ]
-    sources = [table_hbm, *piece_hbm, mine_hbm, *constant_hbm]
-    targets = [table_ref, *[boxes_ref.at[pair] for pair in places], mine, *constants]
-    copies = [pltpu.make_async_copy(s, t, sems.at[i]) for i, (s, t) in enumerate(zip(sources, targets))]
-    for copy in copies:
-        copy.start()
+    table_copy = pltpu.make_async_copy(table_hbm, table_ref, sems.at[0])
+    table_copy.start()
     for pair in places:
         clear_edges(sizes, fields, pair * own_count, own_count)
     for ref in terms:
         clear_edges(sizes, ref, 0, group)
-    table_copy, *piece_copies, mine_copy, mix_copy, gain_copy = copies[: pair_count + 4]
-    there_copies, back_copies = copies[pair_count + 4 : pair_count + 6], copies[pair_count + 6 :]
-    for copy in (table_copy, *piece_copies):
-        copy.wait()
-    for pair in places:
-        spread(sizes, boxes_ref, fields, pair)
-    mine_copy.wait()
+    for piece_ref, pair in zip(piece_refs, places):
+        spread(sizes, piece_ref, fields, pair)
+    table_copy.wait()
 
     row_count = solves * side
     half_tiles = tiles // 2
@@ -317,15 +307,12 @@
         left = jnp.concatenate([high, low, high], axis=1)
         return dot(left, jnp.concatenate([basis, basis, rest], axis=0))
 
-    mix_copy.wait()
     for start in range(0, row_count, group_rows):
         for index in range(start // side, (start + group_rows) // side):
             densities(index)
         columns = slice(0, cells)
         store_split(second, start, group_rows, columns, along_x(start, columns, first))
 
-    for copy in (gain_copy, *there_copies):
-        copy.wait()
     for parity in range(2):
         for column in range(0, half_cells, width):
             columns = slice(column, column + width)
@@ -335,8 +322,6 @@
             value = (value.reshape(solves, side, width) * gain[None]).reshape(row_count, width)
             store_split(first, 0, row_count, columns, value)
 
-    for copy in back_copies:
-        copy.wait()
     for parity in range(2):
         for column in range(0, half_cells, width):
             value = in_plane(parity, slice(column, column + width), first, back_high, back_low)
@@ -422,7 +407,7 @@
 
 def unpack_kernel(sizes, *refs):
     own_count, slab_count, tiles = sizes
-    block_refs, out_ref, blocks, sems = refs[:slab_count], *refs[slab_count:]
+    block_refs, out_hbm, blocks, out_ref, sems, out_sems = refs[:slab_count], *refs[slab_count:]
     slab_index = lax.axis_index("slab")
     copies = []
     for index in range(slab_count):
@@ -433,6 +418,7 @@
         copy.wait()
     row_count = own_count * tiles
     values = {}
+    copies = []
     for slab in range(slab_count):
         header = blocks[slab, row_count:, :].astype(jnp.int32).astype(jnp.float32)
         units = jnp.exp2(header[:8, :])
@@ -451,6 +437,11 @@
                 for tile in range(8):
                     start = (band * tiles + 8 * plane + tile) * 8
                     out_ref[start : start + 8, :] = rows[tile]
+            rows = slice(band * tiles * 8, (band + 1) * tiles * 8)
+            copies.append(pltpu.make_async_copy(out_ref.at[rows], out_hbm.at[rows], out_sems.at[band]))
+            copies[-1].start()
+    for copy in copies:
+        copy.wait()
 
 
 def unpack(blocks, own_count, cells):
@@ -461,10 +452,12 @@
         functools.partial(unpack_kernel, (own_count, slab_count, tiles)),
         out_shape=jax.ShapeDtypeStruct((row_count * tiles, LANES), jnp.float32),
         in_specs=[pl.BlockSpec(memory_space=pl.ANY)] * slab_count,
-        out_specs=pl.BlockSpec(memory_space=pltpu.VMEM),
+        out_specs=pl.BlockSpec(memory_space=pl.ANY),
         scratch_shapes=[
             pltpu.VMEM((slab_count,) + blocks[0].shape, jnp.int16),
+            pltpu.VMEM((row_count * tiles, LANES), jnp.float32),
             pltpu.SemaphoreType.DMA((slab_count,)),
+            pltpu.SemaphoreType.DMA((row_count // 8,)),
         ],
         compiler_params=pltpu.CompilerParams(vmem_limit_bytes=8 * 1024 * 1024),
     )(*blocks)
@@ -502,14 +495,11 @@
             jax.ShapeDtypeStruct(constants[2].shape, jnp.float32),
             *[matrix] * 4,
         ],
-        in_specs=[either] * len(inputs),
+        in_specs=[either] * 2 + [vectors] * 3 + [either],
         out_specs=[vectors, pl.BlockSpec(memory_space=pltpu.SMEM)] + [vectors] * 6,
         scratch_shapes=[
             pltpu.SMEM(match.shape, jnp.int32),
             pltpu.SMEM(centers.shape, jnp.int32),
-            pltpu.VMEM((1,) + boxes.shape, jnp.bfloat16),
-            pltpu.VMEM(constants[0].shape, jnp.float32),
-            pltpu.VMEM(constants[1].shape, jnp.float32),
             pltpu.VMEM((own_count * tiles * pitch, LANES), jnp.float32),
             pltpu.SemaphoreType.DMA((len(inputs),)),
         ],
@@ -533,20 +523,17 @@
     return pl.pallas_call(
         functools.partial(force_kernel, sizes),
         out_shape=[jax.ShapeDtypeStruct((rows + HEADER_ROWS, LANES), jnp.int16)] * slab_count,
-        in_specs=[either] * len(inputs),
+        in_specs=[vectors, either] + [vectors] * (len(pieces) + len(constants)),
         out_specs=[vectors] * slab_count,
         scratch_shapes=[
             pltpu.SMEM(table.shape, jnp.int32),
             pltpu.VMEM(mine.shape, jnp.bfloat16),
-            pltpu.VMEM(mine.shape, jnp.bfloat16),
-            pltpu.VMEM((pair_count, slab_count, rows, LANES), jnp.bfloat16),
-            *[pltpu.VMEM(constant.shape, constant.dtype) for constant in constants],
             pltpu.VMEM((own_count * pair_count * tiles * pitch, LANES), jnp.float32),
             wide,
             wide,
             *[pltpu.VMEM((group * tiles * pitch, LANES), jnp.float32)] * (solves // group),
             pltpu.VMEM((slab_count, rows + HEADER_ROWS, LANES), jnp.int16),
-            pltpu.SemaphoreType.DMA((len(inputs),)),
+            pltpu.SemaphoreType.DMA((1,)),
         ],
         compiler_params=pltpu.CompilerParams(vmem_limit_bytes=32 * 1024 * 1024),
         cost_estimate=pl.CostEstimate(flops=flops, bytes_accessed=8 * 1024 * 1024, transcendentals=0),

time: 51 us -> 49.8 us (0.976)
  Pallas kernels: 15 us -> 13.5 us
    pallas_call x1, Pallas kernels: 9.36 us -> 8.23 us  [team_forces(): pl.pallas_call(functools.partial(force_kernel, sizes), out_shape=[jax.Sha...]
  transfers between devices with their start and end apart: 10 -> 10, of which waited for: 7 -> 7; matrix products, arithmetic and copies ran while one was open for 0% -> 0% of each run, Pallas kernels for 8% -> 7%
where the time goes in v20:
time: 49.8 us; the launch traced here: 49.6 us
  blocking collectives  16.1 us (32%)
  Pallas kernels  13.5 us (27%)
  starting transfers between devices  12.8 us (26%)
  waiting for transfers between devices  6.02 us (12%)
  local copies, waits for them, and re-layouts  1.11 us (2%)
    all_to_all x1, blocking collectives, shards(): lax.all_to_all(blocks, 'slab', split_axis=0, concat_axis=0, tiled=True)  16.1 us
    ppermute x7, starting transfers between devices, shards(): received.append(lax.ppermute(codes[step], 'slab', perm))  11.2 us
    pallas_call x1, Pallas kernels, team_forces(): pl.pallas_call(functools.partial(force_kernel, sizes), out_shape=[jax.Sha...  8.23 us
    pallas_call x1, Pallas kernels, place_own(): pl.pallas_call(functools.partial(own_kernel, sizes), out_shape=[jax.Shape...  3.63 us
    ppermute x7, waiting for transfers between devices, shards(): received.append(lax.ppermute(codes[step], 'slab', perm))  3.35 us
    pallas_call x1, Pallas kernels, unpack(): pl.pallas_call(functools.partial(unpack_kernel, (own_count, slab_count, t...  1.64 us
    ppermute x2, waiting for transfers between devices, swap_cores(): return lax.ppermute(block, 'pair', [(i, i ^ 1) for i in range(pair_count)])  1.53 us
    ppermute x1, starting transfers between devices, gather_chips(): pieces.append(lax.ppermute(boxes, 'pair', perm))  1.49 us
  transfers between devices with their start and end apart: 10, of which 7 were waited for; matrix products, arithmetic and copies ran while one was open for 0% of the time, Pallas kernels for 7%

profile of v20, /device:TPU:0, one launch (start us, length us, event | category | flops | bytes accessed | tf_op | source)
XLA Modules:
  0.0 49.6 jit_solution(17013718542322712626)
XLA Ops:
  0.0 1.1 %reshape.9 = bf16[8,128,128]{2,1,0:T(8,128)(2,1)S(1)} reshape(bf16[32,4096]{1,0:T(8,128)(2,1)} %param.6) | data formatting | bytes 524288 | tf_op jit(solution)/shard_map/reshape | solution.py:549
  1.1 0.0 copy-start.2
  1.1 0.0 copy-start.3
  1.1 0.0 copy-start.4
  1.1 16.1 %all_to_all.5.boxes_ref.refs_0_ = bf16[8,128,128]{2,1,0:T(8,128)(2,1)S(1)} all-to-all(bf16[8,128,128]{2,1,0:T(8,128)(2,1)S(1)} %reshape.9), channel_id=1, replica_groups=mesh['slab'=8,'pair'=4] {'slab'}, dimensions={0} | all-to-all | bytes 524288 | tf_op jit(solution)/shard_map/all_to_all | solution.py:550
  17.3 1.5 %collective-permute-start = (bf16[8,128,128]{2,1,0:T(8,128)(2,1)S(1)}, bf16[8,128,128]{2,1,0:T(8,128)(2,1)S(1)}, u32[]{:S(2)}, u32[]{:S(2)}) collective-permute-start(bf16[8,128,128]{2,1,0:T(8,128)(2,1)S(1)} %all_to_all.5.boxes_ref.refs_0_), channel_id=1, source_target_pairs={{0,2},{1,3},{2,0},{3,1},{4,6},{5,7},{6,4},{7,5},{8,10},{9,11},{10,... | collective-permute-start | bytes 786440 | tf_op jit(solution)/shard_map/ppermute | solution.py:404
  18.8 3.6 %shard_map.64 = (bf16[512,1024]{1,0:T(8,128)(2,1)S(1)}, s32[128]{0:T(128)S(1)}, bf16[256,768]{1,0:T(8,128)(2,1)S(1)}, f32[32,1024]{1,0:T(8,128)S(1)}, bf16[2,512...) custom-call(s32[1,4,16]{2,1,0:T(4,128)S(1)} %copy-done, ...), custom_call_target="tpu_custom_call" | custom-call | flops 5000000000 | bytes 4194304 | tf_op jit(solution)/shard_map/pallas_call | solution.py:489
  22.4 0.1 collective-permute-start.1
  22.5 1.1 %collective-permute-done.refs_1_ = bf16[8,128,128]{2,1,0:T(8,128)(2,1)S(1)} collective-permute-done((bf16[8,128,128]{2,1,0:T(8,128)(2,1)S(1)}, bf16[8,128,128]{2,1,0:T(8,128)(2,1)S(1)}, u32[]{:S(2)}, u32[]{:S(2)}) %collective-permute-start) | collective-permute-done | bytes 262176 | tf_op jit(solution)/shard_map/ppermute | solution.py:404
  23.6 0.4 collective-permute-done.1.refs_2_
  24.0 1.2 %collective-permute-done.2.refs_3_ = bf16[8,128,128]{2,1,0:T(8,128)(2,1)S(1)} collective-permute-done((bf16[8,128,128]{2,1,0:T(8,128)(2,1)S(1)}, bf16[8,128,128]{2,1,0:T(8,128)(2,1)S(1)}, u32[]{:S(2)}, u32[]{:S(2)}) %collective-permute-start.2) | collective-permute-done | bytes 262176 | tf_op jit(solution)/shard_map/ppermute | solution.py:397
  25.2 8.2 %shard_map.65 = (s16[144,128]{1,0:T(8,128)(2,1)S(1)}, s16[144,128]{1,0:T(8,128)(2,1)S(1)}, s16[144,128]{1,0:T(8,128)(2,1)S(1)}, s16[144,128]{1,0:T(8,128)(2,1)S(...) custom-call(bf16[512,1024]{1,0:T(8,128)(2,1)S(1)} %get-tuple-element, ...), custom_call_target="tpu_custom_call" | custom-call | flops 4831838208 | bytes 8388608 | tf_op jit(solution)/shard_map/pallas_call | solution.py:523
  33.4 3.7 %collective-permute-start.3 = (s16[144,128]{1,0:T(8,128)(2,1)S(1)}, s16[144,128]{1,0:T(8,128)(2,1)S(1)}, u32[]{:S(2)}, u32[]{:S(2)}) collective-permute-start(s16[144,128]{1,0:T(8,128)(2,1)S(1)} %get-tuple-element.37), channel_id=1, source_target_pairs={{0,28},{4,24},{8,20},{12,16},{16,12},{20,8},{24,4},{28,0},{1,29},{... | collective-permute-start | bytes 110600 | tf_op jit(solution)/shard_map/ppermute | solution.py:562
  37.1 1.0 %collective-permute-start.4 = (s16[144,128]{1,0:T(8,128)(2,1)S(1)}, s16[144,128]{1,0:T(8,128)(2,1)S(1)}, u32[]{:S(2)}, u32[]{:S(2)}) collective-permute-start(s16[144,128]{1,0:T(8,128)(2,1)S(1)} %get-tuple-element.38), channel_id=1, source_target_pairs={{0,24},{4,28},{8,16},{12,20},{16,8},{20,12},{24,0},{28,4},{1,25},{... | collective-permute-start | bytes 110600 | tf_op jit(solution)/shard_map/ppermute | solution.py:562
  38.2 0.4 collective-permute-start.5
  38.6 2.6 %collective-permute-start.6 = (s16[144,128]{1,0:T(8,128)(2,1)S(1)}, s16[144,128]{1,0:T(8,128)(2,1)S(1)}, u32[]{:S(2)}, u32[]{:S(2)}) collective-permute-start(s16[144,128]{1,0:T(8,128)(2,1)S(1)} %get-tuple-element.40), channel_id=1, source_target_pairs={{0,16},{4,20},{8,24},{12,28},{16,0},{20,4},{24,8},{28,12},{1,17},{... | collective-permute-start | bytes 110600 | tf_op jit(solution)/shard_map/ppermute | solution.py:562
  41.1 1.3 %collective-permute-start.7 = (s16[144,128]{1,0:T(8,128)(2,1)S(1)}, s16[144,128]{1,0:T(8,128)(2,1)S(1)}, u32[]{:S(2)}, u32[]{:S(2)}) collective-permute-start(s16[144,128]{1,0:T(8,128)(2,1)S(1)} %get-tuple-element.41), channel_id=1, source_target_pairs={{0,12},{4,8},{8,4},{12,0},{16,28},{20,24},{24,20},{28,16},{1,13},{... | collective-permute-start | bytes 110600 | tf_op jit(solution)/shard_map/ppermute | solution.py:562
  42.4 1.6 %collective-permute-start.8 = (s16[144,128]{1,0:T(8,128)(2,1)S(1)}, s16[144,128]{1,0:T(8,128)(2,1)S(1)}, u32[]{:S(2)}, u32[]{:S(2)}) collective-permute-start(s16[144,128]{1,0:T(8,128)(2,1)S(1)} %get-tuple-element.42), channel_id=1, source_target_pairs={{0,8},{4,12},{8,0},{12,4},{16,24},{20,28},{24,16},{28,20},{1,9},{5... | collective-permute-start | bytes 110600 | tf_op jit(solution)/shard_map/ppermute | solution.py:562
  44.0 0.6 %collective-permute-start.9 = (s16[144,128]{1,0:T(8,128)(2,1)S(1)}, s16[144,128]{1,0:T(8,128)(2,1)S(1)}, u32[]{:S(2)}, u32[]{:S(2)}) collective-permute-start(s16[144,128]{1,0:T(8,128)(2,1)S(1)} %get-tuple-element.43), channel_id=1, source_target_pairs={{0,4},{4,0},{8,12},{12,8},{16,20},{20,16},{24,28},{28,24},{1,5},{5... | collective-permute-start | bytes 110600 | tf_op jit(solution)/shard_map/ppermute | solution.py:562
  44.6 0.3 collective-permute-done.6.refs_3_
  44.9 1.1 %collective-permute-done.7.refs_4_ = s16[144,128]{1,0:T(8,128)(2,1)S(1)} collective-permute-done((s16[144,128]{1,0:T(8,128)(2,1)S(1)}, s16[144,128]{1,0:T(8,128)(2,1)S(1)}, u32[]{:S(2)}, u32[]{:S(2)}) %collective-permute-start.7) | collective-permute-done | bytes 36896 | tf_op jit(solution)/shard_map/ppermute | solution.py:562
  46.0 0.4 collective-permute-done.8.refs_5_
  46.4 1.6 %collective-permute-done.9.refs_6_ = s16[144,128]{1,0:T(8,128)(2,1)S(1)} collective-permute-done((s16[144,128]{1,0:T(8,128)(2,1)S(1)}, s16[144,128]{1,0:T(8,128)(2,1)S(1)}, u32[]{:S(2)}, u32[]{:S(2)}) %collective-permute-start.9) | collective-permute-done | bytes 36896 | tf_op jit(solution)/shard_map/ppermute | solution.py:562
  48.0 1.6 %shard_map.66 = f32[1024,128]{1,0:T(8,128)} custom-call(s16[144,128]{1,0:T(8,128)(2,1)S(1)} %collective-permute-done.3.refs_0_, s16[144,128]{1,0:T(8,128)(2,1)S(1)} %collective-permute-done.4.refs_1_, s16[144,128]{1,0:T(8,128)(2,1)S(1)} %collective-permute-done.5.refs_2_, s16[144,128]{1,0:T(8,128)(2,1)S(1)} %collective-permute-done.6.refs_3_, ...), custom_call_target="tpu_custom_call" | custom-call | tf_op jit(solution)/shard_map/pallas_call | solution.py:451
  (11 shorter events, 0.0 us)
Async XLA Ops:
  1.1 17.7 %copy-start = (s32[1,4,16]{2,1,0:T(4,128)S(1)}, s32[1,4,16]{2,1,0:T(4,128)}, u32[]{:S(2)}) copy-start(s32[1,4,16]{2,1,0:T(4,128)} %match_hbm.1) | copy-start | bytes 772
  1.1 17.7 %copy-start.1 = (s32[128,3]{0,1:T(4,128)S(1)}, s32[128,3]{0,1:T(4,128)}, u32[]{:S(2)}) copy-start(s32[128,3]{0,1:T(4,128)} %param.7) | copy-start | bytes 4612
  1.1 17.7 %copy-start.2 = (f32[32,1024]{1,0:T(8,128)S(1)}, f32[32,1024]{1,0:T(8,128)}, u32[]{:S(2)}) copy-start(f32[32,1024]{1,0:T(8,128)} %constant.8.clone.refs_2_) | copy-start | bytes 393220
  1.1 17.7 %copy-start.3 = (f32[64,512]{1,0:T(8,128)S(1)}, f32[64,512]{1,0:T(8,128)}, u32[]{:S(2)}) copy-start(f32[64,512]{1,0:T(8,128)} %constant.7.clone.refs_1_) | copy-start | bytes 393220
  1.1 17.6 %copy-start.4 = (f32[32,512]{1,0:T(8,128)S(1)}, f32[32,512]{1,0:T(8,128)}, u32[]{:S(2)}) copy-start(f32[32,512]{1,0:T(8,128)} %constant.6.clone.refs_0_) | copy-start | bytes 196612
  17.3 6.4 %collective-permute-start = (bf16[8,128,128]{2,1,0:T(8,128)(2,1)S(1)}, bf16[8,128,128]{2,1,0:T(8,128)(2,1)S(1)}, u32[]{:S(2)}, u32[]{:S(2)}) collective-permute-start(bf16[8,128,128]{2,1,0:T(8,128)(2,1)S(1)} %all_to_all.5.boxes_ref.refs_0_), channel_id=1, source_target_pairs={{0,2},{1,3},{2,0},{3,1},{4,6},{5,7},{6,4},{7,5},{8,10},{9,11},{10,... | collective-permute-start | bytes 786440 | tf_op jit(solution)/shard_map/ppermute | solution.py:404
  22.4 1.6 %collective-permute-start.1 = (bf16[8,128,128]{2,1,0:T(8,128)(2,1)S(1)}, bf16[8,128,128]{2,1,0:T(8,128)(2,1)S(1)}, u32[]{:S(2)}, u32[]{:S(2)}) collective-permute-start(bf16[8,128,128]{2,1,0:T(8,128)(2,1)S(1)} %all_to_all.5.boxes_ref.refs_0_), channel_id=1, source_target_pairs={{0,1},{1,0},{2,3},{3,2},{4,5},{5,4},{6,7},{7,6},{8,9},{9,8},{10,11... | collective-permute-start | bytes 786440 | tf_op jit(solution)/shard_map/ppermute | solution.py:397
  23.6 1.5 %collective-permute-start.2 = (bf16[8,128,128]{2,1,0:T(8,128)(2,1)S(1)}, bf16[8,128,128]{2,1,0:T(8,128)(2,1)S(1)}, u32[]{:S(2)}, u32[]{:S(2)}) collective-permute-start(bf16[8,128,128]{2,1,0:T(8,128)(2,1)S(1)} %collective-permute-done.refs_1_), channel_id=1, source_target_pairs={{0,1},{1,0},{2,3},{3,2},{4,5},{5,4},{6,7},{7,6},{8,9},{9,8},{10,11... | collective-permute-start | bytes 786440 | tf_op jit(solution)/shard_map/ppermute | solution.py:397
  33.4 9.0 %collective-permute-start.3 = (s16[144,128]{1,0:T(8,128)(2,1)S(1)}, s16[144,128]{1,0:T(8,128)(2,1)S(1)}, u32[]{:S(2)}, u32[]{:S(2)}) collective-permute-start(s16[144,128]{1,0:T(8,128)(2,1)S(1)} %get-tuple-element.37), channel_id=1, source_target_pairs={{0,28},{4,24},{8,20},{12,16},{16,12},{20,8},{24,4},{28,0},{1,29},{... | collective-permute-start | bytes 110600 | tf_op jit(solution)/shard_map/ppermute | solution.py:562
  37.1 6.9 %collective-permute-start.4 = (s16[144,128]{1,0:T(8,128)(2,1)S(1)}, s16[144,128]{1,0:T(8,128)(2,1)S(1)}, u32[]{:S(2)}, u32[]{:S(2)}) collective-permute-start(s16[144,128]{1,0:T(8,128)(2,1)S(1)} %get-tuple-element.38), channel_id=1, source_target_pairs={{0,24},{4,28},{8,16},{12,20},{16,8},{20,12},{24,0},{28,4},{1,25},{... | collective-permute-start | bytes 110600 | tf_op jit(solution)/shard_map/ppermute | solution.py:562
  38.2 6.5 %collective-permute-start.5 = (s16[144,128]{1,0:T(8,128)(2,1)S(1)}, s16[144,128]{1,0:T(8,128)(2,1)S(1)}, u32[]{:S(2)}, u32[]{:S(2)}) collective-permute-start(s16[144,128]{1,0:T(8,128)(2,1)S(1)} %get-tuple-element.39), channel_id=1, source_target_pairs={{0,20},{4,16},{8,28},{12,24},{16,4},{20,0},{24,12},{28,8},{1,21},{... | collective-permute-start | bytes 110600 | tf_op jit(solution)/shard_map/ppermute | solution.py:562
  38.6 6.4 %collective-permute-start.6 = (s16[144,128]{1,0:T(8,128)(2,1)S(1)}, s16[144,128]{1,0:T(8,128)(2,1)S(1)}, u32[]{:S(2)}, u32[]{:S(2)}) collective-permute-start(s16[144,128]{1,0:T(8,128)(2,1)S(1)} %get-tuple-element.40), channel_id=1, source_target_pairs={{0,16},{4,20},{8,24},{12,28},{16,0},{20,4},{24,8},{28,12},{1,17},{... | collective-permute-start | bytes 110600 | tf_op jit(solution)/shard_map/ppermute | solution.py:562
  41.1 4.9 %collective-permute-start.7 = (s16[144,128]{1,0:T(8,128)(2,1)S(1)}, s16[144,128]{1,0:T(8,128)(2,1)S(1)}, u32[]{:S(2)}, u32[]{:S(2)}) collective-permute-start(s16[144,128]{1,0:T(8,128)(2,1)S(1)} %get-tuple-element.41), channel_id=1, source_target_pairs={{0,12},{4,8},{8,4},{12,0},{16,28},{20,24},{24,20},{28,16},{1,13},{... | collective-permute-start | bytes 110600 | tf_op jit(solution)/shard_map/ppermute | solution.py:562
  42.4 4.0 %collective-permute-start.8 = (s16[144,128]{1,0:T(8,128)(2,1)S(1)}, s16[144,128]{1,0:T(8,128)(2,1)S(1)}, u32[]{:S(2)}, u32[]{:S(2)}) collective-permute-start(s16[144,128]{1,0:T(8,128)(2,1)S(1)} %get-tuple-element.42), channel_id=1, source_target_pairs={{0,8},{4,12},{8,0},{12,4},{16,24},{20,28},{24,16},{28,20},{1,9},{5... | collective-permute-start | bytes 110600 | tf_op jit(solution)/shard_map/ppermute | solution.py:562
  44.0 4.0 %collective-permute-start.9 = (s16[144,128]{1,0:T(8,128)(2,1)S(1)}, s16[144,128]{1,0:T(8,128)(2,1)S(1)}, u32[]{:S(2)}, u32[]{:S(2)}) collective-permute-start(s16[144,128]{1,0:T(8,128)(2,1)S(1)} %get-tuple-element.43), channel_id=1, source_target_pairs={{0,4},{4,0},{8,12},{12,8},{16,20},{20,16},{24,28},{28,24},{1,5},{5... | collective-permute-start | bytes 110600 | tf_op jit(solution)/shard_map/ppermute | solution.py:562

commit v21 on v20

--- a/solution.py
+++ b/solution.py
@@ -89,21 +89,13 @@
 
 def box_shape(sizes):
     side = sizes[0]
-    return side * side // LANES, LANES // side, side + 2 * REACH
-
-
-def clear_edges(sizes, ref, first, count):
-    side = sizes[0]
+    return side * side // LANES, LANES // side, side + REACH
+
+
+def clear_edges(sizes, ref, count):
     tiles, _, pitch = box_shape(sizes)
-    zeros = jnp.zeros((REACH, LANES), jnp.float32)
-
-    def clear(index, carry):
-        start = (first * tiles + index) * pitch
-        ref[pl.ds(pl.multiple_of(start, 8), REACH), :] = zeros
-        ref[pl.ds(pl.multiple_of(start + REACH + side, 8), REACH), :] = zeros
-        return carry
-
-    lax.fori_loop(0, count * tiles, clear, 0, unroll=8)
+    for index in range(count * tiles + 1):
+        ref[index * pitch : index * pitch + REACH, :] = jnp.zeros((REACH, LANES), jnp.float32)
 
 
 def turned(tiles):
@@ -201,7 +193,7 @@
     copies = [pltpu.make_async_copy(s, t, sems.at[i]) for i, (s, t) in enumerate(zip(sources, targets))]
     for copy in copies:
         copy.start()
-    clear_edges(sizes, fields, 0, own_count)
+    clear_edges(sizes, fields, own_count)
     make_mix(basis_ref, mix_ref)
     make_matrices(basis_ref, line_ref, 0, there_high, there_low)
     make_matrices(basis_ref, line_ref, side, back_high, back_low)
@@ -250,10 +242,9 @@
     ]
     table_copy = pltpu.make_async_copy(table_hbm, table_ref, sems.at[0])
     table_copy.start()
-    for pair in places:
-        clear_edges(sizes, fields, pair * own_count, own_count)
+    clear_edges(sizes, fields, pair_count * own_count)
     for ref in terms:
-        clear_edges(sizes, ref, 0, group)
+        clear_edges(sizes, ref, group)
     for piece_ref, pair in zip(piece_refs, places):
         spread(sizes, piece_ref, fields, pair)
     table_copy.wait()
@@ -407,39 +398,48 @@
 
 def unpack_kernel(sizes, *refs):
     own_count, slab_count, tiles = sizes
-    block_refs, out_hbm, blocks, out_ref, sems, out_sems = refs[:slab_count], *refs[slab_count:]
+    block_refs, out_hbm, out_ref, out_sems = refs[:slab_count], *refs[slab_count:]
     slab_index = lax.axis_index("slab")
+    band_slabs = 8 // own_count
+    assert slab_count & (slab_count - 1) == 0 and band_slabs * own_count == 8
+    row = lax.broadcasted_iota(jnp.int32, (8, LANES), 0)
+
+    def ordered(value):
+        distance = own_count
+        while distance < 8:
+            near = pltpu.roll(value, 8 - distance, axis=0)
+            far = pltpu.roll(value, distance, axis=0)
+            swapped = jnp.where((row & distance) == 0, near, far)
+            value = jnp.where(slab_index // (distance // own_count) % 2 == 1, swapped, value)
+            distance *= 2
+        return value
+
+    row_count = own_count * tiles
     copies = []
-    for index in range(slab_count):
-        slab = partner_of(slab_index, slab_count - 1 - index, slab_count)[1]
-        copies.append(pltpu.make_async_copy(block_refs[index], blocks.at[slab], sems.at[index]))
+    for band in range(slab_count // band_slabs):
+        values = {}
+        for part in range(band_slabs):
+            block_ref = block_refs[slab_count - 1 - band * band_slabs - part]
+            header = block_ref[row_count:, :].astype(jnp.int32).astype(jnp.float32)
+            units = jnp.exp2(header[:8, :])
+            factors = header[8:, :] * (1.0 / (CODE_LIMIT * FACTOR_UNIT))
+            for pair in range(row_count // 16):
+                codes = block_ref[16 * pair : 16 * pair + 16, :].astype(jnp.int32).astype(jnp.float32)
+                for half in range(2):
+                    chunk = 2 * pair + half
+                    own, plane = divmod(8 * chunk, tiles)
+                    value = codes[8 * half : 8 * half + 8, :] * factors[:, chunk : chunk + 1]
+                    values[part * own_count + own, plane // 8] = value * units[:, chunk : chunk + 1]
+        for plane in range(tiles // 8):
+            rows = turned([values[index, plane] for index in range(8)])
+            for tile in range(8):
+                start = (band * tiles + 8 * plane + tile) * 8
+                out_ref[start : start + 8, :] = ordered(rows[tile])
+        target = (slab_index // band_slabs ^ band) * (tiles * 8)
+        source = out_ref.at[band * tiles * 8 : (band + 1) * tiles * 8]
+        target = out_hbm.at[pl.ds(pl.multiple_of(target, 8), tiles * 8)]
+        copies.append(pltpu.make_async_copy(source, target, out_sems.at[band]))
         copies[-1].start()
-    for copy in copies:
-        copy.wait()
-    row_count = own_count * tiles
-    values = {}
-    copies = []
-    for slab in range(slab_count):
-        header = blocks[slab, row_count:, :].astype(jnp.int32).astype(jnp.float32)
-        units = jnp.exp2(header[:8, :])
-        factors = header[8:, :] * (1.0 / (CODE_LIMIT * FACTOR_UNIT))
-        for pair in range(row_count // 16):
-            codes = blocks[slab, 16 * pair : 16 * pair + 16, :].astype(jnp.int32).astype(jnp.float32)
-            for half in range(2):
-                chunk = 2 * pair + half
-                own, plane = divmod(8 * chunk, tiles)
-                value = codes[8 * half : 8 * half + 8, :] * factors[:, chunk : chunk + 1]
-                values[slab * own_count + own, plane // 8] = value * units[:, chunk : chunk + 1]
-        if (slab + 1) * own_count % 8 == 0:
-            band = (slab + 1) * own_count // 8 - 1
-            for plane in range(tiles // 8):
-                rows = turned([values[8 * band + index, plane] for index in range(8)])
-                for tile in range(8):
-                    start = (band * tiles + 8 * plane + tile) * 8
-                    out_ref[start : start + 8, :] = rows[tile]
-            rows = slice(band * tiles * 8, (band + 1) * tiles * 8)
-            copies.append(pltpu.make_async_copy(out_ref.at[rows], out_hbm.at[rows], out_sems.at[band]))
-            copies[-1].start()
     for copy in copies:
         copy.wait()
 
@@ -451,12 +451,10 @@
     out = pl.pallas_call(
         functools.partial(unpack_kernel, (own_count, slab_count, tiles)),
         out_shape=jax.ShapeDtypeStruct((row_count * tiles, LANES), jnp.float32),
-        in_specs=[pl.BlockSpec(memory_space=pl.ANY)] * slab_count,
+        in_specs=[pl.BlockSpec(memory_space=pltpu.VMEM)] * slab_count,
         out_specs=pl.BlockSpec(memory_space=pl.ANY),
         scratch_shapes=[
-            pltpu.VMEM((slab_count,) + blocks[0].shape, jnp.int16),
             pltpu.VMEM((row_count * tiles, LANES), jnp.float32),
-            pltpu.SemaphoreType.DMA((slab_count,)),
             pltpu.SemaphoreType.DMA((row_count // 8,)),
         ],
         compiler_params=pltpu.CompilerParams(vmem_limit_bytes=8 * 1024 * 1024),
@@ -500,7 +498,7 @@
         scratch_shapes=[
             pltpu.SMEM(match.shape, jnp.int32),
             pltpu.SMEM(centers.shape, jnp.int32),
-            pltpu.VMEM((own_count * tiles * pitch, LANES), jnp.float32),
+            pltpu.VMEM((own_count * tiles * pitch + REACH, LANES), jnp.float32),
             pltpu.SemaphoreType.DMA((len(inputs),)),
         ],
         compiler_params=pltpu.CompilerParams(vmem_limit_bytes=32 * 1024 * 1024),
@@ -528,10 +526,10 @@
         scratch_shapes=[
             pltpu.SMEM(table.shape, jnp.int32),
             pltpu.VMEM(mine.shape, jnp.bfloat16),
-            pltpu.VMEM((own_count * pair_count * tiles * pitch, LANES), jnp.float32),
+            pltpu.VMEM((own_count * pair_count * tiles * pitch + REACH, LANES), jnp.float32),
             wide,
             wide,
-            *[pltpu.VMEM((group * tiles * pitch, LANES), jnp.float32)] * (solves // group),
+            *[pltpu.VMEM((group * tiles * pitch + REACH, LANES), jnp.float32)] * (solves // group),
             pltpu.VMEM((slab_count, rows + HEADER_ROWS, LANES), jnp.int16),
             pltpu.SemaphoreType.DMA((1,)),
         ],

time: 49.8 us -> 49.4 us (level)
  no operation moved by 1% of the time
where the time goes in v21:
time: 49.4 us; the launch traced here: 49.2 us
  blocking collectives  16.1 us (33%)
  Pallas kernels  13.1 us (27%)
  starting transfers between devices  12.8 us (26%)
  waiting for transfers between devices  6.03 us (12%)
  local copies, waits for them, and re-layouts  1.11 us (2%)
    all_to_all x1, blocking collectives, shards(): lax.all_to_all(blocks, 'slab', split_axis=0, concat_axis=0, tiled=True)  16.1 us
    ppermute x7, starting transfers between devices, shards(): received.append(lax.ppermute(codes[step], 'slab', perm))  11.2 us
    pallas_call x1, Pallas kernels, team_forces(): pl.pallas_call(functools.partial(force_kernel, sizes), out_shape=[jax.Sha...  8.24 us
    pallas_call x1, Pallas kernels, place_own(): pl.pallas_call(functools.partial(own_kernel, sizes), out_shape=[jax.Shape...  3.61 us
    ppermute x7, waiting for transfers between devices, shards(): received.append(lax.ppermute(codes[step], 'slab', perm))  3.34 us
    ppermute x2, waiting for transfers between devices, swap_cores(): return lax.ppermute(block, 'pair', [(i, i ^ 1) for i in range(pair_count)])  1.53 us
    ppermute x1, starting transfers between devices, gather_chips(): pieces.append(lax.ppermute(boxes, 'pair', perm))  1.49 us
    pallas_call x1, Pallas kernels, unpack(): pl.pallas_call(functools.partial(unpack_kernel, (own_count, slab_count, t...  1.21 us
  transfers between devices with their start and end apart: 10, of which 7 were waited for; matrix products, arithmetic and copies ran while one was open for 0% of the time, Pallas kernels for 7%

profile of v21, /device:TPU:0, one launch (start us, length us, event | category | flops | bytes accessed | tf_op | source)
XLA Modules:
  0.0 49.2 jit_solution(4956318424378052042)
XLA Ops:
  0.0 1.1 %reshape.9 = bf16[8,128,128]{2,1,0:T(8,128)(2,1)S(1)} reshape(bf16[32,4096]{1,0:T(8,128)(2,1)} %param.6) | data formatting | bytes 524288 | tf_op jit(solution)/shard_map/reshape | solution.py:547
  1.1 0.0 copy-start.2
  1.1 0.0 copy-start.3
  1.1 0.0 copy-start.4
  1.1 16.1 %all_to_all.5.boxes_ref.refs_0_ = bf16[8,128,128]{2,1,0:T(8,128)(2,1)S(1)} all-to-all(bf16[8,128,128]{2,1,0:T(8,128)(2,1)S(1)} %reshape.9), channel_id=1, replica_groups=mesh['slab'=8,'pair'=4] {'slab'}, dimensions={0} | all-to-all | bytes 524288 | tf_op jit(solution)/shard_map/all_to_all | solution.py:548
  17.3 1.5 %collective-permute-start = (bf16[8,128,128]{2,1,0:T(8,128)(2,1)S(1)}, bf16[8,128,128]{2,1,0:T(8,128)(2,1)S(1)}, u32[]{:S(2)}, u32[]{:S(2)}) collective-permute-start(bf16[8,128,128]{2,1,0:T(8,128)(2,1)S(1)} %all_to_all.5.boxes_ref.refs_0_), channel_id=1, source_target_pairs={{0,2},{1,3},{2,0},{3,1},{4,6},{5,7},{6,4},{7,5},{8,10},{9,11},{10,... | collective-permute-start | bytes 786440 | tf_op jit(solution)/shard_map/ppermute | solution.py:395
  18.8 3.6 %shard_map.64 = (bf16[512,1024]{1,0:T(8,128)(2,1)S(1)}, s32[128]{0:T(128)S(1)}, bf16[256,768]{1,0:T(8,128)(2,1)S(1)}, f32[32,1024]{1,0:T(8,128)S(1)}, bf16[2,512...) custom-call(s32[1,4,16]{2,1,0:T(4,128)S(1)} %copy-done, ...), custom_call_target="tpu_custom_call" | custom-call | flops 5000000000 | bytes 4194304 | tf_op jit(solution)/shard_map/pallas_call | solution.py:487
  22.4 0.1 collective-permute-start.1
  22.5 1.2 %collective-permute-done.refs_1_ = bf16[8,128,128]{2,1,0:T(8,128)(2,1)S(1)} collective-permute-done((bf16[8,128,128]{2,1,0:T(8,128)(2,1)S(1)}, bf16[8,128,128]{2,1,0:T(8,128)(2,1)S(1)}, u32[]{:S(2)}, u32[]{:S(2)}) %collective-permute-start) | collective-permute-done | bytes 262176 | tf_op jit(solution)/shard_map/ppermute | solution.py:395
  23.6 0.4 collective-permute-done.1.refs_2_
  24.0 1.2 %collective-permute-done.2.refs_3_ = bf16[8,128,128]{2,1,0:T(8,128)(2,1)S(1)} collective-permute-done((bf16[8,128,128]{2,1,0:T(8,128)(2,1)S(1)}, bf16[8,128,128]{2,1,0:T(8,128)(2,1)S(1)}, u32[]{:S(2)}, u32[]{:S(2)}) %collective-permute-start.2) | collective-permute-done | bytes 262176 | tf_op jit(solution)/shard_map/ppermute | solution.py:388
  25.2 8.2 %shard_map.65 = (s16[144,128]{1,0:T(8,128)(2,1)S(1)}, s16[144,128]{1,0:T(8,128)(2,1)S(1)}, s16[144,128]{1,0:T(8,128)(2,1)S(1)}, s16[144,128]{1,0:T(8,128)(2,1)S(...) custom-call(bf16[512,1024]{1,0:T(8,128)(2,1)S(1)} %get-tuple-element, ...), custom_call_target="tpu_custom_call" | custom-call | flops 4831838208 | bytes 8388608 | tf_op jit(solution)/shard_map/pallas_call | solution.py:521
  33.4 3.7 %collective-permute-start.3 = (s16[144,128]{1,0:T(8,128)(2,1)S(1)}, s16[144,128]{1,0:T(8,128)(2,1)S(1)}, u32[]{:S(2)}, u32[]{:S(2)}) collective-permute-start(s16[144,128]{1,0:T(8,128)(2,1)S(1)} %get-tuple-element.37), channel_id=1, source_target_pairs={{0,28},{4,24},{8,20},{12,16},{16,12},{20,8},{24,4},{28,0},{1,29},{... | collective-permute-start | bytes 110600 | tf_op jit(solution)/shard_map/ppermute | solution.py:560
  37.1 1.0 %collective-permute-start.4 = (s16[144,128]{1,0:T(8,128)(2,1)S(1)}, s16[144,128]{1,0:T(8,128)(2,1)S(1)}, u32[]{:S(2)}, u32[]{:S(2)}) collective-permute-start(s16[144,128]{1,0:T(8,128)(2,1)S(1)} %get-tuple-element.38), channel_id=1, source_target_pairs={{0,24},{4,28},{8,16},{12,20},{16,8},{20,12},{24,0},{28,4},{1,25},{... | collective-permute-start | bytes 110600 | tf_op jit(solution)/shard_map/ppermute | solution.py:560
  38.2 0.4 collective-permute-start.5
  38.6 2.6 %collective-permute-start.6 = (s16[144,128]{1,0:T(8,128)(2,1)S(1)}, s16[144,128]{1,0:T(8,128)(2,1)S(1)}, u32[]{:S(2)}, u32[]{:S(2)}) collective-permute-start(s16[144,128]{1,0:T(8,128)(2,1)S(1)} %get-tuple-element.40), channel_id=1, source_target_pairs={{0,16},{4,20},{8,24},{12,28},{16,0},{20,4},{24,8},{28,12},{1,17},{... | collective-permute-start | bytes 110600 | tf_op jit(solution)/shard_map/ppermute | solution.py:560
  41.1 1.3 %collective-permute-start.7 = (s16[144,128]{1,0:T(8,128)(2,1)S(1)}, s16[144,128]{1,0:T(8,128)(2,1)S(1)}, u32[]{:S(2)}, u32[]{:S(2)}) collective-permute-start(s16[144,128]{1,0:T(8,128)(2,1)S(1)} %get-tuple-element.41), channel_id=1, source_target_pairs={{0,12},{4,8},{8,4},{12,0},{16,28},{20,24},{24,20},{28,16},{1,13},{... | collective-permute-start | bytes 110600 | tf_op jit(solution)/shard_map/ppermute | solution.py:560
  42.4 1.6 %collective-permute-start.8 = (s16[144,128]{1,0:T(8,128)(2,1)S(1)}, s16[144,128]{1,0:T(8,128)(2,1)S(1)}, u32[]{:S(2)}, u32[]{:S(2)}) collective-permute-start(s16[144,128]{1,0:T(8,128)(2,1)S(1)} %get-tuple-element.42), channel_id=1, source_target_pairs={{0,8},{4,12},{8,0},{12,4},{16,24},{20,28},{24,16},{28,20},{1,9},{5... | collective-permute-start | bytes 110600 | tf_op jit(solution)/shard_map/ppermute | solution.py:560
  44.0 0.6 %collective-permute-start.9 = (s16[144,128]{1,0:T(8,128)(2,1)S(1)}, s16[144,128]{1,0:T(8,128)(2,1)S(1)}, u32[]{:S(2)}, u32[]{:S(2)}) collective-permute-start(s16[144,128]{1,0:T(8,128)(2,1)S(1)} %get-tuple-element.43), channel_id=1, source_target_pairs={{0,4},{4,0},{8,12},{12,8},{16,20},{20,16},{24,28},{28,24},{1,5},{5... | collective-permute-start | bytes 110600 | tf_op jit(solution)/shard_map/ppermute | solution.py:560
  44.6 0.3 collective-permute-done.6.refs_3_
  44.9 1.1 %collective-permute-done.7.refs_4_ = s16[144,128]{1,0:T(8,128)(2,1)S(1)} collective-permute-done((s16[144,128]{1,0:T(8,128)(2,1)S(1)}, s16[144,128]{1,0:T(8,128)(2,1)S(1)}, u32[]{:S(2)}, u32[]{:S(2)}) %collective-permute-start.7) | collective-permute-done | bytes 36896 | tf_op jit(solution)/shard_map/ppermute | solution.py:560
  46.0 0.4 collective-permute-done.8.refs_5_
  46.4 1.6 %collective-permute-done.9.refs_6_ = s16[144,128]{1,0:T(8,128)(2,1)S(1)} collective-permute-done((s16[144,128]{1,0:T(8,128)(2,1)S(1)}, s16[144,128]{1,0:T(8,128)(2,1)S(1)}, u32[]{:S(2)}, u32[]{:S(2)}) %collective-permute-start.9) | collective-permute-done | bytes 36896 | tf_op jit(solution)/shard_map/ppermute | solution.py:560
  48.0 1.2 %shard_map.66 = f32[1024,128]{1,0:T(8,128)} custom-call(s16[144,128]{1,0:T(8,128)(2,1)S(1)} %collective-permute-done.3.refs_0_, s16[144,128]{1,0:T(8,128)(2,1)S(1)} %collective-permute-done.4.refs_1_, s16[144,128]{1,0:T(8,128)(2,1)S(1)} %collective-permute-done.5.refs_2_, s16[144,128]{1,0:T(8,128)(2,1)S(1)} %collective-permute-done.6.refs_3_, ...), custom_call_target="tpu_custom_call" | custom-call | tf_op jit(solution)/shard_map/pallas_call | solution.py:451
  (11 shorter events, 0.0 us)
Async XLA Ops:
  1.1 17.7 %copy-start = (s32[1,4,16]{2,1,0:T(4,128)S(1)}, s32[1,4,16]{2,1,0:T(4,128)}, u32[]{:S(2)}) copy-start(s32[1,4,16]{2,1,0:T(4,128)} %match_hbm.1) | copy-start | bytes 772
  1.1 17.7 %copy-start.1 = (s32[128,3]{0,1:T(4,128)S(1)}, s32[128,3]{0,1:T(4,128)}, u32[]{:S(2)}) copy-start(s32[128,3]{0,1:T(4,128)} %param.7) | copy-start | bytes 4612
  1.1 17.7 %copy-start.2 = (f32[32,1024]{1,0:T(8,128)S(1)}, f32[32,1024]{1,0:T(8,128)}, u32[]{:S(2)}) copy-start(f32[32,1024]{1,0:T(8,128)} %constant.8.clone.refs_2_) | copy-start | bytes 393220
  1.1 17.7 %copy-start.3 = (f32[64,512]{1,0:T(8,128)S(1)}, f32[64,512]{1,0:T(8,128)}, u32[]{:S(2)}) copy-start(f32[64,512]{1,0:T(8,128)} %constant.7.clone.refs_1_) | copy-start | bytes 393220
  1.1 17.6 %copy-start.4 = (f32[32,512]{1,0:T(8,128)S(1)}, f32[32,512]{1,0:T(8,128)}, u32[]{:S(2)}) copy-start(f32[32,512]{1,0:T(8,128)} %constant.6.clone.refs_0_) | copy-start | bytes 196612
  17.3 6.4 %collective-permute-start = (bf16[8,128,128]{2,1,0:T(8,128)(2,1)S(1)}, bf16[8,128,128]{2,1,0:T(8,128)(2,1)S(1)}, u32[]{:S(2)}, u32[]{:S(2)}) collective-permute-start(bf16[8,128,128]{2,1,0:T(8,128)(2,1)S(1)} %all_to_all.5.boxes_ref.refs_0_), channel_id=1, source_target_pairs={{0,2},{1,3},{2,0},{3,1},{4,6},{5,7},{6,4},{7,5},{8,10},{9,11},{10,... | collective-permute-start | bytes 786440 | tf_op jit(solution)/shard_map/ppermute | solution.py:395
  22.4 1.6 %collective-permute-start.1 = (bf16[8,128,128]{2,1,0:T(8,128)(2,1)S(1)}, bf16[8,128,128]{2,1,0:T(8,128)(2,1)S(1)}, u32[]{:S(2)}, u32[]{:S(2)}) collective-permute-start(bf16[8,128,128]{2,1,0:T(8,128)(2,1)S(1)} %all_to_all.5.boxes_ref.refs_0_), channel_id=1, source_target_pairs={{0,1},{1,0},{2,3},{3,2},{4,5},{5,4},{6,7},{7,6},{8,9},{9,8},{10,11... | collective-permute-start | bytes 786440 | tf_op jit(solution)/shard_map/ppermute | solution.py:388
  23.6 1.5 %collective-permute-start.2 = (bf16[8,128,128]{2,1,0:T(8,128)(2,1)S(1)}, bf16[8,128,128]{2,1,0:T(8,128)(2,1)S(1)}, u32[]{:S(2)}, u32[]{:S(2)}) collective-permute-start(bf16[8,128,128]{2,1,0:T(8,128)(2,1)S(1)} %collective-permute-done.refs_1_), channel_id=1, source_target_pairs={{0,1},{1,0},{2,3},{3,2},{4,5},{5,4},{6,7},{7,6},{8,9},{9,8},{10,11... | collective-permute-start | bytes 786440 | tf_op jit(solution)/shard_map/ppermute | solution.py:388
  33.4 9.0 %collective-permute-start.3 = (s16[144,128]{1,0:T(8,128)(2,1)S(1)}, s16[144,128]{1,0:T(8,128)(2,1)S(1)}, u32[]{:S(2)}, u32[]{:S(2)}) collective-permute-start(s16[144,128]{1,0:T(8,128)(2,1)S(1)} %get-tuple-element.37), channel_id=1, source_target_pairs={{0,28},{4,24},{8,20},{12,16},{16,12},{20,8},{24,4},{28,0},{1,29},{... | collective-permute-start | bytes 110600 | tf_op jit(solution)/shard_map/ppermute | solution.py:560
  37.1 6.9 %collective-permute-start.4 = (s16[144,128]{1,0:T(8,128)(2,1)S(1)}, s16[144,128]{1,0:T(8,128)(2,1)S(1)}, u32[]{:S(2)}, u32[]{:S(2)}) collective-permute-start(s16[144,128]{1,0:T(8,128)(2,1)S(1)} %get-tuple-element.38), channel_id=1, source_target_pairs={{0,24},{4,28},{8,16},{12,20},{16,8},{20,12},{24,0},{28,4},{1,25},{... | collective-permute-start | bytes 110600 | tf_op jit(solution)/shard_map/ppermute | solution.py:560
  38.2 6.5 %collective-permute-start.5 = (s16[144,128]{1,0:T(8,128)(2,1)S(1)}, s16[144,128]{1,0:T(8,128)(2,1)S(1)}, u32[]{:S(2)}, u32[]{:S(2)}) collective-permute-start(s16[144,128]{1,0:T(8,128)(2,1)S(1)} %get-tuple-element.39), channel_id=1, source_target_pairs={{0,20},{4,16},{8,28},{12,24},{16,4},{20,0},{24,12},{28,8},{1,21},{... | collective-permute-start | bytes 110600 | tf_op jit(solution)/shard_map/ppermute | solution.py:560
  38.6 6.4 %collective-permute-start.6 = (s16[144,128]{1,0:T(8,128)(2,1)S(1)}, s16[144,128]{1,0:T(8,128)(2,1)S(1)}, u32[]{:S(2)}, u32[]{:S(2)}) collective-permute-start(s16[144,128]{1,0:T(8,128)(2,1)S(1)} %get-tuple-element.40), channel_id=1, source_target_pairs={{0,16},{4,20},{8,24},{12,28},{16,0},{20,4},{24,8},{28,12},{1,17},{... | collective-permute-start | bytes 110600 | tf_op jit(solution)/shard_map/ppermute | solution.py:560
  41.1 4.9 %collective-permute-start.7 = (s16[144,128]{1,0:T(8,128)(2,1)S(1)}, s16[144,128]{1,0:T(8,128)(2,1)S(1)}, u32[]{:S(2)}, u32[]{:S(2)}) collective-permute-start(s16[144,128]{1,0:T(8,128)(2,1)S(1)} %get-tuple-element.41), channel_id=1, source_target_pairs={{0,12},{4,8},{8,4},{12,0},{16,28},{20,24},{24,20},{28,16},{1,13},{... | collective-permute-start | bytes 110600 | tf_op jit(solution)/shard_map/ppermute | solution.py:560
  42.4 4.0 %collective-permute-start.8 = (s16[144,128]{1,0:T(8,128)(2,1)S(1)}, s16[144,128]{1,0:T(8,128)(2,1)S(1)}, u32[]{:S(2)}, u32[]{:S(2)}) collective-permute-start(s16[144,128]{1,0:T(8,128)(2,1)S(1)} %get-tuple-element.42), channel_id=1, source_target_pairs={{0,8},{4,12},{8,0},{12,4},{16,24},{20,28},{24,16},{28,20},{1,9},{5... | collective-permute-start | bytes 110600 | tf_op jit(solution)/shard_map/ppermute | solution.py:560
  44.0 4.0 %collective-permute-start.9 = (s16[144,128]{1,0:T(8,128)(2,1)S(1)}, s16[144,128]{1,0:T(8,128)(2,1)S(1)}, u32[]{:S(2)}, u32[]{:S(2)}) collective-permute-start(s16[144,128]{1,0:T(8,128)(2,1)S(1)} %get-tuple-element.43), channel_id=1, source_target_pairs={{0,4},{4,0},{8,12},{12,8},{16,20},{20,16},{24,28},{28,24},{1,5},{5... | collective-permute-start | bytes 110600 | tf_op jit(solution)/shard_map/ppermute | solution.py:560

commit v22 on v21

--- a/solution.py
+++ b/solution.py
@@ -228,7 +228,6 @@
     group = min(solves, 8)
     group_rows = group * side
     cells = tiles * LANES
-    width = cells // 2
     slab_index = lax.axis_index("slab")
     pair_index = lax.axis_index("pair")
     core = pair_index % CORES
@@ -289,51 +288,39 @@
         low = source[row_count + start : row_count + start + group_rows, columns]
         return dot(mix_ref[...], jnp.concatenate([high, low, high], axis=0))
 
-    def in_plane(parity, columns, source, high_ref, low_ref):
+    def in_plane(start, parity, source, high_ref, low_ref):
         inner = slice(parity * half_cells, (parity + 1) * half_cells)
-        high = source[:row_count, inner]
-        low = source[row_count:, inner]
-        basis = high_ref[parity, :, columns]
-        rest = low_ref[parity, :, columns]
+        high = source[start : start + group_rows, inner]
+        low = source[row_count + start : row_count + start + group_rows, inner]
+        basis = high_ref[parity]
         left = jnp.concatenate([high, low, high], axis=1)
-        return dot(left, jnp.concatenate([basis, basis, rest], axis=0))
-
-    for start in range(0, row_count, group_rows):
+        return dot(left, jnp.concatenate([basis, basis, low_ref[parity]], axis=0))
+
+    def solve_group(start):
         for index in range(start // side, (start + group_rows) // side):
             densities(index)
         columns = slice(0, cells)
         store_split(second, start, group_rows, columns, along_x(start, columns, first))
-
-    for parity in range(2):
-        for column in range(0, half_cells, width):
-            columns = slice(column, column + width)
-            value = in_plane(parity, columns, second, there_high, there_low)
-            columns = slice(parity * half_cells + column, parity * half_cells + column + width)
-            gain = gain_ref[:, columns]
-            value = (value.reshape(solves, side, width) * gain[None]).reshape(row_count, width)
-            store_split(first, 0, row_count, columns, value)
-
-    for parity in range(2):
-        for column in range(0, half_cells, width):
-            value = in_plane(parity, slice(column, column + width), first, back_high, back_low)
-            columns = slice(parity * half_cells + column, parity * half_cells + column + width)
-            store_split(second, 0, row_count, columns, value)
-
-    for start in range(0, row_count, group_rows):
-        for column in range(0, half_cells, width):
-            even = along_x(start, slice(column, column + width), second)
-            odd = along_x(start, slice(half_cells + column, half_cells + column + width), second)
-            for part in range(width // LANES):
-                tile = column // LANES + part
-                lanes = slice(part * LANES, (part + 1) * LANES)
-                near = even[:, lanes] + odd[:, lanes]
-                far = mirrored(even[:, lanes] - odd[:, lanes])
-                for place, value in ((tile, near), (tiles - 1 - tile, far)):
-                    columns = slice(place * LANES, (place + 1) * LANES)
-                    value = value * partner[start : start + group_rows, columns].astype(jnp.float32)
-                    for solve in range(group):
-                        row = (solve * tiles + place) * pitch + REACH
-                        terms[start // group_rows][row : row + side, :] = value[solve * side : (solve + 1) * side, :]
+        for parity in range(2):
+            columns = slice(parity * half_cells, (parity + 1) * half_cells)
+            value = in_plane(start, parity, second, there_high, there_low)
+            value = value.reshape(group, side, half_cells) * gain_ref[:, columns][None]
+            store_split(first, start, group_rows, columns, value.reshape(group_rows, half_cells))
+        for parity in range(2):
+            columns = slice(parity * half_cells, (parity + 1) * half_cells)
+            store_split(second, start, group_rows, columns, in_plane(start, parity, first, back_high, back_low))
+        even = along_x(start, slice(0, half_cells), second)
+        odd = along_x(start, slice(half_cells, cells), second)
+        for tile in range(half_tiles):
+            lanes = slice(tile * LANES, (tile + 1) * LANES)
+            near = even[:, lanes] + odd[:, lanes]
+            far = mirrored(even[:, lanes] - odd[:, lanes])
+            for place, value in ((tile, near), (tiles - 1 - tile, far)):
+                columns = slice(place * LANES, (place + 1) * LANES)
+                value = value * partner[start : start + group_rows, columns].astype(jnp.float32)
+                for solve in range(group):
+                    row = (solve * tiles + place) * pitch + REACH
+                    terms[start // group_rows][row : row + side, :] = value[solve * side : (solve + 1) * side, :]
 
     step_rows = 16
 
@@ -352,6 +339,8 @@
     factors = [jnp.zeros((tiles, LANES), jnp.float32)] * slab_count
     codes = {}
     for own in range(own_count):
+        if own * rounds % group == 0:
+            solve_group(own * rounds * side)
         for row in range(0, side, step_rows):
             sums = collect(own, row)
             for half in range(0, step_rows, 8):

time: 49.4 us -> 49 us (level)
  no operation moved by 1% of the time
where the time goes in v22:
time: 49 us; the launch traced here: 48.9 us
  blocking collectives  16.1 us (33%)
  starting transfers between devices  12.8 us (26%)
  Pallas kernels  12.7 us (26%)
  waiting for transfers between devices  6.04 us (12%)
  local copies, waits for them, and re-layouts  1.11 us (2%)
    all_to_all x1, blocking collectives, shards(): lax.all_to_all(blocks, 'slab', split_axis=0, concat_axis=0, tiled=True)  16.1 us
    ppermute x7, starting transfers between devices, shards(): received.append(lax.ppermute(codes[step], 'slab', perm))  11.2 us
    pallas_call x1, Pallas kernels, team_forces(): pl.pallas_call(functools.partial(force_kernel, sizes), out_shape=[jax.Sha...  7.91 us
    pallas_call x1, Pallas kernels, place_own(): pl.pallas_call(functools.partial(own_kernel, sizes), out_shape=[jax.Shape...  3.61 us
    ppermute x7, waiting for transfers between devices, shards(): received.append(lax.ppermute(codes[step], 'slab', perm))  3.35 us
    ppermute x2, waiting for transfers between devices, swap_cores(): return lax.ppermute(block, 'pair', [(i, i ^ 1) for i in range(pair_count)])  1.53 us
    ppermute x1, starting transfers between devices, gather_chips(): pieces.append(lax.ppermute(boxes, 'pair', perm))  1.49 us
    pallas_call x1, Pallas kernels, unpack(): pl.pallas_call(functools.partial(unpack_kernel, (own_count, slab_count, t...  1.21 us
  transfers between devices with their start and end apart: 10, of which 7 were waited for; matrix products, arithmetic and copies ran while one was open for 0% of the time, Pallas kernels for 7%

profile of v22, /device:TPU:0, one launch (start us, length us, event | category | flops | bytes accessed | tf_op | source)
XLA Modules:
  0.0 48.9 jit_solution(3469249377699001912)
XLA Ops:
  0.0 1.1 %reshape.9 = bf16[8,128,128]{2,1,0:T(8,128)(2,1)S(1)} reshape(bf16[32,4096]{1,0:T(8,128)(2,1)} %param.6) | data formatting | bytes 524288 | tf_op jit(solution)/shard_map/reshape | solution.py:536
  1.1 0.0 copy-start.2
  1.1 0.0 copy-start.3
  1.1 0.0 copy-start.4
  1.1 16.1 %all_to_all.5.boxes_ref.refs_0_ = bf16[8,128,128]{2,1,0:T(8,128)(2,1)S(1)} all-to-all(bf16[8,128,128]{2,1,0:T(8,128)(2,1)S(1)} %reshape.9), channel_id=1, replica_groups=mesh['slab'=8,'pair'=4] {'slab'}, dimensions={0} | all-to-all | bytes 524288 | tf_op jit(solution)/shard_map/all_to_all | solution.py:537
  17.3 1.5 %collective-permute-start = (bf16[8,128,128]{2,1,0:T(8,128)(2,1)S(1)}, bf16[8,128,128]{2,1,0:T(8,128)(2,1)S(1)}, u32[]{:S(2)}, u32[]{:S(2)}) collective-permute-start(bf16[8,128,128]{2,1,0:T(8,128)(2,1)S(1)} %all_to_all.5.boxes_ref.refs_0_), channel_id=1, source_target_pairs={{0,2},{1,3},{2,0},{3,1},{4,6},{5,7},{6,4},{7,5},{8,10},{9,11},{10,... | collective-permute-start | bytes 786440 | tf_op jit(solution)/shard_map/ppermute | solution.py:384
  18.8 3.6 %shard_map.64 = (bf16[512,1024]{1,0:T(8,128)(2,1)S(1)}, s32[128]{0:T(128)S(1)}, bf16[256,768]{1,0:T(8,128)(2,1)S(1)}, f32[32,1024]{1,0:T(8,128)S(1)}, bf16[2,512...) custom-call(s32[1,4,16]{2,1,0:T(4,128)S(1)} %copy-done, ...), custom_call_target="tpu_custom_call" | custom-call | flops 5000000000 | bytes 4194304 | tf_op jit(solution)/shard_map/pallas_call | solution.py:476
  22.4 0.1 collective-permute-start.1
  22.5 1.2 %collective-permute-done.refs_1_ = bf16[8,128,128]{2,1,0:T(8,128)(2,1)S(1)} collective-permute-done((bf16[8,128,128]{2,1,0:T(8,128)(2,1)S(1)}, bf16[8,128,128]{2,1,0:T(8,128)(2,1)S(1)}, u32[]{:S(2)}, u32[]{:S(2)}) %collective-permute-start) | collective-permute-done | bytes 262176 | tf_op jit(solution)/shard_map/ppermute | solution.py:384
  23.6 0.4 collective-permute-done.1.refs_2_
  24.0 1.2 %collective-permute-done.2.refs_3_ = bf16[8,128,128]{2,1,0:T(8,128)(2,1)S(1)} collective-permute-done((bf16[8,128,128]{2,1,0:T(8,128)(2,1)S(1)}, bf16[8,128,128]{2,1,0:T(8,128)(2,1)S(1)}, u32[]{:S(2)}, u32[]{:S(2)}) %collective-permute-start.2) | collective-permute-done | bytes 262176 | tf_op jit(solution)/shard_map/ppermute | solution.py:377
  25.2 7.9 %shard_map.65 = (s16[144,128]{1,0:T(8,128)(2,1)S(1)}, s16[144,128]{1,0:T(8,128)(2,1)S(1)}, s16[144,128]{1,0:T(8,128)(2,1)S(1)}, s16[144,128]{1,0:T(8,128)(2,1)S(...) custom-call(bf16[512,1024]{1,0:T(8,128)(2,1)S(1)} %get-tuple-element, ...), custom_call_target="tpu_custom_call" | custom-call | flops 4831838208 | bytes 8388608 | tf_op jit(solution)/shard_map/pallas_call | solution.py:510
  33.1 3.7 %collective-permute-start.3 = (s16[144,128]{1,0:T(8,128)(2,1)S(1)}, s16[144,128]{1,0:T(8,128)(2,1)S(1)}, u32[]{:S(2)}, u32[]{:S(2)}) collective-permute-start(s16[144,128]{1,0:T(8,128)(2,1)S(1)} %get-tuple-element.37), channel_id=1, source_target_pairs={{0,28},{4,24},{8,20},{12,16},{16,12},{20,8},{24,4},{28,0},{1,29},{... | collective-permute-start | bytes 110600 | tf_op jit(solution)/shard_map/ppermute | solution.py:549
  36.8 1.0 %collective-permute-start.4 = (s16[144,128]{1,0:T(8,128)(2,1)S(1)}, s16[144,128]{1,0:T(8,128)(2,1)S(1)}, u32[]{:S(2)}, u32[]{:S(2)}) collective-permute-start(s16[144,128]{1,0:T(8,128)(2,1)S(1)} %get-tuple-element.38), channel_id=1, source_target_pairs={{0,24},{4,28},{8,16},{12,20},{16,8},{20,12},{24,0},{28,4},{1,25},{... | collective-permute-start | bytes 110600 | tf_op jit(solution)/shard_map/ppermute | solution.py:549
  37.8 0.4 collective-permute-start.5
  38.2 2.6 %collective-permute-start.6 = (s16[144,128]{1,0:T(8,128)(2,1)S(1)}, s16[144,128]{1,0:T(8,128)(2,1)S(1)}, u32[]{:S(2)}, u32[]{:S(2)}) collective-permute-start(s16[144,128]{1,0:T(8,128)(2,1)S(1)} %get-tuple-element.40), channel_id=1, source_target_pairs={{0,16},{4,20},{8,24},{12,28},{16,0},{20,4},{24,8},{28,12},{1,17},{... | collective-permute-start | bytes 110600 | tf_op jit(solution)/shard_map/ppermute | solution.py:549
  40.8 1.3 %collective-permute-start.7 = (s16[144,128]{1,0:T(8,128)(2,1)S(1)}, s16[144,128]{1,0:T(8,128)(2,1)S(1)}, u32[]{:S(2)}, u32[]{:S(2)}) collective-permute-start(s16[144,128]{1,0:T(8,128)(2,1)S(1)} %get-tuple-element.41), channel_id=1, source_target_pairs={{0,12},{4,8},{8,4},{12,0},{16,28},{20,24},{24,20},{28,16},{1,13},{... | collective-permute-start | bytes 110600 | tf_op jit(solution)/shard_map/ppermute | solution.py:549
  42.1 1.6 %collective-permute-start.8 = (s16[144,128]{1,0:T(8,128)(2,1)S(1)}, s16[144,128]{1,0:T(8,128)(2,1)S(1)}, u32[]{:S(2)}, u32[]{:S(2)}) collective-permute-start(s16[144,128]{1,0:T(8,128)(2,1)S(1)} %get-tuple-element.42), channel_id=1, source_target_pairs={{0,8},{4,12},{8,0},{12,4},{16,24},{20,28},{24,16},{28,20},{1,9},{5... | collective-permute-start | bytes 110600 | tf_op jit(solution)/shard_map/ppermute | solution.py:549
  43.7 0.6 %collective-permute-start.9 = (s16[144,128]{1,0:T(8,128)(2,1)S(1)}, s16[144,128]{1,0:T(8,128)(2,1)S(1)}, u32[]{:S(2)}, u32[]{:S(2)}) collective-permute-start(s16[144,128]{1,0:T(8,128)(2,1)S(1)} %get-tuple-element.43), channel_id=1, source_target_pairs={{0,4},{4,0},{8,12},{12,8},{16,20},{20,16},{24,28},{28,24},{1,5},{5... | collective-permute-start | bytes 110600 | tf_op jit(solution)/shard_map/ppermute | solution.py:549
  44.3 0.3 collective-permute-done.6.refs_3_
  44.6 1.1 %collective-permute-done.7.refs_4_ = s16[144,128]{1,0:T(8,128)(2,1)S(1)} collective-permute-done((s16[144,128]{1,0:T(8,128)(2,1)S(1)}, s16[144,128]{1,0:T(8,128)(2,1)S(1)}, u32[]{:S(2)}, u32[]{:S(2)}) %collective-permute-start.7) | collective-permute-done | bytes 36896 | tf_op jit(solution)/shard_map/ppermute | solution.py:549
  45.7 0.4 collective-permute-done.8.refs_5_
  46.0 1.6 %collective-permute-done.9.refs_6_ = s16[144,128]{1,0:T(8,128)(2,1)S(1)} collective-permute-done((s16[144,128]{1,0:T(8,128)(2,1)S(1)}, s16[144,128]{1,0:T(8,128)(2,1)S(1)}, u32[]{:S(2)}, u32[]{:S(2)}) %collective-permute-start.9) | collective-permute-done | bytes 36896 | tf_op jit(solution)/shard_map/ppermute | solution.py:549
  47.6 1.2 %shard_map.66 = f32[1024,128]{1,0:T(8,128)} custom-call(s16[144,128]{1,0:T(8,128)(2,1)S(1)} %collective-permute-done.3.refs_0_, s16[144,128]{1,0:T(8,128)(2,1)S(1)} %collective-permute-done.4.refs_1_, s16[144,128]{1,0:T(8,128)(2,1)S(1)} %collective-permute-done.5.refs_2_, s16[144,128]{1,0:T(8,128)(2,1)S(1)} %collective-permute-done.6.refs_3_, ...), custom_call_target="tpu_custom_call" | custom-call | tf_op jit(solution)/shard_map/pallas_call | solution.py:440
  (11 shorter events, 0.0 us)
Async XLA Ops:
  1.1 17.7 %copy-start = (s32[1,4,16]{2,1,0:T(4,128)S(1)}, s32[1,4,16]{2,1,0:T(4,128)}, u32[]{:S(2)}) copy-start(s32[1,4,16]{2,1,0:T(4,128)} %match_hbm.1) | copy-start | bytes 772
  1.1 17.7 %copy-start.1 = (s32[128,3]{0,1:T(4,128)S(1)}, s32[128,3]{0,1:T(4,128)}, u32[]{:S(2)}) copy-start(s32[128,3]{0,1:T(4,128)} %param.7) | copy-start | bytes 4612
  1.1 17.7 %copy-start.2 = (f32[32,1024]{1,0:T(8,128)S(1)}, f32[32,1024]{1,0:T(8,128)}, u32[]{:S(2)}) copy-start(f32[32,1024]{1,0:T(8,128)} %constant.8.clone.refs_2_) | copy-start | bytes 393220
  1.1 17.7 %copy-start.3 = (f32[64,512]{1,0:T(8,128)S(1)}, f32[64,512]{1,0:T(8,128)}, u32[]{:S(2)}) copy-start(f32[64,512]{1,0:T(8,128)} %constant.7.clone.refs_1_) | copy-start | bytes 393220
  1.1 17.6 %copy-start.4 = (f32[32,512]{1,0:T(8,128)S(1)}, f32[32,512]{1,0:T(8,128)}, u32[]{:S(2)}) copy-start(f32[32,512]{1,0:T(8,128)} %constant.6.clone.refs_0_) | copy-start | bytes 196612
  17.3 6.4 %collective-permute-start = (bf16[8,128,128]{2,1,0:T(8,128)(2,1)S(1)}, bf16[8,128,128]{2,1,0:T(8,128)(2,1)S(1)}, u32[]{:S(2)}, u32[]{:S(2)}) collective-permute-start(bf16[8,128,128]{2,1,0:T(8,128)(2,1)S(1)} %all_to_all.5.boxes_ref.refs_0_), channel_id=1, source_target_pairs={{0,2},{1,3},{2,0},{3,1},{4,6},{5,7},{6,4},{7,5},{8,10},{9,11},{10,... | collective-permute-start | bytes 786440 | tf_op jit(solution)/shard_map/ppermute | solution.py:384
  22.4 1.6 %collective-permute-start.1 = (bf16[8,128,128]{2,1,0:T(8,128)(2,1)S(1)}, bf16[8,128,128]{2,1,0:T(8,128)(2,1)S(1)}, u32[]{:S(2)}, u32[]{:S(2)}) collective-permute-start(bf16[8,128,128]{2,1,0:T(8,128)(2,1)S(1)} %all_to_all.5.boxes_ref.refs_0_), channel_id=1, source_target_pairs={{0,1},{1,0},{2,3},{3,2},{4,5},{5,4},{6,7},{7,6},{8,9},{9,8},{10,11... | collective-permute-start | bytes 786440 | tf_op jit(solution)/shard_map/ppermute | solution.py:377
  23.6 1.5 %collective-permute-start.2 = (bf16[8,128,128]{2,1,0:T(8,128)(2,1)S(1)}, bf16[8,128,128]{2,1,0:T(8,128)(2,1)S(1)}, u32[]{:S(2)}, u32[]{:S(2)}) collective-permute-start(bf16[8,128,128]{2,1,0:T(8,128)(2,1)S(1)} %collective-permute-done.refs_1_), channel_id=1, source_target_pairs={{0,1},{1,0},{2,3},{3,2},{4,5},{5,4},{6,7},{7,6},{8,9},{9,8},{10,11... | collective-permute-start | bytes 786440 | tf_op jit(solution)/shard_map/ppermute | solution.py:377
  33.1 9.0 %collective-permute-start.3 = (s16[144,128]{1,0:T(8,128)(2,1)S(1)}, s16[144,128]{1,0:T(8,128)(2,1)S(1)}, u32[]{:S(2)}, u32[]{:S(2)}) collective-permute-start(s16[144,128]{1,0:T(8,128)(2,1)S(1)} %get-tuple-element.37), channel_id=1, source_target_pairs={{0,28},{4,24},{8,20},{12,16},{16,12},{20,8},{24,4},{28,0},{1,29},{... | collective-permute-start | bytes 110600 | tf_op jit(solution)/shard_map/ppermute | solution.py:549
  36.8 6.9 %collective-permute-start.4 = (s16[144,128]{1,0:T(8,128)(2,1)S(1)}, s16[144,128]{1,0:T(8,128)(2,1)S(1)}, u32[]{:S(2)}, u32[]{:S(2)}) collective-permute-start(s16[144,128]{1,0:T(8,128)(2,1)S(1)} %get-tuple-element.38), channel_id=1, source_target_pairs={{0,24},{4,28},{8,16},{12,20},{16,8},{20,12},{24,0},{28,4},{1,25},{... | collective-permute-start | bytes 110600 | tf_op jit(solution)/shard_map/ppermute | solution.py:549
  37.8 6.5 %collective-permute-start.5 = (s16[144,128]{1,0:T(8,128)(2,1)S(1)}, s16[144,128]{1,0:T(8,128)(2,1)S(1)}, u32[]{:S(2)}, u32[]{:S(2)}) collective-permute-start(s16[144,128]{1,0:T(8,128)(2,1)S(1)} %get-tuple-element.39), channel_id=1, source_target_pairs={{0,20},{4,16},{8,28},{12,24},{16,4},{20,0},{24,12},{28,8},{1,21},{... | collective-permute-start | bytes 110600 | tf_op jit(solution)/shard_map/ppermute | solution.py:549
  38.2 6.4 %collective-permute-start.6 = (s16[144,128]{1,0:T(8,128)(2,1)S(1)}, s16[144,128]{1,0:T(8,128)(2,1)S(1)}, u32[]{:S(2)}, u32[]{:S(2)}) collective-permute-start(s16[144,128]{1,0:T(8,128)(2,1)S(1)} %get-tuple-element.40), channel_id=1, source_target_pairs={{0,16},{4,20},{8,24},{12,28},{16,0},{20,4},{24,8},{28,12},{1,17},{... | collective-permute-start | bytes 110600 | tf_op jit(solution)/shard_map/ppermute | solution.py:549
  40.8 4.9 %collective-permute-start.7 = (s16[144,128]{1,0:T(8,128)(2,1)S(1)}, s16[144,128]{1,0:T(8,128)(2,1)S(1)}, u32[]{:S(2)}, u32[]{:S(2)}) collective-permute-start(s16[144,128]{1,0:T(8,128)(2,1)S(1)} %get-tuple-element.41), channel_id=1, source_target_pairs={{0,12},{4,8},{8,4},{12,0},{16,28},{20,24},{24,20},{28,16},{1,13},{... | collective-permute-start | bytes 110600 | tf_op jit(solution)/shard_map/ppermute | solution.py:549
  42.1 4.0 %collective-permute-start.8 = (s16[144,128]{1,0:T(8,128)(2,1)S(1)}, s16[144,128]{1,0:T(8,128)(2,1)S(1)}, u32[]{:S(2)}, u32[]{:S(2)}) collective-permute-start(s16[144,128]{1,0:T(8,128)(2,1)S(1)} %get-tuple-element.42), channel_id=1, source_target_pairs={{0,8},{4,12},{8,0},{12,4},{16,24},{20,28},{24,16},{28,20},{1,9},{5... | collective-permute-start | bytes 110600 | tf_op jit(solution)/shard_map/ppermute | solution.py:549
  43.7 4.0 %collective-permute-start.9 = (s16[144,128]{1,0:T(8,128)(2,1)S(1)}, s16[144,128]{1,0:T(8,128)(2,1)S(1)}, u32[]{:S(2)}, u32[]{:S(2)}) collective-permute-start(s16[144,128]{1,0:T(8,128)(2,1)S(1)} %get-tuple-element.43), channel_id=1, source_target_pairs={{0,4},{4,0},{8,12},{12,8},{16,20},{20,16},{24,28},{28,24},{1,5},{5... | collective-permute-start | bytes 110600 | tf_op jit(solution)/shard_map/ppermute | solution.py:549

commit v23 on v22

--- a/solution.py
+++ b/solution.py
@@ -408,7 +408,7 @@
     for band in range(slab_count // band_slabs):
         values = {}
         for part in range(band_slabs):
-            block_ref = block_refs[slab_count - 1 - band * band_slabs - part]
+            block_ref = block_refs[band * band_slabs + part]
             header = block_ref[row_count:, :].astype(jnp.int32).astype(jnp.float32)
             units = jnp.exp2(header[:8, :])
             factors = header[8:, :] * (1.0 / (CODE_LIMIT * FACTOR_UNIT))
@@ -543,11 +543,11 @@
     pieces, mine = lax.optimization_barrier((pieces, mine))
     swapped += [swap_cores(piece, pair_count) for piece in pieces]
     codes = team_forces(sizes, mine, table, constants, [boxes] + pieces + swapped)
-    received = []
-    for step in reversed(range(1, slab_count)):
+    received = [codes[0]]
+    for step in range(1, slab_count):
         perm = [(i, partner_of(i, step, slab_count)[0]) for i in range(slab_count)]
         received.append(lax.ppermute(codes[step], "slab", perm))
-    return unpack(received + [codes[0]], own_count, plane_cells)
+    return unpack(received, own_count, plane_cells)
 
 
 def solution(mesh):

time: 49 us -> 51.3 us (1.047)
  waiting for transfers between devices: 6.04 us -> 8.27 us
    ppermute x7, waiting for transfers between devices: 3.35 us -> 5.58 us  [shards(): received.append(lax.ppermute(codes[step], 'slab', perm))]
  transfers between devices with their start and end apart: 10 -> 10, of which waited for: 7 -> 6; matrix products, arithmetic and copies ran while one was open for 0% -> 0% of each run, Pallas kernels for 7% -> 7%
where the time goes in v23:
time: 51.3 us; the launch traced here: 51.1 us
  blocking collectives  16.1 us (31%)
  starting transfers between devices  12.8 us (25%)
  Pallas kernels  12.7 us (25%)
  waiting for transfers between devices  8.27 us (16%)
  local copies, waits for them, and re-layouts  1.11 us (2%)
    all_to_all x1, blocking collectives, shards(): lax.all_to_all(blocks, 'slab', split_axis=0, concat_axis=0, tiled=True)  16.1 us
    ppermute x7, starting transfers between devices, shards(): received.append(lax.ppermute(codes[step], 'slab', perm))  11.2 us
    pallas_call x1, Pallas kernels, team_forces(): pl.pallas_call(functools.partial(force_kernel, sizes), out_shape=[jax.Sha...  7.9 us
    ppermute x7, waiting for transfers between devices, shards(): received.append(lax.ppermute(codes[step], 'slab', perm))  5.58 us
    pallas_call x1, Pallas kernels, place_own(): pl.pallas_call(functools.partial(own_kernel, sizes), out_shape=[jax.Shape...  3.61 us
    ppermute x2, waiting for transfers between devices, swap_cores(): return lax.ppermute(block, 'pair', [(i, i ^ 1) for i in range(pair_count)])  1.53 us
    ppermute x1, starting transfers between devices, gather_chips(): pieces.append(lax.ppermute(boxes, 'pair', perm))  1.49 us
    pallas_call x1, Pallas kernels, unpack(): pl.pallas_call(functools.partial(unpack_kernel, (own_count, slab_count, t...  1.21 us
  transfers between devices with their start and end apart: 10, of which 6 were waited for; matrix products, arithmetic and copies ran while one was open for 0% of the time, Pallas kernels for 7%

profile of v23, /device:TPU:0, one launch (start us, length us, event | category | flops | bytes accessed | tf_op | source)
XLA Modules:
  0.0 51.1 jit_solution(1567827153755429371)
XLA Ops:
  0.0 1.1 %reshape.9 = bf16[8,128,128]{2,1,0:T(8,128)(2,1)S(1)} reshape(bf16[32,4096]{1,0:T(8,128)(2,1)} %param.6) | data formatting | bytes 524288 | tf_op jit(solution)/shard_map/reshape | solution.py:536
  1.1 0.0 copy-start.1
  1.1 0.0 copy-start.2
  1.1 0.0 copy-start.3
  1.1 0.0 copy-start.4
  1.1 16.1 %all_to_all.5.boxes_ref.refs_0_ = bf16[8,128,128]{2,1,0:T(8,128)(2,1)S(1)} all-to-all(bf16[8,128,128]{2,1,0:T(8,128)(2,1)S(1)} %reshape.9), channel_id=1, replica_groups=mesh['slab'=8,'pair'=4] {'slab'}, dimensions={0} | all-to-all | bytes 524288 | tf_op jit(solution)/shard_map/all_to_all | solution.py:537
  17.3 1.5 %collective-permute-start = (bf16[8,128,128]{2,1,0:T(8,128)(2,1)S(1)}, bf16[8,128,128]{2,1,0:T(8,128)(2,1)S(1)}, u32[]{:S(2)}, u32[]{:S(2)}) collective-permute-start(bf16[8,128,128]{2,1,0:T(8,128)(2,1)S(1)} %all_to_all.5.boxes_ref.refs_0_), channel_id=1, source_target_pairs={{0,2},{1,3},{2,0},{3,1},{4,6},{5,7},{6,4},{7,5},{8,10},{9,11},{10,... | collective-permute-start | bytes 786440 | tf_op jit(solution)/shard_map/ppermute | solution.py:384
  18.8 3.6 %shard_map.64 = (bf16[512,1024]{1,0:T(8,128)(2,1)S(1)}, s32[128]{0:T(128)S(1)}, bf16[256,768]{1,0:T(8,128)(2,1)S(1)}, f32[32,1024]{1,0:T(8,128)S(1)}, bf16[2,512...) custom-call(s32[1,4,16]{2,1,0:T(4,128)S(1)} %copy-done, ...), custom_call_target="tpu_custom_call" | custom-call | flops 5000000000 | bytes 4194304 | tf_op jit(solution)/shard_map/pallas_call | solution.py:476
  22.4 0.1 collective-permute-start.1
  22.5 1.2 %collective-permute-done.refs_1_ = bf16[8,128,128]{2,1,0:T(8,128)(2,1)S(1)} collective-permute-done((bf16[8,128,128]{2,1,0:T(8,128)(2,1)S(1)}, bf16[8,128,128]{2,1,0:T(8,128)(2,1)S(1)}, u32[]{:S(2)}, u32[]{:S(2)}) %collective-permute-start) | collective-permute-done | bytes 262176 | tf_op jit(solution)/shard_map/ppermute | solution.py:384
  23.6 0.4 collective-permute-done.1.refs_2_
  24.0 1.2 %collective-permute-done.2.refs_3_ = bf16[8,128,128]{2,1,0:T(8,128)(2,1)S(1)} collective-permute-done((bf16[8,128,128]{2,1,0:T(8,128)(2,1)S(1)}, bf16[8,128,128]{2,1,0:T(8,128)(2,1)S(1)}, u32[]{:S(2)}, u32[]{:S(2)}) %collective-permute-start.2) | collective-permute-done | bytes 262176 | tf_op jit(solution)/shard_map/ppermute | solution.py:377
  25.2 7.9 %shard_map.65 = (s16[144,128]{1,0:T(8,128)(2,1)S(1)}, s16[144,128]{1,0:T(8,128)(2,1)S(1)}, s16[144,128]{1,0:T(8,128)(2,1)S(1)}, s16[144,128]{1,0:T(8,128)(2,1)S(...) custom-call(bf16[512,1024]{1,0:T(8,128)(2,1)S(1)} %get-tuple-element, ...), custom_call_target="tpu_custom_call" | custom-call | flops 4831838208 | bytes 8388608 | tf_op jit(solution)/shard_map/pallas_call | solution.py:510
  33.1 1.5 %collective-permute-start.3 = (s16[144,128]{1,0:T(8,128)(2,1)S(1)}, s16[144,128]{1,0:T(8,128)(2,1)S(1)}, u32[]{:S(2)}, u32[]{:S(2)}) collective-permute-start(s16[144,128]{1,0:T(8,128)(2,1)S(1)} %get-tuple-element.38), channel_id=1, source_target_pairs={{0,4},{4,0},{8,12},{12,8},{16,20},{20,16},{24,28},{28,24},{1,5},{5... | collective-permute-start | bytes 110600 | tf_op jit(solution)/shard_map/ppermute | solution.py:549
  34.6 0.3 collective-permute-start.4
  34.8 1.8 %collective-permute-start.5 = (s16[144,128]{1,0:T(8,128)(2,1)S(1)}, s16[144,128]{1,0:T(8,128)(2,1)S(1)}, u32[]{:S(2)}, u32[]{:S(2)}) collective-permute-start(s16[144,128]{1,0:T(8,128)(2,1)S(1)} %get-tuple-element.40), channel_id=1, source_target_pairs={{0,12},{4,8},{8,4},{12,0},{16,28},{20,24},{24,20},{28,16},{1,13},{... | collective-permute-start | bytes 110600 | tf_op jit(solution)/shard_map/ppermute | solution.py:549
  36.6 2.2 %collective-permute-start.6 = (s16[144,128]{1,0:T(8,128)(2,1)S(1)}, s16[144,128]{1,0:T(8,128)(2,1)S(1)}, u32[]{:S(2)}, u32[]{:S(2)}) collective-permute-start(s16[144,128]{1,0:T(8,128)(2,1)S(1)} %get-tuple-element.41), channel_id=1, source_target_pairs={{0,16},{4,20},{8,24},{12,28},{16,0},{20,4},{24,8},{28,12},{1,17},{... | collective-permute-start | bytes 110600 | tf_op jit(solution)/shard_map/ppermute | solution.py:549
  38.8 1.6 %collective-permute-start.7 = (s16[144,128]{1,0:T(8,128)(2,1)S(1)}, s16[144,128]{1,0:T(8,128)(2,1)S(1)}, u32[]{:S(2)}, u32[]{:S(2)}) collective-permute-start(s16[144,128]{1,0:T(8,128)(2,1)S(1)} %get-tuple-element.42), channel_id=1, source_target_pairs={{0,20},{4,16},{8,28},{12,24},{16,4},{20,0},{24,12},{28,8},{1,21},{... | collective-permute-start | bytes 110600 | tf_op jit(solution)/shard_map/ppermute | solution.py:549
  40.4 2.8 %collective-permute-start.8 = (s16[144,128]{1,0:T(8,128)(2,1)S(1)}, s16[144,128]{1,0:T(8,128)(2,1)S(1)}, u32[]{:S(2)}, u32[]{:S(2)}) collective-permute-start(s16[144,128]{1,0:T(8,128)(2,1)S(1)} %get-tuple-element.43), channel_id=1, source_target_pairs={{0,24},{4,28},{8,16},{12,20},{16,8},{20,12},{24,0},{28,4},{1,25},{... | collective-permute-start | bytes 110600 | tf_op jit(solution)/shard_map/ppermute | solution.py:549
  43.2 1.1 %collective-permute-start.9 = (s16[144,128]{1,0:T(8,128)(2,1)S(1)}, s16[144,128]{1,0:T(8,128)(2,1)S(1)}, u32[]{:S(2)}, u32[]{:S(2)}) collective-permute-start(s16[144,128]{1,0:T(8,128)(2,1)S(1)} %get-tuple-element.44), channel_id=1, source_target_pairs={{0,28},{4,24},{8,20},{12,16},{16,12},{20,8},{24,4},{28,0},{1,29},{... | collective-permute-start | bytes 110600 | tf_op jit(solution)/shard_map/ppermute | solution.py:549
  44.3 1.1 %collective-permute-done.7.refs_5_ = s16[144,128]{1,0:T(8,128)(2,1)S(1)} collective-permute-done((s16[144,128]{1,0:T(8,128)(2,1)S(1)}, s16[144,128]{1,0:T(8,128)(2,1)S(1)}, u32[]{:S(2)}, u32[]{:S(2)}) %collective-permute-start.7) | collective-permute-done | bytes 36896 | tf_op jit(solution)/shard_map/ppermute | solution.py:549
  45.4 1.1 %collective-permute-done.8.refs_6_ = s16[144,128]{1,0:T(8,128)(2,1)S(1)} collective-permute-done((s16[144,128]{1,0:T(8,128)(2,1)S(1)}, s16[144,128]{1,0:T(8,128)(2,1)S(1)}, u32[]{:S(2)}, u32[]{:S(2)}) %collective-permute-start.8) | collective-permute-done | bytes 36896 | tf_op jit(solution)/shard_map/ppermute | solution.py:549
  46.5 3.4 %collective-permute-done.9.refs_7_ = s16[144,128]{1,0:T(8,128)(2,1)S(1)} collective-permute-done((s16[144,128]{1,0:T(8,128)(2,1)S(1)}, s16[144,128]{1,0:T(8,128)(2,1)S(1)}, u32[]{:S(2)}, u32[]{:S(2)}) %collective-permute-start.9) | collective-permute-done | bytes 36896 | tf_op jit(solution)/shard_map/ppermute | solution.py:549
  49.9 1.2 %shard_map.66 = f32[1024,128]{1,0:T(8,128)} custom-call(s16[144,128]{1,0:T(8,128)(2,1)S(1)} %get-tuple-element.37.refs_0_, s16[144,128]{1,0:T(8,128)(2,1)S(1)} %collective-permute-done.3.refs_1_, s16[144,128]{1,0:T(8,128)(2,1)S(1)} %collective-permute-done.4.refs_2_, s16[144,128]{1,0:T(8,128)(2,1)S(1)} %collective-permute-done.5.refs_3_, ...), custom_call_target="tpu_custom_call" | custom-call | tf_op jit(solution)/shard_map/pallas_call | solution.py:440
  (11 shorter events, 0.0 us)
Async XLA Ops:
  1.1 17.7 %copy-start = (s32[1,4,16]{2,1,0:T(4,128)S(1)}, s32[1,4,16]{2,1,0:T(4,128)}, u32[]{:S(2)}) copy-start(s32[1,4,16]{2,1,0:T(4,128)} %match_hbm.1) | copy-start | bytes 772
  1.1 17.7 %copy-start.1 = (s32[128,3]{0,1:T(4,128)S(1)}, s32[128,3]{0,1:T(4,128)}, u32[]{:S(2)}) copy-start(s32[128,3]{0,1:T(4,128)} %param.7) | copy-start | bytes 4612
  1.1 17.7 %copy-start.2 = (f32[32,1024]{1,0:T(8,128)S(1)}, f32[32,1024]{1,0:T(8,128)}, u32[]{:S(2)}) copy-start(f32[32,1024]{1,0:T(8,128)} %constant.8.clone.refs_2_) | copy-start | bytes 393220
  1.1 17.7 %copy-start.3 = (f32[64,512]{1,0:T(8,128)S(1)}, f32[64,512]{1,0:T(8,128)}, u32[]{:S(2)}) copy-start(f32[64,512]{1,0:T(8,128)} %constant.7.clone.refs_1_) | copy-start | bytes 393220
  1.1 17.6 %copy-start.4 = (f32[32,512]{1,0:T(8,128)S(1)}, f32[32,512]{1,0:T(8,128)}, u32[]{:S(2)}) copy-start(f32[32,512]{1,0:T(8,128)} %constant.6.clone.refs_0_) | copy-start | bytes 196612
  17.3 6.4 %collective-permute-start = (bf16[8,128,128]{2,1,0:T(8,128)(2,1)S(1)}, bf16[8,128,128]{2,1,0:T(8,128)(2,1)S(1)}, u32[]{:S(2)}, u32[]{:S(2)}) collective-permute-start(bf16[8,128,128]{2,1,0:T(8,128)(2,1)S(1)} %all_to_all.5.boxes_ref.refs_0_), channel_id=1, source_target_pairs={{0,2},{1,3},{2,0},{3,1},{4,6},{5,7},{6,4},{7,5},{8,10},{9,11},{10,... | collective-permute-start | bytes 786440 | tf_op jit(solution)/shard_map/ppermute | solution.py:384
  22.4 1.6 %collective-permute-start.1 = (bf16[8,128,128]{2,1,0:T(8,128)(2,1)S(1)}, bf16[8,128,128]{2,1,0:T(8,128)(2,1)S(1)}, u32[]{:S(2)}, u32[]{:S(2)}) collective-permute-start(bf16[8,128,128]{2,1,0:T(8,128)(2,1)S(1)} %all_to_all.5.boxes_ref.refs_0_), channel_id=1, source_target_pairs={{0,1},{1,0},{2,3},{3,2},{4,5},{5,4},{6,7},{7,6},{8,9},{9,8},{10,11... | collective-permute-start | bytes 786440 | tf_op jit(solution)/shard_map/ppermute | solution.py:377
  23.6 1.5 %collective-permute-start.2 = (bf16[8,128,128]{2,1,0:T(8,128)(2,1)S(1)}, bf16[8,128,128]{2,1,0:T(8,128)(2,1)S(1)}, u32[]{:S(2)}, u32[]{:S(2)}) collective-permute-start(bf16[8,128,128]{2,1,0:T(8,128)(2,1)S(1)} %collective-permute-done.refs_1_), channel_id=1, source_target_pairs={{0,1},{1,0},{2,3},{3,2},{4,5},{5,4},{6,7},{7,6},{8,9},{9,8},{10,11... | collective-permute-start | bytes 786440 | tf_op jit(solution)/shard_map/ppermute | solution.py:377
  33.1 7.3 %collective-permute-start.3 = (s16[144,128]{1,0:T(8,128)(2,1)S(1)}, s16[144,128]{1,0:T(8,128)(2,1)S(1)}, u32[]{:S(2)}, u32[]{:S(2)}) collective-permute-start(s16[144,128]{1,0:T(8,128)(2,1)S(1)} %get-tuple-element.38), channel_id=1, source_target_pairs={{0,4},{4,0},{8,12},{12,8},{16,20},{20,16},{24,28},{28,24},{1,5},{5... | collective-permute-start | bytes 110600 | tf_op jit(solution)/shard_map/ppermute | solution.py:549
  34.6 8.7 %collective-permute-start.4 = (s16[144,128]{1,0:T(8,128)(2,1)S(1)}, s16[144,128]{1,0:T(8,128)(2,1)S(1)}, u32[]{:S(2)}, u32[]{:S(2)}) collective-permute-start(s16[144,128]{1,0:T(8,128)(2,1)S(1)} %get-tuple-element.39), channel_id=1, source_target_pairs={{0,8},{4,12},{8,0},{12,4},{16,24},{20,28},{24,16},{28,20},{1,9},{5... | collective-permute-start | bytes 110600 | tf_op jit(solution)/shard_map/ppermute | solution.py:549
  34.8 9.5 %collective-permute-start.5 = (s16[144,128]{1,0:T(8,128)(2,1)S(1)}, s16[144,128]{1,0:T(8,128)(2,1)S(1)}, u32[]{:S(2)}, u32[]{:S(2)}) collective-permute-start(s16[144,128]{1,0:T(8,128)(2,1)S(1)} %get-tuple-element.40), channel_id=1, source_target_pairs={{0,12},{4,8},{8,4},{12,0},{16,28},{20,24},{24,20},{28,16},{1,13},{... | collective-permute-start | bytes 110600 | tf_op jit(solution)/shard_map/ppermute | solution.py:549
  36.6 7.7 %collective-permute-start.6 = (s16[144,128]{1,0:T(8,128)(2,1)S(1)}, s16[144,128]{1,0:T(8,128)(2,1)S(1)}, u32[]{:S(2)}, u32[]{:S(2)}) collective-permute-start(s16[144,128]{1,0:T(8,128)(2,1)S(1)} %get-tuple-element.41), channel_id=1, source_target_pairs={{0,16},{4,20},{8,24},{12,28},{16,0},{20,4},{24,8},{28,12},{1,17},{... | collective-permute-start | bytes 110600 | tf_op jit(solution)/shard_map/ppermute | solution.py:549
  38.8 6.6 %collective-permute-start.7 = (s16[144,128]{1,0:T(8,128)(2,1)S(1)}, s16[144,128]{1,0:T(8,128)(2,1)S(1)}, u32[]{:S(2)}, u32[]{:S(2)}) collective-permute-start(s16[144,128]{1,0:T(8,128)(2,1)S(1)} %get-tuple-element.42), channel_id=1, source_target_pairs={{0,20},{4,16},{8,28},{12,24},{16,4},{20,0},{24,12},{28,8},{1,21},{... | collective-permute-start | bytes 110600 | tf_op jit(solution)/shard_map/ppermute | solution.py:549
  40.4 6.1 %collective-permute-start.8 = (s16[144,128]{1,0:T(8,128)(2,1)S(1)}, s16[144,128]{1,0:T(8,128)(2,1)S(1)}, u32[]{:S(2)}, u32[]{:S(2)}) collective-permute-start(s16[144,128]{1,0:T(8,128)(2,1)S(1)} %get-tuple-element.43), channel_id=1, source_target_pairs={{0,24},{4,28},{8,16},{12,20},{16,8},{20,12},{24,0},{28,4},{1,25},{... | collective-permute-start | bytes 110600 | tf_op jit(solution)/shard_map/ppermute | solution.py:549
  43.2 6.7 %collective-permute-start.9 = (s16[144,128]{1,0:T(8,128)(2,1)S(1)}, s16[144,128]{1,0:T(8,128)(2,1)S(1)}, u32[]{:S(2)}, u32[]{:S(2)}) collective-permute-start(s16[144,128]{1,0:T(8,128)(2,1)S(1)} %get-tuple-element.44), channel_id=1, source_target_pairs={{0,28},{4,24},{8,20},{12,16},{16,12},{20,8},{24,4},{28,0},{1,29},{... | collective-permute-start | bytes 110600 | tf_op jit(solution)/shard_map/ppermute | solution.py:549
